TPU v7x, 256 devices: a whole 4x4x8 slice. The times are simulated.
256 devices in a mesh: dp: 64 (over y_lo, z, x), mp: 4 (over y_hi, core).
Axes of the slice: x: 4, y: 4 (y_hi: 2, y_lo: 2; y = y_hi * 2 + y_lo), z: 8, core: 2. Of those that a mesh axis runs over, the one named last changes fastest.
Arguments:
- tokens: bfloat16 [8192, 3584], P('dp', 'mp'), may hold values from -6 to 6
- routes: int32 [8192, 2], P('dp'), may hold values from 0 to 63, all different within a row; in each aligned block of 128 rows (0 to 127, 128 to 255, ...) at most 5 rows name the same one
- expert_gate_affinity: float32 [8192, 2], P('dp'), may hold values from 0.05 to 1
- expert_gate_weight: bfloat16 [64, 3584, 2048], P('dp', None, 'mp'), may hold values from -0.09375 to 0.09375
- expert_up_weight: bfloat16 [64, 3584, 2048], P('dp', None, 'mp'), may hold values from -0.09375 to 0.09375
- expert_down_weight: bfloat16 [64, 2048, 3584], P('dp', 'mp'), may hold values from -0.125 to 0.125
- proj: bfloat16 [3584, 5120], P('dp', 'mp'), may hold values from -0.09375 to 0.09375
- student_hidden_input: bfloat16 [8192, 5120], P('dp', 'mp'), may hold values from -6 to 6
- student_norm_weight: bfloat16 [5120], P('mp'), may hold values from 0.25 to 1.75
- adapter_down_matrix: bfloat16 [5120, 64], P('mp'), may hold values from -0.078125 to 0.078125
- adapter_up_matrix: bfloat16 [64, 5120], P(None, 'mp'), may hold values from -0.75 to 0.75
Outputs:
- target: float32 [8192, 5120], P('dp', 'mp')
- grad_a: float32 [5120, 64], P('mp')
- up_matrix_gradient: float32 [64, 5120], P(None, 'mp')
- loss: float32 [], replicated
Inputs may be any that keep to these rules, and one draw needn't show every extreme that they name: `routes`: each row names 2 different experts; within the 128 rows of one index of dp no expert is named more than 5 times, and in every draw some index of dp names some expert exactly 5 times.
All inputs are finite; a program needn't handle non-finite values.
Results may differ from a plain program's by a relative error of at most 0.018.
Values may be sent and summed in bfloat16 or wider, within the bound.
No kernel may reach another device: no remote copies, remote signals or barrier semaphores. Data moves between devices by JAX's collectives and lax.ppermute only.
A program may use at most 128 MiB of HBM per device.

v0:
```python
import math

import jax
import jax.numpy as jnp
from jax import lax
from jax.sharding import PartitionSpec as P

route_scale = 2.5
adapter_scale_factor = 0.25


def body(
    tokens,
    routes,
    expert_gate_affinity,
    expert_gate_weight,
    expert_up_weight,
    expert_down_weight,
    proj,
    student_hidden_input,
    student_norm_weight,
    adapter_down_matrix,
    adapter_up_matrix,
):
    experts = lax.axis_size("dp")
    mp_count = lax.axis_size("mp")
    tok_rows = tokens.shape[0]
    part_width = tokens.shape[1]
    topk_count = routes.shape[1]
    assigned = tok_rows * topk_count
    capacity = min(tok_rows, 5 * assigned // (4 * experts))
    slot_count = experts * capacity
    flat_routes = routes.reshape(assigned)
    onehot_e = (flat_routes[:, None] == jnp.arange(experts, dtype=jnp.int32)[None, :]).astype(
        jnp.int32
    )
    position = jnp.sum((jnp.cumsum(onehot_e, axis=0) - onehot_e) * onehot_e, axis=1)
    slot_index = flat_routes * capacity + position
    slot_hit = (jnp.arange(slot_count, dtype=jnp.int32)[:, None] == slot_index[None, :]).astype(
        jnp.bfloat16
    )
    token_hit = (
        jnp.arange(assigned, dtype=jnp.int32)[:, None] // topk_count
        == jnp.arange(tok_rows, dtype=jnp.int32)[None, :]
    ).astype(jnp.bfloat16)
    placing = jnp.dot(slot_hit, token_hit, preferred_element_type=jnp.float32).astype(jnp.bfloat16)
    outgoing = jnp.dot(placing, tokens, preferred_element_type=jnp.float32).astype(jnp.bfloat16)
    arrived = lax.all_to_all(
        outgoing.reshape(experts, capacity, part_width),
        "dp",
        split_axis=0,
        concat_axis=0,
        tiled=True,
    )
    slot_rows = lax.all_gather(arrived.reshape(slot_count, part_width), "mp", axis=1, tiled=True)
    gate_proj = jnp.dot(slot_rows, expert_gate_weight[0], preferred_element_type=jnp.float32)
    up_proj = jnp.dot(slot_rows, expert_up_weight[0], preferred_element_type=jnp.float32)
    hidden = (jax.nn.silu(gate_proj) * up_proj).astype(jnp.bfloat16)
    columns = expert_down_weight[0]
    expert_out = lax.psum_scatter(
        lax.dot_general(
            columns, hidden, (((0,), (1,)), ((), ())), preferred_element_type=jnp.float32
        ).astype(jnp.bfloat16),
        "mp",
        scatter_dimension=0,
        tiled=True,
    )
    returned = lax.all_to_all(
        expert_out.reshape(part_width, experts, capacity),
        "dp",
        split_axis=1,
        concat_axis=1,
        tiled=True,
    )
    returned = returned.reshape(part_width, slot_count)
    weights = (
        route_scale * expert_gate_affinity / jnp.sum(expert_gate_affinity, axis=-1, keepdims=True)
    )
    weights_flat = weights.reshape(assigned)
    combine = jnp.dot(
        slot_hit.astype(jnp.float32) * weights_flat[None, :],
        token_hit.astype(jnp.float32),
        precision=lax.Precision.HIGHEST,
    )
    teacher_cols = jnp.dot(
        returned.astype(jnp.float32), combine, precision=lax.Precision.HIGHEST
    ).astype(jnp.bfloat16)
    teacher_full = lax.all_gather(teacher_cols, "mp", axis=0, tiled=True)
    target = lax.dot_general(
        teacher_full,
        lax.all_gather(proj, "dp", axis=0, tiled=True),
        (((0,), (0,)), ((), ())),
        preferred_element_type=jnp.float32,
    )
    tokens_all = tok_rows * experts
    student_width = student_hidden_input.shape[1] * mp_count
    student_full_width = student_hidden_input.astype(jnp.float32)
    square_sum = lax.psum(jnp.sum(student_full_width * student_full_width, axis=-1), "mp")
    mean_sq = square_sum / student_width
    normalized_states = (
        student_full_width
        * lax.rsqrt(mean_sq[:, None] + 1e-06)
        * student_norm_weight.astype(jnp.float32)
    ).astype(jnp.bfloat16)
    lowrank_piece = jnp.dot(
        normalized_states, adapter_down_matrix, preferred_element_type=jnp.float32
    )
    lowrank_product = lax.psum(lowrank_piece.astype(jnp.bfloat16), "mp")
    output_change = jnp.dot(lowrank_product, adapter_up_matrix, preferred_element_type=jnp.float32)
    output_difference = student_full_width + adapter_scale_factor * output_change - target
    scaled_states = (output_difference * (1.0 / math.sqrt(tokens_all))).astype(jnp.bfloat16)
    local_up_gradient = adapter_scale_factor * jnp.dot(
        lowrank_product.T, scaled_states, preferred_element_type=jnp.float32
    )
    backward_piece = jnp.dot(scaled_states, adapter_up_matrix.T, preferred_element_type=jnp.float32)
    backward_lowrank = (
        adapter_scale_factor
        * lax.psum(backward_piece.astype(jnp.bfloat16), "mp").astype(jnp.float32)
    ).astype(jnp.bfloat16)
    local_grad_a = jnp.dot(
        normalized_states.T, backward_lowrank, preferred_element_type=jnp.float32
    )
    grad_a, up_matrix_gradient = lax.psum((local_grad_a, local_up_gradient), "dp")
    loss_total = lax.psum(jnp.sum(output_difference * output_difference), ("dp", "mp"))
    loss = loss_total / (tokens_all * student_width)
    return (target, grad_a, up_matrix_gradient, loss)


def solution(mesh):
    placed = (
        P("dp", "mp"),
        P("dp", None),
        P("dp", None),
        P("dp", None, "mp"),
        P("dp", None, "mp"),
        P("dp", "mp", None),
        P("dp", "mp"),
        P("dp", "mp"),
        P("mp"),
        P("mp", None),
        P(None, "mp"),
    )
    return jax.shard_map(
        body,
        mesh=mesh,
        in_specs=placed,
        out_specs=(P("dp", "mp"), P("mp", None), P(None, "mp"), P()),
        check_vma=False,
    )
```

profile of v0, /device:TPU:32, one launch (start us, length us, event | category | flops | bytes accessed | tf_op | source)
XLA Modules:
  0.0 1012.2 jit_solution(14878872833809751521)
XLA Ops:
  8.0 0.0 copy-start
  8.0 0.0 all-gather.3.cloned.1.call-start
  8.1 0.8 copy.19
  8.9 0.1 eq.59
  9.0 0.1 reshape.91
  9.2 0.6 reduce-window.6
  9.8 0.2 slice_reduce_fusion
  10.0 0.1 fusion.34
  10.2 0.0 copy-done
  10.2 0.5 convolution_convert_fusion.1
  10.7 0.2 reshape.93
  11.0 38.6 %all_to_all.10 = bf16[64,5,896]{2,1,0:T(8,128)(2,1)S(1)} all-to-all(bf16[64,5,896]{2,1,0:T(8,128)(2,1)S(1)} %reshape.93), channel_id=1, replica_groups=mesh['dp'=64,'mp'=4] {'dp'}, dimensions={0} | all-to-all | bytes 1146880 | tf_op jit(solution)/shard_map/all_to_all | solution.py:48
  49.5 1.0 reshape.94
  50.6 0.0 all-gather.3.cloned.1.call-update
  50.6 0.0 reduce-scatter.4.cloned.1.call-start
  50.7 26.9 %all-gather.3.cloned.1.call-done = bf16[320,3584]{1,0:T(8,128)(2,1)} async-done(((bf16[320,896]{1,0:T(8,128)(2,1)}), bf16[320,3584]{1,0:T(8,128)(2,1)}) %all-gather.3.cloned.1.call-update) | async-done | bytes 2293776 | tf_op jit(solution)/shard_map/all_gather | solution.py:55
  77.6 4.1 fusion.4
  81.7 6.5 fusion
  88.1 2.7 copy.23
  90.8 0.0 copy-start.5
  90.8 0.0 copy-start.4
  90.8 0.0 copy-start.1
  90.8 0.0 copy-start.6
  90.9 0.0 reduce-scatter.4.cloned.1.call-update
  90.9 0.0 all-gather.5.cloned.1.call-start
  90.9 0.5 all-gather.5.cloned.1.call-update
  91.5 46.6 %reduce-scatter.4.cloned.1.call-done = bf16[896,320]{1,0:T(8,128)(2,1)} async-done(((bf16[3584,320]{1,0:T(8,128)(2,1)}), bf16[896,320]{1,0:T(8,128)(2,1)}) %reduce-scatter.4.cloned.1.call-update) | async-done | bytes 573456
  138.0 1.4 copy.24
  139.4 1.1 reshape.95
  140.6 16.2 %all-to-all-start.1 = ((bf16[896,64,5]{0,2,1:T(8,128)(2,1)}), bf16[896,64,5]{0,2,1:T(8,128)(2,1)S(1)}, u32[]{:S(2)}, u32[]{:S(2)}) async-start(bf16[896,64,5]{0,2,1:T(8,128)(2,1)} %reshape.95), calls=%async_computation.1 | async-start | bytes 1835008 | tf_op jit(solution)/shard_map/all_to_all | solution.py:68
  156.8 0.0 all-reduce.3.cloned.1.call-start
  156.9 0.0 copy-done.5
  156.9 0.1 copy.22
  157.0 0.1 mul.89
  157.2 0.0 copy-done.4
  157.2 0.0 copy-done.1
  157.2 0.1 fusion.14
  157.3 8.6 psum.42
  166.0 0.0 copy-done.6
  166.0 0.3 convolution_convert_fusion.5
  166.3 14.1 %psum.43 = bf16[128,64]{0,1:T(8,128)(2,1)S(1)} all-reduce(bf16[128,64]{0,1:T(8,128)(2,1)S(1)} %convolution_convert_fusion.5), channel_id=1, replica_groups=mesh['dp'=64,'mp'=4] {'mp'}, use_global_device_ids=true, to_apply=%region_7.8 | all-reduce | flops 8192 | bytes 32768 | tf_op jit(solution)/shard_map/psum | solution.py:108
  180.4 0.4 fusion.19
  180.7 6.0 all-to-all-done.1
  186.7 0.2 reshape.96
  187.0 0.9 convolution_convert_fusion.2
  187.9 9.1 all_gather.10
  197.0 0.0 copy-start.3
  197.0 211.8 %all-gather.5.cloned.1.call-done = bf16[3584,1280]{1,0:T(8,128)(2,1)} async-done(((bf16[56,1280]{1,0:T(8,128)(2,1)}), bf16[3584,1280]{1,0:T(8,128)(2,1)}) %all-gather.5.cloned.1.call-update) | async-done | bytes 9175056 | tf_op jit(solution)/shard_map/all_gather | solution.py:91
  408.7 5.0 fusion.44
  413.8 0.0 copy-done.3
  413.8 0.0 copy-start.2
  413.8 1.0 multiply_reduce_fusion
  414.7 0.9 convolution_multiply_fusion.1
  415.7 0.2 convolution_convert_fusion.4
  415.9 13.1 %psum.44 = bf16[128,64]{0,1:T(8,128)(2,1)S(1)} all-reduce(bf16[128,64]{0,1:T(8,128)(2,1)S(1)} %convolution_convert_fusion.4), channel_id=1, replica_groups=mesh['dp'=64,'mp'=4] {'mp'}, use_global_device_ids=true, to_apply=%region_8.9 | all-reduce | flops 8192 | bytes 32768 | tf_op jit(solution)/shard_map/psum | solution.py:118
  429.0 1.0 fusion.29
  430.0 0.0 all-reduce.3.cloned.1.call-update
  430.1 80.6 %psum.47 = f32[]{:T(128)} all-reduce(f32[]{:T(128)} %get-tuple-element.6), channel_id=1, replica_groups=mesh['dp'=64,'mp'=4] {'dp','mp'}, use_global_device_ids=true, to_apply=%region_12.13 | all-reduce | flops 1 | bytes 8 | tf_op jit(solution)/shard_map/psum | solution.py:124
  511.3 488.9 %all-reduce.3.cloned.1.call-done = (f32[1280,64]{0,1:T(8,128)}, f32[64,1280]{1,0:T(8,128)}) async-done(((f32[1280,64]{0,1:T(8,128)}, f32[64,1280]{1,0:T(8,128)}), (f32[1280,64]{0,1:T(8,128)}, f32[64,1280]{1,0:T(8,128)})) %all-reduce.3.cloned.1.call-update) | async-done | bytes 655376 | tf_op jit(solution)/shard_map/psum | solution.py:123
  1000.2 1.7 copy.29
  1002.0 1.7 copy.30
  1003.7 0.0 copy-done.2
  (8 shorter events, 0.1 us)
Async XLA Ops:
  8.0 2.2 copy-start
  8.0 69.6 %all-gather.3.cloned.1.call-start = ((), (), s32[]{:S(2)}) async-start(), calls=%async_computation.3 | async-start | bytes 2867200 | tf_op jit(solution)/shard_map/all_gather | solution.py:55
  50.6 87.4 %reduce-scatter.4.cloned.1.call-start = ((), (), s32[]{:S(2)}) async-start(), calls=%async_computation.5 | async-start | bytes 3440640
  90.8 66.0 %copy-start.5 = (f32[128,2]{0,1:T(2,128)S(1)}, f32[128,2]{0,1:T(2,128)}, u32[]{:S(2)}) copy-start(f32[128,2]{0,1:T(2,128)} %param.13) | copy-start | bytes 3076
  90.8 66.3 %copy-start.4 = (bf16[1280]{0:T(1024)(128)(2,1)S(1)}, bf16[1280]{0:T(1024)(128)(2,1)}, u32[]{:S(2)}) copy-start(bf16[1280]{0:T(1024)(128)(2,1)} %param.19) | copy-start | bytes 7684
  90.8 66.3 %copy-start.1 = (bf16[128,1280]{1,0:T(8,128)(2,1)S(1)}, bf16[128,1280]{1,0:T(8,128)(2,1)}, u32[]{:S(2)}) copy-start(bf16[128,1280]{1,0:T(8,128)(2,1)} %param.18) | copy-start | bytes 983044
  90.8 75.2 %copy-start.6 = (bf16[1280,64]{0,1:T(8,128)(2,1)S(1)}, bf16[1280,64]{0,1:T(8,128)(2,1)}, u32[]{:S(2)}) copy-start(bf16[1280,64]{0,1:T(8,128)(2,1)} %param.20) | copy-start | bytes 491524
  90.9 317.8 %all-gather.5.cloned.1.call-start = ((), (), s32[]{:S(2)}) async-start(), calls=%async_computation.4 | async-start | bytes 9318400 | tf_op jit(solution)/shard_map/all_gather | solution.py:91
  140.6 46.1 %all-to-all-start.1 = ((bf16[896,64,5]{0,2,1:T(8,128)(2,1)}), bf16[896,64,5]{0,2,1:T(8,128)(2,1)S(1)}, u32[]{:S(2)}, u32[]{:S(2)}) async-start(bf16[896,64,5]{0,2,1:T(8,128)(2,1)} %reshape.95), calls=%async_computation.1 | async-start | bytes 1835008 | tf_op jit(solution)/shard_map/all_to_all | solution.py:68
  156.8 843.4 %all-reduce.3.cloned.1.call-start = ((), (), s32[]{:S(2)}) async-start(), calls=%async_computation.6 | async-start | bytes 1310720 | tf_op jit(solution)/shard_map/psum | solution.py:123
  197.0 216.8 %copy-start.3 = (bf16[64,1280]{1,0:T(8,128)(2,1)S(1)}, bf16[64,1280]{1,0:T(8,128)(2,1)}, u32[]{:S(2)}) copy-start(bf16[64,1280]{1,0:T(8,128)(2,1)} %param.21) | copy-start | bytes 491524
  413.8 589.9 %copy-start.2 = (f32[128,1280]{1,0:T(8,128)}, f32[128,1280]{1,0:T(8,128)S(1)}, u32[]{:S(2)}) copy-start(f32[128,1280]{1,0:T(8,128)S(1)} %fusion.44) | copy-start | bytes 1966084
Sparse Core Ops, SparseCore 0:
  50.7 26.8 all-gather.2
  91.0 46.9 reduce-scatter.3
Sparse Core Ops, SparseCore 1:
  93.3 315.4 all-gather.4
  430.1 570.0 all-reduce.2
where the time goes:
time: 1020 us; the launch traced here: 1010 us
  waiting for transfers between devices  781 us (77%)
  blocking collectives  164 us (16%)
  matrix products  20.8 us (2%)
  between operations  17.4 us (2%)
  starting transfers between devices  16.4 us (2%)
  local copies, waits for them, and re-layouts  11.8 us (1%)
    psum x1, waiting for transfers between devices, body(): lax.psum((local_grad_a, local_up_gradient), 'dp')  489 us
    all_gather x1, waiting for transfers between devices, body(): lax.all_gather(proj, 'dp', axis=0, tiled=True)  212 us
    psum x1, blocking collectives, body(): lax.psum(jnp.sum(output_difference * output_difference), ('dp', 'mp'))  80.6 us
    unnamed x5, waiting for transfers between devices  47.1 us
    all_to_all x1, blocking collectives, body(): lax.all_to_all(outgoing.reshape(experts, capacity, part_width), 'dp', spl...  38.6 us
    all_gather x1, waiting for transfers between devices, body(): lax.all_gather(arrived.reshape(slot_count, part_width), 'mp', axis=1, til...  26.9 us
  transfers between devices with their start and end apart: 5, of which 5 were waited for; matrix products, arithmetic and copies ran while one was open for 0% of the time, Pallas kernels for 0%

commit v1 on v0

v1 whole, which is shorter than its diff:
```python
import math

import jax
import jax.numpy as jnp
from jax import lax
from jax.sharding import Mesh, PartitionSpec as P

route_scale = 2.5
adapter_scale_factor = 0.25
DP = ("yl", "z", "x")
MP = ("yh", "c")
ALL = DP + MP
SIZES = (2, 8, 4, 2, 2)


def index_of(yl, z, x, yh, c):
    return (((yl * 8 + z) * 4 + x) * 2 + yh) * 2 + c


def coords():
    for yl in range(2):
        for z in range(8):
            for x in range(4):
                for yh in range(2):
                    for c in range(2):
                        yield yl, z, x, yh, c


def proj_perm():
    pairs = []
    for yl, z, x, yh, c in coords():
        d, m = (yl * 8 + z) * 4 + x, yh * 2 + c
        owner, place = d // 16, d % 16
        pairs.append(
            (index_of(yl, z, x, yh, c), index_of(place // 8, place % 8, m, owner // 2, owner % 2))
        )
    return pairs


def home_perm(step):
    pairs = []
    for yl, z, x, yh, c in coords():
        m = yh * 2 + c
        pairs.append(
            (index_of(yl, z, x, yh, c), index_of(yl, z, (x + m + step) % 4, x // 2, x % 2))
        )
    return pairs


def swap(value, axis):
    return lax.ppermute(value, axis, [(0, 1), (1, 0)])


def mp_sum(value):
    value = value + swap(value, "c")
    return value + swap(value, "yh")


def dot(a, b):
    return jnp.dot(a, b, preferred_element_type=jnp.float32)


def exchange_slots(rows):
    count, width = rows.shape
    rows = rows.reshape(64, count * width // (64 * 128), 128)
    return lax.all_to_all(rows, DP, split_axis=0, concat_axis=0, tiled=True).reshape(count, width)


def split_two(value):
    high = lax.reduce_precision(value, 8, 7)
    return high.astype(jnp.bfloat16), (value - high).astype(jnp.bfloat16)


def body(
    tokens,
    routes,
    expert_gate_affinity,
    expert_gate_weight,
    expert_up_weight,
    expert_down_weight,
    proj,
    student_hidden_input,
    student_norm_weight,
    adapter_down_matrix,
    adapter_up_matrix,
):
    experts = 64
    mp_count = 4
    tok_rows, part_width = tokens.shape
    topk_count = routes.shape[1]
    assigned = tok_rows * topk_count
    capacity = 5
    slot_count = experts * capacity
    rank = adapter_up_matrix.shape[0]
    xi, yh, core = lax.axis_index("x"), lax.axis_index("yh"), lax.axis_index("c")
    mi = yh * 2 + core

    flat_routes = routes.reshape(assigned)
    onehot_e = (flat_routes[:, None] == jnp.arange(experts, dtype=jnp.int32)[None, :]).astype(
        jnp.int32
    )
    position = jnp.sum((jnp.cumsum(onehot_e, axis=0) - onehot_e) * onehot_e, axis=1)
    slot_index = flat_routes * capacity + position
    slot_hit = (jnp.arange(slot_count, dtype=jnp.int32)[:, None] == slot_index[None, :]).astype(
        jnp.bfloat16
    )
    token_hit = (
        jnp.arange(assigned, dtype=jnp.int32)[:, None] // topk_count
        == jnp.arange(tok_rows, dtype=jnp.int32)[None, :]
    ).astype(jnp.bfloat16)
    placing = dot(slot_hit, token_hit).astype(jnp.bfloat16)
    outgoing = dot(placing, tokens).astype(jnp.bfloat16)
    arrived = exchange_slots(outgoing)

    student = student_hidden_input.astype(jnp.float32)
    gain = student_norm_weight.astype(jnp.float32)
    student_width = student.shape[1] * mp_count
    square_sum = jnp.sum(student * student, axis=-1, keepdims=True)
    low_part = dot((student * gain).astype(jnp.bfloat16), adapter_down_matrix)
    proj_low = lax.dot_general(
        proj, adapter_up_matrix, (((1,), (1,)), ((), ())), preferred_element_type=jnp.float32
    )
    stats = jnp.concatenate(
        [low_part, jnp.broadcast_to(square_sum, (tok_rows, rank))], axis=1
    )
    shared = mp_sum(
        jnp.concatenate([stats, jnp.concatenate([proj_low, jnp.zeros_like(proj_low)], axis=1)])
    )
    stats, proj_low = shared[:tok_rows], shared[tok_rows:, :rank]
    inverse = lax.rsqrt(stats[:, rank : rank + 1] / student_width + 1e-06)
    lowrank = (stats[:, :rank] * inverse).astype(jnp.bfloat16)
    normed = (student * inverse * gain).astype(jnp.bfloat16)
    student_out = student + adapter_scale_factor * dot(lowrank, adapter_up_matrix)
    student_back = mp_sum(
        lax.dot_general(
            student_out,
            adapter_up_matrix.astype(jnp.float32),
            (((1,), (1,)), ((), ())),
            precision=lax.Precision.HIGHEST,
        )
    )

    proj_block = lax.all_gather(
        lax.ppermute(jnp.concatenate([proj, *split_two(proj_low)], axis=1), ALL, proj_perm()),
        ("yl", "z"),
        axis=0,
        tiled=True,
    )
    arrived, lowrank = lax.optimization_barrier((arrived, lowrank))

    arrived_y = swap(arrived, "yh")
    arrived_c = swap(arrived, "c")
    arrived_yc = swap(arrived_y, "c")
    parts = (
        (arrived, mi),
        (arrived_c, yh * 2 + 1 - core),
        (arrived_y, (1 - yh) * 2 + core),
        (arrived_yc, (1 - yh) * 2 + 1 - core),
    )
    gate_proj = up_proj = 0.0
    for rows, place in parts:
        gate_proj = gate_proj + dot(
            rows, lax.dynamic_slice_in_dim(expert_gate_weight[0], place * part_width, part_width, 0)
        )
        up_proj = up_proj + dot(
            rows, lax.dynamic_slice_in_dim(expert_up_weight[0], place * part_width, part_width, 0)
        )
    hidden = (jax.nn.silu(gate_proj) * up_proj).astype(jnp.bfloat16)

    def out_part(place):
        return dot(
            hidden, lax.dynamic_slice_in_dim(expert_down_weight[0], place * part_width, part_width, 1)
        )

    far = swap(out_part((1 - yh) * 2 + 1 - core).astype(jnp.bfloat16), "c")
    near = swap(out_part(yh * 2 + 1 - core).astype(jnp.bfloat16), "c")
    far = out_part((1 - yh) * 2 + core).astype(jnp.bfloat16).astype(jnp.float32) + far.astype(
        jnp.float32
    )
    far = swap(far.astype(jnp.bfloat16), "yh")
    expert_out = (
        out_part(mi).astype(jnp.bfloat16).astype(jnp.float32)
        + near.astype(jnp.float32)
        + far.astype(jnp.float32)
    ).astype(jnp.bfloat16)
    returned, student_back = lax.optimization_barrier((exchange_slots(expert_out), student_back))

    weights = (
        route_scale * expert_gate_affinity / jnp.sum(expert_gate_affinity, axis=-1, keepdims=True)
    )
    combine = jnp.dot(
        slot_hit.astype(jnp.float32) * weights.reshape(assigned)[None, :],
        token_hit.astype(jnp.float32),
        precision=lax.Precision.HIGHEST,
    )
    teacher = lax.dot_general(
        combine,
        returned.astype(jnp.float32),
        (((0,), (0,)), ((), ())),
        precision=lax.Precision.HIGHEST,
    ).astype(jnp.bfloat16)

    teacher_rows = lax.all_gather(teacher, "x", axis=0, tiled=True)
    product = dot(teacher_rows, proj_block)
    columns = adapter_up_matrix.shape[1]
    low = product[:, columns : columns + rank] + product[:, columns + rank :]
    product = jnp.concatenate(
        [product[:, :columns].astype(jnp.bfloat16), *split_two(low)], axis=1
    )
    total = 0.0
    for step in range(mp_count):
        block = lax.rem(xi + mi + step, 4)
        piece = lax.dynamic_slice_in_dim(product, block * tok_rows, tok_rows, 0)
        total = total + lax.ppermute(piece, ALL, home_perm(step)).astype(jnp.float32)
    target = total[:, :columns]

    output_difference = student_out - target
    tokens_all = tok_rows * experts
    scale = 1.0 / math.sqrt(tokens_all)
    scaled = (output_difference * scale).astype(jnp.bfloat16)
    loss_here = jnp.sum(output_difference * output_difference)
    teacher_back = total[:, columns : columns + rank] + total[:, columns + rank :]
    back_low = (adapter_scale_factor * scale * (student_back - teacher_back)).astype(jnp.bfloat16)
    over_tokens = (((0,), (0,)), ((), ()))
    up_part = adapter_scale_factor * lax.dot_general(
        lowrank, scaled, over_tokens, preferred_element_type=jnp.float32
    )
    down_part = lax.dot_general(back_low, normed, over_tokens, preferred_element_type=jnp.float32)

    lanes = 128
    blocks = columns // lanes
    first = lax.reduce_precision(loss_here, 8, 7)
    second = lax.reduce_precision(loss_here - first, 8, 7)
    third = loss_here - first - second
    lane = jnp.arange(lanes)
    loss_row = jnp.where(
        lane == 0, first, jnp.where(lane == 1, second, jnp.where(lane == 2, third, 0.0))
    )
    bundle = jnp.concatenate(
        [
            up_part.reshape(rank, blocks, lanes),
            down_part.reshape(rank, blocks, lanes),
            jnp.broadcast_to(loss_row, (rank, 1, lanes)),
        ],
        axis=1,
    ).astype(jnp.bfloat16)
    bundle = lax.all_to_all(bundle, DP, split_axis=0, concat_axis=0, tiled=True)
    summed = jnp.sum(bundle.astype(jnp.float32), axis=0)
    loss_row = summed[2 * blocks :]
    cross = [(i, 3 - i) for i in range(4)]
    loss_row = (loss_row + swap(loss_row, "c")) + (
        swap(loss_row, "yh") + lax.ppermute(loss_row, MP, cross)
    )
    loss = jnp.sum(loss_row) / (tokens_all * student_width)
    grads = jnp.broadcast_to(
        summed[: 2 * blocks].astype(jnp.bfloat16), (rank, 2 * blocks, lanes)
    )
    grads = lax.all_to_all(grads, DP, split_axis=0, concat_axis=0, tiled=True).astype(jnp.float32)
    up_matrix_gradient = grads[:, :blocks].reshape(rank, columns)
    grad_a = grads[:, blocks:].reshape(rank, columns).T
    return (target, grad_a, up_matrix_gradient, loss)


def solution(mesh):
    fine = Mesh(mesh.devices.reshape(SIZES), ALL)
    placed = (
        P(DP, MP),
        P(DP, None),
        P(DP, None),
        P(DP, None, MP),
        P(DP, None, MP),
        P(DP, MP, None),
        P(DP, MP),
        P(DP, MP),
        P(MP),
        P(MP, None),
        P(None, MP),
    )
    return jax.shard_map(
        body,
        mesh=fine,
        in_specs=placed,
        out_specs=(P(DP, MP), P(MP, None), P(None, MP), P()),
        check_vma=False,
    )
```

time: 1020 us -> 242 us (0.24)
  waiting for transfers between devices: 781 us -> 73.2 us
  blocking collectives: 164 us -> 40.3 us
  starting transfers between devices: 16.4 us -> 72.5 us
    psum x1 -> x0, waiting for transfers between devices: 489 us -> none  [body(): lax.psum((local_grad_a, local_up_gradient), 'dp')]
    all_gather x2 -> x1, waiting for transfers between devices: 239 us -> 0.01 us  [body(): lax.all_gather(lax.ppermute(jnp.concatenate([proj, *split_two(proj_low)],...]
    psum x4 -> x0, blocking collectives: 116 us -> none  [the longest x1 80.6 us: body(): lax.psum(jnp.sum(output_difference * output_difference), ('dp', 'mp'))]
    unnamed x5 -> x1, waiting for transfers between devices: 47.1 us -> 0.02 us
    ppermute x0 -> x18, waiting for transfers between devices: none -> 45.3 us  [the longest x12 36.1 us: swap(): return lax.ppermute(value, axis, [(0, 1), (1, 0)])]
    ppermute x0 -> x18, starting transfers between devices: none -> 35.9 us  [the longest x4 14.8 us: body(): lax.ppermute(piece, ALL, home_perm(step)).astype(jnp.float32)]
    all_to_all x1 -> x3, waiting for transfers between devices: 5.96 us -> 27.9 us  [the longest x2 18.4 us: exchange_slots(): lax.all_to_all(rows, DP, split_axis=0, concat_axis=0, tiled=True)]
    all_to_all x1 -> x3, starting transfers between devices: 16.2 us -> 36.6 us  [the longest x2 30.8 us: exchange_slots(): lax.all_to_all(rows, DP, split_axis=0, concat_axis=0, tiled=True)]
  transfers between devices with their start and end apart: 5 -> 22, of which waited for: 5 -> 15; matrix products, arithmetic and copies ran while one was open for 0% -> 7% of each run, Pallas kernels for 0% -> 0%
where the time goes in v1:
time: 242 us
  waiting for transfers between devices  73.2 us (30%)
  starting transfers between devices  72.5 us (30%)
  blocking collectives  40.3 us (17%)
  between operations  20.1 us (8%)
  matrix products  16.5 us (7%)
  local copies, waits for them, and re-layouts  14.2 us (6%)
  other arithmetic  4.89 us (2%)
    ppermute x12, waiting for transfers between devices, swap(): return lax.ppermute(value, axis, [(0, 1), (1, 0)])  36.1 us
    all_to_all x2, starting transfers between devices, exchange_slots(): lax.all_to_all(rows, DP, split_axis=0, concat_axis=0, tiled=True)  30.8 us
    all_to_all x1, blocking collectives, body(): bundle = lax.all_to_all(bundle, DP, split_axis=0, concat_axis=0, tiled=True)  25.9 us
    all_to_all x2, waiting for transfers between devices, exchange_slots(): lax.all_to_all(rows, DP, split_axis=0, concat_axis=0, tiled=True)  18.4 us
    ppermute x4, starting transfers between devices, body(): lax.ppermute(piece, ALL, home_perm(step)).astype(jnp.float32)  14.8 us
    all_gather x1, blocking collectives, body(): teacher_rows = lax.all_gather(teacher, 'x', axis=0, tiled=True)  14.4 us
    dot_general x16, matrix products, dot(): return jnp.dot(a, b, preferred_element_type=jnp.float32)  14.4 us
    ppermute x12, starting transfers between devices, swap(): return lax.ppermute(value, axis, [(0, 1), (1, 0)])  12.1 us
  transfers between devices with their start and end apart: 22, of which 15 were waited for; matrix products, arithmetic and copies ran while one was open for 7% of the time, Pallas kernels for 0%

profile of v1, /device:TPU:32, one launch (start us, length us, event | category | flops | bytes accessed | tf_op | source)
XLA Modules:
  0.0 241.6 jit_solution(3430422727752176032)
XLA Ops:
  7.2 0.9 copy.36
  8.4 0.6 reduce-window.6
  9.4 0.6 convolution_convert_fusion.5
  9.9 1.4 reshape.117
  11.4 12.6 %all-to-all-start = ((bf16[64,35,128]{2,1,0:T(8,128)(2,1)}), bf16[64,35,128]{2,1,0:T(8,128)(2,1)S(1)}, u32[]{:S(2)}, u32[]{:S(2)}) async-start(bf16[64,35,128]{2,1,0:T(8,128)(2,1)} %reshape.117), calls=%async_computation | async-start | bytes 1310720 | tf_op jit(solution)/shard_map/all_to_all | solution.py:66
  25.0 1.3 collective-permute-done
  26.3 3.0 %collective-permute-start.1 = (f32[184,128]{1,0:T(8,128)S(1)}, f32[184,128]{1,0:T(8,128)S(1)}, u32[]{:S(2)}, u32[]{:S(2)}) collective-permute-start(f32[184,128]{1,0:T(8,128)S(1)} %fusion.88), channel_id=1, source_target_pairs={{0,2},{2,0},{1,3},{3,1},{4,6},{6,4},{5,7},{7,5},{8,10},{10,8},{9,1... | collective-permute-start | bytes 282632 | tf_op jit(solution)/shard_map/ppermute | solution.py:51
  29.3 6.0 %collective-permute-done.1 = f32[184,128]{1,0:T(8,128)S(1)} collective-permute-done((f32[184,128]{1,0:T(8,128)S(1)}, f32[184,128]{1,0:T(8,128)S(1)}, u32[]{:S(2)}, u32[]{:S(2)}) %collective-permute-start.1) | collective-permute-done | bytes 94240 | tf_op jit(solution)/shard_map/ppermute | solution.py:51
  35.4 5.7 %collective-permute-start.10 = (bf16[56,1408]{1,0:T(8,128)(2,1)S(1)}, bf16[56,1408]{1,0:T(8,128)(2,1)S(1)}, u32[]{:S(2)}, u32[]{:S(2)}) collective-permute-start(bf16[56,1408]{1,0:T(8,128)(2,1)S(1)} %concatenate.22), channel_id=1, source_target_pairs={{0,0},{1,4},{2,8},{3,12},{4,16},{5,20},{6,24},{7,28},{8,32},{9,36}... | collective-permute-start | bytes 473096 | tf_op jit(solution)/shard_map/ppermute | solution.py:144
  41.4 3.6 %all-to-all-done = bf16[64,35,128]{2,1,0:T(8,128)(2,1)S(1)} async-done(((bf16[64,35,128]{2,1,0:T(8,128)(2,1)}), bf16[64,35,128]{2,1,0:T(8,128)(2,1)S(1)}, u32[]{:S(2)}, u32[]{:S(2)}) %all-to-all-start) | async-done | bytes 573472 | tf_op jit(solution)/shard_map/all_to_all | solution.py:66
  44.9 0.6 reshape.118
  45.5 3.0 %collective-permute-start.3 = (bf16[320,896]{1,0:T(8,128)(2,1)S(1)}, bf16[320,896]{1,0:T(8,128)(2,1)S(1)}, u32[]{:S(2)}, u32[]{:S(2)}) collective-permute-start(bf16[320,896]{1,0:T(8,128)(2,1)S(1)} %reshape.118), channel_id=1, source_target_pairs={{0,2},{2,0},{1,3},{3,1},{4,6},{6,4},{5,7},{7,5},{8,10},{10,8},{9,1... | collective-permute-start | bytes 1720328 | tf_op jit(solution)/shard_map/ppermute | solution.py:51
  48.5 0.9 collective-permute-done.10
  49.4 0.7 copy-done.8
  50.1 1.8 fusion.13
  52.0 1.8 fusion.18
  53.8 6.9 %collective-permute-done.3 = bf16[320,896]{1,0:T(8,128)(2,1)S(1)} collective-permute-done((bf16[320,896]{1,0:T(8,128)(2,1)S(1)}, bf16[320,896]{1,0:T(8,128)(2,1)S(1)}, u32[]{:S(2)}, u32[]{:S(2)}) %collective-permute-start.3) | collective-permute-done | bytes 573472 | tf_op jit(solution)/shard_map/ppermute | solution.py:51
  60.7 1.7 convolution_add_fusion.2
  62.4 0.5 convolution_add_fusion.5
  62.9 0.5 convolution_add_fusion.1
  63.4 0.5 convolution_add_fusion.4
  64.0 0.5 convolution_add_fusion.3
  64.5 0.6 multiply_convert_fusion.1
  65.1 0.9 copy-done.2
  66.0 0.5 convolution_convert_fusion.1
  66.5 0.6 collective-permute-start.6
  67.1 0.5 convolution_convert_fusion.3
  67.7 1.0 collective-permute-done.6
  68.7 0.5 add_convert_fusion.1
  69.2 4.3 %collective-permute-start.7 = (bf16[320,896]{1,0:T(8,128)(2,1)S(1)}, bf16[320,896]{1,0:T(8,128)(2,1)S(1)}, u32[]{:S(2)}, u32[]{:S(2)}) collective-permute-start(bf16[320,896]{1,0:T(8,128)(2,1)S(1)} %add_convert_fusion.1), channel_id=1, source_target_pairs={{0,2},{2,0},{1,3},{3,1},{4,6},{6,4},{5,7},{7,5},{8,10},{10,8},{9,1... | collective-permute-start | bytes 1720328 | tf_op jit(solution)/shard_map/ppermute | solution.py:51
  73.5 0.5 fusion.3
  74.1 13.0 %collective-permute-done.7 = bf16[320,896]{1,0:T(8,128)(2,1)S(1)} collective-permute-done((bf16[320,896]{1,0:T(8,128)(2,1)S(1)}, bf16[320,896]{1,0:T(8,128)(2,1)S(1)}, u32[]{:S(2)}, u32[]{:S(2)}) %collective-permute-start.7) | collective-permute-done | bytes 573472 | tf_op jit(solution)/shard_map/ppermute | solution.py:51
  87.2 1.4 reshape.119
  88.7 18.2 %all-to-all-start.1 = ((bf16[64,35,128]{2,1,0:T(8,128)(2,1)}), bf16[64,35,128]{2,1,0:T(8,128)(2,1)S(1)}, u32[]{:S(2)}, u32[]{:S(2)}) async-start(bf16[64,35,128]{2,1,0:T(8,128)(2,1)} %reshape.119), calls=%async_computation.1 | async-start | bytes 1310720 | tf_op jit(solution)/shard_map/all_to_all | solution.py:66
  107.1 0.4 fusion.91
  107.9 1.0 collective-permute-done.8
  108.9 0.7 collective-permute-start.9
  109.6 0.4 fusion.43
  110.0 5.3 %collective-permute-done.9 = f32[128,64]{1,0:T(8,128)S(1)} collective-permute-done((f32[128,64]{1,0:T(8,128)S(1)}, f32[128,64]{1,0:T(8,128)S(1)}, u32[]{:S(2)}, u32[]{:S(2)}) %collective-permute-start.9) | collective-permute-done | bytes 32800 | tf_op jit(solution)/shard_map/ppermute | solution.py:51
  115.3 14.8 %all-to-all-done.1 = bf16[64,35,128]{2,1,0:T(8,128)(2,1)S(1)} async-done(((bf16[64,35,128]{2,1,0:T(8,128)(2,1)}), bf16[64,35,128]{2,1,0:T(8,128)(2,1)S(1)}, u32[]{:S(2)}, u32[]{:S(2)}) %all-to-all-start.1) | async-done | bytes 573472 | tf_op jit(solution)/shard_map/all_to_all | solution.py:66
  130.1 0.6 reshape.120
  130.7 0.6 convolution_convert_fusion.6
  131.3 14.4 %all_gather.6 = bf16[512,896]{1,0:T(8,128)(2,1)S(1)} all-gather(bf16[128,896]{1,0:T(8,128)(2,1)S(1)} %convolution_convert_fusion.6), channel_id=1, replica_groups=mesh['yl'=2,'z'=8,'x'=4,'yh'=2,'c'=2] {'x'}, dimensions={0}, use_global_device_ids=true | all-gather | bytes 1146880 | tf_op jit(solution)/shard_map/all_gather | solution.py:203
  145.8 3.5 %fusion.92 = f32[512,1408]{1,0:T(8,128)S(1)} fusion(bf16[512,896]{1,0:T(8,128)(2,1)S(1)} %all_gather.6, bf16[896,1408]{1,0:T(8,128)(2,1)} %all-gather.2.cloned.1.call-done), kind=kOutput, calls=%fused_computation.144 | convolution fusion | flops 1291845632 | bytes 6324224 | tf_op jit(solution)/shard_map/dot_general | solution.py:60
  149.2 1.2 slice.115
  150.6 2.5 %concatenate.23 = bf16[512,1408]{1,0:T(8,128)(2,1)S(1)} concatenate(bf16[512,1280]{1,0:T(8,128)(2,1)} %slice.115, bf16[512,64]{1,0:T(8,128)(2,1)S(1)} %get-tuple-element.15, bf16[512,64]{1,0:T(8,128)(2,1)S(1)} %get-tuple-element.14), dimensions={1} | concatenate | bytes 2883584 | tf_op jit(solution)/shard_map/concatenate | solution.py:207
  153.3 0.7 collective-permute-start.11
  153.9 3.8 %collective-permute-start.12 = (bf16[128,1408]{1,0:T(8,128)(2,1)S(1)}, bf16[128,1408]{1,0:T(8,128)(2,1)S(1)}, u32[]{:S(2)}, u32[]{:S(2)}) collective-permute-start(bf16[128,1408]{1,0:T(8,128)(2,1)S(1)} %get-tuple-element.19), channel_id=1, source_target_pairs={{0,4},{1,8},{2,12},{3,0},{4,9},{5,13},{6,1},{7,5},{8,14},{9,2},{10... | collective-permute-start | bytes 1081352 | tf_op jit(solution)/shard_map/ppermute | solution.py:214
  157.7 5.5 %collective-permute-start.13 = (bf16[128,1408]{1,0:T(8,128)(2,1)S(1)}, bf16[128,1408]{1,0:T(8,128)(2,1)S(1)}, u32[]{:S(2)}, u32[]{:S(2)}) collective-permute-start(bf16[128,1408]{1,0:T(8,128)(2,1)S(1)} %get-tuple-element.18), channel_id=1, source_target_pairs={{0,8},{1,12},{2,0},{3,4},{4,13},{5,1},{6,5},{7,9},{8,2},{9,6},{10,... | collective-permute-start | bytes 1081352 | tf_op jit(solution)/shard_map/ppermute | solution.py:214
  163.2 4.9 %collective-permute-start.14 = (bf16[128,1408]{1,0:T(8,128)(2,1)S(1)}, bf16[128,1408]{1,0:T(8,128)(2,1)S(1)}, u32[]{:S(2)}, u32[]{:S(2)}) collective-permute-start(bf16[128,1408]{1,0:T(8,128)(2,1)S(1)} %get-tuple-element.17), channel_id=1, source_target_pairs={{0,12},{1,0},{2,4},{3,8},{4,1},{5,5},{6,9},{7,13},{8,6},{9,10},{10... | collective-permute-start | bytes 1081352 | tf_op jit(solution)/shard_map/ppermute | solution.py:214
  168.1 5.6 %collective-permute-done.12 = bf16[128,1408]{1,0:T(8,128)(2,1)S(1)} collective-permute-done((bf16[128,1408]{1,0:T(8,128)(2,1)S(1)}, bf16[128,1408]{1,0:T(8,128)(2,1)S(1)}, u32[]{:S(2)}, u32[]{:S(2)}) %collective-permute-start.12) | collective-permute-done | bytes 360480 | tf_op jit(solution)/shard_map/ppermute | solution.py:214
  173.7 0.7 collective-permute-done.13
  174.4 2.0 collective-permute-done.14
  176.6 0.8 multiply_reduce_fusion
  181.8 1.3 fusion.85
  183.3 25.9 %all_to_all.20 = bf16[64,21,128]{2,1,0:T(8,128)(2,1)S(1)} all-to-all(bf16[64,21,128]{2,1,0:T(8,128)(2,1)S(1)} %pad_maximum_fusion), channel_id=1, replica_groups=mesh['yl'=2,'z'=8,'x'=4,'yh'=2,'c'=2] {'yl','z','x'}, dimensions={0} | all-to-all | bytes 688128 | tf_op jit(solution)/shard_map/all_to_all | solution.py:247
  209.3 0.8 broadcast_in_dim.42
  210.1 5.8 %all-to-all-start.3 = ((bf16[64,20,128]{2,1,0:T(8,128)(2,1)}), bf16[64,20,128]{2,1,0:T(8,128)(2,1)S(1)}, u32[]{:S(2)}, u32[]{:S(2)}) async-start(bf16[64,20,128]{2,1,0:T(8,128)(2,1)} %broadcast_in_dim.42), calls=%async_computation.3 | async-start | bytes 786432 | tf_op jit(solution)/shard_map/all_to_all | solution.py:258
  216.1 3.3 %collective-permute-start.17 = (f32[1,128]{1,0:T(1,128)S(1)}, f32[1,128]{1,0:T(1,128)S(1)}, u32[]{:S(2)}, u32[]{:S(2)}) collective-permute-start(f32[1,128]{1,0:T(1,128)S(1)} %slice.78), channel_id=1, source_target_pairs={{0,3},{1,2},{2,1},{3,0},{4,7},{5,6},{6,5},{7,4},{8,11},{9,10},{10,... | collective-permute-start | bytes 1544 | tf_op jit(solution)/shard_map/ppermute | solution.py:252
  219.4 1.8 collective-permute-done.16
  221.1 0.6 add_reduce_fusion
  222.4 9.5 %all-to-all-done.3 = bf16[64,20,128]{2,1,0:T(8,128)(2,1)S(1)} async-done(((bf16[64,20,128]{2,1,0:T(8,128)(2,1)}), bf16[64,20,128]{2,1,0:T(8,128)(2,1)S(1)}, u32[]{:S(2)}, u32[]{:S(2)}) %all-to-all-start.3) | async-done | bytes 327712 | tf_op jit(solution)/shard_map/all_to_all | solution.py:258
  232.0 0.8 copy.51
  232.8 0.8 copy.52
  (79 shorter events, 4.7 us)
Async XLA Ops:
  7.2 2.2 copy-start
  7.2 16.9 %copy-start.9 = (bf16[1280]{0:T(1024)(128)(2,1)S(1)}, bf16[1280]{0:T(1024)(128)(2,1)}, u32[]{:S(2)}) copy-start(bf16[1280]{0:T(1024)(128)(2,1)} %param.19) | copy-start | bytes 7684
  7.2 16.9 %copy-start.7 = (bf16[56,1280]{1,0:T(8,128)(2,1)S(1)}, bf16[56,1280]{1,0:T(8,128)(2,1)}, u32[]{:S(2)}) copy-start(bf16[56,1280]{1,0:T(8,128)(2,1)} %param.17) | copy-start | bytes 430084
  7.2 16.9 %copy-start.5 = (bf16[64,1280]{1,0:T(8,128)(2,1)S(1)}, bf16[64,1280]{1,0:T(8,128)(2,1)}, u32[]{:S(2)}) copy-start(bf16[64,1280]{1,0:T(8,128)(2,1)} %param.21) | copy-start | bytes 491524
  7.2 17.1 %copy-start.6 = (bf16[128,1280]{1,0:T(8,128)(2,1)S(1)}, bf16[128,1280]{1,0:T(8,128)(2,1)}, u32[]{:S(2)}) copy-start(bf16[128,1280]{1,0:T(8,128)(2,1)} %param.18) | copy-start | bytes 983044
  7.2 17.1 %copy-start.11 = (bf16[1280,64]{0,1:T(8,128)(2,1)S(1)}, bf16[1280,64]{0,1:T(8,128)(2,1)}, u32[]{:S(2)}) copy-start(bf16[1280,64]{0,1:T(8,128)(2,1)} %param.20) | copy-start | bytes 491524
  11.4 33.6 %all-to-all-start = ((bf16[64,35,128]{2,1,0:T(8,128)(2,1)}), bf16[64,35,128]{2,1,0:T(8,128)(2,1)S(1)}, u32[]{:S(2)}, u32[]{:S(2)}) async-start(bf16[64,35,128]{2,1,0:T(8,128)(2,1)} %reshape.117), calls=%async_computation | async-start | bytes 1310720 | tf_op jit(solution)/shard_map/all_to_all | solution.py:66
  24.0 121.8 %all-gather.2.cloned.1.call-start = ((), (), s32[]{:S(2)}) async-start(), calls=%async_computation.4 | async-start | bytes 2680832 | tf_op jit(solution)/shard_map/all_gather | solution.py:143
  24.9 1.4 collective-permute-start
  26.3 9.0 %collective-permute-start.1 = (f32[184,128]{1,0:T(8,128)S(1)}, f32[184,128]{1,0:T(8,128)S(1)}, u32[]{:S(2)}, u32[]{:S(2)}) collective-permute-start(f32[184,128]{1,0:T(8,128)S(1)} %fusion.88), channel_id=1, source_target_pairs={{0,2},{2,0},{1,3},{3,1},{4,6},{6,4},{5,7},{7,5},{8,10},{10,8},{9,1... | collective-permute-start | bytes 282632 | tf_op jit(solution)/shard_map/ppermute | solution.py:51
  35.4 14.0 %collective-permute-start.10 = (bf16[56,1408]{1,0:T(8,128)(2,1)S(1)}, bf16[56,1408]{1,0:T(8,128)(2,1)S(1)}, u32[]{:S(2)}, u32[]{:S(2)}) collective-permute-start(bf16[56,1408]{1,0:T(8,128)(2,1)S(1)} %concatenate.22), channel_id=1, source_target_pairs={{0,0},{1,4},{2,8},{3,12},{4,16},{5,20},{6,24},{7,28},{8,32},{9,36}... | collective-permute-start | bytes 473096 | tf_op jit(solution)/shard_map/ppermute | solution.py:144
  45.5 15.2 %collective-permute-start.3 = (bf16[320,896]{1,0:T(8,128)(2,1)S(1)}, bf16[320,896]{1,0:T(8,128)(2,1)S(1)}, u32[]{:S(2)}, u32[]{:S(2)}) collective-permute-start(bf16[320,896]{1,0:T(8,128)(2,1)S(1)} %reshape.118), channel_id=1, source_target_pairs={{0,2},{2,0},{1,3},{3,1},{4,6},{6,4},{5,7},{7,5},{8,10},{10,8},{9,1... | collective-permute-start | bytes 1720328 | tf_op jit(solution)/shard_map/ppermute | solution.py:51
  48.5 12.2 %collective-permute-start.2 = (bf16[320,896]{1,0:T(8,128)(2,1)S(1)}, bf16[320,896]{1,0:T(8,128)(2,1)S(1)}, u32[]{:S(2)}, u32[]{:S(2)}) collective-permute-start(bf16[320,896]{1,0:T(8,128)(2,1)S(1)} %reshape.118), channel_id=1, source_target_pairs={{0,1},{1,0},{2,3},{3,2},{4,5},{5,4},{6,7},{7,6},{8,9},{9,8},{10,11... | collective-permute-start | bytes 1720328 | tf_op jit(solution)/shard_map/ppermute | solution.py:51
  49.4 0.7 copy-start.8
  50.1 12.3 %copy-start.1 = (bf16[1,3584,512]{2,1,0:T(8,128)(2,1)S(1)}, bf16[1,3584,512]{2,1,0:T(8,128)(2,1)}, u32[]{:S(2)}) copy-start(bf16[1,3584,512]{2,1,0:T(8,128)(2,1)} %param.14) | copy-start | bytes 11010052
  52.0 10.9 %copy-start.4 = (bf16[1,3584,512]{2,1,0:T(8,128)(2,1)S(1)}, bf16[1,3584,512]{2,1,0:T(8,128)(2,1)}, u32[]{:S(2)}) copy-start(bf16[1,3584,512]{2,1,0:T(8,128)(2,1)} %param.15) | copy-start | bytes 11010052
  60.7 3.3 %collective-permute-start.4 = (bf16[320,896]{1,0:T(8,128)(2,1)S(1)}, bf16[320,896]{1,0:T(8,128)(2,1)S(1)}, u32[]{:S(2)}, u32[]{:S(2)}) collective-permute-start(bf16[320,896]{1,0:T(8,128)(2,1)S(1)} %collective-permute-done.3), channel_id=1, source_target_pairs={{0,1},{1,0},{2,3},{3,2},{4,5},{5,4},{6,7},{7,6},{8,9},{9,8},{10,11... | collective-permute-start | bytes 1720328 | tf_op jit(solution)/shard_map/ppermute | solution.py:51
  64.0 2.0 copy-start.2
  66.5 2.2 collective-permute-start.6
  67.6 6.4 %collective-permute-start.5 = (bf16[320,896]{1,0:T(8,128)(2,1)S(1)}, bf16[320,896]{1,0:T(8,128)(2,1)S(1)}, u32[]{:S(2)}, u32[]{:S(2)}) collective-permute-start(bf16[320,896]{1,0:T(8,128)(2,1)S(1)} %convolution_convert_fusion.3), channel_id=1, source_target_pairs={{0,1},{1,0},{2,3},{3,2},{4,5},{5,4},{6,7},{7,6},{8,9},{9,8},{10,11... | collective-permute-start | bytes 1720328 | tf_op jit(solution)/shard_map/ppermute | solution.py:51
  69.2 37.6 %copy-start.10 = (f32[128,2]{0,1:T(2,128)S(1)}, f32[128,2]{0,1:T(2,128)}, u32[]{:S(2)}) copy-start(f32[128,2]{0,1:T(2,128)} %param.13) | copy-start | bytes 3076
  69.2 17.8 %collective-permute-start.7 = (bf16[320,896]{1,0:T(8,128)(2,1)S(1)}, bf16[320,896]{1,0:T(8,128)(2,1)S(1)}, u32[]{:S(2)}, u32[]{:S(2)}) collective-permute-start(bf16[320,896]{1,0:T(8,128)(2,1)S(1)} %add_convert_fusion.1), channel_id=1, source_target_pairs={{0,2},{2,0},{1,3},{3,1},{4,6},{6,4},{5,7},{7,5},{8,10},{10,8},{9,1... | collective-permute-start | bytes 1720328 | tf_op jit(solution)/shard_map/ppermute | solution.py:51
  88.7 41.5 %all-to-all-start.1 = ((bf16[64,35,128]{2,1,0:T(8,128)(2,1)}), bf16[64,35,128]{2,1,0:T(8,128)(2,1)S(1)}, u32[]{:S(2)}, u32[]{:S(2)}) async-start(bf16[64,35,128]{2,1,0:T(8,128)(2,1)} %reshape.119), calls=%async_computation.1 | async-start | bytes 1310720 | tf_op jit(solution)/shard_map/all_to_all | solution.py:66
  107.5 1.3 collective-permute-start.8
  108.9 6.4 %collective-permute-start.9 = (f32[128,64]{1,0:T(8,128)S(1)}, f32[128,64]{1,0:T(8,128)S(1)}, u32[]{:S(2)}, u32[]{:S(2)}) collective-permute-start(f32[128,64]{1,0:T(8,128)S(1)} %add.177), channel_id=1, source_target_pairs={{0,2},{2,0},{1,3},{3,1},{4,6},{6,4},{5,7},{7,5},{8,10},{10,8},{9,1... | collective-permute-start | bytes 98312 | tf_op jit(solution)/shard_map/ppermute | solution.py:51
  153.3 14.9 %collective-permute-start.11 = (bf16[128,1408]{1,0:T(8,128)(2,1)S(1)}, bf16[128,1408]{1,0:T(8,128)(2,1)S(1)}, u32[]{:S(2)}, u32[]{:S(2)}) collective-permute-start(bf16[128,1408]{1,0:T(8,128)(2,1)S(1)} %get-tuple-element.16), channel_id=1, source_target_pairs={{0,0},{1,4},{2,8},{3,12},{4,5},{5,9},{6,13},{7,1},{8,10},{9,14},{1... | collective-permute-start | bytes 1081352 | tf_op jit(solution)/shard_map/ppermute | solution.py:214
  153.9 19.8 %collective-permute-start.12 = (bf16[128,1408]{1,0:T(8,128)(2,1)S(1)}, bf16[128,1408]{1,0:T(8,128)(2,1)S(1)}, u32[]{:S(2)}, u32[]{:S(2)}) collective-permute-start(bf16[128,1408]{1,0:T(8,128)(2,1)S(1)} %get-tuple-element.19), channel_id=1, source_target_pairs={{0,4},{1,8},{2,12},{3,0},{4,9},{5,13},{6,1},{7,5},{8,14},{9,2},{10... | collective-permute-start | bytes 1081352 | tf_op jit(solution)/shard_map/ppermute | solution.py:214
  157.7 16.7 %collective-permute-start.13 = (bf16[128,1408]{1,0:T(8,128)(2,1)S(1)}, bf16[128,1408]{1,0:T(8,128)(2,1)S(1)}, u32[]{:S(2)}, u32[]{:S(2)}) collective-permute-start(bf16[128,1408]{1,0:T(8,128)(2,1)S(1)} %get-tuple-element.18), channel_id=1, source_target_pairs={{0,8},{1,12},{2,0},{3,4},{4,13},{5,1},{6,5},{7,9},{8,2},{9,6},{10,... | collective-permute-start | bytes 1081352 | tf_op jit(solution)/shard_map/ppermute | solution.py:214
  163.2 13.2 %collective-permute-start.14 = (bf16[128,1408]{1,0:T(8,128)(2,1)S(1)}, bf16[128,1408]{1,0:T(8,128)(2,1)S(1)}, u32[]{:S(2)}, u32[]{:S(2)}) collective-permute-start(bf16[128,1408]{1,0:T(8,128)(2,1)S(1)} %get-tuple-element.17), channel_id=1, source_target_pairs={{0,12},{1,0},{2,4},{3,8},{4,1},{5,5},{6,9},{7,13},{8,6},{9,10},{10... | collective-permute-start | bytes 1081352 | tf_op jit(solution)/shard_map/ppermute | solution.py:214
  177.4 54.6 %copy-start.3 = (f32[128,1280]{1,0:T(8,128)}, f32[128,1280]{1,0:T(8,128)S(1)}, u32[]{:S(2)}) copy-start(f32[128,1280]{1,0:T(8,128)S(1)} %get-tuple-element.13) | copy-start | bytes 1966084
  210.1 21.8 %all-to-all-start.3 = ((bf16[64,20,128]{2,1,0:T(8,128)(2,1)}), bf16[64,20,128]{2,1,0:T(8,128)(2,1)S(1)}, u32[]{:S(2)}, u32[]{:S(2)}) async-start(bf16[64,20,128]{2,1,0:T(8,128)(2,1)} %broadcast_in_dim.42), calls=%async_computation.3 | async-start | bytes 786432 | tf_op jit(solution)/shard_map/all_to_all | solution.py:258
  215.9 3.5 %collective-permute-start.15 = (f32[1,128]{1,0:T(1,128)S(1)}, f32[1,128]{1,0:T(1,128)S(1)}, u32[]{:S(2)}, u32[]{:S(2)}) collective-permute-start(f32[1,128]{1,0:T(1,128)S(1)} %slice.78), channel_id=1, source_target_pairs={{0,1},{1,0},{2,3},{3,2},{4,5},{5,4},{6,7},{7,6},{8,9},{9,8},{10,11... | collective-permute-start | bytes 1544 | tf_op jit(solution)/shard_map/ppermute | solution.py:51
  216.0 5.1 %collective-permute-start.16 = (f32[1,128]{1,0:T(1,128)S(1)}, f32[1,128]{1,0:T(1,128)S(1)}, u32[]{:S(2)}, u32[]{:S(2)}) collective-permute-start(f32[1,128]{1,0:T(1,128)S(1)} %slice.78), channel_id=1, source_target_pairs={{0,2},{2,0},{1,3},{3,1},{4,6},{6,4},{5,7},{7,5},{8,10},{10,8},{9,1... | collective-permute-start | bytes 1544 | tf_op jit(solution)/shard_map/ppermute | solution.py:51
  216.1 5.0 %collective-permute-start.17 = (f32[1,128]{1,0:T(1,128)S(1)}, f32[1,128]{1,0:T(1,128)S(1)}, u32[]{:S(2)}, u32[]{:S(2)}) collective-permute-start(f32[1,128]{1,0:T(1,128)S(1)} %slice.78), channel_id=1, source_target_pairs={{0,3},{1,2},{2,1},{3,0},{4,7},{5,6},{6,5},{7,4},{8,11},{9,10},{10,... | collective-permute-start | bytes 1544 | tf_op jit(solution)/shard_map/ppermute | solution.py:252
Sparse Core Ops, SparseCore 0:
  50.3 79.6 all-gather.1

commit v2 on v1

--- a/solution.py
+++ b/solution.py
@@ -3,6 +3,8 @@
 import jax
 import jax.numpy as jnp
 from jax import lax
+from jax.experimental import pallas as pl
+from jax.experimental.pallas import tpu as pltpu
 from jax.sharding import Mesh, PartitionSpec as P
 
 route_scale = 2.5
@@ -26,13 +28,11 @@
                         yield yl, z, x, yh, c
 
 
-def proj_perm():
+def proj_perm(step):
     pairs = []
     for yl, z, x, yh, c in coords():
-        d, m = (yl * 8 + z) * 4 + x, yh * 2 + c
-        owner, place = d // 16, d % 16
         pairs.append(
-            (index_of(yl, z, x, yh, c), index_of(place // 8, place % 8, m, owner // 2, owner % 2))
+            (index_of(yl, z, x, yh, c), index_of(x // 2, z, yh * 2 + c, yl, step ^ (x % 2)))
         )
     return pairs
 
@@ -42,7 +42,7 @@
     for yl, z, x, yh, c in coords():
         m = yh * 2 + c
         pairs.append(
-            (index_of(yl, z, x, yh, c), index_of(yl, z, (x + m + step) % 4, x // 2, x % 2))
+            (index_of(yl, z, x, yh, c), index_of(yl, z, x ^ m ^ step, x // 2, x % 2))
         )
     return pairs
 
@@ -69,6 +69,41 @@
 def split_two(value):
     high = lax.reduce_precision(value, 8, 7)
     return high.astype(jnp.bfloat16), (value - high).astype(jnp.bfloat16)
+
+
+def product_kernel(order_ref, own_ref, other_ref, block_ref, *refs):
+    outs, total = refs[:4], refs[4]
+    width = own_ref.shape[1]
+    rows = own_ref.shape[0] // 4
+    wide = block_ref.shape[1] - 128
+    core = order_ref[4]
+    near = block_ref[pl.ds(pl.multiple_of(core * width, 128), width), :]
+    far = block_ref[pl.ds(pl.multiple_of((1 - core) * width, 128), width), :]
+    total[...] = dot(own_ref[...], near) + dot(other_ref[...], far)
+    for step in range(4):
+        here = pl.ds(pl.multiple_of(order_ref[step] * rows, 128), rows)
+        outs[step][:, :wide] = total[here, :wide].astype(jnp.bfloat16)
+        low = total[here, wide:]
+        low = low + pltpu.roll(low, 64, 1)
+        lane = lax.broadcasted_iota(jnp.int32, low.shape, 1)
+        rest = low - low.astype(jnp.bfloat16).astype(jnp.float32)
+        outs[step][:, wide:] = jnp.where(lane < 64, low, rest).astype(jnp.bfloat16)
+
+
+def product_pieces(order, own, other, block):
+    rows, wide = own.shape[0], block.shape[1]
+    vmem = pl.BlockSpec(memory_space=pltpu.VMEM)
+    return pl.pallas_call(
+        product_kernel,
+        out_shape=[jax.ShapeDtypeStruct((rows // 4, wide), jnp.bfloat16)] * 4,
+        in_specs=[pl.BlockSpec(memory_space=pltpu.SMEM), vmem, vmem, vmem],
+        out_specs=[vmem] * 4,
+        scratch_shapes=[pltpu.VMEM((rows, wide), jnp.float32)],
+        compiler_params=pltpu.CompilerParams(vmem_limit_bytes=40 * 1024 * 1024),
+        cost_estimate=pl.CostEstimate(
+            flops=4 * rows * own.shape[1] * wide, bytes_accessed=8_000_000, transcendentals=0
+        ),
+    )(order, own, other, block)
 
 
 def body(
@@ -93,6 +128,7 @@
     slot_count = experts * capacity
     rank = adapter_up_matrix.shape[0]
     xi, yh, core = lax.axis_index("x"), lax.axis_index("yh"), lax.axis_index("c")
+    yl = lax.axis_index("yl")
     mi = yh * 2 + core
 
     flat_routes = routes.reshape(assigned)
@@ -110,7 +146,6 @@
     ).astype(jnp.bfloat16)
     placing = dot(slot_hit, token_hit).astype(jnp.bfloat16)
     outgoing = dot(placing, tokens).astype(jnp.bfloat16)
-    arrived = exchange_slots(outgoing)
 
     student = student_hidden_input.astype(jnp.float32)
     gain = student_norm_weight.astype(jnp.float32)
@@ -123,10 +158,31 @@
     stats = jnp.concatenate(
         [low_part, jnp.broadcast_to(square_sum, (tok_rows, rank))], axis=1
     )
-    shared = mp_sum(
-        jnp.concatenate([stats, jnp.concatenate([proj_low, jnp.zeros_like(proj_low)], axis=1)])
-    )
+    shared = jnp.concatenate(
+        [stats, jnp.concatenate([proj_low, jnp.zeros_like(proj_low)], axis=1)]
+    )
+    outgoing, shared = lax.optimization_barrier((outgoing, shared + swap(shared, "c")))
+    arrived = exchange_slots(outgoing)
+    shared = shared + swap(shared, "yh")
     stats, proj_low = shared[:tok_rows], shared[tok_rows:, :rank]
+
+    half = proj.shape[1] // 2
+    extra = split_two(proj_low)
+    halves = []
+    for step in range(2):
+        mine = lax.dynamic_slice_in_dim(proj, (step ^ (xi & 1)) * half, half, 1)
+        halves.append(
+            lax.ppermute(jnp.concatenate([mine, *extra], axis=1), ALL, proj_perm(step))
+        )
+    halves = jnp.where(
+        core == 0, jnp.concatenate(halves), jnp.concatenate([halves[1], halves[0]])
+    )
+    others = swap(halves, "yl")
+    halves = jnp.where(
+        yl == 0, jnp.concatenate([halves, others]), jnp.concatenate([others, halves])
+    )
+    proj_block = lax.all_gather(halves, "z", axis=0, tiled=True)
+
     inverse = lax.rsqrt(stats[:, rank : rank + 1] / student_width + 1e-06)
     lowrank = (stats[:, :rank] * inverse).astype(jnp.bfloat16)
     normed = (student * inverse * gain).astype(jnp.bfloat16)
@@ -140,14 +196,6 @@
         )
     )
 
-    proj_block = lax.all_gather(
-        lax.ppermute(jnp.concatenate([proj, *split_two(proj_low)], axis=1), ALL, proj_perm()),
-        ("yl", "z"),
-        axis=0,
-        tiled=True,
-    )
-    arrived, lowrank = lax.optimization_barrier((arrived, lowrank))
-
     arrived_y = swap(arrived, "yh")
     arrived_c = swap(arrived, "c")
     arrived_yc = swap(arrived_y, "c")
@@ -201,25 +249,27 @@
     ).astype(jnp.bfloat16)
 
     teacher_rows = lax.all_gather(teacher, "x", axis=0, tiled=True)
-    product = dot(teacher_rows, proj_block)
-    columns = adapter_up_matrix.shape[1]
-    low = product[:, columns : columns + rank] + product[:, columns + rank :]
-    product = jnp.concatenate(
-        [product[:, :columns].astype(jnp.bfloat16), *split_two(low)], axis=1
-    )
-    total = 0.0
-    for step in range(mp_count):
-        block = lax.rem(xi + mi + step, 4)
-        piece = lax.dynamic_slice_in_dim(product, block * tok_rows, tok_rows, 0)
-        total = total + lax.ppermute(piece, ALL, home_perm(step)).astype(jnp.float32)
-    target = total[:, :columns]
+    order = jnp.stack([xi ^ mi ^ step for step in range(mp_count)] + [core])
+    pieces = product_pieces(order, teacher_rows, swap(teacher_rows, "c"), proj_block)
+    pieces = [
+        lax.ppermute(piece, ALL, home_perm(step)).astype(jnp.float32)
+        for step, piece in enumerate(pieces)
+    ]
+    even, odd = pieces[0] + pieces[2], pieces[1] + pieces[3]
+    first_even = (xi ^ mi) & 1 == 0
+    left, right = even[:, :half], odd[:, :half]
+    target = jnp.where(
+        first_even,
+        jnp.concatenate([left, right], axis=1),
+        jnp.concatenate([right, left], axis=1),
+    )
+    teacher_back = even[:, half : half + rank] + even[:, half + rank :]
 
     output_difference = student_out - target
     tokens_all = tok_rows * experts
     scale = 1.0 / math.sqrt(tokens_all)
     scaled = (output_difference * scale).astype(jnp.bfloat16)
     loss_here = jnp.sum(output_difference * output_difference)
-    teacher_back = total[:, columns : columns + rank] + total[:, columns + rank :]
     back_low = (adapter_scale_factor * scale * (student_back - teacher_back)).astype(jnp.bfloat16)
     over_tokens = (((0,), (0,)), ((), ()))
     up_part = adapter_scale_factor * lax.dot_general(
@@ -228,7 +278,8 @@
     down_part = lax.dot_general(back_low, normed, over_tokens, preferred_element_type=jnp.float32)
 
     lanes = 128
-    blocks = columns // lanes
+    columns = up_part.shape[1]
+    tiles = rank // 8 * (columns // lanes)
     first = lax.reduce_precision(loss_here, 8, 7)
     second = lax.reduce_precision(loss_here - first, 8, 7)
     third = loss_here - first - second
@@ -236,28 +287,42 @@
     loss_row = jnp.where(
         lane == 0, first, jnp.where(lane == 1, second, jnp.where(lane == 2, third, 0.0))
     )
+
+    def to_tiles(value):
+        value = value.astype(jnp.bfloat16).reshape(rank // 8, 8, columns // lanes, lanes)
+        return value.transpose(0, 2, 1, 3).reshape(tiles, 8, lanes)
+
+    def from_tiles(value):
+        value = value.reshape(rank // 8, columns // lanes, 8, lanes).transpose(0, 2, 1, 3)
+        return value.reshape(rank, columns).astype(jnp.float32)
+
+    bundle = jnp.concatenate([to_tiles(up_part), to_tiles(down_part)])
     bundle = jnp.concatenate(
         [
-            up_part.reshape(rank, blocks, lanes),
-            down_part.reshape(rank, blocks, lanes),
-            jnp.broadcast_to(loss_row, (rank, 1, lanes)),
+            bundle[: 2 * experts].reshape(experts, 16, lanes),
+            bundle[2 * experts :].reshape(experts, 4, lanes),
+            jnp.broadcast_to(loss_row.astype(jnp.bfloat16), (experts, 4, lanes)),
         ],
         axis=1,
-    ).astype(jnp.bfloat16)
+    )
     bundle = lax.all_to_all(bundle, DP, split_axis=0, concat_axis=0, tiled=True)
     summed = jnp.sum(bundle.astype(jnp.float32), axis=0)
-    loss_row = summed[2 * blocks :]
+    grads = jnp.broadcast_to(summed.astype(jnp.bfloat16), (experts, 24, lanes))
+    grads = lax.all_to_all(grads, DP, split_axis=0, concat_axis=0, tiled=True)
+    loss_row = summed[20:21]
     cross = [(i, 3 - i) for i in range(4)]
     loss_row = (loss_row + swap(loss_row, "c")) + (
         swap(loss_row, "yh") + lax.ppermute(loss_row, MP, cross)
     )
     loss = jnp.sum(loss_row) / (tokens_all * student_width)
-    grads = jnp.broadcast_to(
-        summed[: 2 * blocks].astype(jnp.bfloat16), (rank, 2 * blocks, lanes)
-    )
-    grads = lax.all_to_all(grads, DP, split_axis=0, concat_axis=0, tiled=True).astype(jnp.float32)
-    up_matrix_gradient = grads[:, :blocks].reshape(rank, columns)
-    grad_a = grads[:, blocks:].reshape(rank, columns).T
+    grads = jnp.concatenate(
+        [
+            grads[:, :16].reshape(2 * experts, 8, lanes),
+            grads[:, 16:20].reshape(experts // 2, 8, lanes),
+        ]
+    )
+    up_matrix_gradient = from_tiles(grads[:tiles])
+    grad_a = from_tiles(grads[tiles:]).T
     return (target, grad_a, up_matrix_gradient, loss)
 
 

time: 242 us -> 235 us (0.971)
  the two profiles are of different devices: /device:TPU:32 before, /device:TPU:48 now
where the time goes in v2:
time: 235 us; the launch traced here: 234 us
  waiting for transfers between devices  79.6 us (34%)
  starting transfers between devices  60.7 us (26%)
  blocking collectives  36.5 us (16%)
  between operations  20.1 us (9%)
  matrix products  15.9 us (7%)
  local copies, waits for them, and re-layouts  9.49 us (4%)
  other arithmetic  9.35 us (4%)
  Pallas kernels  2.49 us (1%)
    ppermute x14, waiting for transfers between devices, swap(): return lax.ppermute(value, axis, [(0, 1), (1, 0)])  46.6 us
    all_to_all x1, blocking collectives, body(): bundle = lax.all_to_all(bundle, DP, split_axis=0, concat_axis=0, tiled=True)  21.7 us
    all_to_all x2, starting transfers between devices, exchange_slots(): lax.all_to_all(rows, DP, split_axis=0, concat_axis=0, tiled=True)  21.2 us
    all_gather x1, blocking collectives, body(): teacher_rows = lax.all_gather(teacher, 'x', axis=0, tiled=True)  14.8 us
    ppermute x4, starting transfers between devices, body(): lax.ppermute(piece, ALL, home_perm(step)).astype(jnp.float32)  14 us
    dot_general x15, matrix products, dot(): return jnp.dot(a, b, preferred_element_type=jnp.float32)  11.9 us
    all_to_all x2, waiting for transfers between devices, exchange_slots(): lax.all_to_all(rows, DP, split_axis=0, concat_axis=0, tiled=True)  10.7 us
    ppermute x14, starting transfers between devices, swap(): return lax.ppermute(value, axis, [(0, 1), (1, 0)])  9.98 us
  transfers between devices with their start and end apart: 25, of which 16 were waited for; matrix products, arithmetic and copies ran while one was open for 8% of the time, Pallas kernels for 0%

profile of v2, /device:TPU:48, one launch (start us, length us, event | category | flops | bytes accessed | tf_op | source)
XLA Modules:
  0.0 234.2 jit_solution(5207624673775687429)
XLA Ops:
  7.2 0.7 convert_element_type.145
  7.9 1.1 fusion.33
  9.0 1.2 fusion.37
  10.3 1.2 fusion.90
  11.8 0.8 copy.18
  12.8 0.6 reduce-window.6
  13.8 0.5 convolution_convert_fusion.5
  14.5 1.4 reshape.141
  15.9 12.3 %all-to-all-start = ((bf16[64,35,128]{2,1,0:T(8,128)(2,1)}), bf16[64,35,128]{2,1,0:T(8,128)(2,1)S(1)}, u32[]{:S(2)}, u32[]{:S(2)}) async-start(bf16[64,35,128]{2,1,0:T(8,128)(2,1)} %reshape.141), calls=%async_computation | async-start | bytes 1310720 | tf_op jit(solution)/shard_map/all_to_all | solution.py:66
  28.3 0.7 collective-permute-start.7
  29.0 8.2 %collective-permute-done.7 = f32[184,128]{1,0:T(8,128)S(1)} collective-permute-done((f32[184,128]{1,0:T(8,128)S(1)}, f32[184,128]{1,0:T(8,128)S(1)}, u32[]{:S(2)}, u32[]{:S(2)}) %collective-permute-start.7) | collective-permute-done | bytes 94240 | tf_op jit(solution)/shard_map/ppermute | solution.py:51
  37.3 4.7 %collective-permute-start.11 = (bf16[56,768]{1,0:T(8,128)(2,1)S(1)}, bf16[56,768]{1,0:T(8,128)(2,1)S(1)}, u32[]{:S(2)}, u32[]{:S(2)}) collective-permute-start(bf16[56,768]{1,0:T(8,128)(2,1)S(1)} %get-tuple-element.26), channel_id=1, source_target_pairs={{0,0},{1,4},{2,8},{3,12},{4,1},{5,5},{6,9},{7,13},{8,128},{9,132},... | collective-permute-start | bytes 258056 | tf_op jit(solution)/shard_map/ppermute | solution.py:175
  42.1 1.7 collective-permute-start.12
  43.8 0.8 collective-permute-done.11
  44.6 3.0 %collective-permute-done.12 = bf16[56,768]{1,0:T(8,128)(2,1)S(1)} collective-permute-done((bf16[56,768]{1,0:T(8,128)(2,1)S(1)}, bf16[56,768]{1,0:T(8,128)(2,1)S(1)}, u32[]{:S(2)}, u32[]{:S(2)}) %collective-permute-start.12) | collective-permute-done | bytes 86048 | tf_op jit(solution)/shard_map/ppermute | solution.py:175
  47.6 5.0 %collective-permute-start.13 = (bf16[112,768]{1,0:T(8,128)(2,1)S(1)}, bf16[112,768]{1,0:T(8,128)(2,1)S(1)}, u32[]{:S(2)}, u32[]{:S(2)}) collective-permute-start(bf16[112,768]{1,0:T(8,128)(2,1)S(1)} %maximum_select_fusion.2), channel_id=1, source_target_pairs={{0,128},{128,0},{1,129},{129,1},{2,130},{130,2},{3,131},{131,3},{4... | collective-permute-start | bytes 516104 | tf_op jit(solution)/shard_map/ppermute | solution.py:51
  52.7 0.6 reshape.142
  53.5 4.0 %collective-permute-done.13 = bf16[112,768]{1,0:T(8,128)(2,1)S(1)} collective-permute-done((bf16[112,768]{1,0:T(8,128)(2,1)S(1)}, bf16[112,768]{1,0:T(8,128)(2,1)S(1)}, u32[]{:S(2)}, u32[]{:S(2)}) %collective-permute-start.13) | collective-permute-done | bytes 172064 | tf_op jit(solution)/shard_map/ppermute | solution.py:51
  57.4 0.8 maximum_select_fusion.1
  58.3 1.8 fusion.18
  60.1 1.7 fusion.13
  61.8 8.4 %collective-permute-done.2 = bf16[320,896]{1,0:T(8,128)(2,1)S(1)} collective-permute-done((bf16[320,896]{1,0:T(8,128)(2,1)S(1)}, bf16[320,896]{1,0:T(8,128)(2,1)S(1)}, u32[]{:S(2)}, u32[]{:S(2)}) %collective-permute-start.2) | collective-permute-done | bytes 573472 | tf_op jit(solution)/shard_map/ppermute | solution.py:51
  70.3 0.5 convolution_add_fusion.5
  70.8 1.7 convolution_add_fusion.2
  72.5 0.5 convolution_add_fusion.4
  73.6 0.5 convolution_add_fusion.3
  74.1 0.6 multiply_convert_fusion.1
  74.6 1.0 copy-done.3
  76.1 0.6 collective-permute-start.5
  77.5 0.8 collective-permute-done.5
  78.9 1.7 collective-permute-start.6
  81.1 14.7 %collective-permute-done.6 = bf16[320,896]{1,0:T(8,128)(2,1)S(1)} collective-permute-done((bf16[320,896]{1,0:T(8,128)(2,1)S(1)}, bf16[320,896]{1,0:T(8,128)(2,1)S(1)}, u32[]{:S(2)}, u32[]{:S(2)}) %collective-permute-start.6) | collective-permute-done | bytes 573472 | tf_op jit(solution)/shard_map/ppermute | solution.py:51
  95.9 1.4 reshape.143
  97.3 8.9 %all-to-all-start.1 = ((bf16[64,35,128]{2,1,0:T(8,128)(2,1)}), bf16[64,35,128]{2,1,0:T(8,128)(2,1)S(1)}, u32[]{:S(2)}, u32[]{:S(2)}) async-start(bf16[64,35,128]{2,1,0:T(8,128)(2,1)} %reshape.143), calls=%async_computation.1 | async-start | bytes 1310720 | tf_op jit(solution)/shard_map/all_to_all | solution.py:66
  107.5 1.0 collective-permute-done.8
  108.5 1.1 collective-permute-start.9
  110.0 5.4 %collective-permute-done.9 = f32[128,64]{1,0:T(8,128)S(1)} collective-permute-done((f32[128,64]{1,0:T(8,128)S(1)}, f32[128,64]{1,0:T(8,128)S(1)}, u32[]{:S(2)}, u32[]{:S(2)}) %collective-permute-start.9) | collective-permute-done | bytes 32800 | tf_op jit(solution)/shard_map/ppermute | solution.py:51
  115.5 0.6 add.151
  116.1 10.7 %all-to-all-done.1 = bf16[64,35,128]{2,1,0:T(8,128)(2,1)S(1)} async-done(((bf16[64,35,128]{2,1,0:T(8,128)(2,1)}), bf16[64,35,128]{2,1,0:T(8,128)(2,1)S(1)}, u32[]{:S(2)}, u32[]{:S(2)}) %all-to-all-start.1) | async-done | bytes 573472 | tf_op jit(solution)/shard_map/all_to_all | solution.py:66
  126.8 0.6 reshape.144
  127.4 0.6 convolution_convert_fusion.6
  128.0 14.8 %all_gather.6.own_ref = bf16[512,896]{1,0:T(8,128)(2,1)S(1)} all-gather(bf16[128,896]{1,0:T(8,128)(2,1)S(1)} %convolution_convert_fusion.6), channel_id=1, replica_groups=mesh['yl'=2,'z'=8,'x'=4,'yh'=2,'c'=2] {'x'}, dimensions={0}, use_global_device_ids=true | all-gather | bytes 1146880 | tf_op jit(solution)/shard_map/all_gather | solution.py:251
  142.9 2.4 %collective-permute-done.10.other_ref = bf16[512,896]{1,0:T(8,128)(2,1)S(1)} collective-permute-done((bf16[512,896]{1,0:T(8,128)(2,1)S(1)}, bf16[512,896]{1,0:T(8,128)(2,1)S(1)}, u32[]{:S(2)}, u32[]{:S(2)}) %collective-permute-start.10) | collective-permute-done | bytes 917536 | tf_op jit(solution)/shard_map/ppermute | solution.py:51
  145.3 1.8 copy-done.1
  147.1 2.5 %shard_map.138 = (bf16[128,768]{1,0:T(8,128)(2,1)S(1)}, bf16[128,768]{1,0:T(8,128)(2,1)S(1)}, bf16[128,768]{1,0:T(8,128)(2,1)S(1)}, bf16[128,768]{1,0:T(8,128)(2,1)S(1)}) custom-call(s32[5]{0:T(128)S(1)} %stack.23.order_ref, bf16[512,896]{1,0:T(8,128)(2,1)S(1)} %all_gather.6.own_ref, bf16[512,896]{1,0:T(8,128)(2,1)S(1)} %collective-permute-done.10.other_ref, ...), custom_call_target="tpu_custom_call" | custom-call | flops 1409286144 | bytes 8000000 | tf_op jit(solution)/shard_map/pallas_call | solution.py:96
  149.6 3.8 %collective-permute-start.14 = (bf16[128,768]{1,0:T(8,128)(2,1)S(1)}, bf16[128,768]{1,0:T(8,128)(2,1)S(1)}, u32[]{:S(2)}, u32[]{:S(2)}) collective-permute-start(bf16[128,768]{1,0:T(8,128)(2,1)S(1)} %get-tuple-element.15), channel_id=1, source_target_pairs={{0,0},{1,4},{2,8},{3,12},{4,5},{5,1},{6,13},{7,9},{8,10},{9,14},{1... | collective-permute-start | bytes 589832 | tf_op jit(solution)/shard_map/ppermute | solution.py:255
  153.4 1.9 collective-permute-start.15
  155.3 6.4 %collective-permute-start.16 = (bf16[128,768]{1,0:T(8,128)(2,1)S(1)}, bf16[128,768]{1,0:T(8,128)(2,1)S(1)}, u32[]{:S(2)}, u32[]{:S(2)}) collective-permute-start(bf16[128,768]{1,0:T(8,128)(2,1)S(1)} %get-tuple-element.17), channel_id=1, source_target_pairs={{0,4},{1,0},{2,12},{3,8},{4,1},{5,5},{6,9},{7,13},{8,14},{9,10},{1... | collective-permute-start | bytes 589832 | tf_op jit(solution)/shard_map/ppermute | solution.py:255
  161.7 1.9 collective-permute-start.17
  163.7 1.3 collective-permute-done.15
  165.0 1.9 collective-permute-done.16
  166.9 5.8 %collective-permute-done.17 = bf16[128,768]{1,0:T(8,128)(2,1)S(1)} collective-permute-done((bf16[128,768]{1,0:T(8,128)(2,1)S(1)}, bf16[128,768]{1,0:T(8,128)(2,1)S(1)}, u32[]{:S(2)}, u32[]{:S(2)}) %collective-permute-start.17) | collective-permute-done | bytes 196640 | tf_op jit(solution)/shard_map/ppermute | solution.py:255
  172.7 0.8 multiply_reduce_fusion
  173.6 1.2 fusion.1
  178.7 1.3 fusion.84
  180.2 21.7 %all_to_all.20 = bf16[64,24,128]{2,1,0:T(8,128)(2,1)S(1)} all-to-all(bf16[64,24,128]{2,1,0:T(8,128)(2,1)S(1)} %pad_maximum_fusion), channel_id=1, replica_groups=mesh['yl'=2,'z'=8,'x'=4,'yh'=2,'c'=2] {'yl','z','x'}, dimensions={0} | all-to-all | bytes 786432 | tf_op jit(solution)/shard_map/all_to_all | solution.py:308
  202.0 0.8 broadcast_in_dim.42
  202.8 5.8 %all-to-all-start.3 = ((bf16[64,24,128]{2,1,0:T(8,128)(2,1)}), bf16[64,24,128]{2,1,0:T(8,128)(2,1)S(1)}, u32[]{:S(2)}, u32[]{:S(2)}) async-start(bf16[64,24,128]{2,1,0:T(8,128)(2,1)} %broadcast_in_dim.42), calls=%async_computation.3 | async-start | bytes 786432 | tf_op jit(solution)/shard_map/all_to_all | solution.py:311
  208.8 3.3 %collective-permute-start.20 = (f32[1,128]{1,0:T(1,128)S(1)}, f32[1,128]{1,0:T(1,128)S(1)}, u32[]{:S(2)}, u32[]{:S(2)}) collective-permute-start(f32[1,128]{1,0:T(1,128)S(1)} %slice.82), channel_id=1, source_target_pairs={{0,3},{1,2},{2,1},{3,0},{4,7},{5,6},{6,5},{7,4},{8,11},{9,10},{10,... | collective-permute-start | bytes 1544 | tf_op jit(solution)/shard_map/ppermute | solution.py:315
  212.1 1.8 collective-permute-done.19
  213.8 0.6 add_reduce_fusion
  215.1 9.5 %all-to-all-done.3 = bf16[64,24,128]{2,1,0:T(8,128)(2,1)S(1)} async-done(((bf16[64,24,128]{2,1,0:T(8,128)(2,1)}), bf16[64,24,128]{2,1,0:T(8,128)(2,1)S(1)}, u32[]{:S(2)}, u32[]{:S(2)}) %all-to-all-start.3) | async-done | bytes 393248 | tf_op jit(solution)/shard_map/all_to_all | solution.py:311
  224.7 0.7 convert_bitcast_fusion.1
  225.4 0.7 convert_bitcast_fusion
  (91 shorter events, 7.1 us)
Async XLA Ops:
  7.2 6.6 %copy-start = (bf16[128,896]{1,0:T(8,128)(2,1)S(1)}, bf16[128,896]{1,0:T(8,128)(2,1)}, u32[]{:S(2)}) copy-start(bf16[128,896]{1,0:T(8,128)(2,1)} %param.11) | copy-start | bytes 688132
  7.2 21.8 %copy-start.10 = (bf16[56,1280]{1,0:T(8,128)(2,1)S(1)}, bf16[56,1280]{1,0:T(8,128)(2,1)}, u32[]{:S(2)}) copy-start(bf16[56,1280]{1,0:T(8,128)(2,1)} %param.17) | copy-start | bytes 430084
  11.7 2.7 %collective-permute-start = (f32[184,128]{1,0:T(8,128)S(1)}, f32[184,128]{1,0:T(8,128)S(1)}, u32[]{:S(2)}, u32[]{:S(2)}) collective-permute-start(f32[184,128]{1,0:T(8,128)S(1)} %select_maximum_fusion), channel_id=1, source_target_pairs={{0,1},{1,0},{2,3},{3,2},{4,5},{5,4},{6,7},{7,6},{8,9},{9,8},{10,11... | collective-permute-start | bytes 282632 | tf_op jit(solution)/shard_map/ppermute | solution.py:51
  15.9 36.8 %all-to-all-start = ((bf16[64,35,128]{2,1,0:T(8,128)(2,1)}), bf16[64,35,128]{2,1,0:T(8,128)(2,1)S(1)}, u32[]{:S(2)}, u32[]{:S(2)}) async-start(bf16[64,35,128]{2,1,0:T(8,128)(2,1)} %reshape.141), calls=%async_computation | async-start | bytes 1310720 | tf_op jit(solution)/shard_map/all_to_all | solution.py:66
  28.2 114.7 %all-gather.2.cloned.1.call-start = ((), (), s32[]{:S(2)}) async-start(), calls=%async_computation.4 | async-start | bytes 3096576 | tf_op jit(solution)/shard_map/all_gather | solution.py:184
  28.3 8.9 %collective-permute-start.7 = (f32[184,128]{1,0:T(8,128)S(1)}, f32[184,128]{1,0:T(8,128)S(1)}, u32[]{:S(2)}, u32[]{:S(2)}) collective-permute-start(f32[184,128]{1,0:T(8,128)S(1)} %fusion.89), channel_id=1, source_target_pairs={{0,2},{2,0},{1,3},{3,1},{4,6},{6,4},{5,7},{7,5},{8,10},{10,8},{9,1... | collective-permute-start | bytes 282632 | tf_op jit(solution)/shard_map/ppermute | solution.py:51
  37.2 69.2 %copy-start.9 = (f32[184,128]{1,0:T(8,128)}, f32[184,128]{1,0:T(8,128)S(1)}, u32[]{:S(2)}) copy-start(f32[184,128]{1,0:T(8,128)S(1)} %add.146) | copy-start | bytes 282628
  37.3 7.3 %collective-permute-start.11 = (bf16[56,768]{1,0:T(8,128)(2,1)S(1)}, bf16[56,768]{1,0:T(8,128)(2,1)S(1)}, u32[]{:S(2)}, u32[]{:S(2)}) collective-permute-start(bf16[56,768]{1,0:T(8,128)(2,1)S(1)} %get-tuple-element.26), channel_id=1, source_target_pairs={{0,0},{1,4},{2,8},{3,12},{4,1},{5,5},{6,9},{7,13},{8,128},{9,132},... | collective-permute-start | bytes 258056 | tf_op jit(solution)/shard_map/ppermute | solution.py:175
  42.1 5.5 %collective-permute-start.12 = (bf16[56,768]{1,0:T(8,128)(2,1)S(1)}, bf16[56,768]{1,0:T(8,128)(2,1)S(1)}, u32[]{:S(2)}, u32[]{:S(2)}) collective-permute-start(bf16[56,768]{1,0:T(8,128)(2,1)S(1)} %get-tuple-element.27), channel_id=1, source_target_pairs={{0,1},{1,5},{2,9},{3,13},{4,0},{5,4},{6,8},{7,12},{8,129},{9,133},... | collective-permute-start | bytes 258056 | tf_op jit(solution)/shard_map/ppermute | solution.py:175
  47.6 9.8 %collective-permute-start.13 = (bf16[112,768]{1,0:T(8,128)(2,1)S(1)}, bf16[112,768]{1,0:T(8,128)(2,1)S(1)}, u32[]{:S(2)}, u32[]{:S(2)}) collective-permute-start(bf16[112,768]{1,0:T(8,128)(2,1)S(1)} %maximum_select_fusion.2), channel_id=1, source_target_pairs={{0,128},{128,0},{1,129},{129,1},{2,130},{130,2},{3,131},{131,3},{4... | collective-permute-start | bytes 516104 | tf_op jit(solution)/shard_map/ppermute | solution.py:51
  53.3 17.0 %collective-permute-start.1 = (bf16[320,896]{1,0:T(8,128)(2,1)S(1)}, bf16[320,896]{1,0:T(8,128)(2,1)S(1)}, u32[]{:S(2)}, u32[]{:S(2)}) collective-permute-start(bf16[320,896]{1,0:T(8,128)(2,1)S(1)} %reshape.142), channel_id=1, source_target_pairs={{0,1},{1,0},{2,3},{3,2},{4,5},{5,4},{6,7},{7,6},{8,9},{9,8},{10,11... | collective-permute-start | bytes 1720328 | tf_op jit(solution)/shard_map/ppermute | solution.py:51
  53.4 16.9 %collective-permute-start.2 = (bf16[320,896]{1,0:T(8,128)(2,1)S(1)}, bf16[320,896]{1,0:T(8,128)(2,1)S(1)}, u32[]{:S(2)}, u32[]{:S(2)}) collective-permute-start(bf16[320,896]{1,0:T(8,128)(2,1)S(1)} %reshape.142), channel_id=1, source_target_pairs={{0,2},{2,0},{1,3},{3,1},{4,6},{6,4},{5,7},{7,5},{8,10},{10,8},{9,1... | collective-permute-start | bytes 1720328 | tf_op jit(solution)/shard_map/ppermute | solution.py:51
  58.3 12.0 %copy-start.2 = (bf16[1,3584,512]{2,1,0:T(8,128)(2,1)S(1)}, bf16[1,3584,512]{2,1,0:T(8,128)(2,1)}, u32[]{:S(2)}) copy-start(bf16[1,3584,512]{2,1,0:T(8,128)(2,1)} %param.14) | copy-start | bytes 11010052
  61.8 11.2 %copy-start.5 = (bf16[1,3584,512]{2,1,0:T(8,128)(2,1)S(1)}, bf16[1,3584,512]{2,1,0:T(8,128)(2,1)}, u32[]{:S(2)}) copy-start(bf16[1,3584,512]{2,1,0:T(8,128)(2,1)} %param.15) | copy-start | bytes 11010052
  70.3 3.3 %collective-permute-start.3 = (bf16[320,896]{1,0:T(8,128)(2,1)S(1)}, bf16[320,896]{1,0:T(8,128)(2,1)S(1)}, u32[]{:S(2)}, u32[]{:S(2)}) collective-permute-start(bf16[320,896]{1,0:T(8,128)(2,1)S(1)} %collective-permute-done.2), channel_id=1, source_target_pairs={{0,1},{1,0},{2,3},{3,2},{4,5},{5,4},{6,7},{7,6},{8,9},{9,8},{10,11... | collective-permute-start | bytes 1720328 | tf_op jit(solution)/shard_map/ppermute | solution.py:51
  73.5 2.1 copy-start.3
  76.1 2.2 collective-permute-start.5
  77.2 3.8 %collective-permute-start.4 = (bf16[320,896]{1,0:T(8,128)(2,1)S(1)}, bf16[320,896]{1,0:T(8,128)(2,1)S(1)}, u32[]{:S(2)}, u32[]{:S(2)}) collective-permute-start(bf16[320,896]{1,0:T(8,128)(2,1)S(1)} %convolution_convert_fusion.3), channel_id=1, source_target_pairs={{0,1},{1,0},{2,3},{3,2},{4,5},{5,4},{6,7},{7,6},{8,9},{9,8},{10,11... | collective-permute-start | bytes 1720328 | tf_op jit(solution)/shard_map/ppermute | solution.py:51
  78.8 27.4 %copy-start.12 = (f32[128,2]{0,1:T(2,128)S(1)}, f32[128,2]{0,1:T(2,128)}, u32[]{:S(2)}) copy-start(f32[128,2]{0,1:T(2,128)} %param.13) | copy-start | bytes 3076
  78.8 27.6 %copy-start.6 = (bf16[64,1280]{1,0:T(8,128)(2,1)S(1)}, bf16[64,1280]{1,0:T(8,128)(2,1)}, u32[]{:S(2)}) copy-start(bf16[64,1280]{1,0:T(8,128)(2,1)} %param.21) | copy-start | bytes 491524
  78.9 27.6 %copy-start.7 = (bf16[128,1280]{1,0:T(8,128)(2,1)S(1)}, bf16[128,1280]{1,0:T(8,128)(2,1)}, u32[]{:S(2)}) copy-start(bf16[128,1280]{1,0:T(8,128)(2,1)} %param.18) | copy-start | bytes 983044
  78.9 16.9 %collective-permute-start.6 = (bf16[320,896]{1,0:T(8,128)(2,1)S(1)}, bf16[320,896]{1,0:T(8,128)(2,1)S(1)}, u32[]{:S(2)}, u32[]{:S(2)}) collective-permute-start(bf16[320,896]{1,0:T(8,128)(2,1)S(1)} %add_convert_fusion.1), channel_id=1, source_target_pairs={{0,2},{2,0},{1,3},{3,1},{4,6},{6,4},{5,7},{7,5},{8,10},{10,8},{9,1... | collective-permute-start | bytes 1720328 | tf_op jit(solution)/shard_map/ppermute | solution.py:51
  97.3 29.5 %all-to-all-start.1 = ((bf16[64,35,128]{2,1,0:T(8,128)(2,1)}), bf16[64,35,128]{2,1,0:T(8,128)(2,1)S(1)}, u32[]{:S(2)}, u32[]{:S(2)}) async-start(bf16[64,35,128]{2,1,0:T(8,128)(2,1)} %reshape.143), calls=%async_computation.1 | async-start | bytes 1310720 | tf_op jit(solution)/shard_map/all_to_all | solution.py:66
  107.2 1.3 collective-permute-start.8
  108.5 6.9 %collective-permute-start.9 = (f32[128,64]{1,0:T(8,128)S(1)}, f32[128,64]{1,0:T(8,128)S(1)}, u32[]{:S(2)}, u32[]{:S(2)}) collective-permute-start(f32[128,64]{1,0:T(8,128)S(1)} %add.150), channel_id=1, source_target_pairs={{0,2},{2,0},{1,3},{3,1},{4,6},{6,4},{5,7},{7,5},{8,10},{10,8},{9,1... | collective-permute-start | bytes 98312 | tf_op jit(solution)/shard_map/ppermute | solution.py:51
  142.8 2.5 %collective-permute-start.10 = (bf16[512,896]{1,0:T(8,128)(2,1)S(1)}, bf16[512,896]{1,0:T(8,128)(2,1)S(1)}, u32[]{:S(2)}, u32[]{:S(2)}) collective-permute-start(bf16[512,896]{1,0:T(8,128)(2,1)S(1)} %all_gather.6.own_ref), channel_id=1, source_target_pairs={{0,1},{1,0},{2,3},{3,2},{4,5},{5,4},{6,7},{7,6},{8,9},{9,8},{10,11... | collective-permute-start | bytes 2752520 | tf_op jit(solution)/shard_map/ppermute | solution.py:51
  145.3 1.8 copy-start.1
  149.6 25.2 %copy-start.8 = (bf16[128,1280]{1,0:T(8,128)(2,1)S(1)}, bf16[128,1280]{1,0:T(8,128)(2,1)}, u32[]{:S(2)}) copy-start(bf16[128,1280]{1,0:T(8,128)(2,1)} %param.18) | copy-start | bytes 983044
  149.6 25.2 %copy-start.11 = (f32[128,64]{1,0:T(8,128)S(1)}, f32[128,64]{1,0:T(8,128)}, u32[]{:S(2)}) copy-start(f32[128,64]{1,0:T(8,128)} %add.151) | copy-start | bytes 98308
  149.6 14.1 %collective-permute-start.14 = (bf16[128,768]{1,0:T(8,128)(2,1)S(1)}, bf16[128,768]{1,0:T(8,128)(2,1)S(1)}, u32[]{:S(2)}, u32[]{:S(2)}) collective-permute-start(bf16[128,768]{1,0:T(8,128)(2,1)S(1)} %get-tuple-element.15), channel_id=1, source_target_pairs={{0,0},{1,4},{2,8},{3,12},{4,5},{5,1},{6,13},{7,9},{8,10},{9,14},{1... | collective-permute-start | bytes 589832 | tf_op jit(solution)/shard_map/ppermute | solution.py:255
  153.4 11.6 %collective-permute-start.15 = (bf16[128,768]{1,0:T(8,128)(2,1)S(1)}, bf16[128,768]{1,0:T(8,128)(2,1)S(1)}, u32[]{:S(2)}, u32[]{:S(2)}) collective-permute-start(bf16[128,768]{1,0:T(8,128)(2,1)S(1)} %get-tuple-element.16), channel_id=1, source_target_pairs={{0,8},{1,12},{2,0},{3,4},{4,13},{5,9},{6,5},{7,1},{8,2},{9,6},{10,... | collective-permute-start | bytes 589832 | tf_op jit(solution)/shard_map/ppermute | solution.py:255
  155.3 11.6 %collective-permute-start.16 = (bf16[128,768]{1,0:T(8,128)(2,1)S(1)}, bf16[128,768]{1,0:T(8,128)(2,1)S(1)}, u32[]{:S(2)}, u32[]{:S(2)}) collective-permute-start(bf16[128,768]{1,0:T(8,128)(2,1)S(1)} %get-tuple-element.17), channel_id=1, source_target_pairs={{0,4},{1,0},{2,12},{3,8},{4,1},{5,5},{6,9},{7,13},{8,14},{9,10},{1... | collective-permute-start | bytes 589832 | tf_op jit(solution)/shard_map/ppermute | solution.py:255
  161.7 11.0 %collective-permute-start.17 = (bf16[128,768]{1,0:T(8,128)(2,1)S(1)}, bf16[128,768]{1,0:T(8,128)(2,1)S(1)}, u32[]{:S(2)}, u32[]{:S(2)}) collective-permute-start(bf16[128,768]{1,0:T(8,128)(2,1)S(1)} %get-tuple-element.18), channel_id=1, source_target_pairs={{0,12},{1,8},{2,4},{3,0},{4,9},{5,13},{6,1},{7,5},{8,6},{9,2},{10,... | collective-permute-start | bytes 589832 | tf_op jit(solution)/shard_map/ppermute | solution.py:255
  173.6 51.1 %copy-start.4 = (f32[128,1280]{1,0:T(8,128)}, f32[128,1280]{1,0:T(8,128)S(1)}, u32[]{:S(2)}) copy-start(f32[128,1280]{1,0:T(8,128)S(1)} %get-tuple-element.21) | copy-start | bytes 1966084
  202.8 21.8 %all-to-all-start.3 = ((bf16[64,24,128]{2,1,0:T(8,128)(2,1)}), bf16[64,24,128]{2,1,0:T(8,128)(2,1)S(1)}, u32[]{:S(2)}, u32[]{:S(2)}) async-start(bf16[64,24,128]{2,1,0:T(8,128)(2,1)} %broadcast_in_dim.42), calls=%async_computation.3 | async-start | bytes 786432 | tf_op jit(solution)/shard_map/all_to_all | solution.py:311
  208.6 3.5 %collective-permute-start.18 = (f32[1,128]{1,0:T(1,128)S(1)}, f32[1,128]{1,0:T(1,128)S(1)}, u32[]{:S(2)}, u32[]{:S(2)}) collective-permute-start(f32[1,128]{1,0:T(1,128)S(1)} %slice.82), channel_id=1, source_target_pairs={{0,1},{1,0},{2,3},{3,2},{4,5},{5,4},{6,7},{7,6},{8,9},{9,8},{10,11... | collective-permute-start | bytes 1544 | tf_op jit(solution)/shard_map/ppermute | solution.py:51
  208.7 5.1 %collective-permute-start.19 = (f32[1,128]{1,0:T(1,128)S(1)}, f32[1,128]{1,0:T(1,128)S(1)}, u32[]{:S(2)}, u32[]{:S(2)}) collective-permute-start(f32[1,128]{1,0:T(1,128)S(1)} %slice.82), channel_id=1, source_target_pairs={{0,2},{2,0},{1,3},{3,1},{4,6},{6,4},{5,7},{7,5},{8,10},{10,8},{9,1... | collective-permute-start | bytes 1544 | tf_op jit(solution)/shard_map/ppermute | solution.py:51
  208.8 5.0 %collective-permute-start.20 = (f32[1,128]{1,0:T(1,128)S(1)}, f32[1,128]{1,0:T(1,128)S(1)}, u32[]{:S(2)}, u32[]{:S(2)}) collective-permute-start(f32[1,128]{1,0:T(1,128)S(1)} %slice.82), channel_id=1, source_target_pairs={{0,3},{1,2},{2,1},{3,0},{4,7},{5,6},{6,5},{7,4},{8,11},{9,10},{10,... | collective-permute-start | bytes 1544 | tf_op jit(solution)/shard_map/ppermute | solution.py:315
Sparse Core Ops, SparseCore 0:
  58.4 42.2 all-gather.1

commit v3 on v2

v3 whole, which is shorter than its diff:
```python
import itertools
import math

import jax
import jax.numpy as jnp
from jax import lax
from jax.experimental import pallas as pl
from jax.experimental.pallas import tpu as pltpu
from jax.sharding import Mesh, PartitionSpec as P

route_scale = 2.5
adapter_scale_factor = 0.25
DP = ("yl", "z", "xh", "xl")
MP = ("yh", "c")
ALL = DP + MP
SIZES = (2, 8, 2, 2, 2, 2)


def permutation(target):
    places = list(itertools.product(*(range(size) for size in SIZES)))
    return [(place, places.index(target(*here))) for place, here in enumerate(places)]


def proj_target(yl, z, xh, xl, yh, c):
    return (xh, z, xl, yh, yl, c)


def home_target(step):
    return lambda yl, z, xh, xl, yh, c: (yl, z, xh, yh ^ step, xl, c)


def swap(value, axis):
    return lax.ppermute(value, axis, [(0, 1), (1, 0)])


def mp_sum(value):
    value = value + swap(value, "c")
    return value + swap(value, "yh")


def dot(a, b):
    return jnp.dot(a, b, preferred_element_type=jnp.float32)


def pair_rows(value, axis, index):
    other = swap(value, axis)
    return jnp.where(
        index == 0, jnp.concatenate([value, other]), jnp.concatenate([other, value])
    )


def exchange_slots(rows):
    count, width = rows.shape
    rows = rows.reshape(64, count * width // (64 * 128), 128)
    return lax.all_to_all(rows, DP, split_axis=0, concat_axis=0, tiled=True).reshape(count, width)


def product_kernel(order_ref, own_ref, own_far_ref, pair_ref, pair_far_ref, block_ref, *refs):
    outs, near_rows, far_rows, total = refs[:2], refs[2], refs[3], refs[4]
    rows, width = own_ref.shape

    @pl.when(pl.program_id(0) == 0)
    def _():
        near_rows[:rows] = own_ref[...]
        near_rows[rows:] = pair_ref[...]
        far_rows[:rows] = own_far_ref[...]
        far_rows[rows:] = pair_far_ref[...]

    core = order_ref[2]
    near = block_ref[pl.ds(pl.multiple_of(core * width, 128), width), :]
    far = block_ref[pl.ds(pl.multiple_of((1 - core) * width, 128), width), :]
    total[...] = dot(near_rows[...], near) + dot(far_rows[...], far)
    for step in range(2):
        here = pl.ds(pl.multiple_of(order_ref[step] * rows, 128), rows)
        outs[step][...] = total[here, :].astype(jnp.bfloat16)


def product_pieces(order, own, own_far, pair, pair_far, block):
    rows, width = own.shape
    depth, wide = block.shape
    cut = 256
    whole = pl.BlockSpec((rows, width), lambda i: (0, 0))
    return pl.pallas_call(
        product_kernel,
        grid=(wide // cut,),
        out_shape=[jax.ShapeDtypeStruct((rows, wide), jnp.bfloat16)] * 2,
        in_specs=[pl.BlockSpec(memory_space=pltpu.SMEM)]
        + [whole] * 4
        + [pl.BlockSpec((depth, cut), lambda i: (0, i))],
        out_specs=[pl.BlockSpec((rows, cut), lambda i: (0, i))] * 2,
        scratch_shapes=[
            pltpu.VMEM((2 * rows, width), jnp.bfloat16),
            pltpu.VMEM((2 * rows, width), jnp.bfloat16),
            pltpu.VMEM((2 * rows, cut), jnp.float32),
        ],
        compiler_params=pltpu.CompilerParams(vmem_limit_bytes=24 * 1024 * 1024),
        cost_estimate=pl.CostEstimate(
            flops=4 * rows * depth * wide, bytes_accessed=6_000_000, transcendentals=0
        ),
    )(order, own, own_far, pair, pair_far, block)


def body(
    tokens,
    routes,
    expert_gate_affinity,
    expert_gate_weight,
    expert_up_weight,
    expert_down_weight,
    proj,
    student_hidden_input,
    student_norm_weight,
    adapter_down_matrix,
    adapter_up_matrix,
):
    experts = 64
    mp_count = 4
    tok_rows, part_width = tokens.shape
    topk_count = routes.shape[1]
    assigned = tok_rows * topk_count
    capacity = 5
    slot_count = experts * capacity
    rank = adapter_up_matrix.shape[0]
    yl, xh, xl, yh, core = (lax.axis_index(name) for name in ("yl", "xh", "xl", "yh", "c"))
    mi = yh * 2 + core

    proj_rows = lax.ppermute(proj, ALL, permutation(proj_target))

    flat_routes = routes.reshape(assigned)
    onehot_e = (flat_routes[:, None] == jnp.arange(experts, dtype=jnp.int32)[None, :]).astype(
        jnp.int32
    )
    position = jnp.sum((jnp.cumsum(onehot_e, axis=0) - onehot_e) * onehot_e, axis=1)
    slot_index = flat_routes * capacity + position
    slot_hit = (jnp.arange(slot_count, dtype=jnp.int32)[:, None] == slot_index[None, :]).astype(
        jnp.bfloat16
    )
    token_hit = (
        jnp.arange(assigned, dtype=jnp.int32)[:, None] // topk_count
        == jnp.arange(tok_rows, dtype=jnp.int32)[None, :]
    ).astype(jnp.bfloat16)
    placing = dot(slot_hit, token_hit).astype(jnp.bfloat16)
    outgoing = dot(placing, tokens).astype(jnp.bfloat16)

    outgoing, proj_rows = lax.optimization_barrier((outgoing, proj_rows))
    arrived = exchange_slots(outgoing)
    proj_rows = pair_rows(proj_rows, "xh", xh)
    proj_rows = pair_rows(proj_rows, "yl", yl)
    arrived, proj_rows = lax.optimization_barrier((arrived, proj_rows))
    proj_block = lax.all_gather(proj_rows, "z", axis=0, tiled=True)

    arrived_y = swap(arrived, "yh")
    arrived_c = swap(arrived, "c")
    arrived_yc = swap(arrived_y, "c")
    parts = (
        (arrived, mi),
        (arrived_c, yh * 2 + 1 - core),
        (arrived_y, (1 - yh) * 2 + core),
        (arrived_yc, (1 - yh) * 2 + 1 - core),
    )
    gate_proj = up_proj = 0.0
    for rows, place in parts:
        gate_proj = gate_proj + dot(
            rows, lax.dynamic_slice_in_dim(expert_gate_weight[0], place * part_width, part_width, 0)
        )
        up_proj = up_proj + dot(
            rows, lax.dynamic_slice_in_dim(expert_up_weight[0], place * part_width, part_width, 0)
        )
    hidden = (jax.nn.silu(gate_proj) * up_proj).astype(jnp.bfloat16)

    def out_part(place):
        return dot(
            hidden, lax.dynamic_slice_in_dim(expert_down_weight[0], place * part_width, part_width, 1)
        )

    far = swap(out_part((1 - yh) * 2 + 1 - core).astype(jnp.bfloat16), "c")
    near = swap(out_part(yh * 2 + 1 - core).astype(jnp.bfloat16), "c")
    far = out_part((1 - yh) * 2 + core).astype(jnp.bfloat16).astype(jnp.float32) + far.astype(
        jnp.float32
    )
    far = swap(far.astype(jnp.bfloat16), "yh")
    expert_out = (
        out_part(mi).astype(jnp.bfloat16).astype(jnp.float32)
        + near.astype(jnp.float32)
        + far.astype(jnp.float32)
    ).astype(jnp.bfloat16)
    returned = exchange_slots(expert_out)

    expert_out, student_hidden_input = lax.optimization_barrier((expert_out, student_hidden_input))
    student = student_hidden_input.astype(jnp.float32)
    gain = student_norm_weight.astype(jnp.float32)
    student_width = student.shape[1] * mp_count
    square_sum = jnp.sum(student * student, axis=-1, keepdims=True)
    low_part = dot((student * gain).astype(jnp.bfloat16), adapter_down_matrix)
    stats = mp_sum(
        jnp.concatenate([low_part, jnp.broadcast_to(square_sum, (tok_rows, rank))], axis=1)
    )
    inverse = lax.rsqrt(stats[:, rank : rank + 1] / student_width + 1e-06)
    lowrank = (stats[:, :rank] * inverse).astype(jnp.bfloat16)
    normed = (student * inverse * gain).astype(jnp.bfloat16)
    student_out = student + adapter_scale_factor * dot(lowrank, adapter_up_matrix)
    returned, lowrank, normed, student_out = lax.optimization_barrier(
        (returned, lowrank, normed, student_out)
    )


    weights = (
        route_scale * expert_gate_affinity / jnp.sum(expert_gate_affinity, axis=-1, keepdims=True)
    )
    combine = jnp.dot(
        slot_hit.astype(jnp.float32) * weights.reshape(assigned)[None, :],
        token_hit.astype(jnp.float32),
        precision=lax.Precision.HIGHEST,
    )
    teacher = lax.dot_general(
        combine,
        returned.astype(jnp.float32),
        (((0,), (0,)), ((), ())),
        precision=lax.Precision.HIGHEST,
    ).astype(jnp.bfloat16)

    teacher_far = swap(teacher, "c")
    pair = swap(teacher, "xl")
    order = jnp.stack([yh ^ xl, yh ^ xl ^ 1, core])
    pieces = product_pieces(order, teacher, teacher_far, pair, swap(pair, "c"), proj_block)
    pieces = [
        lax.ppermute(piece, ALL, permutation(home_target(step))).astype(jnp.float32)
        for step, piece in enumerate(pieces)
    ]
    target = pieces[0] + pieces[1]

    output_difference = student_out - target
    tokens_all = tok_rows * experts
    scale = 1.0 / math.sqrt(tokens_all)
    scaled = (output_difference * scale).astype(jnp.bfloat16)
    loss_here = jnp.sum(output_difference * output_difference)
    back_part = lax.dot_general(
        scaled, adapter_up_matrix, (((1,), (1,)), ((), ())), preferred_element_type=jnp.float32
    )
    back_low = (adapter_scale_factor * mp_sum(back_part)).astype(jnp.bfloat16)
    over_tokens = (((0,), (0,)), ((), ()))
    up_part = adapter_scale_factor * lax.dot_general(
        lowrank, scaled, over_tokens, preferred_element_type=jnp.float32
    )
    down_part = lax.dot_general(back_low, normed, over_tokens, preferred_element_type=jnp.float32)

    lanes = 128
    columns = up_part.shape[1]
    tiles = rank // 8 * (columns // lanes)
    first = lax.reduce_precision(loss_here, 8, 7)
    second = lax.reduce_precision(loss_here - first, 8, 7)
    third = loss_here - first - second
    lane = jnp.arange(lanes)
    loss_row = jnp.where(
        lane == 0, first, jnp.where(lane == 1, second, jnp.where(lane == 2, third, 0.0))
    )

    def to_tiles(value):
        value = value.astype(jnp.bfloat16).reshape(rank // 8, 8, columns // lanes, lanes)
        return value.transpose(0, 2, 1, 3).reshape(tiles, 8, lanes)

    def from_tiles(value):
        value = value.reshape(rank // 8, columns // lanes, 8, lanes).transpose(0, 2, 1, 3)
        return value.reshape(rank, columns).astype(jnp.float32)

    bundle = jnp.concatenate([to_tiles(up_part), to_tiles(down_part)])
    bundle = jnp.concatenate(
        [
            bundle[: 2 * experts].reshape(experts, 16, lanes),
            bundle[2 * experts :].reshape(experts, 4, lanes),
            jnp.broadcast_to(loss_row.astype(jnp.bfloat16), (experts, 4, lanes)),
        ],
        axis=1,
    )
    bundle = lax.all_to_all(bundle, DP, split_axis=0, concat_axis=0, tiled=True)
    summed = jnp.sum(bundle.astype(jnp.float32), axis=0)
    grads = jnp.broadcast_to(summed.astype(jnp.bfloat16), (experts, 24, lanes))
    grads = lax.all_to_all(grads, DP, split_axis=0, concat_axis=0, tiled=True)
    loss_row = summed[20:21]
    cross = [(i, 3 - i) for i in range(4)]
    loss_row = (loss_row + swap(loss_row, "c")) + (
        swap(loss_row, "yh") + lax.ppermute(loss_row, MP, cross)
    )
    loss = jnp.sum(loss_row) / (tokens_all * student_width)
    grads = jnp.concatenate(
        [
            grads[:, :16].reshape(2 * experts, 8, lanes),
            grads[:, 16:20].reshape(experts // 2, 8, lanes),
        ]
    )
    up_matrix_gradient = from_tiles(grads[:tiles])
    grad_a = from_tiles(grads[tiles:]).T
    return (target, grad_a, up_matrix_gradient, loss)


def solution(mesh):
    fine = Mesh(mesh.devices.reshape(SIZES), ALL)
    placed = (
        P(DP, MP),
        P(DP, None),
        P(DP, None),
        P(DP, None, MP),
        P(DP, None, MP),
        P(DP, MP, None),
        P(DP, MP),
        P(DP, MP),
        P(MP),
        P(MP, None),
        P(None, MP),
    )
    return jax.shard_map(
        body,
        mesh=fine,
        in_specs=placed,
        out_specs=(P(DP, MP), P(MP, None), P(None, MP), P()),
        check_vma=False,
    )
```

time: 235 us -> 222 us (0.945)
  the two profiles are of different devices: /device:TPU:48 before, /device:TPU:32 now
where the time goes in v3:
time: 222 us; the launch traced here: 221 us
  waiting for transfers between devices  82.9 us (37%)
  starting transfers between devices  62.2 us (28%)
  blocking collectives  21.4 us (10%)
  between operations  20 us (9%)
  matrix products  13.8 us (6%)
  local copies, waits for them, and re-layouts  9.82 us (4%)
  other arithmetic  8.02 us (4%)
  Pallas kernels  3.28 us (1%)
    ppermute x17, waiting for transfers between devices, swap(): return lax.ppermute(value, axis, [(0, 1), (1, 0)])  43.6 us
    all_to_all x2, starting transfers between devices, exchange_slots(): lax.all_to_all(rows, DP, split_axis=0, concat_axis=0, tiled=True)  29.7 us
    all_to_all x2, waiting for transfers between devices, exchange_slots(): lax.all_to_all(rows, DP, split_axis=0, concat_axis=0, tiled=True)  22.5 us
    all_to_all x1, blocking collectives, body(): bundle = lax.all_to_all(bundle, DP, split_axis=0, concat_axis=0, tiled=True)  21.4 us
    ppermute x17, starting transfers between devices, swap(): return lax.ppermute(value, axis, [(0, 1), (1, 0)])  19.7 us
    dot_general x15, matrix products, dot(): return jnp.dot(a, b, preferred_element_type=jnp.float32)  12.2 us
    ppermute x2, waiting for transfers between devices, body(): lax.ppermute(piece, ALL, permutation(home_target(step))).astype(jnp.float32)  8.59 us
    all_to_all x1, waiting for transfers between devices, body(): grads = lax.all_to_all(grads, DP, split_axis=0, concat_axis=0, tiled=True)  6.44 us
  transfers between devices with their start and end apart: 25, of which 15 were waited for; matrix products, arithmetic and copies ran while one was open for 10% of the time, Pallas kernels for 0%

profile of v3, /device:TPU:32, one launch (start us, length us, event | category | flops | bytes accessed | tf_op | source)
XLA Modules:
  0.0 221.3 jit_solution(6234645814579203138)
XLA Ops:
  7.2 1.7 collective-permute-start
  8.9 0.8 copy.15
  10.0 0.6 reduce-window.6
  10.9 0.6 convolution_convert_fusion.5
  11.5 1.4 reshape.141
  12.9 18.6 %all-to-all-start = ((bf16[64,35,128]{2,1,0:T(8,128)(2,1)}), bf16[64,35,128]{2,1,0:T(8,128)(2,1)S(1)}, u32[]{:S(2)}, u32[]{:S(2)}) async-start(bf16[64,35,128]{2,1,0:T(8,128)(2,1)} %reshape.141), calls=%async_computation | async-start | bytes 1310720 | tf_op jit(solution)/shard_map/all_to_all | solution.py:55
  31.6 3.1 %collective-permute-start.1 = (bf16[56,1280]{1,0:T(8,128)(2,1)S(1)}, bf16[56,1280]{1,0:T(8,128)(2,1)S(1)}, u32[]{:S(2)}, u32[]{:S(2)}) collective-permute-start(bf16[56,1280]{1,0:T(8,128)(2,1)S(1)} %collective-permute-done), channel_id=1, source_target_pairs={{0,8},{8,0},{1,9},{9,1},{2,10},{10,2},{3,11},{11,3},{4,12},{12,4},... | collective-permute-start | bytes 430088 | tf_op jit(solution)/shard_map/ppermute | solution.py:33
  34.7 5.1 %collective-permute-done.1 = bf16[56,1280]{1,0:T(8,128)(2,1)S(1)} collective-permute-done((bf16[56,1280]{1,0:T(8,128)(2,1)S(1)}, bf16[56,1280]{1,0:T(8,128)(2,1)S(1)}, u32[]{:S(2)}, u32[]{:S(2)}) %collective-permute-start.1) | collective-permute-done | bytes 143392 | tf_op jit(solution)/shard_map/ppermute | solution.py:33
  39.8 1.5 collective-permute-start.2
  41.4 7.2 %collective-permute-done.2 = bf16[112,1280]{1,0:T(8,128)(2,1)S(1)} collective-permute-done((bf16[112,1280]{1,0:T(8,128)(2,1)S(1)}, bf16[112,1280]{1,0:T(8,128)(2,1)S(1)}, u32[]{:S(2)}, u32[]{:S(2)}) %collective-permute-start.2) | collective-permute-done | bytes 286752 | tf_op jit(solution)/shard_map/ppermute | solution.py:33
  48.6 0.9 maximum_select_fusion
  49.5 2.0 all-to-all-done
  51.5 0.6 reshape.142
  52.2 2.8 %collective-permute-start.4 = (bf16[320,896]{1,0:T(8,128)(2,1)S(1)}, bf16[320,896]{1,0:T(8,128)(2,1)S(1)}, u32[]{:S(2)}, u32[]{:S(2)}) collective-permute-start(bf16[320,896]{1,0:T(8,128)(2,1)S(1)} %reshape.142), channel_id=1, source_target_pairs={{0,2},{2,0},{1,3},{3,1},{4,6},{6,4},{5,7},{7,5},{8,10},{10,8},{9,1... | collective-permute-start | bytes 1720328 | tf_op jit(solution)/shard_map/ppermute | solution.py:33
  55.0 1.8 fusion.13
  56.9 1.8 fusion.18
  58.7 6.5 %collective-permute-done.4 = bf16[320,896]{1,0:T(8,128)(2,1)S(1)} collective-permute-done((bf16[320,896]{1,0:T(8,128)(2,1)S(1)}, bf16[320,896]{1,0:T(8,128)(2,1)S(1)}, u32[]{:S(2)}, u32[]{:S(2)}) %collective-permute-start.4) | collective-permute-done | bytes 573472 | tf_op jit(solution)/shard_map/ppermute | solution.py:33
  65.2 1.7 convolution_add_fusion.2
  66.9 0.5 convolution_add_fusion.5
  67.5 0.5 convolution_add_fusion.1
  68.0 0.5 convolution_add_fusion.4
  68.5 0.5 convolution_add_fusion.3
  69.0 0.6 multiply_convert_fusion.1
  69.6 1.0 copy-done.3
  70.6 0.5 convolution_convert_fusion.1
  71.1 0.6 collective-permute-start.7
  71.7 0.5 convolution_convert_fusion.3
  72.3 1.0 collective-permute-done.7
  73.3 0.5 add_convert_fusion.1
  73.8 2.8 %collective-permute-start.8 = (bf16[320,896]{1,0:T(8,128)(2,1)S(1)}, bf16[320,896]{1,0:T(8,128)(2,1)}, u32[]{:S(2)}, u32[]{:S(2)}) collective-permute-start(bf16[320,896]{1,0:T(8,128)(2,1)S(1)} %add_convert_fusion.1), channel_id=1, source_target_pairs={{0,2},{2,0},{1,3},{3,1},{4,6},{6,4},{5,7},{7,5},{8,10},{10,8},{9,1... | collective-permute-start | bytes 1720328 | tf_op jit(solution)/shard_map/ppermute | solution.py:33
  76.6 1.7 fusion.3
  78.3 12.4 %collective-permute-done.8 = bf16[320,896]{1,0:T(8,128)(2,1)} collective-permute-done((bf16[320,896]{1,0:T(8,128)(2,1)S(1)}, bf16[320,896]{1,0:T(8,128)(2,1)}, u32[]{:S(2)}, u32[]{:S(2)}) %collective-permute-start.8) | collective-permute-done | bytes 573472 | tf_op jit(solution)/shard_map/ppermute | solution.py:33
  90.7 1.3 add_convert_fusion
  93.0 1.0 collective-permute-done.9
  94.0 2.8 %collective-permute-start.10 = (f32[128,128]{0,1:T(8,128)S(1)}, f32[128,128]{0,1:T(8,128)S(1)}, u32[]{:S(2)}, u32[]{:S(2)}) collective-permute-start(f32[128,128]{0,1:T(8,128)S(1)} %fusion.57), channel_id=1, source_target_pairs={{0,2},{2,0},{1,3},{3,1},{4,6},{6,4},{5,7},{7,5},{8,10},{10,8},{9,1... | collective-permute-start | bytes 196616 | tf_op jit(solution)/shard_map/ppermute | solution.py:33
  96.8 0.4 fusion.39
  97.1 1.4 reshape.143
  98.6 11.1 %all-to-all-start.1 = ((bf16[64,35,128]{2,1,0:T(8,128)(2,1)}), bf16[64,35,128]{2,1,0:T(8,128)(2,1)S(1)}, u32[]{:S(2)}, u32[]{:S(2)}) async-start(bf16[64,35,128]{2,1,0:T(8,128)(2,1)} %reshape.143), calls=%async_computation.1 | async-start | bytes 1310720 | tf_op jit(solution)/shard_map/all_to_all | solution.py:55
  110.2 20.5 %all-to-all-done.1 = bf16[64,35,128]{2,1,0:T(8,128)(2,1)S(1)} async-done(((bf16[64,35,128]{2,1,0:T(8,128)(2,1)}), bf16[64,35,128]{2,1,0:T(8,128)(2,1)S(1)}, u32[]{:S(2)}, u32[]{:S(2)}) %all-to-all-start.1) | async-done | bytes 573472 | tf_op jit(solution)/shard_map/all_to_all | solution.py:55
  130.7 0.6 reshape.144
  131.3 0.6 convolution_convert_fusion.6.own_ref
  131.9 1.0 collective-permute-start.12
  132.9 5.1 %collective-permute-done.12.pair_ref = bf16[128,896]{1,0:T(8,128)(2,1)S(1)} collective-permute-done((bf16[128,896]{1,0:T(8,128)(2,1)S(1)}, bf16[128,896]{1,0:T(8,128)(2,1)S(1)}, u32[]{:S(2)}, u32[]{:S(2)}) %collective-permute-start.12) | collective-permute-done | bytes 229408 | tf_op jit(solution)/shard_map/ppermute | solution.py:33
  138.1 1.4 collective-permute-done.13.pair_far_ref
  139.5 2.3 %copy-done.1 = bf16[1792,1280]{1,0:T(8,128)(2,1)S(1)} copy-done((bf16[1792,1280]{1,0:T(8,128)(2,1)S(1)}, bf16[1792,1280]{1,0:T(8,128)(2,1)}, u32[]{:S(2)}) %copy-start.1) | copy-done | bytes 4587544
  141.8 3.3 %shard_map.138 = (bf16[128,1280]{1,0:T(8,128)(2,1)S(1)}, bf16[128,1280]{1,0:T(8,128)(2,1)S(1)}) custom-call(s32[3]{0:T(128)S(1)} %pad_add_fusion.order_ref, bf16[128,896]{1,0:T(8,128)(2,1)S(1)} %convolution_convert_fusion.6.own_ref, bf16[128,896]{1,0:T(8,128)(2,1)S(1)} %collective-permute-done.11.own_far_ref, ...), custom_call_target="tpu_custom_call" | custom-call | flops 1174405120 | bytes 6000000 | tf_op jit(solution)/shard_map/pallas_call | solution.py:83
  145.1 0.7 collective-permute-start.14
  145.8 4.3 %collective-permute-start.15 = (bf16[128,1280]{1,0:T(8,128)(2,1)S(1)}, bf16[128,1280]{1,0:T(8,128)(2,1)S(1)}, u32[]{:S(2)}, u32[]{:S(2)}) collective-permute-start(bf16[128,1280]{1,0:T(8,128)(2,1)S(1)} %get-tuple-element.22), channel_id=1, source_target_pairs={{0,4},{1,5},{2,0},{3,1},{4,6},{5,7},{6,2},{7,3},{8,12},{9,13},{10,... | collective-permute-start | bytes 983048 | tf_op jit(solution)/shard_map/ppermute | solution.py:227
  150.1 8.6 %collective-permute-done.15 = bf16[128,1280]{1,0:T(8,128)(2,1)S(1)} collective-permute-done((bf16[128,1280]{1,0:T(8,128)(2,1)S(1)}, bf16[128,1280]{1,0:T(8,128)(2,1)S(1)}, u32[]{:S(2)}, u32[]{:S(2)}) %collective-permute-start.15) | collective-permute-done | bytes 327712 | tf_op jit(solution)/shard_map/ppermute | solution.py:227
  159.4 0.8 multiply_reduce_fusion
  163.8 2.1 collective-permute-start.17
  165.9 1.3 fusion.72
  167.2 2.1 collective-permute-done.17
  169.7 21.4 %all_to_all.20 = bf16[64,24,128]{2,1,0:T(8,128)(2,1)S(1)} all-to-all(bf16[64,24,128]{2,1,0:T(8,128)(2,1)S(1)} %pad_maximum_fusion), channel_id=1, replica_groups=mesh['yl'=2,'z'=8,'xh'=2,'xl'=2,'yh'=2,'c'=2] {'yl','z','xh','xl'}, dimensions={0} | all-to-all | bytes 786432 | tf_op jit(solution)/shard_map/all_to_all | solution.py:275
  191.2 0.8 broadcast_in_dim.41
  192.0 5.0 %all-to-all-start.3 = ((bf16[64,24,128]{2,1,0:T(8,128)(2,1)}), bf16[64,24,128]{2,1,0:T(8,128)(2,1)S(1)}, u32[]{:S(2)}, u32[]{:S(2)}) async-start(bf16[64,24,128]{2,1,0:T(8,128)(2,1)} %broadcast_in_dim.41), calls=%async_computation.3 | async-start | bytes 786432 | tf_op jit(solution)/shard_map/all_to_all | solution.py:278
  197.2 2.4 %collective-permute-start.19 = (f32[1,128]{1,0:T(1,128)S(1)}, f32[1,128]{1,0:T(1,128)S(1)}, u32[]{:S(2)}, u32[]{:S(2)}) collective-permute-start(f32[1,128]{1,0:T(1,128)S(1)} %slice.53), channel_id=1, source_target_pairs={{0,2},{2,0},{1,3},{3,1},{4,6},{6,4},{5,7},{7,5},{8,10},{10,8},{9,1... | collective-permute-start | bytes 1544 | tf_op jit(solution)/shard_map/ppermute | solution.py:33
  199.6 0.9 collective-permute-start.20
  200.5 1.8 collective-permute-done.19
  202.3 1.8 collective-permute-done.20
  204.1 0.6 add_reduce_fusion
  205.3 6.4 %all-to-all-done.3 = bf16[64,24,128]{2,1,0:T(8,128)(2,1)S(1)} async-done(((bf16[64,24,128]{2,1,0:T(8,128)(2,1)}), bf16[64,24,128]{2,1,0:T(8,128)(2,1)S(1)}, u32[]{:S(2)}, u32[]{:S(2)}) %all-to-all-start.3) | async-done | bytes 393248 | tf_op jit(solution)/shard_map/all_to_all | solution.py:278
  211.8 0.7 convert_bitcast_fusion.1
  212.6 0.7 convert_bitcast_fusion
  (81 shorter events, 3.7 us)
Async XLA Ops:
  7.2 3.8 %copy-start = (bf16[128,896]{1,0:T(8,128)(2,1)S(1)}, bf16[128,896]{1,0:T(8,128)(2,1)}, u32[]{:S(2)}) copy-start(bf16[128,896]{1,0:T(8,128)(2,1)} %param.11) | copy-start | bytes 688132
  7.2 4.3 %collective-permute-start = (bf16[56,1280]{1,0:T(8,128)(2,1)}, bf16[56,1280]{1,0:T(8,128)(2,1)S(1)}, u32[]{:S(2)}, u32[]{:S(2)}) collective-permute-start(bf16[56,1280]{1,0:T(8,128)(2,1)} %param.17), channel_id=1, source_target_pairs={{0,0},{1,1},{2,4},{3,5},{4,8},{5,9},{6,12},{7,13},{8,128},{9,129},... | collective-permute-start | bytes 430088 | tf_op jit(solution)/shard_map/ppermute | solution.py:127
  12.9 38.6 %all-to-all-start = ((bf16[64,35,128]{2,1,0:T(8,128)(2,1)}), bf16[64,35,128]{2,1,0:T(8,128)(2,1)S(1)}, u32[]{:S(2)}, u32[]{:S(2)}) async-start(bf16[64,35,128]{2,1,0:T(8,128)(2,1)} %reshape.141), calls=%async_computation | async-start | bytes 1310720 | tf_op jit(solution)/shard_map/all_to_all | solution.py:55
  31.6 107.9 %all-gather.2.cloned.1.call-start = ((), (), s32[]{:S(2)}) async-start(), calls=%async_computation.4 | async-start | bytes 5160960 | tf_op jit(solution)/shard_map/all_gather | solution.py:150
  31.6 8.2 %collective-permute-start.1 = (bf16[56,1280]{1,0:T(8,128)(2,1)S(1)}, bf16[56,1280]{1,0:T(8,128)(2,1)S(1)}, u32[]{:S(2)}, u32[]{:S(2)}) collective-permute-start(bf16[56,1280]{1,0:T(8,128)(2,1)S(1)} %collective-permute-done), channel_id=1, source_target_pairs={{0,8},{8,0},{1,9},{9,1},{2,10},{10,2},{3,11},{11,3},{4,12},{12,4},... | collective-permute-start | bytes 430088 | tf_op jit(solution)/shard_map/ppermute | solution.py:33
  39.8 8.7 %collective-permute-start.2 = (bf16[112,1280]{1,0:T(8,128)(2,1)S(1)}, bf16[112,1280]{1,0:T(8,128)(2,1)S(1)}, u32[]{:S(2)}, u32[]{:S(2)}) collective-permute-start(bf16[112,1280]{1,0:T(8,128)(2,1)S(1)} %maximum_select_fusion.1), channel_id=1, source_target_pairs={{0,128},{128,0},{1,129},{129,1},{2,130},{130,2},{3,131},{131,3},{4... | collective-permute-start | bytes 860168 | tf_op jit(solution)/shard_map/ppermute | solution.py:33
  52.2 13.1 %collective-permute-start.4 = (bf16[320,896]{1,0:T(8,128)(2,1)S(1)}, bf16[320,896]{1,0:T(8,128)(2,1)S(1)}, u32[]{:S(2)}, u32[]{:S(2)}) collective-permute-start(bf16[320,896]{1,0:T(8,128)(2,1)S(1)} %reshape.142), channel_id=1, source_target_pairs={{0,2},{2,0},{1,3},{3,1},{4,6},{6,4},{5,7},{7,5},{8,10},{10,8},{9,1... | collective-permute-start | bytes 1720328 | tf_op jit(solution)/shard_map/ppermute | solution.py:33
  55.0 10.2 %collective-permute-start.3 = (bf16[320,896]{1,0:T(8,128)(2,1)S(1)}, bf16[320,896]{1,0:T(8,128)(2,1)S(1)}, u32[]{:S(2)}, u32[]{:S(2)}) collective-permute-start(bf16[320,896]{1,0:T(8,128)(2,1)S(1)} %reshape.142), channel_id=1, source_target_pairs={{0,1},{1,0},{2,3},{3,2},{4,5},{5,4},{6,7},{7,6},{8,9},{9,8},{10,11... | collective-permute-start | bytes 1720328 | tf_op jit(solution)/shard_map/ppermute | solution.py:33
  55.0 11.9 %copy-start.2 = (bf16[1,3584,512]{2,1,0:T(8,128)(2,1)S(1)}, bf16[1,3584,512]{2,1,0:T(8,128)(2,1)}, u32[]{:S(2)}) copy-start(bf16[1,3584,512]{2,1,0:T(8,128)(2,1)} %param.14) | copy-start | bytes 11010052
  56.9 10.6 %copy-start.6 = (bf16[1,3584,512]{2,1,0:T(8,128)(2,1)S(1)}, bf16[1,3584,512]{2,1,0:T(8,128)(2,1)}, u32[]{:S(2)}) copy-start(bf16[1,3584,512]{2,1,0:T(8,128)(2,1)} %param.15) | copy-start | bytes 11010052
  65.2 3.3 %collective-permute-start.5 = (bf16[320,896]{1,0:T(8,128)(2,1)S(1)}, bf16[320,896]{1,0:T(8,128)(2,1)S(1)}, u32[]{:S(2)}, u32[]{:S(2)}) collective-permute-start(bf16[320,896]{1,0:T(8,128)(2,1)S(1)} %collective-permute-done.4), channel_id=1, source_target_pairs={{0,1},{1,0},{2,3},{3,2},{4,5},{5,4},{6,7},{7,6},{8,9},{9,8},{10,11... | collective-permute-start | bytes 1720328 | tf_op jit(solution)/shard_map/ppermute | solution.py:33
  68.5 2.1 copy-start.3
  70.6 6.0 %copy-start.8 = (bf16[1280]{0:T(1024)(128)(2,1)S(1)}, bf16[1280]{0:T(1024)(128)(2,1)}, u32[]{:S(2)}) copy-start(bf16[1280]{0:T(1024)(128)(2,1)} %param.19) | copy-start | bytes 7684
  70.6 6.0 %copy-start.9 = (f32[128,2]{0,1:T(2,128)S(1)}, f32[128,2]{0,1:T(2,128)}, u32[]{:S(2)}) copy-start(f32[128,2]{0,1:T(2,128)} %param.13) | copy-start | bytes 3076
  71.1 2.2 collective-permute-start.7
  72.2 19.8 %copy-start.4 = (bf16[128,1280]{1,0:T(8,128)(2,1)S(1)}, bf16[128,1280]{1,0:T(8,128)(2,1)}, u32[]{:S(2)}) copy-start(bf16[128,1280]{1,0:T(8,128)(2,1)} %param.18) | copy-start | bytes 983044
  72.2 20.0 %copy-start.10 = (bf16[1280,64]{0,1:T(8,128)(2,1)S(1)}, bf16[1280,64]{0,1:T(8,128)(2,1)}, u32[]{:S(2)}) copy-start(bf16[1280,64]{0,1:T(8,128)(2,1)} %param.20) | copy-start | bytes 491524
  72.2 6.1 %collective-permute-start.6 = (bf16[320,896]{1,0:T(8,128)(2,1)S(1)}, bf16[320,896]{1,0:T(8,128)(2,1)S(1)}, u32[]{:S(2)}, u32[]{:S(2)}) collective-permute-start(bf16[320,896]{1,0:T(8,128)(2,1)S(1)} %convolution_convert_fusion.3), channel_id=1, source_target_pairs={{0,1},{1,0},{2,3},{3,2},{4,5},{5,4},{6,7},{7,6},{8,9},{9,8},{10,11... | collective-permute-start | bytes 1720328 | tf_op jit(solution)/shard_map/ppermute | solution.py:33
  73.8 17.0 %collective-permute-start.8 = (bf16[320,896]{1,0:T(8,128)(2,1)S(1)}, bf16[320,896]{1,0:T(8,128)(2,1)}, u32[]{:S(2)}, u32[]{:S(2)}) collective-permute-start(bf16[320,896]{1,0:T(8,128)(2,1)S(1)} %add_convert_fusion.1), channel_id=1, source_target_pairs={{0,2},{2,0},{1,3},{3,1},{4,6},{6,4},{5,7},{7,5},{8,10},{10,8},{9,1... | collective-permute-start | bytes 1720328 | tf_op jit(solution)/shard_map/ppermute | solution.py:33
  78.3 31.4 %copy-start.7 = (bf16[64,1280]{1,0:T(8,128)(2,1)S(1)}, bf16[64,1280]{1,0:T(8,128)(2,1)}, u32[]{:S(2)}) copy-start(bf16[64,1280]{1,0:T(8,128)(2,1)} %param.21) | copy-start | bytes 491524
  92.5 1.5 collective-permute-start.9
  94.0 15.7 %collective-permute-start.10 = (f32[128,128]{0,1:T(8,128)S(1)}, f32[128,128]{0,1:T(8,128)S(1)}, u32[]{:S(2)}, u32[]{:S(2)}) collective-permute-start(f32[128,128]{0,1:T(8,128)S(1)} %fusion.57), channel_id=1, source_target_pairs={{0,2},{2,0},{1,3},{3,1},{4,6},{6,4},{5,7},{7,5},{8,10},{10,8},{9,1... | collective-permute-start | bytes 196616 | tf_op jit(solution)/shard_map/ppermute | solution.py:33
  98.6 32.1 %all-to-all-start.1 = ((bf16[64,35,128]{2,1,0:T(8,128)(2,1)}), bf16[64,35,128]{2,1,0:T(8,128)(2,1)S(1)}, u32[]{:S(2)}, u32[]{:S(2)}) async-start(bf16[64,35,128]{2,1,0:T(8,128)(2,1)} %reshape.143), calls=%async_computation.1 | async-start | bytes 1310720 | tf_op jit(solution)/shard_map/all_to_all | solution.py:55
  131.9 6.1 %collective-permute-start.12 = (bf16[128,896]{1,0:T(8,128)(2,1)S(1)}, bf16[128,896]{1,0:T(8,128)(2,1)S(1)}, u32[]{:S(2)}, u32[]{:S(2)}) collective-permute-start(bf16[128,896]{1,0:T(8,128)(2,1)S(1)} %convolution_convert_fusion.6.own_ref), channel_id=1, source_target_pairs={{0,4},{4,0},{1,5},{5,1},{2,6},{6,2},{3,7},{7,3},{8,12},{12,8},{9,1... | collective-permute-start | bytes 688136 | tf_op jit(solution)/shard_map/ppermute | solution.py:33
  132.9 5.1 %collective-permute-start.11 = (bf16[128,896]{1,0:T(8,128)(2,1)S(1)}, bf16[128,896]{1,0:T(8,128)(2,1)S(1)}, u32[]{:S(2)}, u32[]{:S(2)}) collective-permute-start(bf16[128,896]{1,0:T(8,128)(2,1)S(1)} %convolution_convert_fusion.6.own_ref), channel_id=1, source_target_pairs={{0,1},{1,0},{2,3},{3,2},{4,5},{5,4},{6,7},{7,6},{8,9},{9,8},{10,11... | collective-permute-start | bytes 688136 | tf_op jit(solution)/shard_map/ppermute | solution.py:33
  138.0 1.5 collective-permute-start.13
  139.5 2.3 %copy-start.1 = (bf16[1792,1280]{1,0:T(8,128)(2,1)S(1)}, bf16[1792,1280]{1,0:T(8,128)(2,1)}, u32[]{:S(2)}) copy-start(bf16[1792,1280]{1,0:T(8,128)(2,1)} %all-gather.2.cloned.1.call-done.block_ref) | copy-start | bytes 13762564
  145.1 5.0 %collective-permute-start.14 = (bf16[128,1280]{1,0:T(8,128)(2,1)S(1)}, bf16[128,1280]{1,0:T(8,128)(2,1)S(1)}, u32[]{:S(2)}, u32[]{:S(2)}) collective-permute-start(bf16[128,1280]{1,0:T(8,128)(2,1)S(1)} %get-tuple-element.21), channel_id=1, source_target_pairs={{0,0},{1,1},{2,4},{3,5},{4,2},{5,3},{6,6},{7,7},{8,8},{9,9},{10,12... | collective-permute-start | bytes 983048 | tf_op jit(solution)/shard_map/ppermute | solution.py:227
  145.8 12.9 %collective-permute-start.15 = (bf16[128,1280]{1,0:T(8,128)(2,1)S(1)}, bf16[128,1280]{1,0:T(8,128)(2,1)S(1)}, u32[]{:S(2)}, u32[]{:S(2)}) collective-permute-start(bf16[128,1280]{1,0:T(8,128)(2,1)S(1)} %get-tuple-element.22), channel_id=1, source_target_pairs={{0,4},{1,5},{2,0},{3,1},{4,6},{5,7},{6,2},{7,3},{8,12},{9,13},{10,... | collective-permute-start | bytes 983048 | tf_op jit(solution)/shard_map/ppermute | solution.py:227
  158.8 53.0 %copy-start.5 = (f32[128,1280]{1,0:T(8,128)}, f32[128,1280]{1,0:T(8,128)S(1)}, u32[]{:S(2)}) copy-start(f32[128,1280]{1,0:T(8,128)S(1)} %get-tuple-element.27) | copy-start | bytes 1966084
  159.3 4.5 %collective-permute-start.16 = (f32[128,64]{0,1:T(8,128)S(1)}, f32[128,64]{0,1:T(8,128)S(1)}, u32[]{:S(2)}, u32[]{:S(2)}) collective-permute-start(f32[128,64]{0,1:T(8,128)S(1)} %fusion.77), channel_id=1, source_target_pairs={{0,1},{1,0},{2,3},{3,2},{4,5},{5,4},{6,7},{7,6},{8,9},{9,8},{10,11... | collective-permute-start | bytes 98312 | tf_op jit(solution)/shard_map/ppermute | solution.py:33
  163.8 5.5 %collective-permute-start.17 = (f32[128,64]{0,1:T(8,128)S(1)}, f32[128,64]{0,1:T(8,128)S(1)}, u32[]{:S(2)}, u32[]{:S(2)}) collective-permute-start(f32[128,64]{0,1:T(8,128)S(1)} %add.137), channel_id=1, source_target_pairs={{0,2},{2,0},{1,3},{3,1},{4,6},{6,4},{5,7},{7,5},{8,10},{10,8},{9,1... | collective-permute-start | bytes 98312 | tf_op jit(solution)/shard_map/ppermute | solution.py:33
  192.0 19.7 %all-to-all-start.3 = ((bf16[64,24,128]{2,1,0:T(8,128)(2,1)}), bf16[64,24,128]{2,1,0:T(8,128)(2,1)S(1)}, u32[]{:S(2)}, u32[]{:S(2)}) async-start(bf16[64,24,128]{2,1,0:T(8,128)(2,1)} %broadcast_in_dim.41), calls=%async_computation.3 | async-start | bytes 786432 | tf_op jit(solution)/shard_map/all_to_all | solution.py:278
  197.1 3.5 %collective-permute-start.18 = (f32[1,128]{1,0:T(1,128)S(1)}, f32[1,128]{1,0:T(1,128)S(1)}, u32[]{:S(2)}, u32[]{:S(2)}) collective-permute-start(f32[1,128]{1,0:T(1,128)S(1)} %slice.53), channel_id=1, source_target_pairs={{0,1},{1,0},{2,3},{3,2},{4,5},{5,4},{6,7},{7,6},{8,9},{9,8},{10,11... | collective-permute-start | bytes 1544 | tf_op jit(solution)/shard_map/ppermute | solution.py:33
  197.2 5.1 %collective-permute-start.19 = (f32[1,128]{1,0:T(1,128)S(1)}, f32[1,128]{1,0:T(1,128)S(1)}, u32[]{:S(2)}, u32[]{:S(2)}) collective-permute-start(f32[1,128]{1,0:T(1,128)S(1)} %slice.53), channel_id=1, source_target_pairs={{0,2},{2,0},{1,3},{3,1},{4,6},{6,4},{5,7},{7,5},{8,10},{10,8},{9,1... | collective-permute-start | bytes 1544 | tf_op jit(solution)/shard_map/ppermute | solution.py:33
  199.6 4.5 %collective-permute-start.20 = (f32[1,128]{1,0:T(1,128)S(1)}, f32[1,128]{1,0:T(1,128)S(1)}, u32[]{:S(2)}, u32[]{:S(2)}) collective-permute-start(f32[1,128]{1,0:T(1,128)S(1)} %slice.53), channel_id=1, source_target_pairs={{0,3},{1,2},{2,1},{3,0},{4,7},{5,6},{6,5},{7,4},{8,11},{9,10},{10,... | collective-permute-start | bytes 1544 | tf_op jit(solution)/shard_map/ppermute | solution.py:282
Sparse Core Ops, SparseCore 0:
  52.3 56.1 all-gather.1

commit v4 on v3

--- a/solution.py
+++ b/solution.py
@@ -1,3 +1,4 @@
+import functools
 import itertools
 import math
 
@@ -22,7 +23,7 @@
 
 
 def proj_target(yl, z, xh, xl, yh, c):
-    return (xh, z, xl, yh, yl, c)
+    return (xl, z, xh, yh, yl, c)
 
 
 def home_target(step):
@@ -56,48 +57,91 @@
 
 
 def product_kernel(order_ref, own_ref, own_far_ref, pair_ref, pair_far_ref, block_ref, *refs):
-    outs, near_rows, far_rows, total = refs[:2], refs[2], refs[3], refs[4]
+    outs, near_rows, far_rows, total, held, arrived = refs[:2], *refs[2:]
     rows, width = own_ref.shape
-
-    @pl.when(pl.program_id(0) == 0)
-    def _():
-        near_rows[:rows] = own_ref[...]
-        near_rows[rows:] = pair_ref[...]
-        far_rows[:rows] = own_far_ref[...]
-        far_rows[rows:] = pair_far_ref[...]
-
+    count, cut = held.shape[0], held.shape[2]
+    copies = [
+        pltpu.make_async_copy(
+            block_ref.at[:, pl.ds(index * cut, cut)], held.at[index], arrived.at[index]
+        )
+        for index in range(count)
+    ]
+    for copy in copies:
+        copy.start()
+    near_rows[:rows] = own_ref[...]
+    near_rows[rows:] = pair_ref[...]
+    far_rows[:rows] = own_far_ref[...]
+    far_rows[rows:] = pair_far_ref[...]
     core = order_ref[2]
-    near = block_ref[pl.ds(pl.multiple_of(core * width, 128), width), :]
-    far = block_ref[pl.ds(pl.multiple_of((1 - core) * width, 128), width), :]
-    total[...] = dot(near_rows[...], near) + dot(far_rows[...], far)
-    for step in range(2):
-        here = pl.ds(pl.multiple_of(order_ref[step] * rows, 128), rows)
-        outs[step][...] = total[here, :].astype(jnp.bfloat16)
+    near = pl.ds(pl.multiple_of(core * width, 128), width)
+    far = pl.ds(pl.multiple_of((1 - core) * width, 128), width)
+    for index, copy in enumerate(copies):
+        copy.wait()
+        total[...] = dot(near_rows[...], held[index, near, :]) + dot(
+            far_rows[...], held[index, far, :]
+        )
+        for step in range(2):
+            here = pl.ds(pl.multiple_of(order_ref[step] * rows, 128), rows)
+            outs[step][:, index * cut : (index + 1) * cut] = total[here, :].astype(jnp.bfloat16)
 
 
 def product_pieces(order, own, own_far, pair, pair_far, block):
     rows, width = own.shape
     depth, wide = block.shape
     cut = 256
-    whole = pl.BlockSpec((rows, width), lambda i: (0, 0))
+    vmem = pl.BlockSpec(memory_space=pltpu.VMEM)
     return pl.pallas_call(
         product_kernel,
-        grid=(wide // cut,),
         out_shape=[jax.ShapeDtypeStruct((rows, wide), jnp.bfloat16)] * 2,
         in_specs=[pl.BlockSpec(memory_space=pltpu.SMEM)]
-        + [whole] * 4
-        + [pl.BlockSpec((depth, cut), lambda i: (0, i))],
-        out_specs=[pl.BlockSpec((rows, cut), lambda i: (0, i))] * 2,
+        + [vmem] * 4
+        + [pl.BlockSpec(memory_space=pltpu.HBM)],
+        out_specs=[vmem] * 2,
         scratch_shapes=[
             pltpu.VMEM((2 * rows, width), jnp.bfloat16),
             pltpu.VMEM((2 * rows, width), jnp.bfloat16),
             pltpu.VMEM((2 * rows, cut), jnp.float32),
+            pltpu.VMEM((wide // cut, depth, cut), jnp.bfloat16),
+            pltpu.SemaphoreType.DMA((wide // cut,)),
         ],
         compiler_params=pltpu.CompilerParams(vmem_limit_bytes=24 * 1024 * 1024),
         cost_estimate=pl.CostEstimate(
             flops=4 * rows * depth * wide, bytes_accessed=6_000_000, transcendentals=0
         ),
     )(order, own, own_far, pair, pair_far, block)
+
+
+def stats_kernel(student_ref, gain_ref, down_ref, out_ref):
+    student = student_ref[...].astype(jnp.float32)
+    scaled = (student * gain_ref[...].astype(jnp.float32)).astype(jnp.bfloat16)
+    rank = down_ref.shape[0]
+    out_ref[:, :rank] = lax.dot_general(
+        scaled, down_ref[...], (((1,), (1,)), ((), ())), preferred_element_type=jnp.float32
+    )
+    total = jnp.sum(student * student, axis=-1, keepdims=True)
+    out_ref[:, rank:] = jnp.broadcast_to(total, (student.shape[0], rank))
+
+
+def student_kernel(width, stats_ref, student_ref, gain_ref, up_ref, low_ref, normed_ref, out_ref):
+    rank = up_ref.shape[0]
+    inverse = lax.rsqrt(stats_ref[:, rank : rank + 1] / width + 1e-06)
+    low = (stats_ref[:, :rank] * inverse).astype(jnp.bfloat16)
+    student = student_ref[...].astype(jnp.float32)
+    low_ref[...] = low
+    normed_ref[...] = (student * inverse * gain_ref[...].astype(jnp.float32)).astype(jnp.bfloat16)
+    out_ref[...] = student + adapter_scale_factor * dot(low, up_ref[...])
+
+
+def local_kernel(kernel, shapes, *args):
+    vmem = pl.BlockSpec(memory_space=pltpu.VMEM)
+    return pl.pallas_call(
+        kernel,
+        out_shape=shapes,
+        in_specs=[vmem] * len(args),
+        out_specs=jax.tree.map(lambda _: vmem, shapes),
+        compiler_params=pltpu.CompilerParams(vmem_limit_bytes=16 * 1024 * 1024),
+        cost_estimate=pl.CostEstimate(flops=100, bytes_accessed=100, transcendentals=0),
+    )(*args)
 
 
 def body(
@@ -124,8 +168,6 @@
     yl, xh, xl, yh, core = (lax.axis_index(name) for name in ("yl", "xh", "xl", "yh", "c"))
     mi = yh * 2 + core
 
-    proj_rows = lax.ppermute(proj, ALL, permutation(proj_target))
-
     flat_routes = routes.reshape(assigned)
     onehot_e = (flat_routes[:, None] == jnp.arange(experts, dtype=jnp.int32)[None, :]).astype(
         jnp.int32
@@ -142,15 +184,28 @@
     placing = dot(slot_hit, token_hit).astype(jnp.bfloat16)
     outgoing = dot(placing, tokens).astype(jnp.bfloat16)
 
-    outgoing, proj_rows = lax.optimization_barrier((outgoing, proj_rows))
+    outgoing, proj = lax.optimization_barrier((outgoing, proj))
     arrived = exchange_slots(outgoing)
-    proj_rows = pair_rows(proj_rows, "xh", xh)
+
+    proj_rows = lax.ppermute(proj, ALL, permutation(proj_target))
     proj_rows = pair_rows(proj_rows, "yl", yl)
     arrived, proj_rows = lax.optimization_barrier((arrived, proj_rows))
-    proj_block = lax.all_gather(proj_rows, "z", axis=0, tiled=True)
 
     arrived_y = swap(arrived, "yh")
     arrived_c = swap(arrived, "c")
+    proj_rows = pair_rows(proj_rows, "xh", xh)
+
+    gain = student_norm_weight.reshape(1, -1)
+    stats = local_kernel(
+        stats_kernel,
+        jax.ShapeDtypeStruct((tok_rows, 2 * rank), jnp.float32),
+        student_hidden_input,
+        gain,
+        adapter_down_matrix.T,
+    )
+    stats = stats + swap(stats, "c")
+    arrived_y, proj_rows, stats = lax.optimization_barrier((arrived_y, proj_rows, stats))
+    proj_block = lax.all_gather(proj_rows, "z", axis=0, tiled=True)
     arrived_yc = swap(arrived_y, "c")
     parts = (
         (arrived, mi),
@@ -186,23 +241,23 @@
     ).astype(jnp.bfloat16)
     returned = exchange_slots(expert_out)
 
-    expert_out, student_hidden_input = lax.optimization_barrier((expert_out, student_hidden_input))
-    student = student_hidden_input.astype(jnp.float32)
-    gain = student_norm_weight.astype(jnp.float32)
-    student_width = student.shape[1] * mp_count
-    square_sum = jnp.sum(student * student, axis=-1, keepdims=True)
-    low_part = dot((student * gain).astype(jnp.bfloat16), adapter_down_matrix)
-    stats = mp_sum(
-        jnp.concatenate([low_part, jnp.broadcast_to(square_sum, (tok_rows, rank))], axis=1)
-    )
-    inverse = lax.rsqrt(stats[:, rank : rank + 1] / student_width + 1e-06)
-    lowrank = (stats[:, :rank] * inverse).astype(jnp.bfloat16)
-    normed = (student * inverse * gain).astype(jnp.bfloat16)
-    student_out = student + adapter_scale_factor * dot(lowrank, adapter_up_matrix)
+    stats = stats + swap(stats, "yh")
+    student_width = student_hidden_input.shape[1] * mp_count
+    lowrank, normed, student_out = local_kernel(
+        functools.partial(student_kernel, student_width),
+        [
+            jax.ShapeDtypeStruct((tok_rows, rank), jnp.bfloat16),
+            jax.ShapeDtypeStruct(student_hidden_input.shape, jnp.bfloat16),
+            jax.ShapeDtypeStruct(student_hidden_input.shape, jnp.float32),
+        ],
+        stats,
+        student_hidden_input,
+        gain,
+        adapter_up_matrix,
+    )
     returned, lowrank, normed, student_out = lax.optimization_barrier(
         (returned, lowrank, normed, student_out)
     )
-
 
     weights = (
         route_scale * expert_gate_affinity / jnp.sum(expert_gate_affinity, axis=-1, keepdims=True)

time: 222 us -> 219 us (0.986)
  waiting for transfers between devices: 82.9 us -> 76.5 us
  starting transfers between devices: 62.2 us -> 64.8 us
  blocking collectives: 21.4 us -> 23.8 us
    ppermute x17, starting transfers between devices: 19.7 us -> 31.2 us  [swap(): return lax.ppermute(value, axis, [(0, 1), (1, 0)])]
    all_to_all x2, starting transfers between devices: 29.7 us -> 21.1 us  [exchange_slots(): lax.all_to_all(rows, DP, split_axis=0, concat_axis=0, tiled=True)]
    ppermute x17, waiting for transfers between devices: 43.6 us -> 38.7 us  [swap(): return lax.ppermute(value, axis, [(0, 1), (1, 0)])]
    all_to_all x1, blocking collectives: 21.4 us -> 23.8 us  [body(): bundle = lax.all_to_all(bundle, DP, split_axis=0, concat_axis=0, tiled=True)]
    dot_general x15 -> x13, matrix products: 12.2 us -> 10.6 us  [dot(): return jnp.dot(a, b, preferred_element_type=jnp.float32)]
    pallas_call x1 -> x3, Pallas kernels: 3.28 us -> 4.78 us  [the longest x1 4.22 us: product_pieces(): pl.pallas_call(product_kernel, out_shape=[jax.ShapeDtypeStruct((rows, wid...]
  transfers between devices with their start and end apart: 25 -> 25, of which waited for: 15 -> 16; matrix products, arithmetic and copies ran while one was open for 10% -> 8% of each run, Pallas kernels for 0% -> 0%
where the time goes in v4:
time: 219 us
  waiting for transfers between devices  76.5 us (35%)
  starting transfers between devices  64.8 us (30%)
  blocking collectives  23.8 us (11%)
  between operations  20 us (9%)
  matrix products  12.3 us (6%)
  local copies, waits for them, and re-layouts  9.84 us (4%)
  other arithmetic  6.61 us (3%)
  Pallas kernels  4.78 us (2%)
    ppermute x17, waiting for transfers between devices, swap(): return lax.ppermute(value, axis, [(0, 1), (1, 0)])  38.7 us
    ppermute x17, starting transfers between devices, swap(): return lax.ppermute(value, axis, [(0, 1), (1, 0)])  31.2 us
    all_to_all x1, blocking collectives, body(): bundle = lax.all_to_all(bundle, DP, split_axis=0, concat_axis=0, tiled=True)  23.8 us
    all_to_all x2, waiting for transfers between devices, exchange_slots(): lax.all_to_all(rows, DP, split_axis=0, concat_axis=0, tiled=True)  21.8 us
    all_to_all x2, starting transfers between devices, exchange_slots(): lax.all_to_all(rows, DP, split_axis=0, concat_axis=0, tiled=True)  21.1 us
    dot_general x13, matrix products, dot(): return jnp.dot(a, b, preferred_element_type=jnp.float32)  10.6 us
    ppermute x2, waiting for transfers between devices, body(): lax.ppermute(piece, ALL, permutation(home_target(step))).astype(jnp.float32)  7.8 us
    all_to_all x1, waiting for transfers between devices, body(): grads = lax.all_to_all(grads, DP, split_axis=0, concat_axis=0, tiled=True)  6.2 us
  transfers between devices with their start and end apart: 25, of which 16 were waited for; matrix products, arithmetic and copies ran while one was open for 8% of the time, Pallas kernels for 0%

profile of v4, /device:TPU:32, one launch (start us, length us, event | category | flops | bytes accessed | tf_op | source)
XLA Modules:
  0.0 218.7 jit_solution(15493406657849144402)
XLA Ops:
  7.2 0.9 copy.15
  8.4 0.6 reduce-window.6
  9.3 0.6 convolution_convert_fusion.5
  9.9 1.4 reshape.142
  11.3 12.6 %all-to-all-start = ((bf16[64,35,128]{2,1,0:T(8,128)(2,1)}), bf16[64,35,128]{2,1,0:T(8,128)(2,1)S(1)}, u32[]{:S(2)}, u32[]{:S(2)}) async-start(bf16[64,35,128]{2,1,0:T(8,128)(2,1)} %reshape.142), calls=%async_computation | async-start | bytes 1310720 | tf_op jit(solution)/shard_map/all_to_all | solution.py:56
  24.0 0.7 collective-permute-start
  24.7 11.9 %collective-permute-start.1 = (bf16[56,1280]{1,0:T(8,128)(2,1)S(1)}, bf16[56,1280]{1,0:T(8,128)(2,1)S(1)}, u32[]{:S(2)}, u32[]{:S(2)}) collective-permute-start(bf16[56,1280]{1,0:T(8,128)(2,1)S(1)} %collective-permute-done), channel_id=1, source_target_pairs={{0,128},{128,0},{1,129},{129,1},{2,130},{130,2},{3,131},{131,3},{4... | collective-permute-start | bytes 430088 | tf_op jit(solution)/shard_map/ppermute | solution.py:34
  36.6 4.2 %collective-permute-done.1 = bf16[56,1280]{1,0:T(8,128)(2,1)S(1)} collective-permute-done((bf16[56,1280]{1,0:T(8,128)(2,1)S(1)}, bf16[56,1280]{1,0:T(8,128)(2,1)S(1)}, u32[]{:S(2)}, u32[]{:S(2)}) %collective-permute-start.1) | collective-permute-done | bytes 143392 | tf_op jit(solution)/shard_map/ppermute | solution.py:34
  40.9 4.0 %all-to-all-done = bf16[64,35,128]{2,1,0:T(8,128)(2,1)S(1)} async-done(((bf16[64,35,128]{2,1,0:T(8,128)(2,1)}), bf16[64,35,128]{2,1,0:T(8,128)(2,1)S(1)}, u32[]{:S(2)}, u32[]{:S(2)}) %all-to-all-start) | async-done | bytes 573472 | tf_op jit(solution)/shard_map/all_to_all | solution.py:56
  44.9 0.6 reshape.143
  45.5 3.0 %collective-permute-start.3 = (bf16[320,896]{1,0:T(8,128)(2,1)S(1)}, bf16[320,896]{1,0:T(8,128)(2,1)S(1)}, u32[]{:S(2)}, u32[]{:S(2)}) collective-permute-start(bf16[320,896]{1,0:T(8,128)(2,1)S(1)} %reshape.143), channel_id=1, source_target_pairs={{0,2},{2,0},{1,3},{3,1},{4,6},{6,4},{5,7},{7,5},{8,10},{10,8},{9,1... | collective-permute-start | bytes 1720328 | tf_op jit(solution)/shard_map/ppermute | solution.py:34
  48.5 1.9 collective-permute-start.4
  50.8 1.2 collective-permute-done.5
  52.1 4.6 %collective-permute-done.4 = bf16[112,1280]{1,0:T(8,128)(2,1)S(1)} collective-permute-done((bf16[112,1280]{1,0:T(8,128)(2,1)S(1)}, bf16[112,1280]{1,0:T(8,128)(2,1)S(1)}, u32[]{:S(2)}, u32[]{:S(2)}) %collective-permute-start.4) | collective-permute-done | bytes 286752 | tf_op jit(solution)/shard_map/ppermute | solution.py:34
  56.6 0.9 maximum_select_fusion
  57.6 1.9 collective-permute-done.3
  59.6 1.8 fusion.21
  61.4 0.5 collective-permute-start.6
  62.0 1.7 fusion.15
  63.7 0.5 convolution_add_fusion.3
  64.2 2.0 convolution_add_fusion.1
  66.2 0.5 fusion.17
  66.7 0.5 fusion.11
  67.2 0.5 fusion.4
  67.7 0.6 multiply_convert_fusion.1
  68.3 0.9 copy-done.6
  69.2 0.5 convolution_convert_fusion.1
  69.9 0.5 convolution_convert_fusion.3
  70.4 0.5 collective-permute-start.7
  70.9 0.9 collective-permute-done.8
  71.8 0.5 add_convert_fusion.1
  72.3 3.2 %collective-permute-start.9 = (bf16[320,896]{1,0:T(8,128)(2,1)S(1)}, bf16[320,896]{1,0:T(8,128)(2,1)S(1)}, u32[]{:S(2)}, u32[]{:S(2)}) collective-permute-start(bf16[320,896]{1,0:T(8,128)(2,1)S(1)} %add_convert_fusion.1), channel_id=1, source_target_pairs={{0,2},{2,0},{1,3},{3,1},{4,6},{6,4},{5,7},{7,5},{8,10},{10,8},{9,1... | collective-permute-start | bytes 1720328 | tf_op jit(solution)/shard_map/ppermute | solution.py:34
  75.5 0.5 fusion.2
  76.0 13.1 %collective-permute-done.9 = bf16[320,896]{1,0:T(8,128)(2,1)S(1)} collective-permute-done((bf16[320,896]{1,0:T(8,128)(2,1)S(1)}, bf16[320,896]{1,0:T(8,128)(2,1)S(1)}, u32[]{:S(2)}, u32[]{:S(2)}) %collective-permute-start.9) | collective-permute-done | bytes 573472 | tf_op jit(solution)/shard_map/ppermute | solution.py:34
  89.3 1.4 reshape.145
  90.7 8.5 %all-to-all-start.1 = ((bf16[64,35,128]{2,1,0:T(8,128)(2,1)}), bf16[64,35,128]{2,1,0:T(8,128)(2,1)S(1)}, u32[]{:S(2)}, u32[]{:S(2)}) async-start(bf16[64,35,128]{2,1,0:T(8,128)(2,1)} %reshape.145), calls=%async_computation.1 | async-start | bytes 1310720 | tf_op jit(solution)/shard_map/all_to_all | solution.py:56
  99.5 2.7 %collective-permute-start.10 = (f32[128,128]{1,0:T(8,128)S(1)}, f32[128,128]{1,0:T(8,128)S(1)}, u32[]{:S(2)}, u32[]{:S(2)}) collective-permute-start(f32[128,128]{1,0:T(8,128)S(1)} %add.109), channel_id=1, source_target_pairs={{0,2},{2,0},{1,3},{3,1},{4,6},{6,4},{5,7},{7,5},{8,10},{10,8},{9,1... | collective-permute-start | bytes 196616 | tf_op jit(solution)/shard_map/ppermute | solution.py:34
  102.6 3.5 %collective-permute-done.10 = f32[128,128]{1,0:T(8,128)S(1)} collective-permute-done((f32[128,128]{1,0:T(8,128)S(1)}, f32[128,128]{1,0:T(8,128)S(1)}, u32[]{:S(2)}, u32[]{:S(2)}) %collective-permute-start.10) | collective-permute-done | bytes 65568 | tf_op jit(solution)/shard_map/ppermute | solution.py:34
  106.5 17.8 %all-to-all-done.1 = bf16[64,35,128]{2,1,0:T(8,128)(2,1)S(1)} async-done(((bf16[64,35,128]{2,1,0:T(8,128)(2,1)}), bf16[64,35,128]{2,1,0:T(8,128)(2,1)S(1)}, u32[]{:S(2)}, u32[]{:S(2)}) %all-to-all-start.1) | async-done | bytes 573472 | tf_op jit(solution)/shard_map/all_to_all | solution.py:56
  124.3 0.6 reshape.146
  124.9 0.6 convolution_convert_fusion.6.own_ref
  125.5 1.3 collective-permute-start.12
  126.9 4.8 %collective-permute-done.12.pair_ref = bf16[128,896]{1,0:T(8,128)(2,1)S(1)} collective-permute-done((bf16[128,896]{1,0:T(8,128)(2,1)S(1)}, bf16[128,896]{1,0:T(8,128)(2,1)S(1)}, u32[]{:S(2)}, u32[]{:S(2)}) %collective-permute-start.12) | collective-permute-done | bytes 229408 | tf_op jit(solution)/shard_map/ppermute | solution.py:34
  131.7 1.4 collective-permute-done.13.pair_far_ref
  133.1 2.3 %copy-done.1 = bf16[1792,1280]{1,0:T(8,128)(2,1)S(1)} copy-done((bf16[1792,1280]{1,0:T(8,128)(2,1)S(1)}, bf16[1792,1280]{1,0:T(8,128)(2,1)}, u32[]{:S(2)}) %copy-start.1) | copy-done | bytes 4587544
  135.4 4.2 %shard_map.140 = (bf16[128,1280]{1,0:T(8,128)(2,1)S(1)}, bf16[128,1280]{1,0:T(8,128)(2,1)S(1)}) custom-call(s32[3]{0:T(128)S(1)} %pad_add_fusion.order_ref, bf16[128,896]{1,0:T(8,128)(2,1)S(1)} %convolution_convert_fusion.6.own_ref, bf16[128,896]{1,0:T(8,128)(2,1)S(1)} %collective-permute-done.11.own_far_ref, ...), custom_call_target="tpu_custom_call" | custom-call | flops 1174405120 | bytes 6000000 | tf_op jit(solution)/shard_map/pallas_call | solution.py:93
  139.7 0.7 collective-permute-start.14
  140.4 5.4 %collective-permute-start.15 = (bf16[128,1280]{1,0:T(8,128)(2,1)S(1)}, bf16[128,1280]{1,0:T(8,128)(2,1)S(1)}, u32[]{:S(2)}, u32[]{:S(2)}) collective-permute-start(bf16[128,1280]{1,0:T(8,128)(2,1)S(1)} %get-tuple-element.32), channel_id=1, source_target_pairs={{0,4},{1,5},{2,0},{3,1},{4,6},{5,7},{6,2},{7,3},{8,12},{9,13},{10,... | collective-permute-start | bytes 983048 | tf_op jit(solution)/shard_map/ppermute | solution.py:282
  145.8 7.8 %collective-permute-done.15 = bf16[128,1280]{1,0:T(8,128)(2,1)S(1)} collective-permute-done((bf16[128,1280]{1,0:T(8,128)(2,1)S(1)}, bf16[128,1280]{1,0:T(8,128)(2,1)S(1)}, u32[]{:S(2)}, u32[]{:S(2)}) %collective-permute-start.15) | collective-permute-done | bytes 327712 | tf_op jit(solution)/shard_map/ppermute | solution.py:282
  154.3 0.8 multiply_reduce_fusion
  158.7 2.9 %collective-permute-start.17 = (f32[128,64]{0,1:T(8,128)S(1)}, f32[128,64]{0,1:T(8,128)S(1)}, u32[]{:S(2)}, u32[]{:S(2)}) collective-permute-start(f32[128,64]{0,1:T(8,128)S(1)} %add.125), channel_id=1, source_target_pairs={{0,2},{2,0},{1,3},{3,1},{4,6},{6,4},{5,7},{7,5},{8,10},{10,8},{9,1... | collective-permute-start | bytes 98312 | tf_op jit(solution)/shard_map/ppermute | solution.py:34
  161.6 1.3 fusion.66
  162.9 1.3 collective-permute-done.17
  164.6 23.8 %all_to_all.20 = bf16[64,24,128]{2,1,0:T(8,128)(2,1)S(1)} all-to-all(bf16[64,24,128]{2,1,0:T(8,128)(2,1)S(1)} %pad_maximum_fusion), channel_id=1, replica_groups=mesh['yl'=2,'z'=8,'xh'=2,'xl'=2,'yh'=2,'c'=2] {'yl','z','xh','xl'}, dimensions={0} | all-to-all | bytes 786432 | tf_op jit(solution)/shard_map/all_to_all | solution.py:330
  188.5 0.8 broadcast_in_dim.32
  189.3 5.0 %all-to-all-start.3 = ((bf16[64,24,128]{2,1,0:T(8,128)(2,1)}), bf16[64,24,128]{2,1,0:T(8,128)(2,1)S(1)}, u32[]{:S(2)}, u32[]{:S(2)}) async-start(bf16[64,24,128]{2,1,0:T(8,128)(2,1)} %broadcast_in_dim.32), calls=%async_computation.3 | async-start | bytes 786432 | tf_op jit(solution)/shard_map/all_to_all | solution.py:333
  194.5 2.7 %collective-permute-start.19 = (f32[1,128]{1,0:T(1,128)S(1)}, f32[1,128]{1,0:T(1,128)S(1)}, u32[]{:S(2)}, u32[]{:S(2)}) collective-permute-start(f32[1,128]{1,0:T(1,128)S(1)} %slice.43), channel_id=1, source_target_pairs={{0,2},{2,0},{1,3},{3,1},{4,6},{6,4},{5,7},{7,5},{8,10},{10,8},{9,1... | collective-permute-start | bytes 1544 | tf_op jit(solution)/shard_map/ppermute | solution.py:34
  197.2 0.7 collective-permute-start.20
  197.9 1.8 collective-permute-done.19
  199.6 2.0 collective-permute-done.20
  201.6 0.6 add_reduce_fusion
  202.9 6.2 %all-to-all-done.3 = bf16[64,24,128]{2,1,0:T(8,128)(2,1)S(1)} async-done(((bf16[64,24,128]{2,1,0:T(8,128)(2,1)}), bf16[64,24,128]{2,1,0:T(8,128)(2,1)S(1)}, u32[]{:S(2)}, u32[]{:S(2)}) %all-to-all-start.3) | async-done | bytes 393248 | tf_op jit(solution)/shard_map/all_to_all | solution.py:333
  209.2 0.7 convert_bitcast_fusion.1
  209.9 0.7 convert_bitcast_fusion
  (77 shorter events, 4.0 us)
Async XLA Ops:
  7.2 2.2 copy-start
  7.2 16.8 %copy-start.11 = (bf16[56,1280]{1,0:T(8,128)(2,1)S(1)}, bf16[56,1280]{1,0:T(8,128)(2,1)}, u32[]{:S(2)}) copy-start(bf16[56,1280]{1,0:T(8,128)(2,1)} %param.17) | copy-start | bytes 430084
  7.2 43.3 %copy-start.9 = (bf16[1280]{0:T(1024)(128)(2,1)S(1)}, bf16[1280]{0:T(1024)(128)(2,1)}, u32[]{:S(2)}) copy-start(bf16[1280]{0:T(1024)(128)(2,1)} %param.19) | copy-start | bytes 7684
  7.2 43.3 %copy-start.4 = (bf16[1280,64]{0,1:T(8,128)(2,1)S(1)}, bf16[1280,64]{0,1:T(8,128)(2,1)}, u32[]{:S(2)}) copy-start(bf16[1280,64]{0,1:T(8,128)(2,1)} %param.20) | copy-start | bytes 491524
  7.2 43.3 %copy-start.2 = (bf16[128,1280]{1,0:T(8,128)(2,1)S(1)}, bf16[128,1280]{1,0:T(8,128)(2,1)}, u32[]{:S(2)}) copy-start(bf16[128,1280]{1,0:T(8,128)(2,1)} %student_ref.3) | copy-start | bytes 983044
  11.3 33.6 %all-to-all-start = ((bf16[64,35,128]{2,1,0:T(8,128)(2,1)}), bf16[64,35,128]{2,1,0:T(8,128)(2,1)S(1)}, u32[]{:S(2)}, u32[]{:S(2)}) async-start(bf16[64,35,128]{2,1,0:T(8,128)(2,1)} %reshape.142), calls=%async_computation | async-start | bytes 1310720 | tf_op jit(solution)/shard_map/all_to_all | solution.py:56
  24.0 109.2 %all-gather.2.cloned.1.call-start = ((), (), s32[]{:S(2)}) async-start(), calls=%async_computation.4 | async-start | bytes 5160960 | tf_op jit(solution)/shard_map/all_gather | solution.py:208
  24.0 0.7 collective-permute-start
  24.7 16.1 %collective-permute-start.1 = (bf16[56,1280]{1,0:T(8,128)(2,1)S(1)}, bf16[56,1280]{1,0:T(8,128)(2,1)S(1)}, u32[]{:S(2)}, u32[]{:S(2)}) collective-permute-start(bf16[56,1280]{1,0:T(8,128)(2,1)S(1)} %collective-permute-done), channel_id=1, source_target_pairs={{0,128},{128,0},{1,129},{129,1},{2,130},{130,2},{3,131},{131,3},{4... | collective-permute-start | bytes 430088 | tf_op jit(solution)/shard_map/ppermute | solution.py:34
  45.5 13.9 %collective-permute-start.3 = (bf16[320,896]{1,0:T(8,128)(2,1)S(1)}, bf16[320,896]{1,0:T(8,128)(2,1)S(1)}, u32[]{:S(2)}, u32[]{:S(2)}) collective-permute-start(bf16[320,896]{1,0:T(8,128)(2,1)S(1)} %reshape.143), channel_id=1, source_target_pairs={{0,2},{2,0},{1,3},{3,1},{4,6},{6,4},{5,7},{7,5},{8,10},{10,8},{9,1... | collective-permute-start | bytes 1720328 | tf_op jit(solution)/shard_map/ppermute | solution.py:34
  48.5 8.1 %collective-permute-start.4 = (bf16[112,1280]{1,0:T(8,128)(2,1)S(1)}, bf16[112,1280]{1,0:T(8,128)(2,1)S(1)}, u32[]{:S(2)}, u32[]{:S(2)}) collective-permute-start(bf16[112,1280]{1,0:T(8,128)(2,1)S(1)} %maximum_select_fusion.1), channel_id=1, source_target_pairs={{0,8},{8,0},{1,9},{9,1},{2,10},{10,2},{3,11},{11,3},{4,12},{12,4},... | collective-permute-start | bytes 860168 | tf_op jit(solution)/shard_map/ppermute | solution.py:34
  50.7 1.3 collective-permute-start.5
  59.4 4.2 %collective-permute-start.2 = (bf16[320,896]{1,0:T(8,128)(2,1)S(1)}, bf16[320,896]{1,0:T(8,128)(2,1)S(1)}, u32[]{:S(2)}, u32[]{:S(2)}) collective-permute-start(bf16[320,896]{1,0:T(8,128)(2,1)S(1)} %reshape.143), channel_id=1, source_target_pairs={{0,1},{1,0},{2,3},{3,2},{4,5},{5,4},{6,7},{7,6},{8,9},{9,8},{10,11... | collective-permute-start | bytes 1720328 | tf_op jit(solution)/shard_map/ppermute | solution.py:34
  59.6 4.1 %copy-start.5 = (bf16[1,3584,512]{2,1,0:T(8,128)(2,1)S(1)}, bf16[1,3584,512]{2,1,0:T(8,128)(2,1)}, u32[]{:S(2)}) copy-start(bf16[1,3584,512]{2,1,0:T(8,128)(2,1)} %param.14) | copy-start | bytes 11010052
  61.4 4.7 %collective-permute-start.6 = (bf16[320,896]{1,0:T(8,128)(2,1)S(1)}, bf16[320,896]{1,0:T(8,128)(2,1)S(1)}, u32[]{:S(2)}, u32[]{:S(2)}) collective-permute-start(bf16[320,896]{1,0:T(8,128)(2,1)S(1)} %collective-permute-done.3), channel_id=1, source_target_pairs={{0,1},{1,0},{2,3},{3,2},{4,5},{5,4},{6,7},{7,6},{8,9},{9,8},{10,11... | collective-permute-start | bytes 1720328 | tf_op jit(solution)/shard_map/ppermute | solution.py:34
  63.6 3.0 %copy-start.8 = (bf16[1,3584,512]{2,1,0:T(8,128)(2,1)S(1)}, bf16[1,3584,512]{2,1,0:T(8,128)(2,1)}, u32[]{:S(2)}) copy-start(bf16[1,3584,512]{2,1,0:T(8,128)(2,1)} %param.15) | copy-start | bytes 11010052
  67.2 2.0 copy-start.6
  69.7 2.1 collective-permute-start.8
  70.4 5.6 %collective-permute-start.7 = (bf16[320,896]{1,0:T(8,128)(2,1)S(1)}, bf16[320,896]{1,0:T(8,128)(2,1)S(1)}, u32[]{:S(2)}, u32[]{:S(2)}) collective-permute-start(bf16[320,896]{1,0:T(8,128)(2,1)S(1)} %convolution_convert_fusion.3), channel_id=1, source_target_pairs={{0,1},{1,0},{2,3},{3,2},{4,5},{5,4},{6,7},{7,6},{8,9},{9,8},{10,11... | collective-permute-start | bytes 1720328 | tf_op jit(solution)/shard_map/ppermute | solution.py:34
  72.3 26.9 %copy-start.10 = (f32[128,2]{0,1:T(2,128)S(1)}, f32[128,2]{0,1:T(2,128)}, u32[]{:S(2)}) copy-start(f32[128,2]{0,1:T(2,128)} %param.13) | copy-start | bytes 3076
  72.3 33.8 %copy-start.3 = (bf16[64,1280]{1,0:T(8,128)(2,1)S(1)}, bf16[64,1280]{1,0:T(8,128)(2,1)}, u32[]{:S(2)}) copy-start(bf16[64,1280]{1,0:T(8,128)(2,1)} %up_ref.1) | copy-start | bytes 491524
  72.3 16.8 %collective-permute-start.9 = (bf16[320,896]{1,0:T(8,128)(2,1)S(1)}, bf16[320,896]{1,0:T(8,128)(2,1)S(1)}, u32[]{:S(2)}, u32[]{:S(2)}) collective-permute-start(bf16[320,896]{1,0:T(8,128)(2,1)S(1)} %add_convert_fusion.1), channel_id=1, source_target_pairs={{0,2},{2,0},{1,3},{3,1},{4,6},{6,4},{5,7},{7,5},{8,10},{10,8},{9,1... | collective-permute-start | bytes 1720328 | tf_op jit(solution)/shard_map/ppermute | solution.py:34
  90.7 33.6 %all-to-all-start.1 = ((bf16[64,35,128]{2,1,0:T(8,128)(2,1)}), bf16[64,35,128]{2,1,0:T(8,128)(2,1)S(1)}, u32[]{:S(2)}, u32[]{:S(2)}) async-start(bf16[64,35,128]{2,1,0:T(8,128)(2,1)} %reshape.145), calls=%async_computation.1 | async-start | bytes 1310720 | tf_op jit(solution)/shard_map/all_to_all | solution.py:56
  99.5 6.6 %collective-permute-start.10 = (f32[128,128]{1,0:T(8,128)S(1)}, f32[128,128]{1,0:T(8,128)S(1)}, u32[]{:S(2)}, u32[]{:S(2)}) collective-permute-start(f32[128,128]{1,0:T(8,128)S(1)} %add.109), channel_id=1, source_target_pairs={{0,2},{2,0},{1,3},{3,1},{4,6},{6,4},{5,7},{7,5},{8,10},{10,8},{9,1... | collective-permute-start | bytes 196616 | tf_op jit(solution)/shard_map/ppermute | solution.py:34
  125.5 6.1 %collective-permute-start.12 = (bf16[128,896]{1,0:T(8,128)(2,1)S(1)}, bf16[128,896]{1,0:T(8,128)(2,1)S(1)}, u32[]{:S(2)}, u32[]{:S(2)}) collective-permute-start(bf16[128,896]{1,0:T(8,128)(2,1)S(1)} %convolution_convert_fusion.6.own_ref), channel_id=1, source_target_pairs={{0,4},{4,0},{1,5},{5,1},{2,6},{6,2},{3,7},{7,3},{8,12},{12,8},{9,1... | collective-permute-start | bytes 688136 | tf_op jit(solution)/shard_map/ppermute | solution.py:34
  126.9 4.9 %collective-permute-start.11 = (bf16[128,896]{1,0:T(8,128)(2,1)S(1)}, bf16[128,896]{1,0:T(8,128)(2,1)S(1)}, u32[]{:S(2)}, u32[]{:S(2)}) collective-permute-start(bf16[128,896]{1,0:T(8,128)(2,1)S(1)} %convolution_convert_fusion.6.own_ref), channel_id=1, source_target_pairs={{0,1},{1,0},{2,3},{3,2},{4,5},{5,4},{6,7},{7,6},{8,9},{9,8},{10,11... | collective-permute-start | bytes 688136 | tf_op jit(solution)/shard_map/ppermute | solution.py:34
  131.6 1.5 collective-permute-start.13
  133.1 2.3 %copy-start.1 = (bf16[1792,1280]{1,0:T(8,128)(2,1)S(1)}, bf16[1792,1280]{1,0:T(8,128)(2,1)}, u32[]{:S(2)}) copy-start(bf16[1792,1280]{1,0:T(8,128)(2,1)} %all-gather.2.cloned.1.call-done.block_ref) | copy-start | bytes 13762564
  139.7 6.1 %collective-permute-start.14 = (bf16[128,1280]{1,0:T(8,128)(2,1)S(1)}, bf16[128,1280]{1,0:T(8,128)(2,1)S(1)}, u32[]{:S(2)}, u32[]{:S(2)}) collective-permute-start(bf16[128,1280]{1,0:T(8,128)(2,1)S(1)} %get-tuple-element.31), channel_id=1, source_target_pairs={{0,0},{1,1},{2,4},{3,5},{4,2},{5,3},{6,6},{7,7},{8,8},{9,9},{10,12... | collective-permute-start | bytes 983048 | tf_op jit(solution)/shard_map/ppermute | solution.py:282
  140.4 13.2 %collective-permute-start.15 = (bf16[128,1280]{1,0:T(8,128)(2,1)S(1)}, bf16[128,1280]{1,0:T(8,128)(2,1)S(1)}, u32[]{:S(2)}, u32[]{:S(2)}) collective-permute-start(bf16[128,1280]{1,0:T(8,128)(2,1)S(1)} %get-tuple-element.32), channel_id=1, source_target_pairs={{0,4},{1,5},{2,0},{3,1},{4,6},{5,7},{6,2},{7,3},{8,12},{9,13},{10,... | collective-permute-start | bytes 983048 | tf_op jit(solution)/shard_map/ppermute | solution.py:282
  153.7 55.4 %copy-start.7 = (f32[128,1280]{1,0:T(8,128)}, f32[128,1280]{1,0:T(8,128)S(1)}, u32[]{:S(2)}) copy-start(f32[128,1280]{1,0:T(8,128)S(1)} %get-tuple-element.37) | copy-start | bytes 1966084
  154.2 4.5 %collective-permute-start.16 = (f32[128,64]{0,1:T(8,128)S(1)}, f32[128,64]{0,1:T(8,128)S(1)}, u32[]{:S(2)}, u32[]{:S(2)}) collective-permute-start(f32[128,64]{0,1:T(8,128)S(1)} %fusion.68), channel_id=1, source_target_pairs={{0,1},{1,0},{2,3},{3,2},{4,5},{5,4},{6,7},{7,6},{8,9},{9,8},{10,11... | collective-permute-start | bytes 98312 | tf_op jit(solution)/shard_map/ppermute | solution.py:34
  158.7 5.5 %collective-permute-start.17 = (f32[128,64]{0,1:T(8,128)S(1)}, f32[128,64]{0,1:T(8,128)S(1)}, u32[]{:S(2)}, u32[]{:S(2)}) collective-permute-start(f32[128,64]{0,1:T(8,128)S(1)} %add.125), channel_id=1, source_target_pairs={{0,2},{2,0},{1,3},{3,1},{4,6},{6,4},{5,7},{7,5},{8,10},{10,8},{9,1... | collective-permute-start | bytes 98312 | tf_op jit(solution)/shard_map/ppermute | solution.py:34
  189.3 19.7 %all-to-all-start.3 = ((bf16[64,24,128]{2,1,0:T(8,128)(2,1)}), bf16[64,24,128]{2,1,0:T(8,128)(2,1)S(1)}, u32[]{:S(2)}, u32[]{:S(2)}) async-start(bf16[64,24,128]{2,1,0:T(8,128)(2,1)} %broadcast_in_dim.32), calls=%async_computation.3 | async-start | bytes 786432 | tf_op jit(solution)/shard_map/all_to_all | solution.py:333
  194.4 3.5 %collective-permute-start.18 = (f32[1,128]{1,0:T(1,128)S(1)}, f32[1,128]{1,0:T(1,128)S(1)}, u32[]{:S(2)}, u32[]{:S(2)}) collective-permute-start(f32[1,128]{1,0:T(1,128)S(1)} %slice.43), channel_id=1, source_target_pairs={{0,1},{1,0},{2,3},{3,2},{4,5},{5,4},{6,7},{7,6},{8,9},{9,8},{10,11... | collective-permute-start | bytes 1544 | tf_op jit(solution)/shard_map/ppermute | solution.py:34
  194.5 5.1 %collective-permute-start.19 = (f32[1,128]{1,0:T(1,128)S(1)}, f32[1,128]{1,0:T(1,128)S(1)}, u32[]{:S(2)}, u32[]{:S(2)}) collective-permute-start(f32[1,128]{1,0:T(1,128)S(1)} %slice.43), channel_id=1, source_target_pairs={{0,2},{2,0},{1,3},{3,1},{4,6},{6,4},{5,7},{7,5},{8,10},{10,8},{9,1... | collective-permute-start | bytes 1544 | tf_op jit(solution)/shard_map/ppermute | solution.py:34
  197.2 4.5 %collective-permute-start.20 = (f32[1,128]{1,0:T(1,128)S(1)}, f32[1,128]{1,0:T(1,128)S(1)}, u32[]{:S(2)}, u32[]{:S(2)}) collective-permute-start(f32[1,128]{1,0:T(1,128)S(1)} %slice.43), channel_id=1, source_target_pairs={{0,3},{1,2},{2,1},{3,0},{4,7},{5,6},{6,5},{7,4},{8,11},{9,10},{10,... | collective-permute-start | bytes 1544 | tf_op jit(solution)/shard_map/ppermute | solution.py:337
Sparse Core Ops, SparseCore 0:
  59.6 69.6 all-gather.1

commit v5 on v4

--- a/solution.py
+++ b/solution.py
@@ -22,8 +22,8 @@
     return [(place, places.index(target(*here))) for place, here in enumerate(places)]
 
 
-def proj_target(yl, z, xh, xl, yh, c):
-    return (xl, z, xh, yh, yl, c)
+def proj_target(step):
+    return lambda yl, z, xh, xl, yh, c: (xl ^ (step & 1), z, xh ^ (step >> 1), yh, yl, c)
 
 
 def home_target(step):
@@ -34,19 +34,18 @@
     return lax.ppermute(value, axis, [(0, 1), (1, 0)])
 
 
-def mp_sum(value):
-    value = value + swap(value, "c")
-    return value + swap(value, "yh")
-
-
 def dot(a, b):
     return jnp.dot(a, b, preferred_element_type=jnp.float32)
 
 
-def pair_rows(value, axis, index):
-    other = swap(value, axis)
+def mp_sum(value):
+    cross = lax.ppermute(value, MP, [(place, 3 - place) for place in range(4)])
+    return (value + swap(value, "c")) + (swap(value, "yh") + cross)
+
+
+def ordered(first, second, index):
     return jnp.where(
-        index == 0, jnp.concatenate([value, other]), jnp.concatenate([other, value])
+        index == 0, jnp.concatenate([first, second]), jnp.concatenate([second, first])
     )
 
 
@@ -144,6 +143,112 @@
     )(*args)
 
 
+def core_halves(core, width):
+    return (
+        pl.ds(pl.multiple_of(core * width, 128), width),
+        pl.ds(pl.multiple_of((1 - core) * width, 128), width),
+    )
+
+
+def near_kernel(place_ref, own_ref, other_ref, gate_ref, up_ref, *refs):
+    outs, held, arrived = refs[:2], refs[2], refs[3]
+    depth = held.shape[1]
+    here = pl.ds(pl.multiple_of(place_ref[0] * depth, 128), depth)
+    copies = [
+        pltpu.make_async_copy(weight.at[here, :], held.at[index], arrived.at[index])
+        for index, weight in enumerate((gate_ref, up_ref))
+    ]
+    for copy in copies:
+        copy.start()
+    own, other = core_halves(place_ref[1], own_ref.shape[1])
+    for index, copy in enumerate(copies):
+        copy.wait()
+        outs[index][...] = dot(own_ref[...], held[index, own, :]) + dot(
+            other_ref[...], held[index, other, :]
+        )
+
+
+def expert_kernel(
+    place_ref, gate_near_ref, up_near_ref, own_ref, other_ref, gate_ref, up_ref, down_ref, *refs
+):
+    outs, held, held_down, arrived = refs[:4], refs[4], refs[5], refs[6]
+    depth, width = held.shape[1], own_ref.shape[1]
+    yh, core = place_ref[0], place_ref[1]
+    here = pl.ds(pl.multiple_of((1 - yh) * depth, 128), depth)
+    copies = [
+        pltpu.make_async_copy(weight.at[here, :], held.at[index], arrived.at[index])
+        for index, weight in enumerate((gate_ref, up_ref))
+    ]
+    parts = (yh * 2 + core, yh * 2 + 1 - core, (1 - yh) * 2 + core, (1 - yh) * 2 + 1 - core)
+    down_copies = [
+        pltpu.make_async_copy(
+            down_ref.at[:, pl.ds(pl.multiple_of(part * width, 128), width)],
+            held_down.at[index],
+            arrived.at[2 + index],
+        )
+        for index, part in enumerate(parts)
+    ]
+    for copy in copies + down_copies[::-1]:
+        copy.start()
+    own, other = core_halves(core, width)
+    sums = []
+    for index, near in enumerate((gate_near_ref, up_near_ref)):
+        copies[index].wait()
+        sums.append(
+            near[...]
+            + dot(own_ref[...], held[index, own, :])
+            + dot(other_ref[...], held[index, other, :])
+        )
+    gate, up = sums
+    hidden = (gate / (1.0 + jnp.exp(-gate)) * up).astype(jnp.bfloat16)
+    for index in (3, 2, 1, 0):
+        down_copies[index].wait()
+        outs[index][...] = dot(hidden, held_down[index]).astype(jnp.bfloat16)
+
+
+def expert_call(kernel, shapes, place, local, weights, scratch):
+    vmem = pl.BlockSpec(memory_space=pltpu.VMEM)
+    return pl.pallas_call(
+        kernel,
+        out_shape=shapes,
+        in_specs=[pl.BlockSpec(memory_space=pltpu.SMEM)]
+        + [vmem] * len(local)
+        + [pl.BlockSpec(memory_space=pltpu.HBM)] * len(weights),
+        out_specs=[vmem] * len(shapes),
+        scratch_shapes=scratch,
+        compiler_params=pltpu.CompilerParams(vmem_limit_bytes=32 * 1024 * 1024),
+        cost_estimate=pl.CostEstimate(flops=100, bytes_accessed=100, transcendentals=0),
+    )(place, *local, *weights)
+
+
+def near_products(place, own, other, gate, up):
+    depth, units = gate.shape[0] // 2, gate.shape[1]
+    return expert_call(
+        near_kernel,
+        [jax.ShapeDtypeStruct((own.shape[0], units), jnp.float32)] * 2,
+        place,
+        (own, other),
+        (gate, up),
+        [pltpu.VMEM((2, depth, units), jnp.bfloat16), pltpu.SemaphoreType.DMA((2,))],
+    )
+
+
+def expert_products(place, near_gate, near_up, own, other, gate, up, down):
+    depth, units = gate.shape[0] // 2, gate.shape[1]
+    return expert_call(
+        expert_kernel,
+        [jax.ShapeDtypeStruct(own.shape, jnp.bfloat16)] * 4,
+        place,
+        (near_gate, near_up, own, other),
+        (gate, up, down),
+        [
+            pltpu.VMEM((2, depth, units), jnp.bfloat16),
+            pltpu.VMEM((4, units, own.shape[1]), jnp.bfloat16),
+            pltpu.SemaphoreType.DMA((6,)),
+        ],
+    )
+
+
 def body(
     tokens,
     routes,
@@ -187,13 +292,13 @@
     outgoing, proj = lax.optimization_barrier((outgoing, proj))
     arrived = exchange_slots(outgoing)
 
-    proj_rows = lax.ppermute(proj, ALL, permutation(proj_target))
-    proj_rows = pair_rows(proj_rows, "yl", yl)
+    blocks = [lax.ppermute(proj, ALL, permutation(proj_target(step))) for step in range(4)]
+    proj_rows = ordered(ordered(*blocks[:2], yl), ordered(*blocks[2:], yl), xh)
     arrived, proj_rows = lax.optimization_barrier((arrived, proj_rows))
+    proj_block = lax.all_gather(proj_rows, "z", axis=0, tiled=True)
 
     arrived_y = swap(arrived, "yh")
     arrived_c = swap(arrived, "c")
-    proj_rows = pair_rows(proj_rows, "xh", xh)
 
     gain = student_norm_weight.reshape(1, -1)
     stats = local_kernel(
@@ -204,38 +309,27 @@
         adapter_down_matrix.T,
     )
     stats = stats + swap(stats, "c")
-    arrived_y, proj_rows, stats = lax.optimization_barrier((arrived_y, proj_rows, stats))
-    proj_block = lax.all_gather(proj_rows, "z", axis=0, tiled=True)
-    arrived_yc = swap(arrived_y, "c")
-    parts = (
-        (arrived, mi),
-        (arrived_c, yh * 2 + 1 - core),
-        (arrived_y, (1 - yh) * 2 + core),
-        (arrived_yc, (1 - yh) * 2 + 1 - core),
-    )
-    gate_proj = up_proj = 0.0
-    for rows, place in parts:
-        gate_proj = gate_proj + dot(
-            rows, lax.dynamic_slice_in_dim(expert_gate_weight[0], place * part_width, part_width, 0)
-        )
-        up_proj = up_proj + dot(
-            rows, lax.dynamic_slice_in_dim(expert_up_weight[0], place * part_width, part_width, 0)
-        )
-    hidden = (jax.nn.silu(gate_proj) * up_proj).astype(jnp.bfloat16)
-
-    def out_part(place):
-        return dot(
-            hidden, lax.dynamic_slice_in_dim(expert_down_weight[0], place * part_width, part_width, 1)
-        )
-
-    far = swap(out_part((1 - yh) * 2 + 1 - core).astype(jnp.bfloat16), "c")
-    near = swap(out_part(yh * 2 + 1 - core).astype(jnp.bfloat16), "c")
-    far = out_part((1 - yh) * 2 + core).astype(jnp.bfloat16).astype(jnp.float32) + far.astype(
-        jnp.float32
-    )
-    far = swap(far.astype(jnp.bfloat16), "yh")
+    near_gate, near_up = near_products(
+        jnp.stack([yh, core]), arrived, arrived_c, expert_gate_weight[0], expert_up_weight[0]
+    )
+    arrived_y, stats, near_gate, near_up = lax.optimization_barrier(
+        (arrived_y, stats, near_gate, near_up)
+    )
+    out_own, out_near, out_far, out_far_near = expert_products(
+        jnp.stack([yh, core]),
+        near_gate,
+        near_up,
+        arrived_y,
+        swap(arrived_y, "c"),
+        expert_gate_weight[0],
+        expert_up_weight[0],
+        expert_down_weight[0],
+    )
+    far = swap(out_far_near, "c")
+    near = swap(out_near, "c")
+    far = swap((out_far.astype(jnp.float32) + far.astype(jnp.float32)).astype(jnp.bfloat16), "yh")
     expert_out = (
-        out_part(mi).astype(jnp.bfloat16).astype(jnp.float32)
+        out_own.astype(jnp.float32)
         + near.astype(jnp.float32)
         + far.astype(jnp.float32)
     ).astype(jnp.bfloat16)
@@ -255,8 +349,8 @@
         gain,
         adapter_up_matrix,
     )
-    returned, lowrank, normed, student_out = lax.optimization_barrier(
-        (returned, lowrank, normed, student_out)
+    returned, lowrank, normed, student_out, proj_block = lax.optimization_barrier(
+        (returned, lowrank, normed, student_out, proj_block)
     )
 
     weights = (
@@ -331,12 +425,7 @@
     summed = jnp.sum(bundle.astype(jnp.float32), axis=0)
     grads = jnp.broadcast_to(summed.astype(jnp.bfloat16), (experts, 24, lanes))
     grads = lax.all_to_all(grads, DP, split_axis=0, concat_axis=0, tiled=True)
-    loss_row = summed[20:21]
-    cross = [(i, 3 - i) for i in range(4)]
-    loss_row = (loss_row + swap(loss_row, "c")) + (
-        swap(loss_row, "yh") + lax.ppermute(loss_row, MP, cross)
-    )
-    loss = jnp.sum(loss_row) / (tokens_all * student_width)
+    loss = jnp.sum(mp_sum(summed[20:21])) / (tokens_all * student_width)
     grads = jnp.concatenate(
         [
             grads[:, :16].reshape(2 * experts, 8, lanes),

time: 219 us -> 220 us (level)
  matrix products: 12.3 us -> 2.16 us
  Pallas kernels: 4.78 us -> 12.2 us
  local copies, waits for them, and re-layouts: 9.84 us -> 15 us
    ppermute x17 -> x15, starting transfers between devices: 31.2 us -> 16.3 us  [swap(): return lax.ppermute(value, axis, [(0, 1), (1, 0)])]
    ppermute x2 -> x6, waiting for transfers between devices: 2.02 us -> 14.7 us  [the longest x4 12.9 us: body(): lax.ppermute(proj, ALL, permutation(proj_target(step)))]
    ppermute x2 -> x6, starting transfers between devices: 1.37 us -> 13.1 us  [the longest x4 11.2 us: body(): lax.ppermute(proj, ALL, permutation(proj_target(step)))]
    dot_general x13 -> x1, matrix products: 10.6 us -> 0.56 us  [dot(): return jnp.dot(a, b, preferred_element_type=jnp.float32)]
    all_to_all x2, waiting for transfers between devices: 21.8 us -> 12.6 us  [exchange_slots(): lax.all_to_all(rows, DP, split_axis=0, concat_axis=0, tiled=True)]
    pallas_call x0 -> x2, Pallas kernels: none -> 7.42 us  [expert_call(): pl.pallas_call(kernel, out_shape=shapes, in_specs=[pl.BlockSpec(memory_sp...]
    unnamed x25 -> x29, local copies, waits for them, and re-layouts: 4.15 us -> 9.32 us
    ppermute x17 -> x15, waiting for transfers between devices: 38.7 us -> 35.7 us  [swap(): return lax.ppermute(value, axis, [(0, 1), (1, 0)])]
  transfers between devices with their start and end apart: 25 -> 27, of which waited for: 16 -> 15; matrix products, arithmetic and copies ran while one was open for 8% -> 3% of each run, Pallas kernels for 0% -> 4%
where the time goes in v5:
time: 220 us
  waiting for transfers between devices  78.2 us (36%)
  starting transfers between devices  62.8 us (29%)
  blocking collectives  22.3 us (10%)
  between operations  19.9 us (9%)
  local copies, waits for them, and re-layouts  15 us (7%)
  Pallas kernels  12.2 us (6%)
  other arithmetic  6.93 us (3%)
    ppermute x15, waiting for transfers between devices, swap(): return lax.ppermute(value, axis, [(0, 1), (1, 0)])  35.7 us
    all_to_all x2, starting transfers between devices, exchange_slots(): lax.all_to_all(rows, DP, split_axis=0, concat_axis=0, tiled=True)  22.8 us
    all_to_all x1, blocking collectives, body(): bundle = lax.all_to_all(bundle, DP, split_axis=0, concat_axis=0, tiled=True)  22.3 us
    ppermute x15, starting transfers between devices, swap(): return lax.ppermute(value, axis, [(0, 1), (1, 0)])  16.3 us
    ppermute x4, waiting for transfers between devices, body(): lax.ppermute(proj, ALL, permutation(proj_target(step)))  12.9 us
    all_to_all x2, waiting for transfers between devices, exchange_slots(): lax.all_to_all(rows, DP, split_axis=0, concat_axis=0, tiled=True)  12.6 us
    ppermute x4, starting transfers between devices, body(): lax.ppermute(proj, ALL, permutation(proj_target(step)))  11.2 us
    unnamed x29, local copies, waits for them, and re-layouts  9.32 us
  transfers between devices with their start and end apart: 27, of which 15 were waited for; matrix products, arithmetic and copies ran while one was open for 3% of the time, Pallas kernels for 4%

profile of v5, /device:TPU:32, one launch (start us, length us, event | category | flops | bytes accessed | tf_op | source)
XLA Modules:
  0.0 219.5 jit_solution(4894405401100132773)
XLA Ops:
  7.2 0.8 copy.15
  8.3 0.6 reduce-window.6
  9.3 0.6 convolution_convert_fusion.1
  9.9 1.4 reshape.130
  11.3 12.6 %all-to-all-start = ((bf16[64,35,128]{2,1,0:T(8,128)(2,1)}), bf16[64,35,128]{2,1,0:T(8,128)(2,1)S(1)}, u32[]{:S(2)}, u32[]{:S(2)}) async-start(bf16[64,35,128]{2,1,0:T(8,128)(2,1)} %reshape.130), calls=%async_computation | async-start | bytes 1310720 | tf_op jit(solution)/shard_map/all_to_all | solution.py:55
  23.9 0.7 collective-permute-start
  24.6 4.2 %collective-permute-start.1 = (bf16[56,1280]{1,0:T(8,128)(2,1)S(1)}, bf16[56,1280]{1,0:T(8,128)(2,1)S(1)}, u32[]{:S(2)}, u32[]{:S(2)}) collective-permute-start(bf16[56,1280]{1,0:T(8,128)(2,1)S(1)} %copy-done.13), channel_id=1, source_target_pairs={{0,128},{1,129},{2,132},{3,133},{4,0},{5,1},{6,4},{7,5},{8,136},{9... | collective-permute-start | bytes 430088 | tf_op jit(solution)/shard_map/ppermute | solution.py:295
  28.8 3.0 %collective-permute-start.2 = (bf16[56,1280]{1,0:T(8,128)(2,1)S(1)}, bf16[56,1280]{1,0:T(8,128)(2,1)S(1)}, u32[]{:S(2)}, u32[]{:S(2)}) collective-permute-start(bf16[56,1280]{1,0:T(8,128)(2,1)S(1)} %copy-done.13), channel_id=1, source_target_pairs={{0,8},{1,9},{2,12},{3,13},{4,136},{5,137},{6,140},{7,141},{8,0},{9... | collective-permute-start | bytes 430088 | tf_op jit(solution)/shard_map/ppermute | solution.py:295
  31.8 3.4 %collective-permute-start.3 = (bf16[56,1280]{1,0:T(8,128)(2,1)S(1)}, bf16[56,1280]{1,0:T(8,128)(2,1)S(1)}, u32[]{:S(2)}, u32[]{:S(2)}) collective-permute-start(bf16[56,1280]{1,0:T(8,128)(2,1)S(1)} %copy-done.13), channel_id=1, source_target_pairs={{0,136},{1,137},{2,140},{3,141},{4,8},{5,9},{6,12},{7,13},{8,128},... | collective-permute-start | bytes 430088 | tf_op jit(solution)/shard_map/ppermute | solution.py:295
  35.2 10.0 %collective-permute-done.1 = bf16[56,1280]{1,0:T(8,128)(2,1)S(1)} collective-permute-done((bf16[56,1280]{1,0:T(8,128)(2,1)S(1)}, bf16[56,1280]{1,0:T(8,128)(2,1)S(1)}, u32[]{:S(2)}, u32[]{:S(2)}) %collective-permute-start.1) | collective-permute-done | bytes 143392 | tf_op jit(solution)/shard_map/ppermute | solution.py:295
  45.2 2.9 %collective-permute-done.3 = bf16[56,1280]{1,0:T(8,128)(2,1)S(1)} collective-permute-done((bf16[56,1280]{1,0:T(8,128)(2,1)S(1)}, bf16[56,1280]{1,0:T(8,128)(2,1)S(1)}, u32[]{:S(2)}, u32[]{:S(2)}) %collective-permute-start.3) | collective-permute-done | bytes 143392 | tf_op jit(solution)/shard_map/ppermute | solution.py:295
  48.2 0.9 maximum_select_fusion
  49.1 0.6 reshape.131.own_ref
  49.8 3.4 %collective-permute-start.4 = (bf16[320,896]{1,0:T(8,128)(2,1)S(1)}, bf16[320,896]{1,0:T(8,128)(2,1)S(1)}, u32[]{:S(2)}, u32[]{:S(2)}) collective-permute-start(bf16[320,896]{1,0:T(8,128)(2,1)S(1)} %reshape.131.own_ref), channel_id=1, source_target_pairs={{0,2},{2,0},{1,3},{3,1},{4,6},{6,4},{5,7},{7,5},{8,10},{10,8},{9,1... | collective-permute-start | bytes 1720328 | tf_op jit(solution)/shard_map/ppermute | solution.py:34
  53.3 0.2 shard_map.138
  53.5 0.2 collective-permute-start.5
  53.8 1.0 collective-permute-done.5
  54.9 2.0 copy-done.1
  56.9 2.0 copy-done.3
  59.0 2.5 %shard_map.139 = (f32[320,512]{1,0:T(8,128)S(1)}, f32[320,512]{1,0:T(8,128)S(1)}) custom-call(s32[2]{0:T(128)S(1)} %pad_add_fusion.1.place_ref, bf16[320,896]{1,0:T(8,128)(2,1)S(1)} %reshape.131.own_ref, bf16[320,896]{1,0:T(8,128)(2,1)S(1)} %collective-permute-done.6.other_ref, bf16[3584,512]{1,0:T(8,128)(2,1)S(1)} %bitcast.63, bf16[3584,512]{1,0:T(8,128)(2,1)S(1)} %bitcast.65), custom_call_target="tpu_custom_call" | custom-call | flops 100 | bytes 100 | tf_op jit(solution)/shard_map/pallas_call | solution.py:211
  61.5 5.3 %collective-permute-done.4.own_ref = bf16[320,896]{1,0:T(8,128)(2,1)S(1)} collective-permute-done((bf16[320,896]{1,0:T(8,128)(2,1)S(1)}, bf16[320,896]{1,0:T(8,128)(2,1)S(1)}, u32[]{:S(2)}, u32[]{:S(2)}) %collective-permute-start.4) | collective-permute-done | bytes 573472 | tf_op jit(solution)/shard_map/ppermute | solution.py:34
  66.8 2.0 collective-permute-done.7.other_ref
  68.8 2.1 copy-done.6
  70.8 4.9 %shard_map.140 = (bf16[320,896]{1,0:T(8,128)(2,1)S(1)}, bf16[320,896]{1,0:T(8,128)(2,1)S(1)}, bf16[320,896]{1,0:T(8,128)(2,1)S(1)}, bf16[320,896]{1,0:T(8,128)(2,1)S(1)}) custom-call(s32[2]{0:T(128)S(1)} %pad_add_fusion.1.place_ref, f32[320,512]{1,0:T(8,128)S(1)} %get-tuple-element.33.gate_near_ref, f32[320,512]{1,0:T(8,128)S(1)} %get-tuple-element.34.up_near_ref, ...), custom_call_target="tpu_custom_call" | custom-call | flops 100 | bytes 100 | tf_op jit(solution)/shard_map/pallas_call | solution.py:211
  75.8 0.4 collective-permute-start.9
  76.2 0.4 collective-permute-start.8
  76.5 1.5 collective-permute-done.9
  78.2 3.4 %collective-permute-start.10 = (bf16[320,896]{1,0:T(8,128)(2,1)S(1)}, bf16[320,896]{1,0:T(8,128)(2,1)S(1)}, u32[]{:S(2)}, u32[]{:S(2)}) collective-permute-start(bf16[320,896]{1,0:T(8,128)(2,1)S(1)} %add_convert_fusion.1), channel_id=1, source_target_pairs={{0,2},{2,0},{1,3},{3,1},{4,6},{6,4},{5,7},{7,5},{8,10},{10,8},{9,1... | collective-permute-start | bytes 1720328 | tf_op jit(solution)/shard_map/ppermute | solution.py:34
  81.5 13.3 %collective-permute-done.10 = bf16[320,896]{1,0:T(8,128)(2,1)S(1)} collective-permute-done((bf16[320,896]{1,0:T(8,128)(2,1)S(1)}, bf16[320,896]{1,0:T(8,128)(2,1)S(1)}, u32[]{:S(2)}, u32[]{:S(2)}) %collective-permute-start.10) | collective-permute-done | bytes 573472 | tf_op jit(solution)/shard_map/ppermute | solution.py:34
  94.8 0.2 add_convert_fusion
  95.1 1.4 reshape.133
  96.5 10.2 %all-to-all-start.1 = ((bf16[64,35,128]{2,1,0:T(8,128)(2,1)}), bf16[64,35,128]{2,1,0:T(8,128)(2,1)S(1)}, u32[]{:S(2)}, u32[]{:S(2)}) async-start(bf16[64,35,128]{2,1,0:T(8,128)(2,1)} %reshape.133), calls=%async_computation.1 | async-start | bytes 1310720 | tf_op jit(solution)/shard_map/all_to_all | solution.py:55
  107.0 2.2 %collective-permute-start.11 = (f32[128,128]{1,0:T(8,128)S(1)}, f32[128,128]{1,0:T(8,128)S(1)}, u32[]{:S(2)}, u32[]{:S(2)}) collective-permute-start(f32[128,128]{1,0:T(8,128)S(1)} %add.50), channel_id=1, source_target_pairs={{0,2},{2,0},{1,3},{3,1},{4,6},{6,4},{5,7},{7,5},{8,10},{10,8},{9,1... | collective-permute-start | bytes 196616 | tf_op jit(solution)/shard_map/ppermute | solution.py:34
  109.2 0.4 fusion.1
  109.6 4.5 %collective-permute-done.11 = f32[128,128]{1,0:T(8,128)S(1)} collective-permute-done((f32[128,128]{1,0:T(8,128)S(1)}, f32[128,128]{1,0:T(8,128)S(1)}, u32[]{:S(2)}, u32[]{:S(2)}) %collective-permute-start.11) | collective-permute-done | bytes 65568 | tf_op jit(solution)/shard_map/ppermute | solution.py:34
  114.1 0.3 shard_map.141
  114.4 12.6 %all-to-all-done.1 = bf16[64,35,128]{2,1,0:T(8,128)(2,1)S(1)} async-done(((bf16[64,35,128]{2,1,0:T(8,128)(2,1)}), bf16[64,35,128]{2,1,0:T(8,128)(2,1)S(1)}, u32[]{:S(2)}, u32[]{:S(2)}) %all-to-all-start.1) | async-done | bytes 573472 | tf_op jit(solution)/shard_map/all_to_all | solution.py:55
  127.1 0.6 reshape.134
  127.7 0.6 convolution_convert_fusion.2.own_ref
  128.3 1.2 collective-permute-start.13
  129.5 4.9 %collective-permute-done.13.pair_ref = bf16[128,896]{1,0:T(8,128)(2,1)S(1)} collective-permute-done((bf16[128,896]{1,0:T(8,128)(2,1)S(1)}, bf16[128,896]{1,0:T(8,128)(2,1)S(1)}, u32[]{:S(2)}, u32[]{:S(2)}) %collective-permute-start.13) | collective-permute-done | bytes 229408 | tf_op jit(solution)/shard_map/ppermute | solution.py:34
  134.5 1.4 collective-permute-done.14.pair_far_ref
  135.9 2.3 %copy-done.5 = bf16[1792,1280]{1,0:T(8,128)(2,1)S(1)} copy-done((bf16[1792,1280]{1,0:T(8,128)(2,1)S(1)}, bf16[1792,1280]{1,0:T(8,128)(2,1)}, u32[]{:S(2)}) %copy-start.5) | copy-done | bytes 4587544
  138.2 4.2 %shard_map.142 = (bf16[128,1280]{1,0:T(8,128)(2,1)S(1)}, bf16[128,1280]{1,0:T(8,128)(2,1)S(1)}) custom-call(s32[3]{0:T(128)S(1)} %pad_add_fusion.order_ref, bf16[128,896]{1,0:T(8,128)(2,1)S(1)} %convolution_convert_fusion.2.own_ref, bf16[128,896]{1,0:T(8,128)(2,1)S(1)} %collective-permute-done.12.own_far_ref, ...), custom_call_target="tpu_custom_call" | custom-call | flops 1174405120 | bytes 6000000 | tf_op jit(solution)/shard_map/pallas_call | solution.py:92
  142.4 0.7 collective-permute-start.15
  143.1 4.8 %collective-permute-start.16 = (bf16[128,1280]{1,0:T(8,128)(2,1)S(1)}, bf16[128,1280]{1,0:T(8,128)(2,1)S(1)}, u32[]{:S(2)}, u32[]{:S(2)}) collective-permute-start(bf16[128,1280]{1,0:T(8,128)(2,1)S(1)} %get-tuple-element.48), channel_id=1, source_target_pairs={{0,4},{1,5},{2,0},{3,1},{4,6},{5,7},{6,2},{7,3},{8,12},{9,13},{10,... | collective-permute-start | bytes 983048 | tf_op jit(solution)/shard_map/ppermute | solution.py:376
  148.0 8.2 %collective-permute-done.16 = bf16[128,1280]{1,0:T(8,128)(2,1)S(1)} collective-permute-done((bf16[128,1280]{1,0:T(8,128)(2,1)S(1)}, bf16[128,1280]{1,0:T(8,128)(2,1)S(1)}, u32[]{:S(2)}, u32[]{:S(2)}) %collective-permute-start.16) | collective-permute-done | bytes 327712 | tf_op jit(solution)/shard_map/ppermute | solution.py:376
  156.3 0.2 fusion.20
  156.7 2.4 %collective-permute-start.18 = (f32[128,64]{0,1:T(8,128)S(1)}, f32[128,64]{0,1:T(8,128)S(1)}, u32[]{:S(2)}, u32[]{:S(2)}) collective-permute-start(f32[128,64]{0,1:T(8,128)S(1)} %fusion.20), channel_id=1, source_target_pairs={{0,2},{2,0},{1,3},{3,1},{4,6},{6,4},{5,7},{7,5},{8,10},{10,8},{9,1... | collective-permute-start | bytes 98312 | tf_op jit(solution)/shard_map/ppermute | solution.py:34
  159.1 0.9 collective-permute-start.19
  160.0 0.2 fusion
  160.2 0.8 multiply_reduce_fusion
  164.7 1.3 fusion.18
  166.4 22.3 %all_to_all.20 = bf16[64,24,128]{2,1,0:T(8,128)(2,1)S(1)} all-to-all(bf16[64,24,128]{2,1,0:T(8,128)(2,1)S(1)} %pad_maximum_fusion), channel_id=1, replica_groups=mesh['yl'=2,'z'=8,'xh'=2,'xl'=2,'yh'=2,'c'=2] {'yl','z','xh','xl'}, dimensions={0} | all-to-all | bytes 786432 | tf_op jit(solution)/shard_map/all_to_all | solution.py:424
  188.8 0.8 broadcast_in_dim.32
  189.6 5.1 %all-to-all-start.3 = ((bf16[64,24,128]{2,1,0:T(8,128)(2,1)}), bf16[64,24,128]{2,1,0:T(8,128)(2,1)S(1)}, u32[]{:S(2)}, u32[]{:S(2)}) async-start(bf16[64,24,128]{2,1,0:T(8,128)(2,1)} %broadcast_in_dim.32), calls=%async_computation.3 | async-start | bytes 786432 | tf_op jit(solution)/shard_map/all_to_all | solution.py:427
  194.8 2.4 %collective-permute-start.21 = (f32[1,128]{1,0:T(1,128)S(1)}, f32[1,128]{1,0:T(1,128)S(1)}, u32[]{:S(2)}, u32[]{:S(2)}) collective-permute-start(f32[1,128]{1,0:T(1,128)S(1)} %slice.43), channel_id=1, source_target_pairs={{0,2},{2,0},{1,3},{3,1},{4,6},{6,4},{5,7},{7,5},{8,10},{10,8},{9,1... | collective-permute-start | bytes 1544 | tf_op jit(solution)/shard_map/ppermute | solution.py:34
  197.3 0.9 collective-permute-start.22
  198.2 1.8 collective-permute-done.21
  200.0 1.8 collective-permute-done.22
  201.7 0.6 add_reduce_fusion
  203.0 7.0 %all-to-all-done.3 = bf16[64,24,128]{2,1,0:T(8,128)(2,1)S(1)} async-done(((bf16[64,24,128]{2,1,0:T(8,128)(2,1)}), bf16[64,24,128]{2,1,0:T(8,128)(2,1)S(1)}, u32[]{:S(2)}, u32[]{:S(2)}) %all-to-all-start.3) | async-done | bytes 393248 | tf_op jit(solution)/shard_map/all_to_all | solution.py:427
  210.0 0.7 convert_bitcast_fusion.1
  210.8 0.7 convert_bitcast_fusion
  (77 shorter events, 2.4 us)
Async XLA Ops:
  7.2 2.1 copy-start
  9.8 14.1 %copy-start.13 = (bf16[56,1280]{1,0:T(8,128)(2,1)S(1)}, bf16[56,1280]{1,0:T(8,128)(2,1)}, u32[]{:S(2)}) copy-start(bf16[56,1280]{1,0:T(8,128)(2,1)} %param.17) | copy-start | bytes 430084
  11.3 37.8 %all-to-all-start = ((bf16[64,35,128]{2,1,0:T(8,128)(2,1)}), bf16[64,35,128]{2,1,0:T(8,128)(2,1)S(1)}, u32[]{:S(2)}, u32[]{:S(2)}) async-start(bf16[64,35,128]{2,1,0:T(8,128)(2,1)} %reshape.130), calls=%async_computation | async-start | bytes 1310720 | tf_op jit(solution)/shard_map/all_to_all | solution.py:55
  23.9 103.8 %all-gather.2.cloned.1.call-start = ((), (), s32[]{:S(2)}) async-start(), calls=%async_computation.4 | async-start | bytes 5160960 | tf_op jit(solution)/shard_map/all_gather | solution.py:298
  23.9 11.2 %collective-permute-start = (bf16[56,1280]{1,0:T(8,128)(2,1)S(1)}, bf16[56,1280]{1,0:T(8,128)(2,1)S(1)}, u32[]{:S(2)}, u32[]{:S(2)}) collective-permute-start(bf16[56,1280]{1,0:T(8,128)(2,1)S(1)} %copy-done.13), channel_id=1, source_target_pairs={{0,0},{1,1},{2,4},{3,5},{4,128},{5,129},{6,132},{7,133},{8,8},{9,9... | collective-permute-start | bytes 430088 | tf_op jit(solution)/shard_map/ppermute | solution.py:295
  24.6 20.5 %collective-permute-start.1 = (bf16[56,1280]{1,0:T(8,128)(2,1)S(1)}, bf16[56,1280]{1,0:T(8,128)(2,1)S(1)}, u32[]{:S(2)}, u32[]{:S(2)}) collective-permute-start(bf16[56,1280]{1,0:T(8,128)(2,1)S(1)} %copy-done.13), channel_id=1, source_target_pairs={{0,128},{1,129},{2,132},{3,133},{4,0},{5,1},{6,4},{7,5},{8,136},{9... | collective-permute-start | bytes 430088 | tf_op jit(solution)/shard_map/ppermute | solution.py:295
  28.8 16.4 %collective-permute-start.2 = (bf16[56,1280]{1,0:T(8,128)(2,1)S(1)}, bf16[56,1280]{1,0:T(8,128)(2,1)S(1)}, u32[]{:S(2)}, u32[]{:S(2)}) collective-permute-start(bf16[56,1280]{1,0:T(8,128)(2,1)S(1)} %copy-done.13), channel_id=1, source_target_pairs={{0,8},{1,9},{2,12},{3,13},{4,136},{5,137},{6,140},{7,141},{8,0},{9... | collective-permute-start | bytes 430088 | tf_op jit(solution)/shard_map/ppermute | solution.py:295
  31.8 16.3 %collective-permute-start.3 = (bf16[56,1280]{1,0:T(8,128)(2,1)S(1)}, bf16[56,1280]{1,0:T(8,128)(2,1)S(1)}, u32[]{:S(2)}, u32[]{:S(2)}) collective-permute-start(bf16[56,1280]{1,0:T(8,128)(2,1)S(1)} %copy-done.13), channel_id=1, source_target_pairs={{0,136},{1,137},{2,140},{3,141},{4,8},{5,9},{6,12},{7,13},{8,128},... | collective-permute-start | bytes 430088 | tf_op jit(solution)/shard_map/ppermute | solution.py:295
  49.1 4.1 %copy-start.11 = (bf16[1280]{0:T(1024)(128)(2,1)S(1)}, bf16[1280]{0:T(1024)(128)(2,1)}, u32[]{:S(2)}) copy-start(bf16[1280]{0:T(1024)(128)(2,1)} %param.19) | copy-start | bytes 7684
  49.1 4.1 %copy-start.7 = (bf16[128,1280]{1,0:T(8,128)(2,1)S(1)}, bf16[128,1280]{1,0:T(8,128)(2,1)}, u32[]{:S(2)}) copy-start(bf16[128,1280]{1,0:T(8,128)(2,1)} %student_ref.3) | copy-start | bytes 983044
  49.1 4.2 %copy-start.9 = (bf16[1280,64]{0,1:T(8,128)(2,1)S(1)}, bf16[1280,64]{0,1:T(8,128)(2,1)}, u32[]{:S(2)}) copy-start(bf16[1280,64]{0,1:T(8,128)(2,1)} %param.20) | copy-start | bytes 491524
  49.7 5.1 %collective-permute-start.6 = (bf16[320,896]{1,0:T(8,128)(2,1)S(1)}, bf16[320,896]{1,0:T(8,128)(2,1)S(1)}, u32[]{:S(2)}, u32[]{:S(2)}) collective-permute-start(bf16[320,896]{1,0:T(8,128)(2,1)S(1)} %reshape.131.own_ref), channel_id=1, source_target_pairs={{0,1},{1,0},{2,3},{3,2},{4,5},{5,4},{6,7},{7,6},{8,9},{9,8},{10,11... | collective-permute-start | bytes 1720328 | tf_op jit(solution)/shard_map/ppermute | solution.py:34
  49.8 16.9 %collective-permute-start.4 = (bf16[320,896]{1,0:T(8,128)(2,1)S(1)}, bf16[320,896]{1,0:T(8,128)(2,1)S(1)}, u32[]{:S(2)}, u32[]{:S(2)}) collective-permute-start(bf16[320,896]{1,0:T(8,128)(2,1)S(1)} %reshape.131.own_ref), channel_id=1, source_target_pairs={{0,2},{2,0},{1,3},{3,1},{4,6},{6,4},{5,7},{7,5},{8,10},{10,8},{9,1... | collective-permute-start | bytes 1720328 | tf_op jit(solution)/shard_map/ppermute | solution.py:34
  53.5 1.3 collective-permute-start.5
  54.9 2.0 copy-start.1
  56.9 2.0 copy-start.3
  59.0 9.8 %copy-start.2 = (bf16[1,3584,512]{2,1,0:T(8,128)(2,1)S(1)}, bf16[1,3584,512]{2,1,0:T(8,128)(2,1)}, u32[]{:S(2)}) copy-start(bf16[1,3584,512]{2,1,0:T(8,128)(2,1)} %param.14) | copy-start | bytes 11010052
  59.0 9.8 %copy-start.4 = (bf16[1,3584,512]{2,1,0:T(8,128)(2,1)S(1)}, bf16[1,3584,512]{2,1,0:T(8,128)(2,1)}, u32[]{:S(2)}) copy-start(bf16[1,3584,512]{2,1,0:T(8,128)(2,1)} %param.15) | copy-start | bytes 11010052
  66.8 2.0 collective-permute-start.7
  68.8 2.1 copy-start.6
  75.8 2.2 %collective-permute-start.9 = (bf16[320,896]{1,0:T(8,128)(2,1)S(1)}, bf16[320,896]{1,0:T(8,128)(2,1)S(1)}, u32[]{:S(2)}, u32[]{:S(2)}) collective-permute-start(bf16[320,896]{1,0:T(8,128)(2,1)S(1)} %get-tuple-element.39), channel_id=1, source_target_pairs={{0,1},{1,0},{2,3},{3,2},{4,5},{5,4},{6,7},{7,6},{8,9},{9,8},{10,11... | collective-permute-start | bytes 1720328 | tf_op jit(solution)/shard_map/ppermute | solution.py:34
  76.2 5.4 %collective-permute-start.8 = (bf16[320,896]{1,0:T(8,128)(2,1)S(1)}, bf16[320,896]{1,0:T(8,128)(2,1)S(1)}, u32[]{:S(2)}, u32[]{:S(2)}) collective-permute-start(bf16[320,896]{1,0:T(8,128)(2,1)S(1)} %get-tuple-element.37), channel_id=1, source_target_pairs={{0,1},{1,0},{2,3},{3,2},{4,5},{5,4},{6,7},{7,6},{8,9},{9,8},{10,11... | collective-permute-start | bytes 1720328 | tf_op jit(solution)/shard_map/ppermute | solution.py:34
  78.2 16.6 %collective-permute-start.10 = (bf16[320,896]{1,0:T(8,128)(2,1)S(1)}, bf16[320,896]{1,0:T(8,128)(2,1)S(1)}, u32[]{:S(2)}, u32[]{:S(2)}) collective-permute-start(bf16[320,896]{1,0:T(8,128)(2,1)S(1)} %add_convert_fusion.1), channel_id=1, source_target_pairs={{0,2},{2,0},{1,3},{3,1},{4,6},{6,4},{5,7},{7,5},{8,10},{10,8},{9,1... | collective-permute-start | bytes 1720328 | tf_op jit(solution)/shard_map/ppermute | solution.py:34
  95.0 11.6 %copy-start.12 = (f32[128,2]{0,1:T(2,128)S(1)}, f32[128,2]{0,1:T(2,128)}, u32[]{:S(2)}) copy-start(f32[128,2]{0,1:T(2,128)} %param.13) | copy-start | bytes 3076
  96.5 17.6 %copy-start.8 = (bf16[64,1280]{1,0:T(8,128)(2,1)S(1)}, bf16[64,1280]{1,0:T(8,128)(2,1)}, u32[]{:S(2)}) copy-start(bf16[64,1280]{1,0:T(8,128)(2,1)} %up_ref.1) | copy-start | bytes 491524
  96.5 30.6 %all-to-all-start.1 = ((bf16[64,35,128]{2,1,0:T(8,128)(2,1)}), bf16[64,35,128]{2,1,0:T(8,128)(2,1)S(1)}, u32[]{:S(2)}, u32[]{:S(2)}) async-start(bf16[64,35,128]{2,1,0:T(8,128)(2,1)} %reshape.133), calls=%async_computation.1 | async-start | bytes 1310720 | tf_op jit(solution)/shard_map/all_to_all | solution.py:55
  107.0 7.1 %collective-permute-start.11 = (f32[128,128]{1,0:T(8,128)S(1)}, f32[128,128]{1,0:T(8,128)S(1)}, u32[]{:S(2)}, u32[]{:S(2)}) collective-permute-start(f32[128,128]{1,0:T(8,128)S(1)} %add.50), channel_id=1, source_target_pairs={{0,2},{2,0},{1,3},{3,1},{4,6},{6,4},{5,7},{7,5},{8,10},{10,8},{9,1... | collective-permute-start | bytes 196616 | tf_op jit(solution)/shard_map/ppermute | solution.py:34
  128.3 6.1 %collective-permute-start.13 = (bf16[128,896]{1,0:T(8,128)(2,1)S(1)}, bf16[128,896]{1,0:T(8,128)(2,1)S(1)}, u32[]{:S(2)}, u32[]{:S(2)}) collective-permute-start(bf16[128,896]{1,0:T(8,128)(2,1)S(1)} %convolution_convert_fusion.2.own_ref), channel_id=1, source_target_pairs={{0,4},{4,0},{1,5},{5,1},{2,6},{6,2},{3,7},{7,3},{8,12},{12,8},{9,1... | collective-permute-start | bytes 688136 | tf_op jit(solution)/shard_map/ppermute | solution.py:34
  129.5 5.0 %collective-permute-start.12 = (bf16[128,896]{1,0:T(8,128)(2,1)S(1)}, bf16[128,896]{1,0:T(8,128)(2,1)S(1)}, u32[]{:S(2)}, u32[]{:S(2)}) collective-permute-start(bf16[128,896]{1,0:T(8,128)(2,1)S(1)} %convolution_convert_fusion.2.own_ref), channel_id=1, source_target_pairs={{0,1},{1,0},{2,3},{3,2},{4,5},{5,4},{6,7},{7,6},{8,9},{9,8},{10,11... | collective-permute-start | bytes 688136 | tf_op jit(solution)/shard_map/ppermute | solution.py:34
  134.4 1.5 collective-permute-start.14
  135.9 2.3 %copy-start.5 = (bf16[1792,1280]{1,0:T(8,128)(2,1)S(1)}, bf16[1792,1280]{1,0:T(8,128)(2,1)}, u32[]{:S(2)}) copy-start(bf16[1792,1280]{1,0:T(8,128)(2,1)} %all-gather.2.cloned.1.call-done.block_ref) | copy-start | bytes 13762564
  142.4 5.5 %collective-permute-start.15 = (bf16[128,1280]{1,0:T(8,128)(2,1)S(1)}, bf16[128,1280]{1,0:T(8,128)(2,1)S(1)}, u32[]{:S(2)}, u32[]{:S(2)}) collective-permute-start(bf16[128,1280]{1,0:T(8,128)(2,1)S(1)} %get-tuple-element.47), channel_id=1, source_target_pairs={{0,0},{1,1},{2,4},{3,5},{4,2},{5,3},{6,6},{7,7},{8,8},{9,9},{10,12... | collective-permute-start | bytes 983048 | tf_op jit(solution)/shard_map/ppermute | solution.py:376
  143.1 13.1 %collective-permute-start.16 = (bf16[128,1280]{1,0:T(8,128)(2,1)S(1)}, bf16[128,1280]{1,0:T(8,128)(2,1)S(1)}, u32[]{:S(2)}, u32[]{:S(2)}) collective-permute-start(bf16[128,1280]{1,0:T(8,128)(2,1)S(1)} %get-tuple-element.48), channel_id=1, source_target_pairs={{0,4},{1,5},{2,0},{3,1},{4,6},{5,7},{6,2},{7,3},{8,12},{9,13},{10,... | collective-permute-start | bytes 983048 | tf_op jit(solution)/shard_map/ppermute | solution.py:376
  156.3 4.7 %copy-start.10 = (f32[128,1280]{1,0:T(8,128)}, f32[128,1280]{1,0:T(8,128)S(1)}, u32[]{:S(2)}) copy-start(f32[128,1280]{1,0:T(8,128)S(1)} %get-tuple-element.53) | copy-start | bytes 1966084
  156.6 9.4 %collective-permute-start.17 = (f32[128,64]{0,1:T(8,128)S(1)}, f32[128,64]{0,1:T(8,128)S(1)}, u32[]{:S(2)}, u32[]{:S(2)}) collective-permute-start(f32[128,64]{0,1:T(8,128)S(1)} %fusion.20), channel_id=1, source_target_pairs={{0,1},{1,0},{2,3},{3,2},{4,5},{5,4},{6,7},{7,6},{8,9},{9,8},{10,11... | collective-permute-start | bytes 98312 | tf_op jit(solution)/shard_map/ppermute | solution.py:34
  156.7 9.3 %collective-permute-start.18 = (f32[128,64]{0,1:T(8,128)S(1)}, f32[128,64]{0,1:T(8,128)S(1)}, u32[]{:S(2)}, u32[]{:S(2)}) collective-permute-start(f32[128,64]{0,1:T(8,128)S(1)} %fusion.20), channel_id=1, source_target_pairs={{0,2},{2,0},{1,3},{3,1},{4,6},{6,4},{5,7},{7,5},{8,10},{10,8},{9,1... | collective-permute-start | bytes 98312 | tf_op jit(solution)/shard_map/ppermute | solution.py:34
  159.1 6.9 %collective-permute-start.19 = (f32[128,64]{0,1:T(8,128)S(1)}, f32[128,64]{0,1:T(8,128)S(1)}, u32[]{:S(2)}, u32[]{:S(2)}) collective-permute-start(f32[128,64]{0,1:T(8,128)S(1)} %fusion.20), channel_id=1, source_target_pairs={{0,3},{1,2},{2,1},{3,0},{4,7},{5,6},{6,5},{7,4},{8,11},{9,10},{10,... | collective-permute-start | bytes 98312 | tf_op jit(solution)/shard_map/ppermute | solution.py:42
  189.6 20.3 %all-to-all-start.3 = ((bf16[64,24,128]{2,1,0:T(8,128)(2,1)}), bf16[64,24,128]{2,1,0:T(8,128)(2,1)S(1)}, u32[]{:S(2)}, u32[]{:S(2)}) async-start(bf16[64,24,128]{2,1,0:T(8,128)(2,1)} %broadcast_in_dim.32), calls=%async_computation.3 | async-start | bytes 786432 | tf_op jit(solution)/shard_map/all_to_all | solution.py:427
  194.7 3.5 %collective-permute-start.20 = (f32[1,128]{1,0:T(1,128)S(1)}, f32[1,128]{1,0:T(1,128)S(1)}, u32[]{:S(2)}, u32[]{:S(2)}) collective-permute-start(f32[1,128]{1,0:T(1,128)S(1)} %slice.43), channel_id=1, source_target_pairs={{0,1},{1,0},{2,3},{3,2},{4,5},{5,4},{6,7},{7,6},{8,9},{9,8},{10,11... | collective-permute-start | bytes 1544 | tf_op jit(solution)/shard_map/ppermute | solution.py:34
  194.8 5.1 %collective-permute-start.21 = (f32[1,128]{1,0:T(1,128)S(1)}, f32[1,128]{1,0:T(1,128)S(1)}, u32[]{:S(2)}, u32[]{:S(2)}) collective-permute-start(f32[1,128]{1,0:T(1,128)S(1)} %slice.43), channel_id=1, source_target_pairs={{0,2},{2,0},{1,3},{3,1},{4,6},{6,4},{5,7},{7,5},{8,10},{10,8},{9,1... | collective-permute-start | bytes 1544 | tf_op jit(solution)/shard_map/ppermute | solution.py:34
  197.3 4.5 %collective-permute-start.22 = (f32[1,128]{1,0:T(1,128)S(1)}, f32[1,128]{1,0:T(1,128)S(1)}, u32[]{:S(2)}, u32[]{:S(2)}) collective-permute-start(f32[1,128]{1,0:T(1,128)S(1)} %slice.43), channel_id=1, source_target_pairs={{0,3},{1,2},{2,1},{3,0},{4,7},{5,6},{6,5},{7,4},{8,11},{9,10},{10,... | collective-permute-start | bytes 1544 | tf_op jit(solution)/shard_map/ppermute | solution.py:42
Sparse Core Ops, SparseCore 0:
  49.9 56.0 all-gather.1

commit v6 on v5

--- a/solution.py
+++ b/solution.py
@@ -22,8 +22,8 @@
     return [(place, places.index(target(*here))) for place, here in enumerate(places)]
 
 
-def proj_target(step):
-    return lambda yl, z, xh, xl, yh, c: (xl ^ (step & 1), z, xh ^ (step >> 1), yh, yl, c)
+def proj_target(yl, z, xh, xl, yh, c):
+    return (xl, z, xh, yh, yl, c)
 
 
 def home_target(step):
@@ -103,7 +103,7 @@
             pltpu.VMEM((wide // cut, depth, cut), jnp.bfloat16),
             pltpu.SemaphoreType.DMA((wide // cut,)),
         ],
-        compiler_params=pltpu.CompilerParams(vmem_limit_bytes=24 * 1024 * 1024),
+        compiler_params=pltpu.CompilerParams(vmem_limit_bytes=61 * 1024 * 1024),
         cost_estimate=pl.CostEstimate(
             flops=4 * rows * depth * wide, bytes_accessed=6_000_000, transcendentals=0
         ),
@@ -216,7 +216,7 @@
         + [pl.BlockSpec(memory_space=pltpu.HBM)] * len(weights),
         out_specs=[vmem] * len(shapes),
         scratch_shapes=scratch,
-        compiler_params=pltpu.CompilerParams(vmem_limit_bytes=32 * 1024 * 1024),
+        compiler_params=pltpu.CompilerParams(vmem_limit_bytes=61 * 1024 * 1024),
         cost_estimate=pl.CostEstimate(flops=100, bytes_accessed=100, transcendentals=0),
     )(place, *local, *weights)
 
@@ -292,13 +292,14 @@
     outgoing, proj = lax.optimization_barrier((outgoing, proj))
     arrived = exchange_slots(outgoing)
 
-    blocks = [lax.ppermute(proj, ALL, permutation(proj_target(step))) for step in range(4)]
-    proj_rows = ordered(ordered(*blocks[:2], yl), ordered(*blocks[2:], yl), xh)
+    proj_rows = lax.ppermute(proj, ALL, permutation(proj_target))
+    proj_rows = ordered(proj_rows, swap(proj_rows, "yl"), yl)
     arrived, proj_rows = lax.optimization_barrier((arrived, proj_rows))
-    proj_block = lax.all_gather(proj_rows, "z", axis=0, tiled=True)
 
     arrived_y = swap(arrived, "yh")
     arrived_c = swap(arrived, "c")
+    proj_rows = ordered(proj_rows, swap(proj_rows, "xh"), xh)
+    proj_block = lax.all_gather(proj_rows, "z", axis=0, tiled=True)
 
     gain = student_norm_weight.reshape(1, -1)
     stats = local_kernel(
@@ -396,13 +397,6 @@
     lanes = 128
     columns = up_part.shape[1]
     tiles = rank // 8 * (columns // lanes)
-    first = lax.reduce_precision(loss_here, 8, 7)
-    second = lax.reduce_precision(loss_here - first, 8, 7)
-    third = loss_here - first - second
-    lane = jnp.arange(lanes)
-    loss_row = jnp.where(
-        lane == 0, first, jnp.where(lane == 1, second, jnp.where(lane == 2, third, 0.0))
-    )
 
     def to_tiles(value):
         value = value.astype(jnp.bfloat16).reshape(rank // 8, 8, columns // lanes, lanes)
@@ -412,26 +406,48 @@
         value = value.reshape(rank // 8, columns // lanes, 8, lanes).transpose(0, 2, 1, 3)
         return value.reshape(rank, columns).astype(jnp.float32)
 
+    def to_row(total):
+        first = lax.reduce_precision(total, 8, 7)
+        second = lax.reduce_precision(total - first, 8, 7)
+        third = total - first - second
+        lane = jnp.arange(lanes)
+        row = jnp.where(
+            lane == 0, first, jnp.where(lane == 1, second, jnp.where(lane == 2, third, 0.0))
+        )
+        return row.astype(jnp.bfloat16)
+
+    def exchange(value, axes):
+        return lax.all_to_all(value, axes, split_axis=0, concat_axis=0, tiled=True)
+
+    along_x, across = ("xh", "xl"), ("yl", "z")
+    quarter = 2 * tiles // 4
     bundle = jnp.concatenate([to_tiles(up_part), to_tiles(down_part)])
     bundle = jnp.concatenate(
         [
-            bundle[: 2 * experts].reshape(experts, 16, lanes),
-            bundle[2 * experts :].reshape(experts, 4, lanes),
-            jnp.broadcast_to(loss_row.astype(jnp.bfloat16), (experts, 4, lanes)),
+            bundle.reshape(4, quarter, 8, lanes),
+            jnp.broadcast_to(to_row(loss_here), (4, 1, 8, lanes)),
         ],
         axis=1,
     )
-    bundle = lax.all_to_all(bundle, DP, split_axis=0, concat_axis=0, tiled=True)
-    summed = jnp.sum(bundle.astype(jnp.float32), axis=0)
-    grads = jnp.broadcast_to(summed.astype(jnp.bfloat16), (experts, 24, lanes))
-    grads = lax.all_to_all(grads, DP, split_axis=0, concat_axis=0, tiled=True)
-    loss = jnp.sum(mp_sum(summed[20:21])) / (tokens_all * student_width)
+    bundle = jnp.sum(exchange(bundle, along_x).astype(jnp.float32), axis=0)
+    loss_x = jnp.sum(bundle[quarter, 0])
+    bundle = bundle[:quarter].astype(jnp.bfloat16)
+    bundle = jnp.concatenate(
+        [
+            bundle[:32].reshape(16, 16, lanes),
+            bundle[32:].reshape(16, 4, lanes),
+            jnp.broadcast_to(to_row(loss_x), (16, 4, lanes)),
+        ],
+        axis=1,
+    )
+    summed = jnp.sum(exchange(bundle, across).astype(jnp.float32), axis=0)
+    grads = exchange(jnp.broadcast_to(summed.astype(jnp.bfloat16), (16, 24, lanes)), across)
+    loss = jnp.sum(mp_sum(summed[20:21])) / (tokens_all * student_hidden_input.shape[1] * mp_count)
     grads = jnp.concatenate(
-        [
-            grads[:, :16].reshape(2 * experts, 8, lanes),
-            grads[:, 16:20].reshape(experts // 2, 8, lanes),
-        ]
-    )
+        [grads[:, :16].reshape(32, 8, lanes), grads[:, 16:20].reshape(8, 8, lanes)]
+    )
+    grads = exchange(jnp.broadcast_to(grads, (4, quarter, 8, lanes)), along_x)
+    grads = grads.reshape(2 * tiles, 8, lanes)
     up_matrix_gradient = from_tiles(grads[:tiles])
     grad_a = from_tiles(grads[tiles:]).T
     return (target, grad_a, up_matrix_gradient, loss)

time: 220 us -> 239 us (1.086)
  blocking collectives: 22.3 us -> 34.5 us
  Pallas kernels: 12.2 us -> 20.4 us
  local copies, waits for them, and re-layouts: 15 us -> 8.87 us
  waiting for transfers between devices: 78.2 us -> 73.1 us
  other arithmetic: 6.93 us -> 10.8 us
  between operations: 19.9 us -> 23.6 us
    ppermute x15 -> x17, starting transfers between devices: 16.3 us -> 31.6 us  [swap(): return lax.ppermute(value, axis, [(0, 1), (1, 0)])]
    ppermute x4 -> x1, waiting for transfers between devices: 12.9 us -> 0.01 us  [body(): proj_rows = lax.ppermute(proj, ALL, permutation(proj_target))]
    all_to_all x1 -> x3, blocking collectives: 22.3 us -> 34.5 us  [exchange(): return lax.all_to_all(value, axes, split_axis=0, concat_axis=0, tiled=True)]
    ppermute x4 -> x1, starting transfers between devices: 11.2 us -> 0.67 us  [body(): proj_rows = lax.ppermute(proj, ALL, permutation(proj_target))]
    ppermute x15 -> x17, waiting for transfers between devices: 35.7 us -> 45.3 us  [swap(): return lax.ppermute(value, axis, [(0, 1), (1, 0)])]
    all_to_all x1, waiting for transfers between devices: 6.97 us -> 0.01 us  [exchange(): return lax.all_to_all(value, axes, split_axis=0, concat_axis=0, tiled=True)]
    unnamed x29 -> x35, local copies, waits for them, and re-layouts: 9.32 us -> 3.22 us
    pallas_call x2, Pallas kernels: 7.42 us -> 13.2 us  [expert_call(): pl.pallas_call(kernel, out_shape=shapes, in_specs=[pl.BlockSpec(memory_sp...]
  transfers between devices with their start and end apart: 27 -> 26, of which waited for: 15 -> 15; matrix products, arithmetic and copies ran while one was open for 3% -> 3% of each run, Pallas kernels for 4% -> 6%
where the time goes in v6:
time: 239 us; the launch traced here: 236 us
  waiting for transfers between devices  73.1 us (31%)
  starting transfers between devices  63 us (26%)
  blocking collectives  34.5 us (14%)
  between operations  23.6 us (10%)
  Pallas kernels  20.4 us (9%)
  other arithmetic  10.8 us (5%)
  local copies, waits for them, and re-layouts  8.87 us (4%)
    ppermute x17, waiting for transfers between devices, swap(): return lax.ppermute(value, axis, [(0, 1), (1, 0)])  45.3 us
    all_to_all x3, blocking collectives, exchange(): return lax.all_to_all(value, axes, split_axis=0, concat_axis=0, tiled=True)  34.5 us
    ppermute x17, starting transfers between devices, swap(): return lax.ppermute(value, axis, [(0, 1), (1, 0)])  31.6 us
    all_to_all x2, starting transfers between devices, exchange_slots(): lax.all_to_all(rows, DP, split_axis=0, concat_axis=0, tiled=True)  20.7 us
    all_to_all x2, waiting for transfers between devices, exchange_slots(): lax.all_to_all(rows, DP, split_axis=0, concat_axis=0, tiled=True)  17.2 us
    pallas_call x2, Pallas kernels, expert_call(): pl.pallas_call(kernel, out_shape=shapes, in_specs=[pl.BlockSpec(memory_sp...  13.2 us
    ppermute x2, waiting for transfers between devices, body(): lax.ppermute(piece, ALL, permutation(home_target(step))).astype(jnp.float32)  7.87 us
    pallas_call x1, Pallas kernels, product_pieces(): pl.pallas_call(product_kernel, out_shape=[jax.ShapeDtypeStruct((rows, wid...  6.6 us
  transfers between devices with their start and end apart: 26, of which 15 were waited for; matrix products, arithmetic and copies ran while one was open for 3% of the time, Pallas kernels for 6%

profile of v6, /device:TPU:32, one launch (start us, length us, event | category | flops | bytes accessed | tf_op | source)
XLA Modules:
  0.0 236.4 jit_solution(10214004309600772188)
XLA Ops:
  7.2 0.8 copy.19
  8.3 0.6 reduce-window.6
  9.3 0.6 convolution_convert_fusion.1
  9.9 1.4 reshape.136
  11.3 12.6 %all-to-all-start = ((bf16[64,35,128]{2,1,0:T(8,128)(2,1)}), bf16[64,35,128]{2,1,0:T(8,128)(2,1)S(1)}, u32[]{:S(2)}, u32[]{:S(2)}) async-start(bf16[64,35,128]{2,1,0:T(8,128)(2,1)} %reshape.136), calls=%async_computation | async-start | bytes 1310720 | tf_op jit(solution)/shard_map/all_to_all | solution.py:55
  23.9 0.7 collective-permute-start
  24.6 11.9 %collective-permute-start.1 = (bf16[56,1280]{1,0:T(8,128)(2,1)S(1)}, bf16[56,1280]{1,0:T(8,128)(2,1)S(1)}, u32[]{:S(2)}, u32[]{:S(2)}) collective-permute-start(bf16[56,1280]{1,0:T(8,128)(2,1)S(1)} %collective-permute-done), channel_id=1, source_target_pairs={{0,128},{128,0},{1,129},{129,1},{2,130},{130,2},{3,131},{131,3},{4... | collective-permute-start | bytes 430088 | tf_op jit(solution)/shard_map/ppermute | solution.py:34
  36.6 4.2 %collective-permute-done.1 = bf16[56,1280]{1,0:T(8,128)(2,1)S(1)} collective-permute-done((bf16[56,1280]{1,0:T(8,128)(2,1)S(1)}, bf16[56,1280]{1,0:T(8,128)(2,1)S(1)}, u32[]{:S(2)}, u32[]{:S(2)}) %collective-permute-start.1) | collective-permute-done | bytes 143392 | tf_op jit(solution)/shard_map/ppermute | solution.py:34
  40.8 4.0 %all-to-all-done = bf16[64,35,128]{2,1,0:T(8,128)(2,1)S(1)} async-done(((bf16[64,35,128]{2,1,0:T(8,128)(2,1)}), bf16[64,35,128]{2,1,0:T(8,128)(2,1)S(1)}, u32[]{:S(2)}, u32[]{:S(2)}) %all-to-all-start) | async-done | bytes 573472 | tf_op jit(solution)/shard_map/all_to_all | solution.py:55
  44.8 0.6 reshape.137.own_ref
  45.5 2.0 collective-permute-start.10
  47.5 6.2 %collective-permute-done.10 = bf16[112,1280]{1,0:T(8,128)(2,1)S(1)} collective-permute-done((bf16[112,1280]{1,0:T(8,128)(2,1)S(1)}, bf16[112,1280]{1,0:T(8,128)(2,1)S(1)}, u32[]{:S(2)}, u32[]{:S(2)}) %collective-permute-start.10) | collective-permute-done | bytes 286752 | tf_op jit(solution)/shard_map/ppermute | solution.py:34
  53.7 0.9 maximum_select_fusion
  54.8 3.0 %collective-permute-start.2 = (bf16[320,896]{1,0:T(8,128)(2,1)S(1)}, bf16[320,896]{1,0:T(8,128)(2,1)S(1)}, u32[]{:S(2)}, u32[]{:S(2)}) collective-permute-start(bf16[320,896]{1,0:T(8,128)(2,1)S(1)} %reshape.137.own_ref), channel_id=1, source_target_pairs={{0,2},{2,0},{1,3},{3,1},{4,6},{6,4},{5,7},{7,5},{8,10},{10,8},{9,1... | collective-permute-start | bytes 1720328 | tf_op jit(solution)/shard_map/ppermute | solution.py:34
  57.8 0.2 shard_map.138
  58.1 0.2 collective-permute-start.3
  58.3 0.6 pad_add_fusion.1.place_ref
  58.9 0.5 collective-permute-done.3
  59.4 0.8 copy-done.7
  60.3 5.3 %shard_map.139 = (f32[320,512]{1,0:T(8,128)}, f32[320,512]{1,0:T(8,128)}) custom-call(s32[2]{0:T(128)} %pad_add_fusion.1.place_ref, bf16[320,896]{1,0:T(8,128)(2,1)} %copy-done.5, bf16[320,896]{1,0:T(8,128)(2,1)} %copy-done.7, bf16[3584,512]{1,0:T(8,128)(2,1)} %bitcast.65, bf16[3584,512]{1,0:T(8,128)(2,1)} %bitcast.67), custom_call_target="tpu_custom_call" | custom-call | flops 100 | bytes 100 | tf_op jit(solution)/shard_map/pallas_call | solution.py:211
  65.6 6.1 %collective-permute-done.2.own_ref = bf16[320,896]{1,0:T(8,128)(2,1)S(1)} collective-permute-done((bf16[320,896]{1,0:T(8,128)(2,1)S(1)}, bf16[320,896]{1,0:T(8,128)(2,1)S(1)}, u32[]{:S(2)}, u32[]{:S(2)}) %collective-permute-start.2) | collective-permute-done | bytes 573472 | tf_op jit(solution)/shard_map/ppermute | solution.py:34
  71.7 2.0 collective-permute-done.5.other_ref
  73.7 0.8 copy-done.10
  74.5 7.9 %shard_map.140 = (bf16[320,896]{1,0:T(8,128)(2,1)}, bf16[320,896]{1,0:T(8,128)(2,1)}, bf16[320,896]{1,0:T(8,128)(2,1)}, bf16[320,896]{1,0:T(8,128)(2,1)}) custom-call(s32[2]{0:T(128)} %pad_add_fusion.1.place_ref, f32[320,512]{1,0:T(8,128)} %get-tuple-element.33.gate_near_ref, f32[320,512]{1,0:T(8,128)} %get-tuple-element.34.up_near_ref, ...), custom_call_target="tpu_custom_call" | custom-call | flops 100 | bytes 100 | tf_op jit(solution)/shard_map/pallas_call | solution.py:211
  82.4 0.3 collective-permute-start.7
  82.7 0.3 collective-permute-start.6
  83.0 1.7 collective-permute-done.7
  84.7 1.2 add_convert_fusion.1
  85.9 3.2 %collective-permute-start.8 = (bf16[320,896]{1,0:T(8,128)(2,1)S(1)}, bf16[320,896]{1,0:T(8,128)(2,1)S(1)}, u32[]{:S(2)}, u32[]{:S(2)}) collective-permute-start(bf16[320,896]{1,0:T(8,128)(2,1)S(1)} %add_convert_fusion.1), channel_id=1, source_target_pairs={{0,2},{2,0},{1,3},{3,1},{4,6},{6,4},{5,7},{7,5},{8,10},{10,8},{9,1... | collective-permute-start | bytes 1720328 | tf_op jit(solution)/shard_map/ppermute | solution.py:34
  89.1 13.6 %collective-permute-done.8 = bf16[320,896]{1,0:T(8,128)(2,1)S(1)} collective-permute-done((bf16[320,896]{1,0:T(8,128)(2,1)S(1)}, bf16[320,896]{1,0:T(8,128)(2,1)S(1)}, u32[]{:S(2)}, u32[]{:S(2)}) %collective-permute-start.8) | collective-permute-done | bytes 573472 | tf_op jit(solution)/shard_map/ppermute | solution.py:34
  102.9 1.4 reshape.139
  104.4 8.1 %all-to-all-start.1 = ((bf16[64,35,128]{2,1,0:T(8,128)(2,1)}), bf16[64,35,128]{2,1,0:T(8,128)(2,1)S(1)}, u32[]{:S(2)}, u32[]{:S(2)}) async-start(bf16[64,35,128]{2,1,0:T(8,128)(2,1)} %reshape.139), calls=%async_computation.1 | async-start | bytes 1310720 | tf_op jit(solution)/shard_map/all_to_all | solution.py:55
  112.8 2.8 %collective-permute-start.9 = (f32[128,128]{1,0:T(8,128)S(1)}, f32[128,128]{1,0:T(8,128)S(1)}, u32[]{:S(2)}, u32[]{:S(2)}) collective-permute-start(f32[128,128]{1,0:T(8,128)S(1)} %add.50), channel_id=1, source_target_pairs={{0,2},{2,0},{1,3},{3,1},{4,6},{6,4},{5,7},{7,5},{8,10},{10,8},{9,1... | collective-permute-start | bytes 196616 | tf_op jit(solution)/shard_map/ppermute | solution.py:34
  115.6 0.4 fusion.1
  115.9 3.3 %collective-permute-done.9 = f32[128,128]{1,0:T(8,128)S(1)} collective-permute-done((f32[128,128]{1,0:T(8,128)S(1)}, f32[128,128]{1,0:T(8,128)S(1)}, u32[]{:S(2)}, u32[]{:S(2)}) %collective-permute-start.9) | collective-permute-done | bytes 65568 | tf_op jit(solution)/shard_map/ppermute | solution.py:34
  119.3 0.3 shard_map.141
  119.6 13.2 %all-to-all-done.1 = bf16[64,35,128]{2,1,0:T(8,128)(2,1)S(1)} async-done(((bf16[64,35,128]{2,1,0:T(8,128)(2,1)}), bf16[64,35,128]{2,1,0:T(8,128)(2,1)S(1)}, u32[]{:S(2)}, u32[]{:S(2)}) %all-to-all-start.1) | async-done | bytes 573472 | tf_op jit(solution)/shard_map/all_to_all | solution.py:55
  132.8 0.6 reshape.140
  133.5 0.6 convolution_convert_fusion.2.own_ref
  134.1 1.1 collective-permute-start.12
  135.2 5.0 %collective-permute-done.12.pair_ref = bf16[128,896]{1,0:T(8,128)(2,1)S(1)} collective-permute-done((bf16[128,896]{1,0:T(8,128)(2,1)S(1)}, bf16[128,896]{1,0:T(8,128)(2,1)S(1)}, u32[]{:S(2)}, u32[]{:S(2)}) %collective-permute-start.12) | collective-permute-done | bytes 229408 | tf_op jit(solution)/shard_map/ppermute | solution.py:34
  140.2 0.6 pad_add_fusion.order_ref
  140.8 0.9 collective-permute-done.13.pair_far_ref
  141.7 0.7 copy-done.13
  142.4 6.6 %shard_map.142 = (bf16[128,1280]{1,0:T(8,128)(2,1)}, bf16[128,1280]{1,0:T(8,128)(2,1)}) custom-call(s32[3]{0:T(128)} %pad_add_fusion.order_ref, bf16[128,896]{1,0:T(8,128)(2,1)} %copy-done.6, bf16[128,896]{1,0:T(8,128)(2,1)} %copy-done.12, bf16[128,896]{1,0:T(8,128)(2,1)} %copy-done.11, bf16[128,896]{1,0:T(8,128)(2,1)} %copy-done.13, ...), custom_call_target="tpu_custom_call" | custom-call | flops 1174405120 | bytes 6000000 | tf_op jit(solution)/shard_map/pallas_call | solution.py:92
  149.0 1.6 collective-permute-start.14
  150.6 4.6 %collective-permute-start.15 = (bf16[128,1280]{1,0:T(8,128)(2,1)}, bf16[128,1280]{1,0:T(8,128)(2,1)S(1)}, u32[]{:S(2)}, u32[]{:S(2)}) collective-permute-start(bf16[128,1280]{1,0:T(8,128)(2,1)} %get-tuple-element.48), channel_id=1, source_target_pairs={{0,4},{1,5},{2,0},{3,1},{4,6},{5,7},{6,2},{7,3},{8,12},{9,13},{10,... | collective-permute-start | bytes 983048 | tf_op jit(solution)/shard_map/ppermute | solution.py:377
  155.3 7.9 %collective-permute-done.15 = bf16[128,1280]{1,0:T(8,128)(2,1)S(1)} collective-permute-done((bf16[128,1280]{1,0:T(8,128)(2,1)}, bf16[128,1280]{1,0:T(8,128)(2,1)S(1)}, u32[]{:S(2)}, u32[]{:S(2)}) %collective-permute-start.15) | collective-permute-done | bytes 327712 | tf_op jit(solution)/shard_map/ppermute | solution.py:377
  163.6 3.2 %collective-permute-start.17 = (f32[128,64]{0,1:T(8,128)S(1)}, f32[128,64]{0,1:T(8,128)S(1)}, u32[]{:S(2)}, u32[]{:S(2)}) collective-permute-start(f32[128,64]{0,1:T(8,128)S(1)} %fusion.22), channel_id=1, source_target_pairs={{0,2},{2,0},{1,3},{3,1},{4,6},{6,4},{5,7},{7,5},{8,10},{10,8},{9,1... | collective-permute-start | bytes 98312 | tf_op jit(solution)/shard_map/ppermute | solution.py:34
  167.2 0.8 multiply_reduce_fusion
  171.6 1.3 fusion.18
  173.2 11.6 %all_to_all.30 = bf16[4,41,8,128]{3,2,1,0:T(8,128)(2,1)S(1)} all-to-all(bf16[4,41,8,128]{3,2,1,0:T(8,128)(2,1)S(1)} %pad_maximum_fusion), channel_id=1, replica_groups=mesh['yl'=2,'z'=8,'xh'=2,'xl'=2,'yh'=2,'c'=2] {'xh','xl'}, dimensions={0} | all-to-all | bytes 671744 | tf_op jit(solution)/shard_map/all_to_all | solution.py:420
  184.9 0.6 slice_reduce_fusion.1
  189.1 1.3 fusion.19
  190.5 11.6 %all_to_all.31 = bf16[16,24,128]{2,1,0:T(8,128)(2,1)S(1)} all-to-all(bf16[16,24,128]{2,1,0:T(8,128)(2,1)S(1)} %pad_maximum_fusion.2), channel_id=1, replica_groups=mesh['yl'=2,'z'=8,'xh'=2,'xl'=2,'yh'=2,'c'=2] {'yl','z'}, dimensions={0} | all-to-all | bytes 196608 | tf_op jit(solution)/shard_map/all_to_all | solution.py:420
  202.2 11.3 %all_to_all.32 = bf16[16,24,128]{2,1,0:T(8,128)(2,1)S(1)} all-to-all(bf16[16,24,128]{2,1,0:T(8,128)(2,1)S(1)} %broadcast_in_dim.52), channel_id=1, replica_groups=mesh['yl'=2,'z'=8,'xh'=2,'xl'=2,'yh'=2,'c'=2] {'yl','z'}, dimensions={0} | all-to-all | bytes 196608 | tf_op jit(solution)/shard_map/all_to_all | solution.py:420
  213.5 0.8 broadcast_in_dim.53
  214.3 3.5 %all-to-all-start.5 = ((bf16[4,40,8,128]{3,2,1,0:T(8,128)(2,1)}), bf16[4,40,8,128]{3,2,1,0:T(8,128)(2,1)S(1)}, u32[]{:S(2)}, u32[]{:S(2)}) async-start(bf16[4,40,8,128]{3,2,1,0:T(8,128)(2,1)} %broadcast_in_dim.53), calls=%async_computation.5 | async-start | bytes 655360 | tf_op jit(solution)/shard_map/all_to_all | solution.py:420
  217.8 3.3 %collective-permute-start.20 = (f32[1,128]{1,0:T(1,128)S(1)}, f32[1,128]{1,0:T(1,128)S(1)}, u32[]{:S(2)}, u32[]{:S(2)}) collective-permute-start(f32[1,128]{1,0:T(1,128)S(1)} %slice.54), channel_id=1, source_target_pairs={{0,2},{2,0},{1,3},{3,1},{4,6},{6,4},{5,7},{7,5},{8,10},{10,8},{9,1... | collective-permute-start | bytes 1544 | tf_op jit(solution)/shard_map/ppermute | solution.py:34
  221.2 1.8 collective-permute-done.20
  223.0 2.6 %collective-permute-done.21 = f32[1,128]{1,0:T(1,128)S(1)} collective-permute-done((f32[1,128]{1,0:T(1,128)S(1)}, f32[1,128]{1,0:T(1,128)S(1)}, u32[]{:S(2)}, u32[]{:S(2)}) %collective-permute-start.21) | collective-permute-done | bytes 544 | tf_op jit(solution)/shard_map/ppermute | solution.py:42
  225.6 0.6 add_reduce_fusion
  226.9 0.7 convert_bitcast_fusion
  227.7 0.7 convert_bitcast_fusion.1
  (90 shorter events, 2.9 us)
Async XLA Ops:
  7.2 2.1 copy-start
  9.8 14.1 %copy-start.16 = (bf16[56,1280]{1,0:T(8,128)(2,1)S(1)}, bf16[56,1280]{1,0:T(8,128)(2,1)}, u32[]{:S(2)}) copy-start(bf16[56,1280]{1,0:T(8,128)(2,1)} %param.17) | copy-start | bytes 430084
  11.3 33.5 %all-to-all-start = ((bf16[64,35,128]{2,1,0:T(8,128)(2,1)}), bf16[64,35,128]{2,1,0:T(8,128)(2,1)S(1)}, u32[]{:S(2)}, u32[]{:S(2)}) async-start(bf16[64,35,128]{2,1,0:T(8,128)(2,1)} %reshape.136), calls=%async_computation | async-start | bytes 1310720 | tf_op jit(solution)/shard_map/all_to_all | solution.py:55
  23.9 109.6 %all-gather.2.cloned.1.call-start = ((), (), s32[]{:S(2)}) async-start(), calls=%async_computation.6 | async-start | bytes 5160960 | tf_op jit(solution)/shard_map/all_gather | solution.py:302
  23.9 0.7 collective-permute-start
  24.6 16.1 %collective-permute-start.1 = (bf16[56,1280]{1,0:T(8,128)(2,1)S(1)}, bf16[56,1280]{1,0:T(8,128)(2,1)S(1)}, u32[]{:S(2)}, u32[]{:S(2)}) collective-permute-start(bf16[56,1280]{1,0:T(8,128)(2,1)S(1)} %collective-permute-done), channel_id=1, source_target_pairs={{0,128},{128,0},{1,129},{129,1},{2,130},{130,2},{3,131},{131,3},{4... | collective-permute-start | bytes 430088 | tf_op jit(solution)/shard_map/ppermute | solution.py:34
  45.4 12.6 %copy-start.5 = (bf16[320,896]{1,0:T(8,128)(2,1)}, bf16[320,896]{1,0:T(8,128)(2,1)S(1)}, u32[]{:S(2)}) copy-start(bf16[320,896]{1,0:T(8,128)(2,1)S(1)} %reshape.137.own_ref) | copy-start | bytes 1720324
  45.4 12.3 %copy-start.14 = (bf16[1280]{0:T(1024)(128)(2,1)S(1)}, bf16[1280]{0:T(1024)(128)(2,1)}, u32[]{:S(2)}) copy-start(bf16[1280]{0:T(1024)(128)(2,1)} %param.19) | copy-start | bytes 7684
  45.5 12.3 %copy-start.1 = (bf16[128,1280]{1,0:T(8,128)(2,1)S(1)}, bf16[128,1280]{1,0:T(8,128)(2,1)}, u32[]{:S(2)}) copy-start(bf16[128,1280]{1,0:T(8,128)(2,1)} %student_ref.3) | copy-start | bytes 983044
  45.5 12.3 %copy-start.3 = (bf16[1280,64]{0,1:T(8,128)(2,1)S(1)}, bf16[1280,64]{0,1:T(8,128)(2,1)}, u32[]{:S(2)}) copy-start(bf16[1280,64]{0,1:T(8,128)(2,1)} %param.20) | copy-start | bytes 491524
  45.5 8.2 %collective-permute-start.10 = (bf16[112,1280]{1,0:T(8,128)(2,1)S(1)}, bf16[112,1280]{1,0:T(8,128)(2,1)S(1)}, u32[]{:S(2)}, u32[]{:S(2)}) collective-permute-start(bf16[112,1280]{1,0:T(8,128)(2,1)S(1)} %maximum_select_fusion.1), channel_id=1, source_target_pairs={{0,8},{8,0},{1,9},{9,1},{2,10},{10,2},{3,11},{11,3},{4,12},{12,4},... | collective-permute-start | bytes 860168 | tf_op jit(solution)/shard_map/ppermute | solution.py:34
  54.7 4.7 %collective-permute-start.4 = (bf16[320,896]{1,0:T(8,128)(2,1)S(1)}, bf16[320,896]{1,0:T(8,128)(2,1)S(1)}, u32[]{:S(2)}, u32[]{:S(2)}) collective-permute-start(bf16[320,896]{1,0:T(8,128)(2,1)S(1)} %reshape.137.own_ref), channel_id=1, source_target_pairs={{0,1},{1,0},{2,3},{3,2},{4,5},{5,4},{6,7},{7,6},{8,9},{9,8},{10,11... | collective-permute-start | bytes 1720328 | tf_op jit(solution)/shard_map/ppermute | solution.py:34
  54.8 16.9 %collective-permute-start.2 = (bf16[320,896]{1,0:T(8,128)(2,1)S(1)}, bf16[320,896]{1,0:T(8,128)(2,1)S(1)}, u32[]{:S(2)}, u32[]{:S(2)}) collective-permute-start(bf16[320,896]{1,0:T(8,128)(2,1)S(1)} %reshape.137.own_ref), channel_id=1, source_target_pairs={{0,2},{2,0},{1,3},{3,1},{4,6},{6,4},{5,7},{7,5},{8,10},{10,8},{9,1... | collective-permute-start | bytes 1720328 | tf_op jit(solution)/shard_map/ppermute | solution.py:34
  58.1 1.3 collective-permute-start.3
  59.4 0.8 copy-start.7
  71.7 2.0 copy-start.9
  71.7 2.0 collective-permute-start.5
  73.7 0.8 copy-start.10
  82.4 20.3 %copy-start.8 = (bf16[320,896]{1,0:T(8,128)(2,1)S(1)}, bf16[320,896]{1,0:T(8,128)(2,1)}, u32[]{:S(2)}) copy-start(bf16[320,896]{1,0:T(8,128)(2,1)} %get-tuple-element.36) | copy-start | bytes 1720324
  82.4 2.3 collective-permute-start.7
  82.7 6.4 %collective-permute-start.6 = (bf16[320,896]{1,0:T(8,128)(2,1)}, bf16[320,896]{1,0:T(8,128)(2,1)S(1)}, u32[]{:S(2)}, u32[]{:S(2)}) collective-permute-start(bf16[320,896]{1,0:T(8,128)(2,1)} %get-tuple-element.37), channel_id=1, source_target_pairs={{0,1},{1,0},{2,3},{3,2},{4,5},{5,4},{6,7},{7,6},{8,9},{9,8},{10,11... | collective-permute-start | bytes 1720328 | tf_op jit(solution)/shard_map/ppermute | solution.py:34
  85.9 16.8 %collective-permute-start.8 = (bf16[320,896]{1,0:T(8,128)(2,1)S(1)}, bf16[320,896]{1,0:T(8,128)(2,1)S(1)}, u32[]{:S(2)}, u32[]{:S(2)}) collective-permute-start(bf16[320,896]{1,0:T(8,128)(2,1)S(1)} %add_convert_fusion.1), channel_id=1, source_target_pairs={{0,2},{2,0},{1,3},{3,1},{4,6},{6,4},{5,7},{7,5},{8,10},{10,8},{9,1... | collective-permute-start | bytes 1720328 | tf_op jit(solution)/shard_map/ppermute | solution.py:34
  102.9 9.6 %copy-start.15 = (f32[128,2]{0,1:T(2,128)S(1)}, f32[128,2]{0,1:T(2,128)}, u32[]{:S(2)}) copy-start(f32[128,2]{0,1:T(2,128)} %param.13) | copy-start | bytes 3076
  104.4 14.9 %copy-start.2 = (bf16[64,1280]{1,0:T(8,128)(2,1)S(1)}, bf16[64,1280]{1,0:T(8,128)(2,1)}, u32[]{:S(2)}) copy-start(bf16[64,1280]{1,0:T(8,128)(2,1)} %up_ref.1) | copy-start | bytes 491524
  104.4 28.5 %all-to-all-start.1 = ((bf16[64,35,128]{2,1,0:T(8,128)(2,1)}), bf16[64,35,128]{2,1,0:T(8,128)(2,1)S(1)}, u32[]{:S(2)}, u32[]{:S(2)}) async-start(bf16[64,35,128]{2,1,0:T(8,128)(2,1)} %reshape.139), calls=%async_computation.1 | async-start | bytes 1310720 | tf_op jit(solution)/shard_map/all_to_all | solution.py:55
  112.8 6.4 %collective-permute-start.9 = (f32[128,128]{1,0:T(8,128)S(1)}, f32[128,128]{1,0:T(8,128)S(1)}, u32[]{:S(2)}, u32[]{:S(2)}) collective-permute-start(f32[128,128]{1,0:T(8,128)S(1)} %add.50), channel_id=1, source_target_pairs={{0,2},{2,0},{1,3},{3,1},{4,6},{6,4},{5,7},{7,5},{8,10},{10,8},{9,1... | collective-permute-start | bytes 196616 | tf_op jit(solution)/shard_map/ppermute | solution.py:34
  134.1 7.6 %copy-start.6 = (bf16[128,896]{1,0:T(8,128)(2,1)}, bf16[128,896]{1,0:T(8,128)(2,1)S(1)}, u32[]{:S(2)}) copy-start(bf16[128,896]{1,0:T(8,128)(2,1)S(1)} %convolution_convert_fusion.2.own_ref) | copy-start | bytes 688132
  134.1 6.1 %collective-permute-start.12 = (bf16[128,896]{1,0:T(8,128)(2,1)S(1)}, bf16[128,896]{1,0:T(8,128)(2,1)S(1)}, u32[]{:S(2)}, u32[]{:S(2)}) collective-permute-start(bf16[128,896]{1,0:T(8,128)(2,1)S(1)} %convolution_convert_fusion.2.own_ref), channel_id=1, source_target_pairs={{0,4},{4,0},{1,5},{5,1},{2,6},{6,2},{3,7},{7,3},{8,12},{12,8},{9,1... | collective-permute-start | bytes 688136 | tf_op jit(solution)/shard_map/ppermute | solution.py:34
  135.2 5.6 %collective-permute-start.11 = (bf16[128,896]{1,0:T(8,128)(2,1)S(1)}, bf16[128,896]{1,0:T(8,128)(2,1)S(1)}, u32[]{:S(2)}, u32[]{:S(2)}) collective-permute-start(bf16[128,896]{1,0:T(8,128)(2,1)S(1)} %convolution_convert_fusion.2.own_ref), channel_id=1, source_target_pairs={{0,1},{1,0},{2,3},{3,2},{4,5},{5,4},{6,7},{7,6},{8,9},{9,8},{10,11... | collective-permute-start | bytes 688136 | tf_op jit(solution)/shard_map/ppermute | solution.py:34
  140.2 1.5 copy-start.11
  140.2 1.5 collective-permute-start.13
  140.8 0.9 copy-start.12
  141.7 0.7 copy-start.13
  149.0 6.3 %collective-permute-start.14 = (bf16[128,1280]{1,0:T(8,128)(2,1)}, bf16[128,1280]{1,0:T(8,128)(2,1)S(1)}, u32[]{:S(2)}, u32[]{:S(2)}) collective-permute-start(bf16[128,1280]{1,0:T(8,128)(2,1)} %get-tuple-element.47), channel_id=1, source_target_pairs={{0,0},{1,1},{2,4},{3,5},{4,2},{5,3},{6,6},{7,7},{8,8},{9,9},{10,12... | collective-permute-start | bytes 983048 | tf_op jit(solution)/shard_map/ppermute | solution.py:377
  150.6 12.5 %collective-permute-start.15 = (bf16[128,1280]{1,0:T(8,128)(2,1)}, bf16[128,1280]{1,0:T(8,128)(2,1)S(1)}, u32[]{:S(2)}, u32[]{:S(2)}) collective-permute-start(bf16[128,1280]{1,0:T(8,128)(2,1)} %get-tuple-element.48), channel_id=1, source_target_pairs={{0,4},{1,5},{2,0},{3,1},{4,6},{5,7},{6,2},{7,3},{8,12},{9,13},{10,... | collective-permute-start | bytes 983048 | tf_op jit(solution)/shard_map/ppermute | solution.py:377
  163.3 4.7 %copy-start.4 = (f32[128,1280]{1,0:T(8,128)}, f32[128,1280]{1,0:T(8,128)S(1)}, u32[]{:S(2)}) copy-start(f32[128,1280]{1,0:T(8,128)S(1)} %get-tuple-element.53) | copy-start | bytes 1966084
  163.5 9.4 %collective-permute-start.16 = (f32[128,64]{0,1:T(8,128)S(1)}, f32[128,64]{0,1:T(8,128)S(1)}, u32[]{:S(2)}, u32[]{:S(2)}) collective-permute-start(f32[128,64]{0,1:T(8,128)S(1)} %fusion.22), channel_id=1, source_target_pairs={{0,1},{1,0},{2,3},{3,2},{4,5},{5,4},{6,7},{7,6},{8,9},{9,8},{10,11... | collective-permute-start | bytes 98312 | tf_op jit(solution)/shard_map/ppermute | solution.py:34
  163.6 9.3 %collective-permute-start.17 = (f32[128,64]{0,1:T(8,128)S(1)}, f32[128,64]{0,1:T(8,128)S(1)}, u32[]{:S(2)}, u32[]{:S(2)}) collective-permute-start(f32[128,64]{0,1:T(8,128)S(1)} %fusion.22), channel_id=1, source_target_pairs={{0,2},{2,0},{1,3},{3,1},{4,6},{6,4},{5,7},{7,5},{8,10},{10,8},{9,1... | collective-permute-start | bytes 98312 | tf_op jit(solution)/shard_map/ppermute | solution.py:34
  166.8 6.1 %collective-permute-start.18 = (f32[128,64]{0,1:T(8,128)S(1)}, f32[128,64]{0,1:T(8,128)S(1)}, u32[]{:S(2)}, u32[]{:S(2)}) collective-permute-start(f32[128,64]{0,1:T(8,128)S(1)} %fusion.22), channel_id=1, source_target_pairs={{0,3},{1,2},{2,1},{3,0},{4,7},{5,6},{6,5},{7,4},{8,11},{9,10},{10,... | collective-permute-start | bytes 98312 | tf_op jit(solution)/shard_map/ppermute | solution.py:42
  214.3 12.6 %all-to-all-start.5 = ((bf16[4,40,8,128]{3,2,1,0:T(8,128)(2,1)}), bf16[4,40,8,128]{3,2,1,0:T(8,128)(2,1)S(1)}, u32[]{:S(2)}, u32[]{:S(2)}) async-start(bf16[4,40,8,128]{3,2,1,0:T(8,128)(2,1)} %broadcast_in_dim.53), calls=%async_computation.5 | async-start | bytes 655360 | tf_op jit(solution)/shard_map/all_to_all | solution.py:420
  217.7 3.5 %collective-permute-start.19 = (f32[1,128]{1,0:T(1,128)S(1)}, f32[1,128]{1,0:T(1,128)S(1)}, u32[]{:S(2)}, u32[]{:S(2)}) collective-permute-start(f32[1,128]{1,0:T(1,128)S(1)} %slice.54), channel_id=1, source_target_pairs={{0,1},{1,0},{2,3},{3,2},{4,5},{5,4},{6,7},{7,6},{8,9},{9,8},{10,11... | collective-permute-start | bytes 1544 | tf_op jit(solution)/shard_map/ppermute | solution.py:34
  217.8 5.1 %collective-permute-start.20 = (f32[1,128]{1,0:T(1,128)S(1)}, f32[1,128]{1,0:T(1,128)S(1)}, u32[]{:S(2)}, u32[]{:S(2)}) collective-permute-start(f32[1,128]{1,0:T(1,128)S(1)} %slice.54), channel_id=1, source_target_pairs={{0,2},{2,0},{1,3},{3,1},{4,6},{6,4},{5,7},{7,5},{8,10},{10,8},{9,1... | collective-permute-start | bytes 1544 | tf_op jit(solution)/shard_map/ppermute | solution.py:34
  221.1 4.5 %collective-permute-start.21 = (f32[1,128]{1,0:T(1,128)S(1)}, f32[1,128]{1,0:T(1,128)S(1)}, u32[]{:S(2)}, u32[]{:S(2)}) collective-permute-start(f32[1,128]{1,0:T(1,128)S(1)} %slice.54), channel_id=1, source_target_pairs={{0,3},{1,2},{2,1},{3,0},{4,7},{5,6},{6,5},{7,4},{8,11},{9,10},{10,... | collective-permute-start | bytes 1544 | tf_op jit(solution)/shard_map/ppermute | solution.py:42
Sparse Core Ops, SparseCore 0:
  54.8 55.1 all-gather.1

commit v7 on v4

--- a/solution.py
+++ b/solution.py
@@ -22,8 +22,8 @@
     return [(place, places.index(target(*here))) for place, here in enumerate(places)]
 
 
-def proj_target(yl, z, xh, xl, yh, c):
-    return (xl, z, xh, yh, yl, c)
+def proj_target(step):
+    return lambda yl, z, xh, xl, yh, c: (xl ^ step, z, xh, yh, yl, c)
 
 
 def home_target(step):
@@ -34,19 +34,18 @@
     return lax.ppermute(value, axis, [(0, 1), (1, 0)])
 
 
-def mp_sum(value):
-    value = value + swap(value, "c")
-    return value + swap(value, "yh")
-
-
 def dot(a, b):
     return jnp.dot(a, b, preferred_element_type=jnp.float32)
 
 
-def pair_rows(value, axis, index):
-    other = swap(value, axis)
+def mp_sum(value):
+    cross = lax.ppermute(value, MP, [(place, 3 - place) for place in range(4)])
+    return (value + swap(value, "c")) + (swap(value, "yh") + cross)
+
+
+def ordered(first, second, index):
     return jnp.where(
-        index == 0, jnp.concatenate([value, other]), jnp.concatenate([other, value])
+        index == 0, jnp.concatenate([first, second]), jnp.concatenate([second, first])
     )
 
 
@@ -57,17 +56,8 @@
 
 
 def product_kernel(order_ref, own_ref, own_far_ref, pair_ref, pair_far_ref, block_ref, *refs):
-    outs, near_rows, far_rows, total, held, arrived = refs[:2], *refs[2:]
+    outs, near_rows, far_rows, total = refs[:2], *refs[2:]
     rows, width = own_ref.shape
-    count, cut = held.shape[0], held.shape[2]
-    copies = [
-        pltpu.make_async_copy(
-            block_ref.at[:, pl.ds(index * cut, cut)], held.at[index], arrived.at[index]
-        )
-        for index in range(count)
-    ]
-    for copy in copies:
-        copy.start()
     near_rows[:rows] = own_ref[...]
     near_rows[rows:] = pair_ref[...]
     far_rows[:rows] = own_far_ref[...]
@@ -75,39 +65,33 @@
     core = order_ref[2]
     near = pl.ds(pl.multiple_of(core * width, 128), width)
     far = pl.ds(pl.multiple_of((1 - core) * width, 128), width)
-    for index, copy in enumerate(copies):
-        copy.wait()
-        total[...] = dot(near_rows[...], held[index, near, :]) + dot(
-            far_rows[...], held[index, far, :]
+    cut = total.shape[1]
+    for start in range(0, block_ref.shape[1], cut):
+        columns = slice(start, start + cut)
+        total[...] = dot(near_rows[...], block_ref[near, columns]) + dot(
+            far_rows[...], block_ref[far, columns]
         )
         for step in range(2):
             here = pl.ds(pl.multiple_of(order_ref[step] * rows, 128), rows)
-            outs[step][:, index * cut : (index + 1) * cut] = total[here, :].astype(jnp.bfloat16)
+            outs[step][:, columns] = total[here, :].astype(jnp.bfloat16)
 
 
 def product_pieces(order, own, own_far, pair, pair_far, block):
     rows, width = own.shape
     depth, wide = block.shape
-    cut = 256
     vmem = pl.BlockSpec(memory_space=pltpu.VMEM)
     return pl.pallas_call(
         product_kernel,
         out_shape=[jax.ShapeDtypeStruct((rows, wide), jnp.bfloat16)] * 2,
-        in_specs=[pl.BlockSpec(memory_space=pltpu.SMEM)]
-        + [vmem] * 4
-        + [pl.BlockSpec(memory_space=pltpu.HBM)],
+        in_specs=[pl.BlockSpec(memory_space=pltpu.SMEM)] + [vmem] * 5,
         out_specs=[vmem] * 2,
         scratch_shapes=[
             pltpu.VMEM((2 * rows, width), jnp.bfloat16),
             pltpu.VMEM((2 * rows, width), jnp.bfloat16),
-            pltpu.VMEM((2 * rows, cut), jnp.float32),
-            pltpu.VMEM((wide // cut, depth, cut), jnp.bfloat16),
-            pltpu.SemaphoreType.DMA((wide // cut,)),
+            pltpu.VMEM((2 * rows, 640), jnp.float32),
         ],
         compiler_params=pltpu.CompilerParams(vmem_limit_bytes=24 * 1024 * 1024),
-        cost_estimate=pl.CostEstimate(
-            flops=4 * rows * depth * wide, bytes_accessed=6_000_000, transcendentals=0
-        ),
+        cost_estimate=pl.CostEstimate(flops=100, bytes_accessed=100, transcendentals=0),
     )(order, own, own_far, pair, pair_far, block)
 
 
@@ -122,7 +106,8 @@
     out_ref[:, rank:] = jnp.broadcast_to(total, (student.shape[0], rank))
 
 
-def student_kernel(width, stats_ref, student_ref, gain_ref, up_ref, low_ref, normed_ref, out_ref):
+def student_kernel(width, stats_ref, student_ref, gain_ref, up_ref, block_ref, *outs):
+    low_ref, normed_ref, out_ref = outs
     rank = up_ref.shape[0]
     inverse = lax.rsqrt(stats_ref[:, rank : rank + 1] / width + 1e-06)
     low = (stats_ref[:, :rank] * inverse).astype(jnp.bfloat16)
@@ -142,6 +127,47 @@
         compiler_params=pltpu.CompilerParams(vmem_limit_bytes=16 * 1024 * 1024),
         cost_estimate=pl.CostEstimate(flops=100, bytes_accessed=100, transcendentals=0),
     )(*args)
+
+
+def half_rows(ref, half, core, width):
+    start = half * 2 * width
+    own = pl.ds(pl.multiple_of(start + core * width, 128), width)
+    other = pl.ds(pl.multiple_of(start + (1 - core) * width, 128), width)
+    return ref[own, :], ref[other, :]
+
+
+def near_kernel(place_ref, own_ref, other_ref, gate_ref, up_ref, down_ref, *outs):
+    for out_ref, weight_ref in zip(outs, (gate_ref, up_ref)):
+        own, other = half_rows(weight_ref, place_ref[0], place_ref[1], own_ref.shape[1])
+        out_ref[...] = dot(own_ref[...], own) + dot(other_ref[...], other)
+
+
+def expert_kernel(
+    place_ref, gate_near_ref, up_near_ref, own_ref, other_ref, gate_ref, up_ref, down_ref, *outs
+):
+    yh, core, width = place_ref[0], place_ref[1], own_ref.shape[1]
+    sums = []
+    for near, weight_ref in ((gate_near_ref, gate_ref), (up_near_ref, up_ref)):
+        own, other = half_rows(weight_ref, 1 - yh, core, width)
+        sums.append(near[...] + dot(own_ref[...], own) + dot(other_ref[...], other))
+    gate, up = sums
+    hidden = (gate / (1.0 + jnp.exp(-gate)) * up).astype(jnp.bfloat16)
+    parts = (yh * 2 + core, yh * 2 + 1 - core, (1 - yh) * 2 + core, (1 - yh) * 2 + 1 - core)
+    for out_ref, part in zip(outs, parts):
+        columns = pl.ds(pl.multiple_of(part * width, 128), width)
+        out_ref[...] = dot(hidden, down_ref[:, columns]).astype(jnp.bfloat16)
+
+
+def expert_call(kernel, shapes, place, *args):
+    vmem = pl.BlockSpec(memory_space=pltpu.VMEM)
+    return pl.pallas_call(
+        kernel,
+        out_shape=shapes,
+        in_specs=[pl.BlockSpec(memory_space=pltpu.SMEM)] + [vmem] * len(args),
+        out_specs=[vmem] * len(shapes),
+        compiler_params=pltpu.CompilerParams(vmem_limit_bytes=32 * 1024 * 1024),
+        cost_estimate=pl.CostEstimate(flops=100, bytes_accessed=100, transcendentals=0),
+    )(place, *args)
 
 
 def body(
@@ -187,13 +213,14 @@
     outgoing, proj = lax.optimization_barrier((outgoing, proj))
     arrived = exchange_slots(outgoing)
 
-    proj_rows = lax.ppermute(proj, ALL, permutation(proj_target))
-    proj_rows = pair_rows(proj_rows, "yl", yl)
+    blocks = [lax.ppermute(proj, ALL, permutation(proj_target(step))) for step in range(2)]
+    proj_rows = ordered(*blocks, yl)
+    proj_rows = ordered(proj_rows, swap(proj_rows, "xh"), xh)
     arrived, proj_rows = lax.optimization_barrier((arrived, proj_rows))
+    proj_block = lax.all_gather(proj_rows, "z", axis=0, tiled=True)
 
     arrived_y = swap(arrived, "yh")
     arrived_c = swap(arrived, "c")
-    proj_rows = pair_rows(proj_rows, "xh", xh)
 
     gain = student_norm_weight.reshape(1, -1)
     stats = local_kernel(
@@ -204,38 +231,35 @@
         adapter_down_matrix.T,
     )
     stats = stats + swap(stats, "c")
-    arrived_y, proj_rows, stats = lax.optimization_barrier((arrived_y, proj_rows, stats))
-    proj_block = lax.all_gather(proj_rows, "z", axis=0, tiled=True)
-    arrived_yc = swap(arrived_y, "c")
-    parts = (
-        (arrived, mi),
-        (arrived_c, yh * 2 + 1 - core),
-        (arrived_y, (1 - yh) * 2 + core),
-        (arrived_yc, (1 - yh) * 2 + 1 - core),
-    )
-    gate_proj = up_proj = 0.0
-    for rows, place in parts:
-        gate_proj = gate_proj + dot(
-            rows, lax.dynamic_slice_in_dim(expert_gate_weight[0], place * part_width, part_width, 0)
-        )
-        up_proj = up_proj + dot(
-            rows, lax.dynamic_slice_in_dim(expert_up_weight[0], place * part_width, part_width, 0)
-        )
-    hidden = (jax.nn.silu(gate_proj) * up_proj).astype(jnp.bfloat16)
-
-    def out_part(place):
-        return dot(
-            hidden, lax.dynamic_slice_in_dim(expert_down_weight[0], place * part_width, part_width, 1)
-        )
-
-    far = swap(out_part((1 - yh) * 2 + 1 - core).astype(jnp.bfloat16), "c")
-    near = swap(out_part(yh * 2 + 1 - core).astype(jnp.bfloat16), "c")
-    far = out_part((1 - yh) * 2 + core).astype(jnp.bfloat16).astype(jnp.float32) + far.astype(
-        jnp.float32
-    )
-    far = swap(far.astype(jnp.bfloat16), "yh")
+    place = jnp.stack([yh, core])
+    expert_weights = (expert_gate_weight[0], expert_up_weight[0], expert_down_weight[0])
+    units = expert_weights[0].shape[1]
+    near_gate, near_up = expert_call(
+        near_kernel,
+        [jax.ShapeDtypeStruct((slot_count, units), jnp.float32)] * 2,
+        place,
+        arrived,
+        arrived_c,
+        *expert_weights,
+    )
+    arrived_y, stats, near_gate, near_up = lax.optimization_barrier(
+        (arrived_y, stats, near_gate, near_up)
+    )
+    out_own, out_near, out_far, out_far_near = expert_call(
+        expert_kernel,
+        [jax.ShapeDtypeStruct(arrived.shape, jnp.bfloat16)] * 4,
+        place,
+        near_gate,
+        near_up,
+        arrived_y,
+        swap(arrived_y, "c"),
+        *expert_weights,
+    )
+    far = swap(out_far_near, "c")
+    near = swap(out_near, "c")
+    far = swap((out_far.astype(jnp.float32) + far.astype(jnp.float32)).astype(jnp.bfloat16), "yh")
     expert_out = (
-        out_part(mi).astype(jnp.bfloat16).astype(jnp.float32)
+        out_own.astype(jnp.float32)
         + near.astype(jnp.float32)
         + far.astype(jnp.float32)
     ).astype(jnp.bfloat16)
@@ -254,6 +278,7 @@
         student_hidden_input,
         gain,
         adapter_up_matrix,
+        proj_block,
     )
     returned, lowrank, normed, student_out = lax.optimization_barrier(
         (returned, lowrank, normed, student_out)
@@ -331,12 +356,7 @@
     summed = jnp.sum(bundle.astype(jnp.float32), axis=0)
     grads = jnp.broadcast_to(summed.astype(jnp.bfloat16), (experts, 24, lanes))
     grads = lax.all_to_all(grads, DP, split_axis=0, concat_axis=0, tiled=True)
-    loss_row = summed[20:21]
-    cross = [(i, 3 - i) for i in range(4)]
-    loss_row = (loss_row + swap(loss_row, "c")) + (
-        swap(loss_row, "yh") + lax.ppermute(loss_row, MP, cross)
-    )
-    loss = jnp.sum(loss_row) / (tokens_all * student_width)
+    loss = jnp.sum(mp_sum(summed[20:21])) / (tokens_all * student_width)
     grads = jnp.concatenate(
         [
             grads[:, :16].reshape(2 * experts, 8, lanes),

time: 219 us -> 222 us (1.014)
  matrix products: 12.3 us -> 2.17 us
  local copies, waits for them, and re-layouts: 9.84 us -> 17.3 us
  Pallas kernels: 4.78 us -> 8.52 us
  waiting for transfers between devices: 76.5 us -> 79.4 us
    dot_general x13 -> x1, matrix products: 10.6 us -> 0.56 us  [dot(): return jnp.dot(a, b, preferred_element_type=jnp.float32)]
    unnamed x25 -> x33, local copies, waits for them, and re-layouts: 4.15 us -> 11.6 us
    ppermute x2 -> x4, waiting for transfers between devices: 2.02 us -> 8.68 us  [the longest x2 7.26 us: body(): lax.ppermute(proj, ALL, permutation(proj_target(step)))]
    all_to_all x2, waiting for transfers between devices: 21.8 us -> 15.7 us  [exchange_slots(): lax.all_to_all(rows, DP, split_axis=0, concat_axis=0, tiled=True)]
    pallas_call x0 -> x2, Pallas kernels: none -> 5.63 us  [expert_call(): pl.pallas_call(kernel, out_shape=shapes, in_specs=[pl.BlockSpec(memory_sp...]
    ppermute x2, starting transfers between devices: 6.11 us -> 1.68 us  [body(): lax.ppermute(piece, ALL, permutation(home_target(step))).astype(jnp.float32)]
    all_to_all x2, starting transfers between devices: 21.1 us -> 25.2 us  [exchange_slots(): lax.all_to_all(rows, DP, split_axis=0, concat_axis=0, tiled=True)]
    ppermute x17 -> x16, starting transfers between devices: 31.2 us -> 29.1 us  [swap(): return lax.ppermute(value, axis, [(0, 1), (1, 0)])]
  transfers between devices with their start and end apart: 25 -> 26, of which waited for: 16 -> 15; matrix products, arithmetic and copies ran while one was open for 8% -> 3% of each run, Pallas kernels for 0% -> 3%
where the time goes in v7:
time: 222 us
  waiting for transfers between devices  79.4 us (36%)
  starting transfers between devices  63.6 us (29%)
  blocking collectives  23.8 us (11%)
  between operations  19.9 us (9%)
  local copies, waits for them, and re-layouts  17.3 us (8%)
  Pallas kernels  8.52 us (4%)
  other arithmetic  6.89 us (3%)
    ppermute x16, waiting for transfers between devices, swap(): return lax.ppermute(value, axis, [(0, 1), (1, 0)])  38.1 us
    ppermute x16, starting transfers between devices, swap(): return lax.ppermute(value, axis, [(0, 1), (1, 0)])  29.1 us
    all_to_all x2, starting transfers between devices, exchange_slots(): lax.all_to_all(rows, DP, split_axis=0, concat_axis=0, tiled=True)  25.2 us
    all_to_all x1, blocking collectives, body(): bundle = lax.all_to_all(bundle, DP, split_axis=0, concat_axis=0, tiled=True)  23.8 us
    all_to_all x2, waiting for transfers between devices, exchange_slots(): lax.all_to_all(rows, DP, split_axis=0, concat_axis=0, tiled=True)  15.7 us
    unnamed x33, local copies, waits for them, and re-layouts  11.6 us
    ppermute x2, waiting for transfers between devices, body(): lax.ppermute(piece, ALL, permutation(home_target(step))).astype(jnp.float32)  9.65 us
    ppermute x2, waiting for transfers between devices, body(): lax.ppermute(proj, ALL, permutation(proj_target(step)))  7.26 us
  transfers between devices with their start and end apart: 26, of which 15 were waited for; matrix products, arithmetic and copies ran while one was open for 3% of the time, Pallas kernels for 3%

profile of v7, /device:TPU:32, one launch (start us, length us, event | category | flops | bytes accessed | tf_op | source)
XLA Modules:
  0.0 221.6 jit_solution(9980792545914114796)
XLA Ops:
  7.2 0.8 copy.15
  8.3 0.6 reduce-window.6
  9.3 0.6 convolution_convert_fusion.1
  9.9 1.4 reshape.130
  11.3 12.6 %all-to-all-start = ((bf16[64,35,128]{2,1,0:T(8,128)(2,1)}), bf16[64,35,128]{2,1,0:T(8,128)(2,1)S(1)}, u32[]{:S(2)}, u32[]{:S(2)}) async-start(bf16[64,35,128]{2,1,0:T(8,128)(2,1)} %reshape.130), calls=%async_computation | async-start | bytes 1310720 | tf_op jit(solution)/shard_map/all_to_all | solution.py:55
  23.9 1.7 collective-permute-start.1
  25.6 0.7 collective-permute-start
  26.3 7.3 %collective-permute-done.1 = bf16[56,1280]{1,0:T(8,128)(2,1)S(1)} collective-permute-done((bf16[56,1280]{1,0:T(8,128)(2,1)S(1)}, bf16[56,1280]{1,0:T(8,128)(2,1)S(1)}, u32[]{:S(2)}, u32[]{:S(2)}) %collective-permute-start.1) | collective-permute-done | bytes 143392 | tf_op jit(solution)/shard_map/ppermute | solution.py:216
  33.6 5.8 %collective-permute-start.2 = (bf16[112,1280]{1,0:T(8,128)(2,1)S(1)}, bf16[112,1280]{1,0:T(8,128)(2,1)S(1)}, u32[]{:S(2)}, u32[]{:S(2)}) collective-permute-start(bf16[112,1280]{1,0:T(8,128)(2,1)S(1)} %maximum_select_fusion.1), channel_id=1, source_target_pairs={{0,8},{8,0},{1,9},{9,1},{2,10},{10,2},{3,11},{11,3},{4,12},{12,4},... | collective-permute-start | bytes 860168 | tf_op jit(solution)/shard_map/ppermute | solution.py:34
  39.4 5.2 %collective-permute-done.2 = bf16[112,1280]{1,0:T(8,128)(2,1)S(1)} collective-permute-done((bf16[112,1280]{1,0:T(8,128)(2,1)S(1)}, bf16[112,1280]{1,0:T(8,128)(2,1)S(1)}, u32[]{:S(2)}, u32[]{:S(2)}) %collective-permute-start.2) | collective-permute-done | bytes 286752 | tf_op jit(solution)/shard_map/ppermute | solution.py:34
  44.6 0.9 maximum_select_fusion
  45.6 0.6 reshape.131.own_ref
  46.3 5.4 %collective-permute-start.3 = (bf16[320,896]{1,0:T(8,128)(2,1)S(1)}, bf16[320,896]{1,0:T(8,128)(2,1)S(1)}, u32[]{:S(2)}, u32[]{:S(2)}) collective-permute-start(bf16[320,896]{1,0:T(8,128)(2,1)S(1)} %reshape.131.own_ref), channel_id=1, source_target_pairs={{0,2},{2,0},{1,3},{3,1},{4,6},{6,4},{5,7},{7,5},{8,10},{10,8},{9,1... | collective-permute-start | bytes 1720328 | tf_op jit(solution)/shard_map/ppermute | solution.py:34
  51.7 0.2 shard_map.138
  52.0 0.2 collective-permute-start.4
  52.3 1.0 collective-permute-done.4
  53.3 2.0 copy-done.3
  55.4 2.0 copy-done.5
  57.4 2.0 copy-done.7
  59.4 2.1 shard_map.139
  61.5 3.7 %collective-permute-done.3.own_ref = bf16[320,896]{1,0:T(8,128)(2,1)S(1)} collective-permute-done((bf16[320,896]{1,0:T(8,128)(2,1)S(1)}, bf16[320,896]{1,0:T(8,128)(2,1)S(1)}, u32[]{:S(2)}, u32[]{:S(2)}) %collective-permute-start.3) | collective-permute-done | bytes 573472 | tf_op jit(solution)/shard_map/ppermute | solution.py:34
  65.2 2.0 collective-permute-done.6.other_ref
  67.2 3.6 %shard_map.140 = (bf16[320,896]{1,0:T(8,128)(2,1)S(1)}, bf16[320,896]{1,0:T(8,128)(2,1)S(1)}, bf16[320,896]{1,0:T(8,128)(2,1)S(1)}, bf16[320,896]{1,0:T(8,128)(2,1)S(1)}) custom-call(s32[2]{0:T(128)S(1)} %pad_add_fusion.1.place_ref, f32[320,512]{1,0:T(8,128)S(1)} %get-tuple-element.32.gate_near_ref, f32[320,512]{1,0:T(8,128)S(1)} %get-tuple-element.33.up_near_ref, ...), custom_call_target="tpu_custom_call" | custom-call | flops 100 | bytes 100 | tf_op jit(solution)/shard_map/pallas_call | solution.py:163
  70.8 0.2 collective-permute-start.8
  71.0 0.4 collective-permute-start.7
  71.4 1.5 collective-permute-done.8
  73.0 3.5 %collective-permute-start.9 = (bf16[320,896]{1,0:T(8,128)(2,1)S(1)}, bf16[320,896]{1,0:T(8,128)(2,1)S(1)}, u32[]{:S(2)}, u32[]{:S(2)}) collective-permute-start(bf16[320,896]{1,0:T(8,128)(2,1)S(1)} %add_convert_fusion.1), channel_id=1, source_target_pairs={{0,2},{2,0},{1,3},{3,1},{4,6},{6,4},{5,7},{7,5},{8,10},{10,8},{9,1... | collective-permute-start | bytes 1720328 | tf_op jit(solution)/shard_map/ppermute | solution.py:34
  76.5 13.3 %collective-permute-done.9 = bf16[320,896]{1,0:T(8,128)(2,1)S(1)} collective-permute-done((bf16[320,896]{1,0:T(8,128)(2,1)S(1)}, bf16[320,896]{1,0:T(8,128)(2,1)S(1)}, u32[]{:S(2)}, u32[]{:S(2)}) %collective-permute-start.9) | collective-permute-done | bytes 573472 | tf_op jit(solution)/shard_map/ppermute | solution.py:34
  89.8 0.2 add_convert_fusion
  90.1 1.4 reshape.133
  91.5 12.6 %all-to-all-start.1 = ((bf16[64,35,128]{2,1,0:T(8,128)(2,1)}), bf16[64,35,128]{2,1,0:T(8,128)(2,1)S(1)}, u32[]{:S(2)}, u32[]{:S(2)}) async-start(bf16[64,35,128]{2,1,0:T(8,128)(2,1)} %reshape.133), calls=%async_computation.1 | async-start | bytes 1310720 | tf_op jit(solution)/shard_map/all_to_all | solution.py:55
  104.4 2.4 %collective-permute-start.10 = (f32[128,128]{1,0:T(8,128)S(1)}, f32[128,128]{1,0:T(8,128)S(1)}, u32[]{:S(2)}, u32[]{:S(2)}) collective-permute-start(f32[128,128]{1,0:T(8,128)S(1)} %add.50), channel_id=1, source_target_pairs={{0,2},{2,0},{1,3},{3,1},{4,6},{6,4},{5,7},{7,5},{8,10},{10,8},{9,1... | collective-permute-start | bytes 196616 | tf_op jit(solution)/shard_map/ppermute | solution.py:34
  106.8 0.4 fusion.1
  107.2 3.5 %collective-permute-done.10 = f32[128,128]{1,0:T(8,128)S(1)} collective-permute-done((f32[128,128]{1,0:T(8,128)S(1)}, f32[128,128]{1,0:T(8,128)S(1)}, u32[]{:S(2)}, u32[]{:S(2)}) %collective-permute-start.10) | collective-permute-done | bytes 65568 | tf_op jit(solution)/shard_map/ppermute | solution.py:34
  110.7 15.7 %all-to-all-done.1 = bf16[64,35,128]{2,1,0:T(8,128)(2,1)S(1)} async-done(((bf16[64,35,128]{2,1,0:T(8,128)(2,1)}), bf16[64,35,128]{2,1,0:T(8,128)(2,1)S(1)}, u32[]{:S(2)}, u32[]{:S(2)}) %all-to-all-start.1) | async-done | bytes 573472 | tf_op jit(solution)/shard_map/all_to_all | solution.py:55
  126.4 0.6 reshape.134
  127.0 2.3 %copy-done.1 = bf16[1792,1280]{1,0:T(8,128)(2,1)S(1)} copy-done((bf16[1792,1280]{1,0:T(8,128)(2,1)S(1)}, bf16[1792,1280]{1,0:T(8,128)(2,1)}, u32[]{:S(2)}) %copy-start.1) | copy-done | bytes 4587544
  129.3 0.3 shard_map.141
  129.7 0.6 convolution_convert_fusion.2.own_ref
  130.3 1.0 collective-permute-start.12
  131.3 5.1 %collective-permute-done.12.pair_ref = bf16[128,896]{1,0:T(8,128)(2,1)S(1)} collective-permute-done((bf16[128,896]{1,0:T(8,128)(2,1)S(1)}, bf16[128,896]{1,0:T(8,128)(2,1)S(1)}, u32[]{:S(2)}, u32[]{:S(2)}) %collective-permute-start.12) | collective-permute-done | bytes 229408 | tf_op jit(solution)/shard_map/ppermute | solution.py:34
  136.5 1.4 collective-permute-done.13.pair_far_ref
  137.9 2.3 %copy-done.2 = bf16[1792,1280]{1,0:T(8,128)(2,1)S(1)} copy-done((bf16[1792,1280]{1,0:T(8,128)(2,1)S(1)}, bf16[1792,1280]{1,0:T(8,128)(2,1)}, u32[]{:S(2)}) %copy-start.2) | copy-done | bytes 4587544
  140.2 2.3 %shard_map.142 = (bf16[128,1280]{1,0:T(8,128)(2,1)S(1)}, bf16[128,1280]{1,0:T(8,128)(2,1)S(1)}) custom-call(s32[3]{0:T(128)S(1)} %pad_add_fusion.order_ref, bf16[128,896]{1,0:T(8,128)(2,1)S(1)} %convolution_convert_fusion.2.own_ref, bf16[128,896]{1,0:T(8,128)(2,1)S(1)} %collective-permute-done.11.own_far_ref, ...), custom_call_target="tpu_custom_call" | custom-call | flops 100 | bytes 100 | tf_op jit(solution)/shard_map/pallas_call | solution.py:83
  142.5 1.0 collective-permute-start.15
  143.5 0.7 collective-permute-start.14
  144.2 9.6 %collective-permute-done.15 = bf16[128,1280]{1,0:T(8,128)(2,1)S(1)} collective-permute-done((bf16[128,1280]{1,0:T(8,128)(2,1)S(1)}, bf16[128,1280]{1,0:T(8,128)(2,1)S(1)}, u32[]{:S(2)}, u32[]{:S(2)}) %collective-permute-start.15) | collective-permute-done | bytes 327712 | tf_op jit(solution)/shard_map/ppermute | solution.py:307
  154.0 0.2 fusion.20
  154.2 6.1 %collective-permute-start.17 = (f32[128,64]{0,1:T(8,128)S(1)}, f32[128,64]{0,1:T(8,128)S(1)}, u32[]{:S(2)}, u32[]{:S(2)}) collective-permute-start(f32[128,64]{0,1:T(8,128)S(1)} %fusion.20), channel_id=1, source_target_pairs={{0,2},{2,0},{1,3},{3,1},{4,6},{6,4},{5,7},{7,5},{8,10},{10,8},{9,1... | collective-permute-start | bytes 98312 | tf_op jit(solution)/shard_map/ppermute | solution.py:34
  160.3 0.2 collective-permute-start.16
  160.5 0.8 multiply_reduce_fusion
  164.9 0.2 fusion
  165.2 1.3 fusion.18
  166.9 23.8 %all_to_all.20 = bf16[64,24,128]{2,1,0:T(8,128)(2,1)S(1)} all-to-all(bf16[64,24,128]{2,1,0:T(8,128)(2,1)S(1)} %pad_maximum_fusion), channel_id=1, replica_groups=mesh['yl'=2,'z'=8,'xh'=2,'xl'=2,'yh'=2,'c'=2] {'yl','z','xh','xl'}, dimensions={0} | all-to-all | bytes 786432 | tf_op jit(solution)/shard_map/all_to_all | solution.py:355
  190.8 0.8 broadcast_in_dim.32
  191.6 5.3 %all-to-all-start.3 = ((bf16[64,24,128]{2,1,0:T(8,128)(2,1)}), bf16[64,24,128]{2,1,0:T(8,128)(2,1)S(1)}, u32[]{:S(2)}, u32[]{:S(2)}) async-start(bf16[64,24,128]{2,1,0:T(8,128)(2,1)} %broadcast_in_dim.32), calls=%async_computation.3 | async-start | bytes 786432 | tf_op jit(solution)/shard_map/all_to_all | solution.py:358
  196.9 2.1 collective-permute-start.20
  199.0 1.6 collective-permute-start.19
  200.6 1.4 collective-permute-done.20
  202.1 1.4 collective-permute-done.21
  203.5 0.6 add_reduce_fusion
  204.7 7.3 %all-to-all-done.3 = bf16[64,24,128]{2,1,0:T(8,128)(2,1)S(1)} async-done(((bf16[64,24,128]{2,1,0:T(8,128)(2,1)}), bf16[64,24,128]{2,1,0:T(8,128)(2,1)S(1)}, u32[]{:S(2)}, u32[]{:S(2)}) %all-to-all-start.3) | async-done | bytes 393248 | tf_op jit(solution)/shard_map/all_to_all | solution.py:358
  212.1 0.7 convert_bitcast_fusion.1
  212.8 0.7 convert_bitcast_fusion
  (78 shorter events, 2.2 us)
Async XLA Ops:
  7.2 2.1 copy-start
  9.8 14.1 %copy-start.15 = (bf16[56,1280]{1,0:T(8,128)(2,1)S(1)}, bf16[56,1280]{1,0:T(8,128)(2,1)}, u32[]{:S(2)}) copy-start(bf16[56,1280]{1,0:T(8,128)(2,1)} %param.17) | copy-start | bytes 430084
  11.3 34.3 %all-to-all-start = ((bf16[64,35,128]{2,1,0:T(8,128)(2,1)}), bf16[64,35,128]{2,1,0:T(8,128)(2,1)S(1)}, u32[]{:S(2)}, u32[]{:S(2)}) async-start(bf16[64,35,128]{2,1,0:T(8,128)(2,1)} %reshape.130), calls=%async_computation | async-start | bytes 1310720 | tf_op jit(solution)/shard_map/all_to_all | solution.py:55
  23.9 103.1 %all-gather.2.cloned.1.call-start = ((), (), s32[]{:S(2)}) async-start(), calls=%async_computation.4 | async-start | bytes 5160960 | tf_op jit(solution)/shard_map/all_gather | solution.py:220
  23.9 9.6 %collective-permute-start.1 = (bf16[56,1280]{1,0:T(8,128)(2,1)S(1)}, bf16[56,1280]{1,0:T(8,128)(2,1)S(1)}, u32[]{:S(2)}, u32[]{:S(2)}) collective-permute-start(bf16[56,1280]{1,0:T(8,128)(2,1)S(1)} %copy-done.15), channel_id=1, source_target_pairs={{0,128},{1,129},{2,132},{3,133},{4,0},{5,1},{6,4},{7,5},{8,136},{9... | collective-permute-start | bytes 430088 | tf_op jit(solution)/shard_map/ppermute | solution.py:216
  25.6 7.9 %collective-permute-start = (bf16[56,1280]{1,0:T(8,128)(2,1)S(1)}, bf16[56,1280]{1,0:T(8,128)(2,1)S(1)}, u32[]{:S(2)}, u32[]{:S(2)}) collective-permute-start(bf16[56,1280]{1,0:T(8,128)(2,1)S(1)} %copy-done.15), channel_id=1, source_target_pairs={{0,0},{1,1},{2,4},{3,5},{4,128},{5,129},{6,132},{7,133},{8,8},{9,9... | collective-permute-start | bytes 430088 | tf_op jit(solution)/shard_map/ppermute | solution.py:216
  33.6 11.0 %collective-permute-start.2 = (bf16[112,1280]{1,0:T(8,128)(2,1)S(1)}, bf16[112,1280]{1,0:T(8,128)(2,1)S(1)}, u32[]{:S(2)}, u32[]{:S(2)}) collective-permute-start(bf16[112,1280]{1,0:T(8,128)(2,1)S(1)} %maximum_select_fusion.1), channel_id=1, source_target_pairs={{0,8},{8,0},{1,9},{9,1},{2,10},{10,2},{3,11},{11,3},{4,12},{12,4},... | collective-permute-start | bytes 860168 | tf_op jit(solution)/shard_map/ppermute | solution.py:34
  45.6 6.1 %copy-start.13 = (bf16[1280]{0:T(1024)(128)(2,1)S(1)}, bf16[1280]{0:T(1024)(128)(2,1)}, u32[]{:S(2)}) copy-start(bf16[1280]{0:T(1024)(128)(2,1)} %param.19) | copy-start | bytes 7684
  45.6 6.1 %copy-start.9 = (bf16[128,1280]{1,0:T(8,128)(2,1)S(1)}, bf16[128,1280]{1,0:T(8,128)(2,1)}, u32[]{:S(2)}) copy-start(bf16[128,1280]{1,0:T(8,128)(2,1)} %student_ref.3) | copy-start | bytes 983044
  45.6 6.1 %copy-start.11 = (bf16[1280,64]{0,1:T(8,128)(2,1)S(1)}, bf16[1280,64]{0,1:T(8,128)(2,1)}, u32[]{:S(2)}) copy-start(bf16[1280,64]{0,1:T(8,128)(2,1)} %param.20) | copy-start | bytes 491524
  46.2 7.1 %collective-permute-start.5 = (bf16[320,896]{1,0:T(8,128)(2,1)S(1)}, bf16[320,896]{1,0:T(8,128)(2,1)S(1)}, u32[]{:S(2)}, u32[]{:S(2)}) collective-permute-start(bf16[320,896]{1,0:T(8,128)(2,1)S(1)} %reshape.131.own_ref), channel_id=1, source_target_pairs={{0,1},{1,0},{2,3},{3,2},{4,5},{5,4},{6,7},{7,6},{8,9},{9,8},{10,11... | collective-permute-start | bytes 1720328 | tf_op jit(solution)/shard_map/ppermute | solution.py:34
  46.3 18.9 %collective-permute-start.3 = (bf16[320,896]{1,0:T(8,128)(2,1)S(1)}, bf16[320,896]{1,0:T(8,128)(2,1)S(1)}, u32[]{:S(2)}, u32[]{:S(2)}) collective-permute-start(bf16[320,896]{1,0:T(8,128)(2,1)S(1)} %reshape.131.own_ref), channel_id=1, source_target_pairs={{0,2},{2,0},{1,3},{3,1},{4,6},{6,4},{5,7},{7,5},{8,10},{10,8},{9,1... | collective-permute-start | bytes 1720328 | tf_op jit(solution)/shard_map/ppermute | solution.py:34
  52.0 1.3 collective-permute-start.4
  53.3 2.0 copy-start.3
  55.4 2.0 copy-start.5
  57.4 2.0 copy-start.7
  59.4 7.8 %copy-start.4 = (bf16[1,3584,512]{2,1,0:T(8,128)(2,1)S(1)}, bf16[1,3584,512]{2,1,0:T(8,128)(2,1)}, u32[]{:S(2)}) copy-start(bf16[1,3584,512]{2,1,0:T(8,128)(2,1)} %param.14) | copy-start | bytes 11010052
  59.4 7.8 %copy-start.6 = (bf16[1,3584,512]{2,1,0:T(8,128)(2,1)S(1)}, bf16[1,3584,512]{2,1,0:T(8,128)(2,1)}, u32[]{:S(2)}) copy-start(bf16[1,3584,512]{2,1,0:T(8,128)(2,1)} %param.15) | copy-start | bytes 11010052
  59.4 7.8 %copy-start.8 = (bf16[1,512,3584]{2,1,0:T(8,128)(2,1)S(1)}, bf16[1,512,3584]{2,1,0:T(8,128)(2,1)}, u32[]{:S(2)}) copy-start(bf16[1,512,3584]{2,1,0:T(8,128)(2,1)} %param.16) | copy-start | bytes 11010052
  65.2 2.0 collective-permute-start.6
  70.8 2.1 collective-permute-start.8
  71.0 5.5 %collective-permute-start.7 = (bf16[320,896]{1,0:T(8,128)(2,1)S(1)}, bf16[320,896]{1,0:T(8,128)(2,1)S(1)}, u32[]{:S(2)}, u32[]{:S(2)}) collective-permute-start(bf16[320,896]{1,0:T(8,128)(2,1)S(1)} %get-tuple-element.36), channel_id=1, source_target_pairs={{0,1},{1,0},{2,3},{3,2},{4,5},{5,4},{6,7},{7,6},{8,9},{9,8},{10,11... | collective-permute-start | bytes 1720328 | tf_op jit(solution)/shard_map/ppermute | solution.py:34
  73.0 16.8 %collective-permute-start.9 = (bf16[320,896]{1,0:T(8,128)(2,1)S(1)}, bf16[320,896]{1,0:T(8,128)(2,1)S(1)}, u32[]{:S(2)}, u32[]{:S(2)}) collective-permute-start(bf16[320,896]{1,0:T(8,128)(2,1)S(1)} %add_convert_fusion.1), channel_id=1, source_target_pairs={{0,2},{2,0},{1,3},{3,1},{4,6},{6,4},{5,7},{7,5},{8,10},{10,8},{9,1... | collective-permute-start | bytes 1720328 | tf_op jit(solution)/shard_map/ppermute | solution.py:34
  90.1 14.1 %copy-start.14 = (f32[128,2]{0,1:T(2,128)S(1)}, f32[128,2]{0,1:T(2,128)}, u32[]{:S(2)}) copy-start(f32[128,2]{0,1:T(2,128)} %param.13) | copy-start | bytes 3076
  91.5 34.9 %all-to-all-start.1 = ((bf16[64,35,128]{2,1,0:T(8,128)(2,1)}), bf16[64,35,128]{2,1,0:T(8,128)(2,1)S(1)}, u32[]{:S(2)}, u32[]{:S(2)}) async-start(bf16[64,35,128]{2,1,0:T(8,128)(2,1)} %reshape.133), calls=%async_computation.1 | async-start | bytes 1310720 | tf_op jit(solution)/shard_map/all_to_all | solution.py:55
  104.1 22.9 %copy-start.10 = (bf16[64,1280]{1,0:T(8,128)(2,1)S(1)}, bf16[64,1280]{1,0:T(8,128)(2,1)}, u32[]{:S(2)}) copy-start(bf16[64,1280]{1,0:T(8,128)(2,1)} %up_ref.1) | copy-start | bytes 491524
  104.4 6.2 %collective-permute-start.10 = (f32[128,128]{1,0:T(8,128)S(1)}, f32[128,128]{1,0:T(8,128)S(1)}, u32[]{:S(2)}, u32[]{:S(2)}) collective-permute-start(f32[128,128]{1,0:T(8,128)S(1)} %add.50), channel_id=1, source_target_pairs={{0,2},{2,0},{1,3},{3,1},{4,6},{6,4},{5,7},{7,5},{8,10},{10,8},{9,1... | collective-permute-start | bytes 196616 | tf_op jit(solution)/shard_map/ppermute | solution.py:34
  127.0 2.3 %copy-start.1 = (bf16[1792,1280]{1,0:T(8,128)(2,1)S(1)}, bf16[1792,1280]{1,0:T(8,128)(2,1)}, u32[]{:S(2)}) copy-start(bf16[1792,1280]{1,0:T(8,128)(2,1)} %all-gather.2.cloned.1.call-done.block_ref) | copy-start | bytes 13762564
  130.3 6.1 %collective-permute-start.12 = (bf16[128,896]{1,0:T(8,128)(2,1)S(1)}, bf16[128,896]{1,0:T(8,128)(2,1)S(1)}, u32[]{:S(2)}, u32[]{:S(2)}) collective-permute-start(bf16[128,896]{1,0:T(8,128)(2,1)S(1)} %convolution_convert_fusion.2.own_ref), channel_id=1, source_target_pairs={{0,4},{4,0},{1,5},{5,1},{2,6},{6,2},{3,7},{7,3},{8,12},{12,8},{9,1... | collective-permute-start | bytes 688136 | tf_op jit(solution)/shard_map/ppermute | solution.py:34
  131.3 5.2 %collective-permute-start.11 = (bf16[128,896]{1,0:T(8,128)(2,1)S(1)}, bf16[128,896]{1,0:T(8,128)(2,1)S(1)}, u32[]{:S(2)}, u32[]{:S(2)}) collective-permute-start(bf16[128,896]{1,0:T(8,128)(2,1)S(1)} %convolution_convert_fusion.2.own_ref), channel_id=1, source_target_pairs={{0,1},{1,0},{2,3},{3,2},{4,5},{5,4},{6,7},{7,6},{8,9},{9,8},{10,11... | collective-permute-start | bytes 688136 | tf_op jit(solution)/shard_map/ppermute | solution.py:34
  136.4 1.5 collective-permute-start.13
  137.9 2.3 %copy-start.2 = (bf16[1792,1280]{1,0:T(8,128)(2,1)S(1)}, bf16[1792,1280]{1,0:T(8,128)(2,1)}, u32[]{:S(2)}) copy-start(bf16[1792,1280]{1,0:T(8,128)(2,1)} %all-gather.2.cloned.1.call-done.block_ref) | copy-start | bytes 13762564
  142.5 11.3 %collective-permute-start.15 = (bf16[128,1280]{1,0:T(8,128)(2,1)S(1)}, bf16[128,1280]{1,0:T(8,128)(2,1)S(1)}, u32[]{:S(2)}, u32[]{:S(2)}) collective-permute-start(bf16[128,1280]{1,0:T(8,128)(2,1)S(1)} %get-tuple-element.46), channel_id=1, source_target_pairs={{0,4},{1,5},{2,0},{3,1},{4,6},{5,7},{6,2},{7,3},{8,12},{9,13},{10,... | collective-permute-start | bytes 983048 | tf_op jit(solution)/shard_map/ppermute | solution.py:307
  143.5 10.3 %collective-permute-start.14 = (bf16[128,1280]{1,0:T(8,128)(2,1)S(1)}, bf16[128,1280]{1,0:T(8,128)(2,1)S(1)}, u32[]{:S(2)}, u32[]{:S(2)}) collective-permute-start(bf16[128,1280]{1,0:T(8,128)(2,1)S(1)} %get-tuple-element.45), channel_id=1, source_target_pairs={{0,0},{1,1},{2,4},{3,5},{4,2},{5,3},{6,6},{7,7},{8,8},{9,9},{10,12... | collective-permute-start | bytes 983048 | tf_op jit(solution)/shard_map/ppermute | solution.py:307
  154.0 11.2 %copy-start.12 = (f32[128,1280]{1,0:T(8,128)}, f32[128,1280]{1,0:T(8,128)S(1)}, u32[]{:S(2)}) copy-start(f32[128,1280]{1,0:T(8,128)S(1)} %get-tuple-element.51) | copy-start | bytes 1966084
  154.2 12.3 %collective-permute-start.17 = (f32[128,64]{0,1:T(8,128)S(1)}, f32[128,64]{0,1:T(8,128)S(1)}, u32[]{:S(2)}, u32[]{:S(2)}) collective-permute-start(f32[128,64]{0,1:T(8,128)S(1)} %fusion.20), channel_id=1, source_target_pairs={{0,2},{2,0},{1,3},{3,1},{4,6},{6,4},{5,7},{7,5},{8,10},{10,8},{9,1... | collective-permute-start | bytes 98312 | tf_op jit(solution)/shard_map/ppermute | solution.py:34
  160.3 6.2 %collective-permute-start.18 = (f32[128,64]{0,1:T(8,128)S(1)}, f32[128,64]{0,1:T(8,128)S(1)}, u32[]{:S(2)}, u32[]{:S(2)}) collective-permute-start(f32[128,64]{0,1:T(8,128)S(1)} %fusion.20), channel_id=1, source_target_pairs={{0,3},{1,2},{2,1},{3,0},{4,7},{5,6},{6,5},{7,4},{8,11},{9,10},{10,... | collective-permute-start | bytes 98312 | tf_op jit(solution)/shard_map/ppermute | solution.py:42
  160.3 6.2 %collective-permute-start.16 = (f32[128,64]{0,1:T(8,128)S(1)}, f32[128,64]{0,1:T(8,128)S(1)}, u32[]{:S(2)}, u32[]{:S(2)}) collective-permute-start(f32[128,64]{0,1:T(8,128)S(1)} %fusion.20), channel_id=1, source_target_pairs={{0,1},{1,0},{2,3},{3,2},{4,5},{5,4},{6,7},{7,6},{8,9},{9,8},{10,11... | collective-permute-start | bytes 98312 | tf_op jit(solution)/shard_map/ppermute | solution.py:34
  191.6 20.4 %all-to-all-start.3 = ((bf16[64,24,128]{2,1,0:T(8,128)(2,1)}), bf16[64,24,128]{2,1,0:T(8,128)(2,1)S(1)}, u32[]{:S(2)}, u32[]{:S(2)}) async-start(bf16[64,24,128]{2,1,0:T(8,128)(2,1)} %broadcast_in_dim.32), calls=%async_computation.3 | async-start | bytes 786432 | tf_op jit(solution)/shard_map/all_to_all | solution.py:358
  196.9 5.2 %collective-permute-start.20 = (f32[1,128]{1,0:T(1,128)S(1)}, f32[1,128]{1,0:T(1,128)S(1)}, u32[]{:S(2)}, u32[]{:S(2)}) collective-permute-start(f32[1,128]{1,0:T(1,128)S(1)} %slice.43), channel_id=1, source_target_pairs={{0,2},{2,0},{1,3},{3,1},{4,6},{6,4},{5,7},{7,5},{8,10},{10,8},{9,1... | collective-permute-start | bytes 1544 | tf_op jit(solution)/shard_map/ppermute | solution.py:34
  199.0 4.5 %collective-permute-start.21 = (f32[1,128]{1,0:T(1,128)S(1)}, f32[1,128]{1,0:T(1,128)S(1)}, u32[]{:S(2)}, u32[]{:S(2)}) collective-permute-start(f32[1,128]{1,0:T(1,128)S(1)} %slice.43), channel_id=1, source_target_pairs={{0,3},{1,2},{2,1},{3,0},{4,7},{5,6},{6,5},{7,4},{8,11},{9,10},{10,... | collective-permute-start | bytes 1544 | tf_op jit(solution)/shard_map/ppermute | solution.py:42
  199.0 4.5 %collective-permute-start.19 = (f32[1,128]{1,0:T(1,128)S(1)}, f32[1,128]{1,0:T(1,128)S(1)}, u32[]{:S(2)}, u32[]{:S(2)}) collective-permute-start(f32[1,128]{1,0:T(1,128)S(1)} %slice.43), channel_id=1, source_target_pairs={{0,1},{1,0},{2,3},{3,2},{4,5},{5,4},{6,7},{7,6},{8,9},{9,8},{10,11... | collective-permute-start | bytes 1544 | tf_op jit(solution)/shard_map/ppermute | solution.py:34
Sparse Core Ops, SparseCore 0:
  46.3 63.5 all-gather.1

commit v8 on v7

--- a/solution.py
+++ b/solution.py
@@ -106,8 +106,7 @@
     out_ref[:, rank:] = jnp.broadcast_to(total, (student.shape[0], rank))
 
 
-def student_kernel(width, stats_ref, student_ref, gain_ref, up_ref, block_ref, *outs):
-    low_ref, normed_ref, out_ref = outs
+def student_kernel(width, stats_ref, student_ref, gain_ref, up_ref, low_ref, normed_ref, out_ref):
     rank = up_ref.shape[0]
     inverse = lax.rsqrt(stats_ref[:, rank : rank + 1] / width + 1e-06)
     low = (stats_ref[:, :rank] * inverse).astype(jnp.bfloat16)
@@ -117,13 +116,66 @@
     out_ref[...] = student + adapter_scale_factor * dot(low, up_ref[...])
 
 
-def local_kernel(kernel, shapes, *args):
+def home_kernel(
+    scale, first_ref, second_ref, student_ref, low_ref, up_ref, target_ref, back_ref, grad_ref, loss_ref
+):
+    target = first_ref[...].astype(jnp.float32) + second_ref[...].astype(jnp.float32)
+    target_ref[...] = target
+    diff = student_ref[...] - target
+    scaled = (diff * scale).astype(jnp.bfloat16)
+    back_ref[...] = lax.dot_general(
+        scaled, up_ref[...], (((1,), (1,)), ((), ())), preferred_element_type=jnp.float32
+    )
+    grad_ref[...] = adapter_scale_factor * lax.dot_general(
+        low_ref[...], scaled, (((0,), (0,)), ((), ())), preferred_element_type=jnp.float32
+    )
+    total = jnp.sum(jnp.sum(diff * diff, axis=0, keepdims=True), axis=1, keepdims=True)
+    loss_ref[...] = jnp.broadcast_to(total, loss_ref.shape)
+
+
+def bundle_kernel(own_ref, core_ref, far_ref, cross_ref, normed_ref, grad_ref, loss_ref, out_ref, down_ref):
+    back = (own_ref[...] + core_ref[...]) + (far_ref[...] + cross_ref[...])
+    down_ref[...] = lax.dot_general(
+        (adapter_scale_factor * back).astype(jnp.bfloat16),
+        normed_ref[...],
+        (((0,), (0,)), ((), ())),
+        preferred_element_type=jnp.float32,
+    )
+    total = loss_ref[...]
+    lane = lax.broadcasted_iota(jnp.int32, total.shape, 1)
+    row = lax.broadcasted_iota(jnp.int32, total.shape, 0)
+    first = total.astype(jnp.bfloat16).astype(jnp.float32)
+    second = (total - first).astype(jnp.bfloat16).astype(jnp.float32)
+    third = total - first - second
+    loss = jnp.where(
+        lane == 0, first, jnp.where(lane == 1, second, jnp.where(lane == 2, third, 0.0))
+    )
+    across = down_ref.shape[1] // 128
+    tiles = down_ref.shape[0] // 8 * across
+
+    def tile(number):
+        ref = grad_ref if number < tiles else down_ref
+        high, wide = divmod(number % tiles, across)
+        return ref[high * 8 : high * 8 + 8, wide * 128 : wide * 128 + 128]
+
+    count = out_ref.shape[0]
+    for index in range(count):
+        half = tile(2 * count + index // 2)
+        if index % 2:
+            half = pltpu.roll(half, 4, 0)
+        last = jnp.where(row < 4, half, loss)
+        whole = jnp.concatenate([tile(2 * index), tile(2 * index + 1), last])
+        out_ref[index] = whole.astype(jnp.bfloat16)
+
+
+def local_kernel(kernel, shapes, *args, scratch=()):
     vmem = pl.BlockSpec(memory_space=pltpu.VMEM)
     return pl.pallas_call(
         kernel,
         out_shape=shapes,
         in_specs=[vmem] * len(args),
         out_specs=jax.tree.map(lambda _: vmem, shapes),
+        scratch_shapes=scratch,
         compiler_params=pltpu.CompilerParams(vmem_limit_bytes=16 * 1024 * 1024),
         cost_estimate=pl.CostEstimate(flops=100, bytes_accessed=100, transcendentals=0),
     )(*args)
@@ -278,10 +330,9 @@
         student_hidden_input,
         gain,
         adapter_up_matrix,
-        proj_block,
-    )
-    returned, lowrank, normed, student_out = lax.optimization_barrier(
-        (returned, lowrank, normed, student_out)
+    )
+    returned, lowrank, normed, student_out, proj_block = lax.optimization_barrier(
+        (returned, lowrank, normed, student_out, proj_block)
     )
 
     weights = (
@@ -304,54 +355,45 @@
     order = jnp.stack([yh ^ xl, yh ^ xl ^ 1, core])
     pieces = product_pieces(order, teacher, teacher_far, pair, swap(pair, "c"), proj_block)
     pieces = [
-        lax.ppermute(piece, ALL, permutation(home_target(step))).astype(jnp.float32)
+        lax.ppermute(piece, ALL, permutation(home_target(step)))
         for step, piece in enumerate(pieces)
     ]
-    target = pieces[0] + pieces[1]
-
-    output_difference = student_out - target
     tokens_all = tok_rows * experts
-    scale = 1.0 / math.sqrt(tokens_all)
-    scaled = (output_difference * scale).astype(jnp.bfloat16)
-    loss_here = jnp.sum(output_difference * output_difference)
-    back_part = lax.dot_general(
-        scaled, adapter_up_matrix, (((1,), (1,)), ((), ())), preferred_element_type=jnp.float32
-    )
-    back_low = (adapter_scale_factor * mp_sum(back_part)).astype(jnp.bfloat16)
-    over_tokens = (((0,), (0,)), ((), ()))
-    up_part = adapter_scale_factor * lax.dot_general(
-        lowrank, scaled, over_tokens, preferred_element_type=jnp.float32
-    )
-    down_part = lax.dot_general(back_low, normed, over_tokens, preferred_element_type=jnp.float32)
+    columns = adapter_up_matrix.shape[1]
+    target, back, up_part, loss_here = local_kernel(
+        functools.partial(home_kernel, 1.0 / math.sqrt(tokens_all)),
+        [
+            jax.ShapeDtypeStruct((tok_rows, columns), jnp.float32),
+            jax.ShapeDtypeStruct((tok_rows, rank), jnp.float32),
+            jax.ShapeDtypeStruct((rank, columns), jnp.float32),
+            jax.ShapeDtypeStruct((8, 128), jnp.float32),
+        ],
+        *pieces,
+        student_out,
+        lowrank,
+        adapter_up_matrix,
+    )
 
     lanes = 128
-    columns = up_part.shape[1]
     tiles = rank // 8 * (columns // lanes)
-    first = lax.reduce_precision(loss_here, 8, 7)
-    second = lax.reduce_precision(loss_here - first, 8, 7)
-    third = loss_here - first - second
-    lane = jnp.arange(lanes)
-    loss_row = jnp.where(
-        lane == 0, first, jnp.where(lane == 1, second, jnp.where(lane == 2, third, 0.0))
-    )
-
-    def to_tiles(value):
-        value = value.astype(jnp.bfloat16).reshape(rank // 8, 8, columns // lanes, lanes)
-        return value.transpose(0, 2, 1, 3).reshape(tiles, 8, lanes)
+    cross = [(place, 3 - place) for place in range(4)]
+    bundle = local_kernel(
+        bundle_kernel,
+        jax.ShapeDtypeStruct((experts, 24, lanes), jnp.bfloat16),
+        back,
+        swap(back, "c"),
+        swap(back, "yh"),
+        lax.ppermute(back, MP, cross),
+        normed,
+        up_part,
+        loss_here,
+        scratch=[pltpu.VMEM((rank, columns), jnp.float32)],
+    )
 
     def from_tiles(value):
         value = value.reshape(rank // 8, columns // lanes, 8, lanes).transpose(0, 2, 1, 3)
         return value.reshape(rank, columns).astype(jnp.float32)
 
-    bundle = jnp.concatenate([to_tiles(up_part), to_tiles(down_part)])
-    bundle = jnp.concatenate(
-        [
-            bundle[: 2 * experts].reshape(experts, 16, lanes),
-            bundle[2 * experts :].reshape(experts, 4, lanes),
-            jnp.broadcast_to(loss_row.astype(jnp.bfloat16), (experts, 4, lanes)),
-        ],
-        axis=1,
-    )
     bundle = lax.all_to_all(bundle, DP, split_axis=0, concat_axis=0, tiled=True)
     summed = jnp.sum(bundle.astype(jnp.float32), axis=0)
     grads = jnp.broadcast_to(summed.astype(jnp.bfloat16), (experts, 24, lanes))

time: 222 us -> 219 us (0.986)
  waiting for transfers between devices: 79.4 us -> 87.8 us
  between operations: 19.9 us -> 16.1 us
  other arithmetic: 6.89 us -> 4.53 us
  local copies, waits for them, and re-layouts: 17.3 us -> 15 us
    ppermute x16, starting transfers between devices: 29.1 us -> 19.6 us  [swap(): return lax.ppermute(value, axis, [(0, 1), (1, 0)])]
    ppermute x2 -> x3, starting transfers between devices: 1.68 us -> 6.32 us  [the longest x2 6.18 us: body(): lax.ppermute(piece, ALL, permutation(home_target(step)))]
    ppermute x16, waiting for transfers between devices: 38.1 us -> 42.6 us  [swap(): return lax.ppermute(value, axis, [(0, 1), (1, 0)])]
    ppermute x2, waiting for transfers between devices: 7.26 us -> 11.1 us  [body(): lax.ppermute(proj, ALL, permutation(proj_target(step)))]
    ppermute x2, starting transfers between devices: 2.32 us -> 4.85 us  [body(): lax.ppermute(proj, ALL, permutation(proj_target(step)))]
    unnamed x33 -> x29, local copies, waits for them, and re-layouts: 11.6 us -> 9.28 us
    ppermute x2 -> x3, waiting for transfers between devices: 9.65 us -> 10.2 us  [the longest x2 7.36 us: body(): lax.ppermute(piece, ALL, permutation(home_target(step)))]
  transfers between devices with their start and end apart: 26 -> 26, of which waited for: 15 -> 17; matrix products, arithmetic and copies ran while one was open for 3% -> 2% of each run, Pallas kernels for 3% -> 3%
where the time goes in v8:
time: 219 us
  waiting for transfers between devices  87.8 us (40%)
  starting transfers between devices  62 us (28%)
  blocking collectives  21.8 us (10%)
  between operations  16.1 us (7%)
  local copies, waits for them, and re-layouts  15 us (7%)
  Pallas kernels  9.79 us (4%)
  other arithmetic  4.53 us (2%)
    ppermute x16, waiting for transfers between devices, swap(): return lax.ppermute(value, axis, [(0, 1), (1, 0)])  42.6 us
    all_to_all x2, starting transfers between devices, exchange_slots(): lax.all_to_all(rows, DP, split_axis=0, concat_axis=0, tiled=True)  24.6 us
    all_to_all x1, blocking collectives, body(): bundle = lax.all_to_all(bundle, DP, split_axis=0, concat_axis=0, tiled=True)  21.8 us
    ppermute x16, starting transfers between devices, swap(): return lax.ppermute(value, axis, [(0, 1), (1, 0)])  19.6 us
    all_to_all x2, waiting for transfers between devices, exchange_slots(): lax.all_to_all(rows, DP, split_axis=0, concat_axis=0, tiled=True)  15.3 us
    ppermute x2, waiting for transfers between devices, body(): lax.ppermute(proj, ALL, permutation(proj_target(step)))  11.1 us
    unnamed x29, local copies, waits for them, and re-layouts  9.28 us
    all_to_all x1, waiting for transfers between devices, body(): grads = lax.all_to_all(grads, DP, split_axis=0, concat_axis=0, tiled=True)  7.51 us
  transfers between devices with their start and end apart: 26, of which 17 were waited for; matrix products, arithmetic and copies ran while one was open for 2% of the time, Pallas kernels for 3%

profile of v8, /device:TPU:32, one launch (start us, length us, event | category | flops | bytes accessed | tf_op | source)
XLA Modules:
  0.0 218.7 jit_solution(11940546577625883739)
XLA Ops:
  7.2 0.8 copy.15
  8.3 0.6 reduce-window.6
  8.9 0.2 slice_reduce_fusion
  9.3 0.6 convolution_convert_fusion
  9.9 1.4 reshape.112
  11.3 12.6 %all-to-all-start = ((bf16[64,35,128]{2,1,0:T(8,128)(2,1)}), bf16[64,35,128]{2,1,0:T(8,128)(2,1)S(1)}, u32[]{:S(2)}, u32[]{:S(2)}) async-start(bf16[64,35,128]{2,1,0:T(8,128)(2,1)} %reshape.112), calls=%async_computation | async-start | bytes 1310720 | tf_op jit(solution)/shard_map/all_to_all | solution.py:55
  23.9 0.7 collective-permute-start
  24.6 4.2 %collective-permute-start.1 = (bf16[56,1280]{1,0:T(8,128)(2,1)S(1)}, bf16[56,1280]{1,0:T(8,128)(2,1)S(1)}, u32[]{:S(2)}, u32[]{:S(2)}) collective-permute-start(bf16[56,1280]{1,0:T(8,128)(2,1)S(1)} %copy-done.13), channel_id=1, source_target_pairs={{0,128},{1,129},{2,132},{3,133},{4,0},{5,1},{6,4},{7,5},{8,136},{9... | collective-permute-start | bytes 430088 | tf_op jit(solution)/shard_map/ppermute | solution.py:268
  28.8 11.1 %collective-permute-done.1 = bf16[56,1280]{1,0:T(8,128)(2,1)S(1)} collective-permute-done((bf16[56,1280]{1,0:T(8,128)(2,1)S(1)}, bf16[56,1280]{1,0:T(8,128)(2,1)S(1)}, u32[]{:S(2)}, u32[]{:S(2)}) %collective-permute-start.1) | collective-permute-done | bytes 143392 | tf_op jit(solution)/shard_map/ppermute | solution.py:268
  39.9 2.5 %collective-permute-start.2 = (bf16[112,1280]{1,0:T(8,128)(2,1)S(1)}, bf16[112,1280]{1,0:T(8,128)(2,1)S(1)}, u32[]{:S(2)}, u32[]{:S(2)}) collective-permute-start(bf16[112,1280]{1,0:T(8,128)(2,1)S(1)} %maximum_select_fusion.1), channel_id=1, source_target_pairs={{0,8},{8,0},{1,9},{9,1},{2,10},{10,2},{3,11},{11,3},{4,12},{12,4},... | collective-permute-start | bytes 860168 | tf_op jit(solution)/shard_map/ppermute | solution.py:34
  42.5 7.0 %collective-permute-done.2 = bf16[112,1280]{1,0:T(8,128)(2,1)S(1)} collective-permute-done((bf16[112,1280]{1,0:T(8,128)(2,1)S(1)}, bf16[112,1280]{1,0:T(8,128)(2,1)S(1)}, u32[]{:S(2)}, u32[]{:S(2)}) %collective-permute-start.2) | collective-permute-done | bytes 286752 | tf_op jit(solution)/shard_map/ppermute | solution.py:34
  49.4 0.9 maximum_select_fusion
  50.4 0.6 reshape.113.own_ref
  51.1 3.4 %collective-permute-start.3 = (bf16[320,896]{1,0:T(8,128)(2,1)S(1)}, bf16[320,896]{1,0:T(8,128)(2,1)S(1)}, u32[]{:S(2)}, u32[]{:S(2)}) collective-permute-start(bf16[320,896]{1,0:T(8,128)(2,1)S(1)} %reshape.113.own_ref), channel_id=1, source_target_pairs={{0,2},{2,0},{1,3},{3,1},{4,6},{6,4},{5,7},{7,5},{8,10},{10,8},{9,1... | collective-permute-start | bytes 1720328 | tf_op jit(solution)/shard_map/ppermute | solution.py:34
  54.6 0.2 shard_map.138
  54.8 0.2 collective-permute-start.4
  55.1 1.0 collective-permute-done.4
  56.2 2.0 copy-done.1
  58.2 2.0 copy-done.3
  60.3 2.0 copy-done.5
  62.3 2.1 shard_map.139
  64.4 3.7 %collective-permute-done.3.own_ref = bf16[320,896]{1,0:T(8,128)(2,1)S(1)} collective-permute-done((bf16[320,896]{1,0:T(8,128)(2,1)S(1)}, bf16[320,896]{1,0:T(8,128)(2,1)S(1)}, u32[]{:S(2)}, u32[]{:S(2)}) %collective-permute-start.3) | collective-permute-done | bytes 573472 | tf_op jit(solution)/shard_map/ppermute | solution.py:34
  68.1 2.0 collective-permute-done.6.other_ref
  70.1 3.5 %shard_map.140 = (bf16[320,896]{1,0:T(8,128)(2,1)S(1)}, bf16[320,896]{1,0:T(8,128)(2,1)S(1)}, bf16[320,896]{1,0:T(8,128)(2,1)S(1)}, bf16[320,896]{1,0:T(8,128)(2,1)S(1)}) custom-call(s32[2]{0:T(128)S(1)} %pad_add_fusion.1.place_ref, f32[320,512]{1,0:T(8,128)S(1)} %get-tuple-element.37.gate_near_ref, f32[320,512]{1,0:T(8,128)S(1)} %get-tuple-element.38.up_near_ref, ...), custom_call_target="tpu_custom_call" | custom-call | flops 100 | bytes 100 | tf_op jit(solution)/shard_map/pallas_call | solution.py:215
  73.6 0.2 collective-permute-start.8
  73.8 0.4 collective-permute-start.7
  74.2 1.5 collective-permute-done.8
  75.8 3.5 %collective-permute-start.9 = (bf16[320,896]{1,0:T(8,128)(2,1)S(1)}, bf16[320,896]{1,0:T(8,128)(2,1)S(1)}, u32[]{:S(2)}, u32[]{:S(2)}) collective-permute-start(bf16[320,896]{1,0:T(8,128)(2,1)S(1)} %add_convert_fusion.1), channel_id=1, source_target_pairs={{0,2},{2,0},{1,3},{3,1},{4,6},{6,4},{5,7},{7,5},{8,10},{10,8},{9,1... | collective-permute-start | bytes 1720328 | tf_op jit(solution)/shard_map/ppermute | solution.py:34
  79.4 13.3 %collective-permute-done.9 = bf16[320,896]{1,0:T(8,128)(2,1)S(1)} collective-permute-done((bf16[320,896]{1,0:T(8,128)(2,1)S(1)}, bf16[320,896]{1,0:T(8,128)(2,1)S(1)}, u32[]{:S(2)}, u32[]{:S(2)}) %collective-permute-start.9) | collective-permute-done | bytes 573472 | tf_op jit(solution)/shard_map/ppermute | solution.py:34
  92.7 0.2 add_convert_fusion
  92.9 1.4 reshape.115
  94.3 12.1 %all-to-all-start.1 = ((bf16[64,35,128]{2,1,0:T(8,128)(2,1)}), bf16[64,35,128]{2,1,0:T(8,128)(2,1)S(1)}, u32[]{:S(2)}, u32[]{:S(2)}) async-start(bf16[64,35,128]{2,1,0:T(8,128)(2,1)} %reshape.115), calls=%async_computation.1 | async-start | bytes 1310720 | tf_op jit(solution)/shard_map/all_to_all | solution.py:55
  106.7 3.0 %collective-permute-start.10 = (f32[128,128]{1,0:T(8,128)S(1)}, f32[128,128]{1,0:T(8,128)S(1)}, u32[]{:S(2)}, u32[]{:S(2)}) collective-permute-start(f32[128,128]{1,0:T(8,128)S(1)} %add.38), channel_id=1, source_target_pairs={{0,2},{2,0},{1,3},{3,1},{4,6},{6,4},{5,7},{7,5},{8,10},{10,8},{9,1... | collective-permute-start | bytes 196616 | tf_op jit(solution)/shard_map/ppermute | solution.py:34
  109.7 0.4 fusion
  110.1 3.2 %collective-permute-done.10 = f32[128,128]{1,0:T(8,128)S(1)} collective-permute-done((f32[128,128]{1,0:T(8,128)S(1)}, f32[128,128]{1,0:T(8,128)S(1)}, u32[]{:S(2)}, u32[]{:S(2)}) %collective-permute-start.10) | collective-permute-done | bytes 65568 | tf_op jit(solution)/shard_map/ppermute | solution.py:34
  113.3 0.3 shard_map.141
  113.6 15.3 %all-to-all-done.1 = bf16[64,35,128]{2,1,0:T(8,128)(2,1)S(1)} async-done(((bf16[64,35,128]{2,1,0:T(8,128)(2,1)}), bf16[64,35,128]{2,1,0:T(8,128)(2,1)S(1)}, u32[]{:S(2)}, u32[]{:S(2)}) %all-to-all-start.1) | async-done | bytes 573472 | tf_op jit(solution)/shard_map/all_to_all | solution.py:55
  128.9 0.6 reshape.116
  129.5 0.6 convolution_convert_fusion.1.own_ref
  130.2 0.9 collective-permute-start.12
  131.1 5.2 %collective-permute-done.12.pair_ref = bf16[128,896]{1,0:T(8,128)(2,1)S(1)} collective-permute-done((bf16[128,896]{1,0:T(8,128)(2,1)S(1)}, bf16[128,896]{1,0:T(8,128)(2,1)S(1)}, u32[]{:S(2)}, u32[]{:S(2)}) %collective-permute-start.12) | collective-permute-done | bytes 229408 | tf_op jit(solution)/shard_map/ppermute | solution.py:34
  136.3 1.4 collective-permute-done.13.pair_far_ref
  137.8 2.3 %copy-done.7 = bf16[1792,1280]{1,0:T(8,128)(2,1)S(1)} copy-done((bf16[1792,1280]{1,0:T(8,128)(2,1)S(1)}, bf16[1792,1280]{1,0:T(8,128)(2,1)}, u32[]{:S(2)}) %copy-start.7) | copy-done | bytes 4587544
  140.1 2.3 %shard_map.142 = (bf16[128,1280]{1,0:T(8,128)(2,1)S(1)}, bf16[128,1280]{1,0:T(8,128)(2,1)S(1)}) custom-call(s32[3]{0:T(128)S(1)} %pad_add_fusion.order_ref, bf16[128,896]{1,0:T(8,128)(2,1)S(1)} %convolution_convert_fusion.1.own_ref, bf16[128,896]{1,0:T(8,128)(2,1)S(1)} %collective-permute-done.11.own_far_ref, ...), custom_call_target="tpu_custom_call" | custom-call | flops 100 | bytes 100 | tf_op jit(solution)/shard_map/pallas_call | solution.py:83
  142.4 0.7 collective-permute-start.14
  143.1 5.5 %collective-permute-start.15 = (bf16[128,1280]{1,0:T(8,128)(2,1)S(1)}, bf16[128,1280]{1,0:T(8,128)(2,1)S(1)}, u32[]{:S(2)}, u32[]{:S(2)}) collective-permute-start(bf16[128,1280]{1,0:T(8,128)(2,1)S(1)} %get-tuple-element.52), channel_id=1, source_target_pairs={{0,4},{1,5},{2,0},{3,1},{4,6},{5,7},{6,2},{7,3},{8,12},{9,13},{10,... | collective-permute-start | bytes 983048 | tf_op jit(solution)/shard_map/ppermute | solution.py:358
  148.6 7.4 %collective-permute-done.15.second_ref = bf16[128,1280]{1,0:T(8,128)(2,1)S(1)} collective-permute-done((bf16[128,1280]{1,0:T(8,128)(2,1)S(1)}, bf16[128,1280]{1,0:T(8,128)(2,1)S(1)}, u32[]{:S(2)}, u32[]{:S(2)}) %collective-permute-start.15) | collective-permute-done | bytes 327712 | tf_op jit(solution)/shard_map/ppermute | solution.py:358
  155.9 1.0 shard_map.143
  157.0 3.2 %collective-permute-start.17 = (f32[128,64]{1,0:T(8,128)S(1)}, f32[128,64]{1,0:T(8,128)S(1)}, u32[]{:S(2)}, u32[]{:S(2)}) collective-permute-start(f32[128,64]{1,0:T(8,128)S(1)} %get-tuple-element.56.own_ref), channel_id=1, source_target_pairs={{0,2},{2,0},{1,3},{3,1},{4,6},{6,4},{5,7},{7,5},{8,10},{10,8},{9,1... | collective-permute-start | bytes 98312 | tf_op jit(solution)/shard_map/ppermute | solution.py:34
  160.2 0.1 collective-permute-start.18
  160.4 2.6 %collective-permute-done.17.far_ref = f32[128,64]{1,0:T(8,128)S(1)} collective-permute-done((f32[128,64]{1,0:T(8,128)S(1)}, f32[128,64]{1,0:T(8,128)S(1)}, u32[]{:S(2)}, u32[]{:S(2)}) %collective-permute-start.17) | collective-permute-done | bytes 32800 | tf_op jit(solution)/shard_map/ppermute | solution.py:34
  163.0 2.8 %collective-permute-done.18.cross_ref = f32[128,64]{1,0:T(8,128)S(1)} collective-permute-done((f32[128,64]{1,0:T(8,128)S(1)}, f32[128,64]{1,0:T(8,128)S(1)}, u32[]{:S(2)}, u32[]{:S(2)}) %collective-permute-start.18) | collective-permute-done | bytes 32800 | tf_op jit(solution)/shard_map/ppermute | solution.py:386
  165.8 0.2 shard_map.144
  166.0 21.8 %all_to_all.20 = bf16[64,24,128]{2,1,0:T(8,128)(2,1)S(1)} all-to-all(bf16[64,24,128]{2,1,0:T(8,128)(2,1)S(1)} %shard_map.144), channel_id=1, replica_groups=mesh['yl'=2,'z'=8,'xh'=2,'xl'=2,'yh'=2,'c'=2] {'yl','z','xh','xl'}, dimensions={0} | all-to-all | bytes 786432 | tf_op jit(solution)/shard_map/all_to_all | solution.py:397
  187.9 0.8 broadcast_in_dim.2
  188.8 5.1 %all-to-all-start.3 = ((bf16[64,24,128]{2,1,0:T(8,128)(2,1)}), bf16[64,24,128]{2,1,0:T(8,128)(2,1)S(1)}, u32[]{:S(2)}, u32[]{:S(2)}) async-start(bf16[64,24,128]{2,1,0:T(8,128)(2,1)} %broadcast_in_dim.2), calls=%async_computation.3 | async-start | bytes 786432 | tf_op jit(solution)/shard_map/all_to_all | solution.py:400
  194.0 1.9 collective-permute-start.20
  195.9 1.5 collective-permute-start.21
  197.3 1.8 collective-permute-done.20
  199.2 1.2 collective-permute-done.21
  200.3 0.6 add_reduce_fusion
  201.6 7.5 %all-to-all-done.3 = bf16[64,24,128]{2,1,0:T(8,128)(2,1)S(1)} async-done(((bf16[64,24,128]{2,1,0:T(8,128)(2,1)}), bf16[64,24,128]{2,1,0:T(8,128)(2,1)S(1)}, u32[]{:S(2)}, u32[]{:S(2)}) %all-to-all-start.3) | async-done | bytes 393248 | tf_op jit(solution)/shard_map/all_to_all | solution.py:400
  209.2 0.7 convert_bitcast_fusion.1
  209.9 0.7 convert_bitcast_fusion
  (66 shorter events, 1.6 us)
Async XLA Ops:
  7.2 2.1 copy-start
  9.8 14.1 %copy-start.13 = (bf16[56,1280]{1,0:T(8,128)(2,1)S(1)}, bf16[56,1280]{1,0:T(8,128)(2,1)}, u32[]{:S(2)}) copy-start(bf16[56,1280]{1,0:T(8,128)(2,1)} %param.17) | copy-start | bytes 430084
  11.3 39.1 %all-to-all-start = ((bf16[64,35,128]{2,1,0:T(8,128)(2,1)}), bf16[64,35,128]{2,1,0:T(8,128)(2,1)S(1)}, u32[]{:S(2)}, u32[]{:S(2)}) async-start(bf16[64,35,128]{2,1,0:T(8,128)(2,1)} %reshape.112), calls=%async_computation | async-start | bytes 1310720 | tf_op jit(solution)/shard_map/all_to_all | solution.py:55
  23.9 105.6 %all-gather.2.cloned.1.call-start = ((), (), s32[]{:S(2)}) async-start(), calls=%async_computation.4 | async-start | bytes 5160960 | tf_op jit(solution)/shard_map/all_gather | solution.py:272
  23.9 4.9 %collective-permute-start = (bf16[56,1280]{1,0:T(8,128)(2,1)S(1)}, bf16[56,1280]{1,0:T(8,128)(2,1)S(1)}, u32[]{:S(2)}, u32[]{:S(2)}) collective-permute-start(bf16[56,1280]{1,0:T(8,128)(2,1)S(1)} %copy-done.13), channel_id=1, source_target_pairs={{0,0},{1,1},{2,4},{3,5},{4,128},{5,129},{6,132},{7,133},{8,8},{9,9... | collective-permute-start | bytes 430088 | tf_op jit(solution)/shard_map/ppermute | solution.py:268
  24.6 15.2 %collective-permute-start.1 = (bf16[56,1280]{1,0:T(8,128)(2,1)S(1)}, bf16[56,1280]{1,0:T(8,128)(2,1)S(1)}, u32[]{:S(2)}, u32[]{:S(2)}) collective-permute-start(bf16[56,1280]{1,0:T(8,128)(2,1)S(1)} %copy-done.13), channel_id=1, source_target_pairs={{0,128},{1,129},{2,132},{3,133},{4,0},{5,1},{6,4},{7,5},{8,136},{9... | collective-permute-start | bytes 430088 | tf_op jit(solution)/shard_map/ppermute | solution.py:268
  39.9 9.5 %collective-permute-start.2 = (bf16[112,1280]{1,0:T(8,128)(2,1)S(1)}, bf16[112,1280]{1,0:T(8,128)(2,1)S(1)}, u32[]{:S(2)}, u32[]{:S(2)}) collective-permute-start(bf16[112,1280]{1,0:T(8,128)(2,1)S(1)} %maximum_select_fusion.1), channel_id=1, source_target_pairs={{0,8},{8,0},{1,9},{9,1},{2,10},{10,2},{3,11},{11,3},{4,12},{12,4},... | collective-permute-start | bytes 860168 | tf_op jit(solution)/shard_map/ppermute | solution.py:34
  50.4 4.2 %copy-start.11 = (bf16[1280]{0:T(1024)(128)(2,1)S(1)}, bf16[1280]{0:T(1024)(128)(2,1)}, u32[]{:S(2)}) copy-start(bf16[1280]{0:T(1024)(128)(2,1)} %param.19) | copy-start | bytes 7684
  50.4 4.2 %copy-start.8 = (bf16[128,1280]{1,0:T(8,128)(2,1)S(1)}, bf16[128,1280]{1,0:T(8,128)(2,1)}, u32[]{:S(2)}) copy-start(bf16[128,1280]{1,0:T(8,128)(2,1)} %student_ref.3) | copy-start | bytes 983044
  50.4 4.2 %copy-start.10 = (bf16[1280,64]{0,1:T(8,128)(2,1)S(1)}, bf16[1280,64]{0,1:T(8,128)(2,1)}, u32[]{:S(2)}) copy-start(bf16[1280,64]{0,1:T(8,128)(2,1)} %param.20) | copy-start | bytes 491524
  51.0 5.1 %collective-permute-start.5 = (bf16[320,896]{1,0:T(8,128)(2,1)S(1)}, bf16[320,896]{1,0:T(8,128)(2,1)S(1)}, u32[]{:S(2)}, u32[]{:S(2)}) collective-permute-start(bf16[320,896]{1,0:T(8,128)(2,1)S(1)} %reshape.113.own_ref), channel_id=1, source_target_pairs={{0,1},{1,0},{2,3},{3,2},{4,5},{5,4},{6,7},{7,6},{8,9},{9,8},{10,11... | collective-permute-start | bytes 1720328 | tf_op jit(solution)/shard_map/ppermute | solution.py:34
  51.1 17.0 %collective-permute-start.3 = (bf16[320,896]{1,0:T(8,128)(2,1)S(1)}, bf16[320,896]{1,0:T(8,128)(2,1)S(1)}, u32[]{:S(2)}, u32[]{:S(2)}) collective-permute-start(bf16[320,896]{1,0:T(8,128)(2,1)S(1)} %reshape.113.own_ref), channel_id=1, source_target_pairs={{0,2},{2,0},{1,3},{3,1},{4,6},{6,4},{5,7},{7,5},{8,10},{10,8},{9,1... | collective-permute-start | bytes 1720328 | tf_op jit(solution)/shard_map/ppermute | solution.py:34
  54.8 1.3 collective-permute-start.4
  56.2 2.0 copy-start.1
  58.2 2.0 copy-start.3
  60.3 2.0 copy-start.5
  62.3 7.8 %copy-start.2 = (bf16[1,3584,512]{2,1,0:T(8,128)(2,1)S(1)}, bf16[1,3584,512]{2,1,0:T(8,128)(2,1)}, u32[]{:S(2)}) copy-start(bf16[1,3584,512]{2,1,0:T(8,128)(2,1)} %param.14) | copy-start | bytes 11010052
  62.3 7.8 %copy-start.4 = (bf16[1,3584,512]{2,1,0:T(8,128)(2,1)S(1)}, bf16[1,3584,512]{2,1,0:T(8,128)(2,1)}, u32[]{:S(2)}) copy-start(bf16[1,3584,512]{2,1,0:T(8,128)(2,1)} %param.15) | copy-start | bytes 11010052
  62.3 7.8 %copy-start.6 = (bf16[1,512,3584]{2,1,0:T(8,128)(2,1)S(1)}, bf16[1,512,3584]{2,1,0:T(8,128)(2,1)}, u32[]{:S(2)}) copy-start(bf16[1,512,3584]{2,1,0:T(8,128)(2,1)} %param.16) | copy-start | bytes 11010052
  68.1 2.0 collective-permute-start.6
  73.6 2.1 collective-permute-start.8
  73.8 5.5 %collective-permute-start.7 = (bf16[320,896]{1,0:T(8,128)(2,1)S(1)}, bf16[320,896]{1,0:T(8,128)(2,1)S(1)}, u32[]{:S(2)}, u32[]{:S(2)}) collective-permute-start(bf16[320,896]{1,0:T(8,128)(2,1)S(1)} %get-tuple-element.41), channel_id=1, source_target_pairs={{0,1},{1,0},{2,3},{3,2},{4,5},{5,4},{6,7},{7,6},{8,9},{9,8},{10,11... | collective-permute-start | bytes 1720328 | tf_op jit(solution)/shard_map/ppermute | solution.py:34
  75.8 16.8 %collective-permute-start.9 = (bf16[320,896]{1,0:T(8,128)(2,1)S(1)}, bf16[320,896]{1,0:T(8,128)(2,1)S(1)}, u32[]{:S(2)}, u32[]{:S(2)}) collective-permute-start(bf16[320,896]{1,0:T(8,128)(2,1)S(1)} %add_convert_fusion.1), channel_id=1, source_target_pairs={{0,2},{2,0},{1,3},{3,1},{4,6},{6,4},{5,7},{7,5},{8,10},{10,8},{9,1... | collective-permute-start | bytes 1720328 | tf_op jit(solution)/shard_map/ppermute | solution.py:34
  92.9 13.5 %copy-start.12 = (f32[128,2]{0,1:T(2,128)S(1)}, f32[128,2]{0,1:T(2,128)}, u32[]{:S(2)}) copy-start(f32[128,2]{0,1:T(2,128)} %param.13) | copy-start | bytes 3076
  94.3 19.0 %copy-start.9 = (bf16[64,1280]{1,0:T(8,128)(2,1)S(1)}, bf16[64,1280]{1,0:T(8,128)(2,1)}, u32[]{:S(2)}) copy-start(bf16[64,1280]{1,0:T(8,128)(2,1)} %up_ref.3) | copy-start | bytes 491524
  94.3 34.5 %all-to-all-start.1 = ((bf16[64,35,128]{2,1,0:T(8,128)(2,1)}), bf16[64,35,128]{2,1,0:T(8,128)(2,1)S(1)}, u32[]{:S(2)}, u32[]{:S(2)}) async-start(bf16[64,35,128]{2,1,0:T(8,128)(2,1)} %reshape.115), calls=%async_computation.1 | async-start | bytes 1310720 | tf_op jit(solution)/shard_map/all_to_all | solution.py:55
  106.7 6.6 %collective-permute-start.10 = (f32[128,128]{1,0:T(8,128)S(1)}, f32[128,128]{1,0:T(8,128)S(1)}, u32[]{:S(2)}, u32[]{:S(2)}) collective-permute-start(f32[128,128]{1,0:T(8,128)S(1)} %add.38), channel_id=1, source_target_pairs={{0,2},{2,0},{1,3},{3,1},{4,6},{6,4},{5,7},{7,5},{8,10},{10,8},{9,1... | collective-permute-start | bytes 196616 | tf_op jit(solution)/shard_map/ppermute | solution.py:34
  130.2 6.1 %collective-permute-start.12 = (bf16[128,896]{1,0:T(8,128)(2,1)S(1)}, bf16[128,896]{1,0:T(8,128)(2,1)S(1)}, u32[]{:S(2)}, u32[]{:S(2)}) collective-permute-start(bf16[128,896]{1,0:T(8,128)(2,1)S(1)} %convolution_convert_fusion.1.own_ref), channel_id=1, source_target_pairs={{0,4},{4,0},{1,5},{5,1},{2,6},{6,2},{3,7},{7,3},{8,12},{12,8},{9,1... | collective-permute-start | bytes 688136 | tf_op jit(solution)/shard_map/ppermute | solution.py:34
  131.1 5.2 %collective-permute-start.11 = (bf16[128,896]{1,0:T(8,128)(2,1)S(1)}, bf16[128,896]{1,0:T(8,128)(2,1)S(1)}, u32[]{:S(2)}, u32[]{:S(2)}) collective-permute-start(bf16[128,896]{1,0:T(8,128)(2,1)S(1)} %convolution_convert_fusion.1.own_ref), channel_id=1, source_target_pairs={{0,1},{1,0},{2,3},{3,2},{4,5},{5,4},{6,7},{7,6},{8,9},{9,8},{10,11... | collective-permute-start | bytes 688136 | tf_op jit(solution)/shard_map/ppermute | solution.py:34
  136.3 1.5 collective-permute-start.13
  137.8 2.3 %copy-start.7 = (bf16[1792,1280]{1,0:T(8,128)(2,1)S(1)}, bf16[1792,1280]{1,0:T(8,128)(2,1)}, u32[]{:S(2)}) copy-start(bf16[1792,1280]{1,0:T(8,128)(2,1)} %all-gather.2.cloned.1.call-done.block_ref) | copy-start | bytes 13762564
  142.4 6.2 %collective-permute-start.14 = (bf16[128,1280]{1,0:T(8,128)(2,1)S(1)}, bf16[128,1280]{1,0:T(8,128)(2,1)S(1)}, u32[]{:S(2)}, u32[]{:S(2)}) collective-permute-start(bf16[128,1280]{1,0:T(8,128)(2,1)S(1)} %get-tuple-element.51), channel_id=1, source_target_pairs={{0,0},{1,1},{2,4},{3,5},{4,2},{5,3},{6,6},{7,7},{8,8},{9,9},{10,12... | collective-permute-start | bytes 983048 | tf_op jit(solution)/shard_map/ppermute | solution.py:358
  143.1 12.9 %collective-permute-start.15 = (bf16[128,1280]{1,0:T(8,128)(2,1)S(1)}, bf16[128,1280]{1,0:T(8,128)(2,1)S(1)}, u32[]{:S(2)}, u32[]{:S(2)}) collective-permute-start(bf16[128,1280]{1,0:T(8,128)(2,1)S(1)} %get-tuple-element.52), channel_id=1, source_target_pairs={{0,4},{1,5},{2,0},{3,1},{4,6},{5,7},{6,2},{7,3},{8,12},{9,13},{10,... | collective-permute-start | bytes 983048 | tf_op jit(solution)/shard_map/ppermute | solution.py:358
  157.0 3.4 %collective-permute-start.16 = (f32[128,64]{1,0:T(8,128)S(1)}, f32[128,64]{1,0:T(8,128)S(1)}, u32[]{:S(2)}, u32[]{:S(2)}) collective-permute-start(f32[128,64]{1,0:T(8,128)S(1)} %get-tuple-element.56.own_ref), channel_id=1, source_target_pairs={{0,1},{1,0},{2,3},{3,2},{4,5},{5,4},{6,7},{7,6},{8,9},{9,8},{10,11... | collective-permute-start | bytes 98312 | tf_op jit(solution)/shard_map/ppermute | solution.py:34
  157.0 6.0 %collective-permute-start.17 = (f32[128,64]{1,0:T(8,128)S(1)}, f32[128,64]{1,0:T(8,128)S(1)}, u32[]{:S(2)}, u32[]{:S(2)}) collective-permute-start(f32[128,64]{1,0:T(8,128)S(1)} %get-tuple-element.56.own_ref), channel_id=1, source_target_pairs={{0,2},{2,0},{1,3},{3,1},{4,6},{6,4},{5,7},{7,5},{8,10},{10,8},{9,1... | collective-permute-start | bytes 98312 | tf_op jit(solution)/shard_map/ppermute | solution.py:34
  160.2 5.6 %collective-permute-start.18 = (f32[128,64]{1,0:T(8,128)S(1)}, f32[128,64]{1,0:T(8,128)S(1)}, u32[]{:S(2)}, u32[]{:S(2)}) collective-permute-start(f32[128,64]{1,0:T(8,128)S(1)} %get-tuple-element.56.own_ref), channel_id=1, source_target_pairs={{0,3},{1,2},{2,1},{3,0},{4,7},{5,6},{6,5},{7,4},{8,11},{9,10},{10,... | collective-permute-start | bytes 98312 | tf_op jit(solution)/shard_map/ppermute | solution.py:386
  188.8 20.3 %all-to-all-start.3 = ((bf16[64,24,128]{2,1,0:T(8,128)(2,1)}), bf16[64,24,128]{2,1,0:T(8,128)(2,1)S(1)}, u32[]{:S(2)}, u32[]{:S(2)}) async-start(bf16[64,24,128]{2,1,0:T(8,128)(2,1)} %broadcast_in_dim.2), calls=%async_computation.3 | async-start | bytes 786432 | tf_op jit(solution)/shard_map/all_to_all | solution.py:400
  193.9 3.5 %collective-permute-start.19 = (f32[1,128]{1,0:T(1,128)S(1)}, f32[1,128]{1,0:T(1,128)S(1)}, u32[]{:S(2)}, u32[]{:S(2)}) collective-permute-start(f32[1,128]{1,0:T(1,128)S(1)} %slice.34), channel_id=1, source_target_pairs={{0,1},{1,0},{2,3},{3,2},{4,5},{5,4},{6,7},{7,6},{8,9},{9,8},{10,11... | collective-permute-start | bytes 1544 | tf_op jit(solution)/shard_map/ppermute | solution.py:34
  194.0 5.2 %collective-permute-start.20 = (f32[1,128]{1,0:T(1,128)S(1)}, f32[1,128]{1,0:T(1,128)S(1)}, u32[]{:S(2)}, u32[]{:S(2)}) collective-permute-start(f32[1,128]{1,0:T(1,128)S(1)} %slice.34), channel_id=1, source_target_pairs={{0,2},{2,0},{1,3},{3,1},{4,6},{6,4},{5,7},{7,5},{8,10},{10,8},{9,1... | collective-permute-start | bytes 1544 | tf_op jit(solution)/shard_map/ppermute | solution.py:34
  195.9 4.5 %collective-permute-start.21 = (f32[1,128]{1,0:T(1,128)S(1)}, f32[1,128]{1,0:T(1,128)S(1)}, u32[]{:S(2)}, u32[]{:S(2)}) collective-permute-start(f32[1,128]{1,0:T(1,128)S(1)} %slice.34), channel_id=1, source_target_pairs={{0,3},{1,2},{2,1},{3,0},{4,7},{5,6},{6,5},{7,4},{8,11},{9,10},{10,... | collective-permute-start | bytes 1544 | tf_op jit(solution)/shard_map/ppermute | solution.py:42
Sparse Core Ops, SparseCore 0:
  51.1 61.6 all-gather.1

commit v9 on v8

--- a/solution.py
+++ b/solution.py
@@ -22,8 +22,8 @@
     return [(place, places.index(target(*here))) for place, here in enumerate(places)]
 
 
-def proj_target(step):
-    return lambda yl, z, xh, xl, yh, c: (xl ^ step, z, xh, yh, yl, c)
+def proj_target(yl, z, xh, xl, yh, c):
+    return (xl, z, xh, yh, yl, c)
 
 
 def home_target(step):
@@ -265,14 +265,13 @@
     outgoing, proj = lax.optimization_barrier((outgoing, proj))
     arrived = exchange_slots(outgoing)
 
-    blocks = [lax.ppermute(proj, ALL, permutation(proj_target(step))) for step in range(2)]
-    proj_rows = ordered(*blocks, yl)
-    proj_rows = ordered(proj_rows, swap(proj_rows, "xh"), xh)
+    proj_rows = lax.ppermute(proj, ALL, permutation(proj_target))
+    proj_rows = ordered(proj_rows, swap(proj_rows, "yl"), yl)
     arrived, proj_rows = lax.optimization_barrier((arrived, proj_rows))
-    proj_block = lax.all_gather(proj_rows, "z", axis=0, tiled=True)
 
     arrived_y = swap(arrived, "yh")
     arrived_c = swap(arrived, "c")
+    proj_rows = ordered(proj_rows, swap(proj_rows, "xh"), xh)
 
     gain = student_norm_weight.reshape(1, -1)
     stats = local_kernel(
@@ -294,9 +293,10 @@
         arrived_c,
         *expert_weights,
     )
-    arrived_y, stats, near_gate, near_up = lax.optimization_barrier(
-        (arrived_y, stats, near_gate, near_up)
-    )
+    arrived_y, stats, near_gate, near_up, proj_rows = lax.optimization_barrier(
+        (arrived_y, stats, near_gate, near_up, proj_rows)
+    )
+    proj_block = lax.all_gather(proj_rows, "z", axis=0, tiled=True)
     out_own, out_near, out_far, out_far_near = expert_call(
         expert_kernel,
         [jax.ShapeDtypeStruct(arrived.shape, jnp.bfloat16)] * 4,

time: 219 us -> 230 us (1.050)
  local copies, waits for them, and re-layouts: 15 us -> 22.3 us
  blocking collectives: 21.8 us -> 25.4 us
    ppermute x2 -> x1, waiting for transfers between devices: 11.1 us -> 0.01 us  [body(): proj_rows = lax.ppermute(proj, ALL, permutation(proj_target))]
    ppermute x16 -> x17, starting transfers between devices: 19.6 us -> 26 us  [swap(): return lax.ppermute(value, axis, [(0, 1), (1, 0)])]
    unnamed x29, local copies, waits for them, and re-layouts: 9.28 us -> 15.5 us
    all_to_all x2, waiting for transfers between devices: 15.3 us -> 21.3 us  [exchange_slots(): lax.all_to_all(rows, DP, split_axis=0, concat_axis=0, tiled=True)]
    ppermute x16 -> x17, waiting for transfers between devices: 42.6 us -> 48.3 us  [swap(): return lax.ppermute(value, axis, [(0, 1), (1, 0)])]
    all_to_all x2, starting transfers between devices: 24.6 us -> 19.8 us  [exchange_slots(): lax.all_to_all(rows, DP, split_axis=0, concat_axis=0, tiled=True)]
    ppermute x2 -> x1, starting transfers between devices: 4.85 us -> 0.8 us  [body(): proj_rows = lax.ppermute(proj, ALL, permutation(proj_target))]
    all_to_all x1, blocking collectives: 21.8 us -> 25.4 us  [body(): bundle = lax.all_to_all(bundle, DP, split_axis=0, concat_axis=0, tiled=True)]
  transfers between devices with their start and end apart: 26 -> 26, of which waited for: 17 -> 17; matrix products, arithmetic and copies ran while one was open for 2% -> 3% of each run, Pallas kernels for 3% -> 3%
where the time goes in v9:
time: 230 us; the launch traced here: 229 us
  waiting for transfers between devices  88.5 us (38%)
  starting transfers between devices  59.9 us (26%)
  blocking collectives  25.4 us (11%)
  local copies, waits for them, and re-layouts  22.3 us (10%)
  between operations  16.2 us (7%)
  Pallas kernels  10.3 us (4%)
  other arithmetic  4.52 us (2%)
    ppermute x17, waiting for transfers between devices, swap(): return lax.ppermute(value, axis, [(0, 1), (1, 0)])  48.3 us
    ppermute x17, starting transfers between devices, swap(): return lax.ppermute(value, axis, [(0, 1), (1, 0)])  26 us
    all_to_all x1, blocking collectives, body(): bundle = lax.all_to_all(bundle, DP, split_axis=0, concat_axis=0, tiled=True)  25.4 us
    all_to_all x2, waiting for transfers between devices, exchange_slots(): lax.all_to_all(rows, DP, split_axis=0, concat_axis=0, tiled=True)  21.3 us
    all_to_all x2, starting transfers between devices, exchange_slots(): lax.all_to_all(rows, DP, split_axis=0, concat_axis=0, tiled=True)  19.8 us
    unnamed x29, local copies, waits for them, and re-layouts  15.5 us
    ppermute x2, waiting for transfers between devices, body(): lax.ppermute(piece, ALL, permutation(home_target(step)))  7.69 us
    all_to_all x1, waiting for transfers between devices, body(): grads = lax.all_to_all(grads, DP, split_axis=0, concat_axis=0, tiled=True)  7.19 us
  transfers between devices with their start and end apart: 26, of which 17 were waited for; matrix products, arithmetic and copies ran while one was open for 3% of the time, Pallas kernels for 3%

profile of v9, /device:TPU:32, one launch (start us, length us, event | category | flops | bytes accessed | tf_op | source)
XLA Modules:
  0.0 228.7 jit_solution(5207340675065390101)
XLA Ops:
  7.2 0.8 copy.15
  8.3 0.6 reduce-window.6
  9.3 0.6 convolution_convert_fusion
  9.9 1.4 reshape.112
  11.3 12.6 %all-to-all-start = ((bf16[64,35,128]{2,1,0:T(8,128)(2,1)}), bf16[64,35,128]{2,1,0:T(8,128)(2,1)S(1)}, u32[]{:S(2)}, u32[]{:S(2)}) async-start(bf16[64,35,128]{2,1,0:T(8,128)(2,1)} %reshape.112), calls=%async_computation | async-start | bytes 1310720 | tf_op jit(solution)/shard_map/all_to_all | solution.py:55
  24.0 0.8 collective-permute-start
  24.8 11.9 %collective-permute-start.1 = (bf16[56,1280]{1,0:T(8,128)(2,1)S(1)}, bf16[56,1280]{1,0:T(8,128)(2,1)S(1)}, u32[]{:S(2)}, u32[]{:S(2)}) collective-permute-start(bf16[56,1280]{1,0:T(8,128)(2,1)S(1)} %collective-permute-done), channel_id=1, source_target_pairs={{0,128},{128,0},{1,129},{129,1},{2,130},{130,2},{3,131},{131,3},{4... | collective-permute-start | bytes 430088 | tf_op jit(solution)/shard_map/ppermute | solution.py:34
  36.7 4.3 %collective-permute-done.1 = bf16[56,1280]{1,0:T(8,128)(2,1)S(1)} collective-permute-done((bf16[56,1280]{1,0:T(8,128)(2,1)S(1)}, bf16[56,1280]{1,0:T(8,128)(2,1)S(1)}, u32[]{:S(2)}, u32[]{:S(2)}) %collective-permute-start.1) | collective-permute-done | bytes 143392 | tf_op jit(solution)/shard_map/ppermute | solution.py:34
  41.1 3.8 %all-to-all-done = bf16[64,35,128]{2,1,0:T(8,128)(2,1)S(1)} async-done(((bf16[64,35,128]{2,1,0:T(8,128)(2,1)}), bf16[64,35,128]{2,1,0:T(8,128)(2,1)S(1)}, u32[]{:S(2)}, u32[]{:S(2)}) %all-to-all-start) | async-done | bytes 573472 | tf_op jit(solution)/shard_map/all_to_all | solution.py:55
  44.8 0.6 reshape.113.own_ref
  45.5 3.0 %collective-permute-start.2 = (bf16[320,896]{1,0:T(8,128)(2,1)S(1)}, bf16[320,896]{1,0:T(8,128)(2,1)}, u32[]{:S(2)}, u32[]{:S(2)}) collective-permute-start(bf16[320,896]{1,0:T(8,128)(2,1)S(1)} %reshape.113.own_ref), channel_id=1, source_target_pairs={{0,2},{2,0},{1,3},{3,1},{4,6},{6,4},{5,7},{7,5},{8,10},{10,8},{9,1... | collective-permute-start | bytes 1720328 | tf_op jit(solution)/shard_map/ppermute | solution.py:34
  48.5 1.9 collective-permute-start.5
  50.5 0.2 shard_map.138
  50.9 1.2 collective-permute-done.3
  52.1 6.8 %collective-permute-done.5 = bf16[112,1280]{1,0:T(8,128)(2,1)S(1)} collective-permute-done((bf16[112,1280]{1,0:T(8,128)(2,1)S(1)}, bf16[112,1280]{1,0:T(8,128)(2,1)S(1)}, u32[]{:S(2)}, u32[]{:S(2)}) %collective-permute-start.5) | collective-permute-done | bytes 286752 | tf_op jit(solution)/shard_map/ppermute | solution.py:34
  58.9 0.9 maximum_select_fusion
  59.8 2.0 copy-done.1
  61.9 2.0 copy-done.3
  63.9 2.0 copy-done.5
  66.0 2.1 shard_map.139
  68.2 2.2 collective-permute-done.6.other_ref
  70.4 2.0 copy-done.2
  72.4 2.0 copy-done.4
  74.4 2.2 copy-done.6
  76.6 4.1 %shard_map.140 = (bf16[320,896]{1,0:T(8,128)(2,1)S(1)}, bf16[320,896]{1,0:T(8,128)(2,1)S(1)}, bf16[320,896]{1,0:T(8,128)(2,1)S(1)}, bf16[320,896]{1,0:T(8,128)(2,1)S(1)}) custom-call(s32[2]{0:T(128)S(1)} %pad_add_fusion.1.place_ref, f32[320,512]{1,0:T(8,128)S(1)} %get-tuple-element.39.gate_near_ref, f32[320,512]{1,0:T(8,128)S(1)} %get-tuple-element.40.up_near_ref, ...), custom_call_target="tpu_custom_call" | custom-call | flops 100 | bytes 100 | tf_op jit(solution)/shard_map/pallas_call | solution.py:215
  80.7 0.2 collective-permute-start.8
  80.9 0.3 collective-permute-start.7
  81.3 1.5 collective-permute-done.8
  82.9 0.8 collective-permute-start.9
  83.7 16.1 %collective-permute-done.9 = bf16[320,896]{1,0:T(8,128)(2,1)S(1)} collective-permute-done((bf16[320,896]{1,0:T(8,128)(2,1)S(1)}, bf16[320,896]{1,0:T(8,128)(2,1)S(1)}, u32[]{:S(2)}, u32[]{:S(2)}) %collective-permute-start.9) | collective-permute-done | bytes 573472 | tf_op jit(solution)/shard_map/ppermute | solution.py:34
  100.0 1.4 reshape.115
  101.4 7.2 %all-to-all-start.1 = ((bf16[64,35,128]{2,1,0:T(8,128)(2,1)}), bf16[64,35,128]{2,1,0:T(8,128)(2,1)}, u32[]{:S(2)}, u32[]{:S(2)}) async-start(bf16[64,35,128]{2,1,0:T(8,128)(2,1)} %reshape.115), calls=%async_computation.1 | async-start | bytes 1310720 | tf_op jit(solution)/shard_map/all_to_all | solution.py:55
  108.9 1.0 collective-permute-start.10
  109.9 0.4 fusion
  110.2 5.5 %collective-permute-done.10 = f32[128,128]{1,0:T(8,128)S(1)} collective-permute-done((f32[128,128]{1,0:T(8,128)S(1)}, f32[128,128]{1,0:T(8,128)S(1)}, u32[]{:S(2)}, u32[]{:S(2)}) %collective-permute-start.10) | collective-permute-done | bytes 65568 | tf_op jit(solution)/shard_map/ppermute | solution.py:34
  115.7 0.3 shard_map.141
  116.1 17.6 %all-to-all-done.1 = bf16[64,35,128]{2,1,0:T(8,128)(2,1)} async-done(((bf16[64,35,128]{2,1,0:T(8,128)(2,1)}), bf16[64,35,128]{2,1,0:T(8,128)(2,1)}, u32[]{:S(2)}, u32[]{:S(2)}) %all-to-all-start.1) | async-done | bytes 573472 | tf_op jit(solution)/shard_map/all_to_all | solution.py:55
  133.6 1.7 reshape.116
  135.4 0.6 convolution_convert_fusion.1.own_ref
  136.0 1.3 collective-permute-start.12
  137.4 5.0 %collective-permute-done.12.pair_ref = bf16[128,896]{1,0:T(8,128)(2,1)S(1)} collective-permute-done((bf16[128,896]{1,0:T(8,128)(2,1)S(1)}, bf16[128,896]{1,0:T(8,128)(2,1)S(1)}, u32[]{:S(2)}, u32[]{:S(2)}) %collective-permute-start.12) | collective-permute-done | bytes 229408 | tf_op jit(solution)/shard_map/ppermute | solution.py:34
  142.4 1.4 collective-permute-done.13.pair_far_ref
  143.8 2.3 %copy-done.7 = bf16[1792,1280]{1,0:T(8,128)(2,1)S(1)} copy-done((bf16[1792,1280]{1,0:T(8,128)(2,1)S(1)}, bf16[1792,1280]{1,0:T(8,128)(2,1)}, u32[]{:S(2)}) %copy-start.7) | copy-done | bytes 4587544
  146.1 2.4 %shard_map.142 = (bf16[128,1280]{1,0:T(8,128)(2,1)S(1)}, bf16[128,1280]{1,0:T(8,128)(2,1)S(1)}) custom-call(s32[3]{0:T(128)S(1)} %pad_add_fusion.order_ref, bf16[128,896]{1,0:T(8,128)(2,1)S(1)} %convolution_convert_fusion.1.own_ref, bf16[128,896]{1,0:T(8,128)(2,1)S(1)} %collective-permute-done.11.own_far_ref, ...), custom_call_target="tpu_custom_call" | custom-call | flops 100 | bytes 100 | tf_op jit(solution)/shard_map/pallas_call | solution.py:83
  148.5 0.7 collective-permute-start.14
  149.2 5.9 %collective-permute-start.15 = (bf16[128,1280]{1,0:T(8,128)(2,1)S(1)}, bf16[128,1280]{1,0:T(8,128)(2,1)S(1)}, u32[]{:S(2)}, u32[]{:S(2)}) collective-permute-start(bf16[128,1280]{1,0:T(8,128)(2,1)S(1)} %get-tuple-element.54), channel_id=1, source_target_pairs={{0,4},{1,5},{2,0},{3,1},{4,6},{5,7},{6,2},{7,3},{8,12},{9,13},{10,... | collective-permute-start | bytes 983048 | tf_op jit(solution)/shard_map/ppermute | solution.py:358
  155.1 7.7 %collective-permute-done.15.second_ref = bf16[128,1280]{1,0:T(8,128)(2,1)S(1)} collective-permute-done((bf16[128,1280]{1,0:T(8,128)(2,1)S(1)}, bf16[128,1280]{1,0:T(8,128)(2,1)S(1)}, u32[]{:S(2)}, u32[]{:S(2)}) %collective-permute-start.15) | collective-permute-done | bytes 327712 | tf_op jit(solution)/shard_map/ppermute | solution.py:358
  162.8 1.0 shard_map.143
  163.8 2.9 %collective-permute-start.17 = (f32[128,64]{1,0:T(8,128)S(1)}, f32[128,64]{1,0:T(8,128)S(1)}, u32[]{:S(2)}, u32[]{:S(2)}) collective-permute-start(f32[128,64]{1,0:T(8,128)S(1)} %get-tuple-element.58.own_ref), channel_id=1, source_target_pairs={{0,2},{2,0},{1,3},{3,1},{4,6},{6,4},{5,7},{7,5},{8,10},{10,8},{9,1... | collective-permute-start | bytes 98312 | tf_op jit(solution)/shard_map/ppermute | solution.py:34
  166.7 0.5 collective-permute-start.18
  167.2 2.6 %collective-permute-done.17.far_ref = f32[128,64]{1,0:T(8,128)S(1)} collective-permute-done((f32[128,64]{1,0:T(8,128)S(1)}, f32[128,64]{1,0:T(8,128)S(1)}, u32[]{:S(2)}, u32[]{:S(2)}) %collective-permute-start.17) | collective-permute-done | bytes 32800 | tf_op jit(solution)/shard_map/ppermute | solution.py:34
  169.8 2.5 %collective-permute-done.18.cross_ref = f32[128,64]{1,0:T(8,128)S(1)} collective-permute-done((f32[128,64]{1,0:T(8,128)S(1)}, f32[128,64]{1,0:T(8,128)S(1)}, u32[]{:S(2)}, u32[]{:S(2)}) %collective-permute-start.18) | collective-permute-done | bytes 32800 | tf_op jit(solution)/shard_map/ppermute | solution.py:386
  172.3 0.2 shard_map.144
  172.5 25.4 %all_to_all.20 = bf16[64,24,128]{2,1,0:T(8,128)(2,1)S(1)} all-to-all(bf16[64,24,128]{2,1,0:T(8,128)(2,1)S(1)} %shard_map.144), channel_id=1, replica_groups=mesh['yl'=2,'z'=8,'xh'=2,'xl'=2,'yh'=2,'c'=2] {'yl','z','xh','xl'}, dimensions={0} | all-to-all | bytes 786432 | tf_op jit(solution)/shard_map/all_to_all | solution.py:397
  198.0 0.8 broadcast_in_dim.2
  198.8 5.1 %all-to-all-start.3 = ((bf16[64,24,128]{2,1,0:T(8,128)(2,1)}), bf16[64,24,128]{2,1,0:T(8,128)(2,1)S(1)}, u32[]{:S(2)}, u32[]{:S(2)}) async-start(bf16[64,24,128]{2,1,0:T(8,128)(2,1)} %broadcast_in_dim.2), calls=%async_computation.3 | async-start | bytes 786432 | tf_op jit(solution)/shard_map/all_to_all | solution.py:400
  204.0 2.2 collective-permute-start.20
  206.2 1.2 collective-permute-start.21
  207.4 1.8 collective-permute-done.20
  209.2 1.5 collective-permute-done.21
  210.7 0.6 add_reduce_fusion
  212.0 7.2 %all-to-all-done.3 = bf16[64,24,128]{2,1,0:T(8,128)(2,1)S(1)} async-done(((bf16[64,24,128]{2,1,0:T(8,128)(2,1)}), bf16[64,24,128]{2,1,0:T(8,128)(2,1)S(1)}, u32[]{:S(2)}, u32[]{:S(2)}) %all-to-all-start.3) | async-done | bytes 393248 | tf_op jit(solution)/shard_map/all_to_all | solution.py:400
  219.2 0.7 convert_bitcast_fusion.1
  220.0 0.7 convert_bitcast_fusion
  (66 shorter events, 2.2 us)
Async XLA Ops:
  7.2 2.1 copy-start
  9.8 14.1 %copy-start.13 = (bf16[56,1280]{1,0:T(8,128)(2,1)S(1)}, bf16[56,1280]{1,0:T(8,128)(2,1)}, u32[]{:S(2)}) copy-start(bf16[56,1280]{1,0:T(8,128)(2,1)} %param.17) | copy-start | bytes 430084
  11.3 33.5 %all-to-all-start = ((bf16[64,35,128]{2,1,0:T(8,128)(2,1)}), bf16[64,35,128]{2,1,0:T(8,128)(2,1)S(1)}, u32[]{:S(2)}, u32[]{:S(2)}) async-start(bf16[64,35,128]{2,1,0:T(8,128)(2,1)} %reshape.112), calls=%async_computation | async-start | bytes 1310720 | tf_op jit(solution)/shard_map/all_to_all | solution.py:55
  23.9 26.6 %copy-start.11 = (bf16[1280]{0:T(1024)(128)(2,1)S(1)}, bf16[1280]{0:T(1024)(128)(2,1)}, u32[]{:S(2)}) copy-start(bf16[1280]{0:T(1024)(128)(2,1)} %param.19) | copy-start | bytes 7684
  23.9 26.6 %copy-start.8 = (bf16[128,1280]{1,0:T(8,128)(2,1)S(1)}, bf16[128,1280]{1,0:T(8,128)(2,1)}, u32[]{:S(2)}) copy-start(bf16[128,1280]{1,0:T(8,128)(2,1)} %student_ref.3) | copy-start | bytes 983044
  23.9 26.6 %copy-start.10 = (bf16[1280,64]{0,1:T(8,128)(2,1)S(1)}, bf16[1280,64]{0,1:T(8,128)(2,1)}, u32[]{:S(2)}) copy-start(bf16[1280,64]{0,1:T(8,128)(2,1)} %param.20) | copy-start | bytes 491524
  23.9 111.5 %all-gather.2.cloned.1.call-start = ((), (), s32[]{:S(2)}) async-start(), calls=%async_computation.4 | async-start | bytes 5160960 | tf_op jit(solution)/shard_map/all_gather | solution.py:299
  24.0 0.8 collective-permute-start
  24.8 16.2 %collective-permute-start.1 = (bf16[56,1280]{1,0:T(8,128)(2,1)S(1)}, bf16[56,1280]{1,0:T(8,128)(2,1)S(1)}, u32[]{:S(2)}, u32[]{:S(2)}) collective-permute-start(bf16[56,1280]{1,0:T(8,128)(2,1)S(1)} %collective-permute-done), channel_id=1, source_target_pairs={{0,128},{128,0},{1,129},{129,1},{2,130},{130,2},{3,131},{131,3},{4... | collective-permute-start | bytes 430088 | tf_op jit(solution)/shard_map/ppermute | solution.py:34
  45.4 14.4 %collective-permute-start.4 = (bf16[320,896]{1,0:T(8,128)(2,1)S(1)}, bf16[320,896]{1,0:T(8,128)(2,1)S(1)}, u32[]{:S(2)}, u32[]{:S(2)}) collective-permute-start(bf16[320,896]{1,0:T(8,128)(2,1)S(1)} %reshape.113.own_ref), channel_id=1, source_target_pairs={{0,1},{1,0},{2,3},{3,2},{4,5},{5,4},{6,7},{7,6},{8,9},{9,8},{10,11... | collective-permute-start | bytes 1720328 | tf_op jit(solution)/shard_map/ppermute | solution.py:34
  45.5 22.5 %collective-permute-start.2 = (bf16[320,896]{1,0:T(8,128)(2,1)S(1)}, bf16[320,896]{1,0:T(8,128)(2,1)}, u32[]{:S(2)}, u32[]{:S(2)}) collective-permute-start(bf16[320,896]{1,0:T(8,128)(2,1)S(1)} %reshape.113.own_ref), channel_id=1, source_target_pairs={{0,2},{2,0},{1,3},{3,1},{4,6},{6,4},{5,7},{7,5},{8,10},{10,8},{9,1... | collective-permute-start | bytes 1720328 | tf_op jit(solution)/shard_map/ppermute | solution.py:34
  48.5 10.4 %collective-permute-start.5 = (bf16[112,1280]{1,0:T(8,128)(2,1)S(1)}, bf16[112,1280]{1,0:T(8,128)(2,1)S(1)}, u32[]{:S(2)}, u32[]{:S(2)}) collective-permute-start(bf16[112,1280]{1,0:T(8,128)(2,1)S(1)} %maximum_select_fusion.1), channel_id=1, source_target_pairs={{0,8},{8,0},{1,9},{9,1},{2,10},{10,2},{3,11},{11,3},{4,12},{12,4},... | collective-permute-start | bytes 860168 | tf_op jit(solution)/shard_map/ppermute | solution.py:34
  50.8 1.3 collective-permute-start.3
  59.8 2.0 copy-start.1
  61.9 2.0 copy-start.3
  63.9 2.0 copy-start.5
  68.1 2.3 collective-permute-start.6
  70.3 2.0 copy-start.2
  72.4 2.0 copy-start.4
  74.4 2.2 copy-start.6
  80.7 2.1 collective-permute-start.8
  80.9 2.7 %collective-permute-start.7 = (bf16[320,896]{1,0:T(8,128)(2,1)S(1)}, bf16[320,896]{1,0:T(8,128)(2,1)S(1)}, u32[]{:S(2)}, u32[]{:S(2)}) collective-permute-start(bf16[320,896]{1,0:T(8,128)(2,1)S(1)} %get-tuple-element.43), channel_id=1, source_target_pairs={{0,1},{1,0},{2,3},{3,2},{4,5},{5,4},{6,7},{7,6},{8,9},{9,8},{10,11... | collective-permute-start | bytes 1720328 | tf_op jit(solution)/shard_map/ppermute | solution.py:34
  82.9 16.8 %collective-permute-start.9 = (bf16[320,896]{1,0:T(8,128)(2,1)S(1)}, bf16[320,896]{1,0:T(8,128)(2,1)S(1)}, u32[]{:S(2)}, u32[]{:S(2)}) collective-permute-start(bf16[320,896]{1,0:T(8,128)(2,1)S(1)} %add_convert_fusion.1), channel_id=1, source_target_pairs={{0,2},{2,0},{1,3},{3,1},{4,6},{6,4},{5,7},{7,5},{8,10},{10,8},{9,1... | collective-permute-start | bytes 1720328 | tf_op jit(solution)/shard_map/ppermute | solution.py:34
  100.0 8.6 %copy-start.12 = (f32[128,2]{0,1:T(2,128)S(1)}, f32[128,2]{0,1:T(2,128)}, u32[]{:S(2)}) copy-start(f32[128,2]{0,1:T(2,128)} %param.13) | copy-start | bytes 3076
  101.4 14.3 %copy-start.9 = (bf16[64,1280]{1,0:T(8,128)(2,1)S(1)}, bf16[64,1280]{1,0:T(8,128)(2,1)}, u32[]{:S(2)}) copy-start(bf16[64,1280]{1,0:T(8,128)(2,1)} %up_ref.3) | copy-start | bytes 491524
  101.4 32.2 %all-to-all-start.1 = ((bf16[64,35,128]{2,1,0:T(8,128)(2,1)}), bf16[64,35,128]{2,1,0:T(8,128)(2,1)}, u32[]{:S(2)}, u32[]{:S(2)}) async-start(bf16[64,35,128]{2,1,0:T(8,128)(2,1)} %reshape.115), calls=%async_computation.1 | async-start | bytes 1310720 | tf_op jit(solution)/shard_map/all_to_all | solution.py:55
  108.9 6.8 %collective-permute-start.10 = (f32[128,128]{1,0:T(8,128)S(1)}, f32[128,128]{1,0:T(8,128)S(1)}, u32[]{:S(2)}, u32[]{:S(2)}) collective-permute-start(f32[128,128]{1,0:T(8,128)S(1)} %add.38), channel_id=1, source_target_pairs={{0,2},{2,0},{1,3},{3,1},{4,6},{6,4},{5,7},{7,5},{8,10},{10,8},{9,1... | collective-permute-start | bytes 196616 | tf_op jit(solution)/shard_map/ppermute | solution.py:34
  136.0 6.3 %collective-permute-start.12 = (bf16[128,896]{1,0:T(8,128)(2,1)S(1)}, bf16[128,896]{1,0:T(8,128)(2,1)S(1)}, u32[]{:S(2)}, u32[]{:S(2)}) collective-permute-start(bf16[128,896]{1,0:T(8,128)(2,1)S(1)} %convolution_convert_fusion.1.own_ref), channel_id=1, source_target_pairs={{0,4},{4,0},{1,5},{5,1},{2,6},{6,2},{3,7},{7,3},{8,12},{12,8},{9,1... | collective-permute-start | bytes 688136 | tf_op jit(solution)/shard_map/ppermute | solution.py:34
  137.4 5.1 %collective-permute-start.11 = (bf16[128,896]{1,0:T(8,128)(2,1)S(1)}, bf16[128,896]{1,0:T(8,128)(2,1)S(1)}, u32[]{:S(2)}, u32[]{:S(2)}) collective-permute-start(bf16[128,896]{1,0:T(8,128)(2,1)S(1)} %convolution_convert_fusion.1.own_ref), channel_id=1, source_target_pairs={{0,1},{1,0},{2,3},{3,2},{4,5},{5,4},{6,7},{7,6},{8,9},{9,8},{10,11... | collective-permute-start | bytes 688136 | tf_op jit(solution)/shard_map/ppermute | solution.py:34
  142.4 1.5 collective-permute-start.13
  143.8 2.3 %copy-start.7 = (bf16[1792,1280]{1,0:T(8,128)(2,1)S(1)}, bf16[1792,1280]{1,0:T(8,128)(2,1)}, u32[]{:S(2)}) copy-start(bf16[1792,1280]{1,0:T(8,128)(2,1)} %all-gather.2.cloned.1.call-done.block_ref) | copy-start | bytes 13762564
  148.5 6.6 %collective-permute-start.14 = (bf16[128,1280]{1,0:T(8,128)(2,1)S(1)}, bf16[128,1280]{1,0:T(8,128)(2,1)S(1)}, u32[]{:S(2)}, u32[]{:S(2)}) collective-permute-start(bf16[128,1280]{1,0:T(8,128)(2,1)S(1)} %get-tuple-element.53), channel_id=1, source_target_pairs={{0,0},{1,1},{2,4},{3,5},{4,2},{5,3},{6,6},{7,7},{8,8},{9,9},{10,12... | collective-permute-start | bytes 983048 | tf_op jit(solution)/shard_map/ppermute | solution.py:358
  149.2 13.6 %collective-permute-start.15 = (bf16[128,1280]{1,0:T(8,128)(2,1)S(1)}, bf16[128,1280]{1,0:T(8,128)(2,1)S(1)}, u32[]{:S(2)}, u32[]{:S(2)}) collective-permute-start(bf16[128,1280]{1,0:T(8,128)(2,1)S(1)} %get-tuple-element.54), channel_id=1, source_target_pairs={{0,4},{1,5},{2,0},{3,1},{4,6},{5,7},{6,2},{7,3},{8,12},{9,13},{10,... | collective-permute-start | bytes 983048 | tf_op jit(solution)/shard_map/ppermute | solution.py:358
  163.8 3.4 %collective-permute-start.16 = (f32[128,64]{1,0:T(8,128)S(1)}, f32[128,64]{1,0:T(8,128)S(1)}, u32[]{:S(2)}, u32[]{:S(2)}) collective-permute-start(f32[128,64]{1,0:T(8,128)S(1)} %get-tuple-element.58.own_ref), channel_id=1, source_target_pairs={{0,1},{1,0},{2,3},{3,2},{4,5},{5,4},{6,7},{7,6},{8,9},{9,8},{10,11... | collective-permute-start | bytes 98312 | tf_op jit(solution)/shard_map/ppermute | solution.py:34
  163.8 6.0 %collective-permute-start.17 = (f32[128,64]{1,0:T(8,128)S(1)}, f32[128,64]{1,0:T(8,128)S(1)}, u32[]{:S(2)}, u32[]{:S(2)}) collective-permute-start(f32[128,64]{1,0:T(8,128)S(1)} %get-tuple-element.58.own_ref), channel_id=1, source_target_pairs={{0,2},{2,0},{1,3},{3,1},{4,6},{6,4},{5,7},{7,5},{8,10},{10,8},{9,1... | collective-permute-start | bytes 98312 | tf_op jit(solution)/shard_map/ppermute | solution.py:34
  166.7 5.6 %collective-permute-start.18 = (f32[128,64]{1,0:T(8,128)S(1)}, f32[128,64]{1,0:T(8,128)S(1)}, u32[]{:S(2)}, u32[]{:S(2)}) collective-permute-start(f32[128,64]{1,0:T(8,128)S(1)} %get-tuple-element.58.own_ref), channel_id=1, source_target_pairs={{0,3},{1,2},{2,1},{3,0},{4,7},{5,6},{6,5},{7,4},{8,11},{9,10},{10,... | collective-permute-start | bytes 98312 | tf_op jit(solution)/shard_map/ppermute | solution.py:386
  198.8 20.3 %all-to-all-start.3 = ((bf16[64,24,128]{2,1,0:T(8,128)(2,1)}), bf16[64,24,128]{2,1,0:T(8,128)(2,1)S(1)}, u32[]{:S(2)}, u32[]{:S(2)}) async-start(bf16[64,24,128]{2,1,0:T(8,128)(2,1)} %broadcast_in_dim.2), calls=%async_computation.3 | async-start | bytes 786432 | tf_op jit(solution)/shard_map/all_to_all | solution.py:400
  203.9 3.5 %collective-permute-start.19 = (f32[1,128]{1,0:T(1,128)S(1)}, f32[1,128]{1,0:T(1,128)S(1)}, u32[]{:S(2)}, u32[]{:S(2)}) collective-permute-start(f32[1,128]{1,0:T(1,128)S(1)} %slice.34), channel_id=1, source_target_pairs={{0,1},{1,0},{2,3},{3,2},{4,5},{5,4},{6,7},{7,6},{8,9},{9,8},{10,11... | collective-permute-start | bytes 1544 | tf_op jit(solution)/shard_map/ppermute | solution.py:34
  204.0 5.1 %collective-permute-start.20 = (f32[1,128]{1,0:T(1,128)S(1)}, f32[1,128]{1,0:T(1,128)S(1)}, u32[]{:S(2)}, u32[]{:S(2)}) collective-permute-start(f32[1,128]{1,0:T(1,128)S(1)} %slice.34), channel_id=1, source_target_pairs={{0,2},{2,0},{1,3},{3,1},{4,6},{6,4},{5,7},{7,5},{8,10},{10,8},{9,1... | collective-permute-start | bytes 1544 | tf_op jit(solution)/shard_map/ppermute | solution.py:34
  206.2 4.5 %collective-permute-start.21 = (f32[1,128]{1,0:T(1,128)S(1)}, f32[1,128]{1,0:T(1,128)S(1)}, u32[]{:S(2)}, u32[]{:S(2)}) collective-permute-start(f32[1,128]{1,0:T(1,128)S(1)} %slice.34), channel_id=1, source_target_pairs={{0,3},{1,2},{2,1},{3,0},{4,7},{5,6},{6,5},{7,4},{8,11},{9,10},{10,... | collective-permute-start | bytes 1544 | tf_op jit(solution)/shard_map/ppermute | solution.py:42
Sparse Core Ops, SparseCore 0:
  68.2 66.0 all-gather.1

commit v10 on v4

--- a/solution.py
+++ b/solution.py
@@ -132,13 +132,66 @@
     out_ref[...] = student + adapter_scale_factor * dot(low, up_ref[...])
 
 
-def local_kernel(kernel, shapes, *args):
+def home_kernel(
+    scale, first_ref, second_ref, student_ref, low_ref, up_ref, target_ref, back_ref, grad_ref, loss_ref
+):
+    target = first_ref[...].astype(jnp.float32) + second_ref[...].astype(jnp.float32)
+    target_ref[...] = target
+    diff = student_ref[...] - target
+    scaled = (diff * scale).astype(jnp.bfloat16)
+    back_ref[...] = lax.dot_general(
+        scaled, up_ref[...], (((1,), (1,)), ((), ())), preferred_element_type=jnp.float32
+    )
+    grad_ref[...] = adapter_scale_factor * lax.dot_general(
+        low_ref[...], scaled, (((0,), (0,)), ((), ())), preferred_element_type=jnp.float32
+    )
+    total = jnp.sum(jnp.sum(diff * diff, axis=0, keepdims=True), axis=1, keepdims=True)
+    loss_ref[...] = jnp.broadcast_to(total, loss_ref.shape)
+
+
+def bundle_kernel(own_ref, core_ref, far_ref, cross_ref, normed_ref, grad_ref, loss_ref, out_ref, down_ref):
+    back = (own_ref[...] + core_ref[...]) + (far_ref[...] + cross_ref[...])
+    down_ref[...] = lax.dot_general(
+        (adapter_scale_factor * back).astype(jnp.bfloat16),
+        normed_ref[...],
+        (((0,), (0,)), ((), ())),
+        preferred_element_type=jnp.float32,
+    )
+    total = loss_ref[...]
+    lane = lax.broadcasted_iota(jnp.int32, total.shape, 1)
+    row = lax.broadcasted_iota(jnp.int32, total.shape, 0)
+    first = total.astype(jnp.bfloat16).astype(jnp.float32)
+    second = (total - first).astype(jnp.bfloat16).astype(jnp.float32)
+    third = total - first - second
+    loss = jnp.where(
+        lane == 0, first, jnp.where(lane == 1, second, jnp.where(lane == 2, third, 0.0))
+    )
+    across = down_ref.shape[1] // 128
+    tiles = down_ref.shape[0] // 8 * across
+
+    def tile(number):
+        ref = grad_ref if number < tiles else down_ref
+        high, wide = divmod(number % tiles, across)
+        return ref[high * 8 : high * 8 + 8, wide * 128 : wide * 128 + 128]
+
+    count = out_ref.shape[0]
+    for index in range(count):
+        half = tile(2 * count + index // 2)
+        if index % 2:
+            half = pltpu.roll(half, 4, 0)
+        last = jnp.where(row < 4, half, loss)
+        whole = jnp.concatenate([tile(2 * index), tile(2 * index + 1), last])
+        out_ref[index] = whole.astype(jnp.bfloat16)
+
+
+def local_kernel(kernel, shapes, *args, scratch=()):
     vmem = pl.BlockSpec(memory_space=pltpu.VMEM)
     return pl.pallas_call(
         kernel,
         out_shape=shapes,
         in_specs=[vmem] * len(args),
         out_specs=jax.tree.map(lambda _: vmem, shapes),
+        scratch_shapes=scratch,
         compiler_params=pltpu.CompilerParams(vmem_limit_bytes=16 * 1024 * 1024),
         cost_estimate=pl.CostEstimate(flops=100, bytes_accessed=100, transcendentals=0),
     )(*args)
@@ -279,54 +332,45 @@
     order = jnp.stack([yh ^ xl, yh ^ xl ^ 1, core])
     pieces = product_pieces(order, teacher, teacher_far, pair, swap(pair, "c"), proj_block)
     pieces = [
-        lax.ppermute(piece, ALL, permutation(home_target(step))).astype(jnp.float32)
+        lax.ppermute(piece, ALL, permutation(home_target(step)))
         for step, piece in enumerate(pieces)
     ]
-    target = pieces[0] + pieces[1]
-
-    output_difference = student_out - target
     tokens_all = tok_rows * experts
-    scale = 1.0 / math.sqrt(tokens_all)
-    scaled = (output_difference * scale).astype(jnp.bfloat16)
-    loss_here = jnp.sum(output_difference * output_difference)
-    back_part = lax.dot_general(
-        scaled, adapter_up_matrix, (((1,), (1,)), ((), ())), preferred_element_type=jnp.float32
-    )
-    back_low = (adapter_scale_factor * mp_sum(back_part)).astype(jnp.bfloat16)
-    over_tokens = (((0,), (0,)), ((), ()))
-    up_part = adapter_scale_factor * lax.dot_general(
-        lowrank, scaled, over_tokens, preferred_element_type=jnp.float32
-    )
-    down_part = lax.dot_general(back_low, normed, over_tokens, preferred_element_type=jnp.float32)
+    columns = adapter_up_matrix.shape[1]
+    target, back, up_part, loss_here = local_kernel(
+        functools.partial(home_kernel, 1.0 / math.sqrt(tokens_all)),
+        [
+            jax.ShapeDtypeStruct((tok_rows, columns), jnp.float32),
+            jax.ShapeDtypeStruct((tok_rows, rank), jnp.float32),
+            jax.ShapeDtypeStruct((rank, columns), jnp.float32),
+            jax.ShapeDtypeStruct((8, 128), jnp.float32),
+        ],
+        *pieces,
+        student_out,
+        lowrank,
+        adapter_up_matrix,
+    )
 
     lanes = 128
-    columns = up_part.shape[1]
     tiles = rank // 8 * (columns // lanes)
-    first = lax.reduce_precision(loss_here, 8, 7)
-    second = lax.reduce_precision(loss_here - first, 8, 7)
-    third = loss_here - first - second
-    lane = jnp.arange(lanes)
-    loss_row = jnp.where(
-        lane == 0, first, jnp.where(lane == 1, second, jnp.where(lane == 2, third, 0.0))
-    )
-
-    def to_tiles(value):
-        value = value.astype(jnp.bfloat16).reshape(rank // 8, 8, columns // lanes, lanes)
-        return value.transpose(0, 2, 1, 3).reshape(tiles, 8, lanes)
+    cross = [(place, 3 - place) for place in range(4)]
+    bundle = local_kernel(
+        bundle_kernel,
+        jax.ShapeDtypeStruct((experts, 24, lanes), jnp.bfloat16),
+        back,
+        swap(back, "c"),
+        swap(back, "yh"),
+        lax.ppermute(back, MP, cross),
+        normed,
+        up_part,
+        loss_here,
+        scratch=[pltpu.VMEM((rank, columns), jnp.float32)],
+    )
 
     def from_tiles(value):
         value = value.reshape(rank // 8, columns // lanes, 8, lanes).transpose(0, 2, 1, 3)
         return value.reshape(rank, columns).astype(jnp.float32)
 
-    bundle = jnp.concatenate([to_tiles(up_part), to_tiles(down_part)])
-    bundle = jnp.concatenate(
-        [
-            bundle[: 2 * experts].reshape(experts, 16, lanes),
-            bundle[2 * experts :].reshape(experts, 4, lanes),
-            jnp.broadcast_to(loss_row.astype(jnp.bfloat16), (experts, 4, lanes)),
-        ],
-        axis=1,
-    )
     bundle = lax.all_to_all(bundle, DP, split_axis=0, concat_axis=0, tiled=True)
     summed = jnp.sum(bundle.astype(jnp.float32), axis=0)
     grads = jnp.broadcast_to(summed.astype(jnp.bfloat16), (experts, 24, lanes))

time: 219 us -> 219 us (level)
  waiting for transfers between devices: 76.5 us -> 80.7 us
  between operations: 20 us -> 16.3 us
  other arithmetic: 6.61 us -> 4.23 us
    ppermute x2 -> x3, waiting for transfers between devices: 7.8 us -> 10.2 us  [the longest x2 7.8 us: body(): lax.ppermute(piece, ALL, permutation(home_target(step)))]
    ppermute x2 -> x3, starting transfers between devices: 6.11 us -> 6.68 us  [the longest x2 6.12 us: body(): lax.ppermute(piece, ALL, permutation(home_target(step)))]
  transfers between devices with their start and end apart: 25 -> 26, of which waited for: 16 -> 17; matrix products, arithmetic and copies ran while one was open for 8% -> 7% of each run, Pallas kernels for 0% -> 0%
where the time goes in v10:
time: 219 us; the launch traced here: 218 us
  waiting for transfers between devices  80.7 us (37%)
  starting transfers between devices  65.3 us (30%)
  blocking collectives  24.3 us (11%)
  between operations  16.3 us (7%)
  matrix products  11.6 us (5%)
  local copies, waits for them, and re-layouts  9.8 us (4%)
  Pallas kernels  6.05 us (3%)
  other arithmetic  4.23 us (2%)
    ppermute x17, waiting for transfers between devices, swap(): return lax.ppermute(value, axis, [(0, 1), (1, 0)])  40 us
    ppermute x17, starting transfers between devices, swap(): return lax.ppermute(value, axis, [(0, 1), (1, 0)])  30 us
    all_to_all x1, blocking collectives, body(): bundle = lax.all_to_all(bundle, DP, split_axis=0, concat_axis=0, tiled=True)  24.3 us
    all_to_all x2, waiting for transfers between devices, exchange_slots(): lax.all_to_all(rows, DP, split_axis=0, concat_axis=0, tiled=True)  21.8 us
    all_to_all x2, starting transfers between devices, exchange_slots(): lax.all_to_all(rows, DP, split_axis=0, concat_axis=0, tiled=True)  21.1 us
    dot_general x13, matrix products, dot(): return jnp.dot(a, b, preferred_element_type=jnp.float32)  10.6 us
    ppermute x2, waiting for transfers between devices, body(): lax.ppermute(piece, ALL, permutation(home_target(step)))  7.8 us
    all_to_all x1, waiting for transfers between devices, body(): grads = lax.all_to_all(grads, DP, split_axis=0, concat_axis=0, tiled=True)  7.8 us
  transfers between devices with their start and end apart: 26, of which 17 were waited for; matrix products, arithmetic and copies ran while one was open for 7% of the time, Pallas kernels for 0%

profile of v10, /device:TPU:32, one launch (start us, length us, event | category | flops | bytes accessed | tf_op | source)
XLA Modules:
  0.0 218.3 jit_solution(12317875419782011006)
XLA Ops:
  7.2 0.9 copy.15
  8.4 0.6 reduce-window.6
  9.3 0.6 convolution_convert_fusion.4
  9.9 1.4 reshape.124
  11.3 12.6 %all-to-all-start = ((bf16[64,35,128]{2,1,0:T(8,128)(2,1)}), bf16[64,35,128]{2,1,0:T(8,128)(2,1)S(1)}, u32[]{:S(2)}, u32[]{:S(2)}) async-start(bf16[64,35,128]{2,1,0:T(8,128)(2,1)} %reshape.124), calls=%async_computation | async-start | bytes 1310720 | tf_op jit(solution)/shard_map/all_to_all | solution.py:56
  24.0 0.7 collective-permute-start
  24.7 11.9 %collective-permute-start.1 = (bf16[56,1280]{1,0:T(8,128)(2,1)S(1)}, bf16[56,1280]{1,0:T(8,128)(2,1)S(1)}, u32[]{:S(2)}, u32[]{:S(2)}) collective-permute-start(bf16[56,1280]{1,0:T(8,128)(2,1)S(1)} %collective-permute-done), channel_id=1, source_target_pairs={{0,128},{128,0},{1,129},{129,1},{2,130},{130,2},{3,131},{131,3},{4... | collective-permute-start | bytes 430088 | tf_op jit(solution)/shard_map/ppermute | solution.py:34
  36.6 4.2 %collective-permute-done.1 = bf16[56,1280]{1,0:T(8,128)(2,1)S(1)} collective-permute-done((bf16[56,1280]{1,0:T(8,128)(2,1)S(1)}, bf16[56,1280]{1,0:T(8,128)(2,1)S(1)}, u32[]{:S(2)}, u32[]{:S(2)}) %collective-permute-start.1) | collective-permute-done | bytes 143392 | tf_op jit(solution)/shard_map/ppermute | solution.py:34
  40.9 4.0 %all-to-all-done = bf16[64,35,128]{2,1,0:T(8,128)(2,1)S(1)} async-done(((bf16[64,35,128]{2,1,0:T(8,128)(2,1)}), bf16[64,35,128]{2,1,0:T(8,128)(2,1)S(1)}, u32[]{:S(2)}, u32[]{:S(2)}) %all-to-all-start) | async-done | bytes 573472 | tf_op jit(solution)/shard_map/all_to_all | solution.py:56
  44.9 0.6 reshape.125
  45.5 3.0 %collective-permute-start.3 = (bf16[320,896]{1,0:T(8,128)(2,1)S(1)}, bf16[320,896]{1,0:T(8,128)(2,1)S(1)}, u32[]{:S(2)}, u32[]{:S(2)}) collective-permute-start(bf16[320,896]{1,0:T(8,128)(2,1)S(1)} %reshape.125), channel_id=1, source_target_pairs={{0,2},{2,0},{1,3},{3,1},{4,6},{6,4},{5,7},{7,5},{8,10},{10,8},{9,1... | collective-permute-start | bytes 1720328 | tf_op jit(solution)/shard_map/ppermute | solution.py:34
  48.5 1.9 collective-permute-start.4
  50.8 1.2 collective-permute-done.5
  52.1 4.6 %collective-permute-done.4 = bf16[112,1280]{1,0:T(8,128)(2,1)S(1)} collective-permute-done((bf16[112,1280]{1,0:T(8,128)(2,1)S(1)}, bf16[112,1280]{1,0:T(8,128)(2,1)S(1)}, u32[]{:S(2)}, u32[]{:S(2)}) %collective-permute-start.4) | collective-permute-done | bytes 286752 | tf_op jit(solution)/shard_map/ppermute | solution.py:34
  56.6 0.9 maximum_select_fusion
  57.5 1.9 collective-permute-done.3
  59.6 1.8 fusion.20
  61.4 0.5 collective-permute-start.6
  62.0 1.7 fusion.14
  63.7 0.5 convolution_add_fusion.3
  64.2 2.0 convolution_add_fusion.1
  66.2 0.5 fusion.16
  66.7 0.5 fusion.10
  67.2 0.5 fusion.3
  67.7 0.6 multiply_convert_fusion
  68.3 0.9 copy-done.6
  69.2 0.5 convolution_convert_fusion
  69.9 0.5 convolution_convert_fusion.2
  70.4 0.5 collective-permute-start.7
  70.9 0.9 collective-permute-done.8
  71.8 0.5 add_convert_fusion.1
  72.3 3.2 %collective-permute-start.9 = (bf16[320,896]{1,0:T(8,128)(2,1)S(1)}, bf16[320,896]{1,0:T(8,128)(2,1)S(1)}, u32[]{:S(2)}, u32[]{:S(2)}) collective-permute-start(bf16[320,896]{1,0:T(8,128)(2,1)S(1)} %add_convert_fusion.1), channel_id=1, source_target_pairs={{0,2},{2,0},{1,3},{3,1},{4,6},{6,4},{5,7},{7,5},{8,10},{10,8},{9,1... | collective-permute-start | bytes 1720328 | tf_op jit(solution)/shard_map/ppermute | solution.py:34
  76.0 13.1 %collective-permute-done.9 = bf16[320,896]{1,0:T(8,128)(2,1)S(1)} collective-permute-done((bf16[320,896]{1,0:T(8,128)(2,1)S(1)}, bf16[320,896]{1,0:T(8,128)(2,1)S(1)}, u32[]{:S(2)}, u32[]{:S(2)}) %collective-permute-start.9) | collective-permute-done | bytes 573472 | tf_op jit(solution)/shard_map/ppermute | solution.py:34
  89.3 1.4 reshape.127
  90.7 8.5 %all-to-all-start.1 = ((bf16[64,35,128]{2,1,0:T(8,128)(2,1)}), bf16[64,35,128]{2,1,0:T(8,128)(2,1)S(1)}, u32[]{:S(2)}, u32[]{:S(2)}) async-start(bf16[64,35,128]{2,1,0:T(8,128)(2,1)} %reshape.127), calls=%async_computation.1 | async-start | bytes 1310720 | tf_op jit(solution)/shard_map/all_to_all | solution.py:56
  99.5 2.7 %collective-permute-start.10 = (f32[128,128]{1,0:T(8,128)S(1)}, f32[128,128]{1,0:T(8,128)S(1)}, u32[]{:S(2)}, u32[]{:S(2)}) collective-permute-start(f32[128,128]{1,0:T(8,128)S(1)} %add.100), channel_id=1, source_target_pairs={{0,2},{2,0},{1,3},{3,1},{4,6},{6,4},{5,7},{7,5},{8,10},{10,8},{9,1... | collective-permute-start | bytes 196616 | tf_op jit(solution)/shard_map/ppermute | solution.py:34
  102.6 3.5 %collective-permute-done.10 = f32[128,128]{1,0:T(8,128)S(1)} collective-permute-done((f32[128,128]{1,0:T(8,128)S(1)}, f32[128,128]{1,0:T(8,128)S(1)}, u32[]{:S(2)}, u32[]{:S(2)}) %collective-permute-start.10) | collective-permute-done | bytes 65568 | tf_op jit(solution)/shard_map/ppermute | solution.py:34
  106.5 17.8 %all-to-all-done.1 = bf16[64,35,128]{2,1,0:T(8,128)(2,1)S(1)} async-done(((bf16[64,35,128]{2,1,0:T(8,128)(2,1)}), bf16[64,35,128]{2,1,0:T(8,128)(2,1)S(1)}, u32[]{:S(2)}, u32[]{:S(2)}) %all-to-all-start.1) | async-done | bytes 573472 | tf_op jit(solution)/shard_map/all_to_all | solution.py:56
  124.3 0.6 reshape.128
  124.9 0.6 convolution_convert_fusion.5.own_ref
  125.5 1.3 collective-permute-start.12
  126.9 4.8 %collective-permute-done.12.pair_ref = bf16[128,896]{1,0:T(8,128)(2,1)S(1)} collective-permute-done((bf16[128,896]{1,0:T(8,128)(2,1)S(1)}, bf16[128,896]{1,0:T(8,128)(2,1)S(1)}, u32[]{:S(2)}, u32[]{:S(2)}) %collective-permute-start.12) | collective-permute-done | bytes 229408 | tf_op jit(solution)/shard_map/ppermute | solution.py:34
  131.7 1.4 collective-permute-done.13.pair_far_ref
  133.1 2.3 %copy-done.1 = bf16[1792,1280]{1,0:T(8,128)(2,1)S(1)} copy-done((bf16[1792,1280]{1,0:T(8,128)(2,1)S(1)}, bf16[1792,1280]{1,0:T(8,128)(2,1)}, u32[]{:S(2)}) %copy-start.1) | copy-done | bytes 4587544
  135.4 4.2 %shard_map.140 = (bf16[128,1280]{1,0:T(8,128)(2,1)S(1)}, bf16[128,1280]{1,0:T(8,128)(2,1)S(1)}) custom-call(s32[3]{0:T(128)S(1)} %pad_add_fusion.order_ref, bf16[128,896]{1,0:T(8,128)(2,1)S(1)} %convolution_convert_fusion.5.own_ref, bf16[128,896]{1,0:T(8,128)(2,1)S(1)} %collective-permute-done.11.own_far_ref, ...), custom_call_target="tpu_custom_call" | custom-call | flops 1174405120 | bytes 6000000 | tf_op jit(solution)/shard_map/pallas_call | solution.py:93
  139.7 0.7 collective-permute-start.14
  140.4 5.4 %collective-permute-start.15 = (bf16[128,1280]{1,0:T(8,128)(2,1)S(1)}, bf16[128,1280]{1,0:T(8,128)(2,1)S(1)}, u32[]{:S(2)}, u32[]{:S(2)}) collective-permute-start(bf16[128,1280]{1,0:T(8,128)(2,1)S(1)} %get-tuple-element.36), channel_id=1, source_target_pairs={{0,4},{1,5},{2,0},{3,1},{4,6},{5,7},{6,2},{7,3},{8,12},{9,13},{10,... | collective-permute-start | bytes 983048 | tf_op jit(solution)/shard_map/ppermute | solution.py:335
  145.8 7.8 %collective-permute-done.15.second_ref = bf16[128,1280]{1,0:T(8,128)(2,1)S(1)} collective-permute-done((bf16[128,1280]{1,0:T(8,128)(2,1)S(1)}, bf16[128,1280]{1,0:T(8,128)(2,1)S(1)}, u32[]{:S(2)}, u32[]{:S(2)}) %collective-permute-start.15) | collective-permute-done | bytes 327712 | tf_op jit(solution)/shard_map/ppermute | solution.py:335
  153.6 1.0 shard_map.141
  154.6 2.8 %collective-permute-start.17 = (f32[128,64]{1,0:T(8,128)S(1)}, f32[128,64]{1,0:T(8,128)S(1)}, u32[]{:S(2)}, u32[]{:S(2)}) collective-permute-start(f32[128,64]{1,0:T(8,128)S(1)} %get-tuple-element.40.own_ref), channel_id=1, source_target_pairs={{0,2},{2,0},{1,3},{3,1},{4,6},{6,4},{5,7},{7,5},{8,10},{10,8},{9,1... | collective-permute-start | bytes 98312 | tf_op jit(solution)/shard_map/ppermute | solution.py:34
  157.4 0.6 collective-permute-start.18
  158.0 2.6 %collective-permute-done.17.far_ref = f32[128,64]{1,0:T(8,128)S(1)} collective-permute-done((f32[128,64]{1,0:T(8,128)S(1)}, f32[128,64]{1,0:T(8,128)S(1)}, u32[]{:S(2)}, u32[]{:S(2)}) %collective-permute-start.17) | collective-permute-done | bytes 32800 | tf_op jit(solution)/shard_map/ppermute | solution.py:34
  160.6 2.4 %collective-permute-done.18.cross_ref = f32[128,64]{1,0:T(8,128)S(1)} collective-permute-done((f32[128,64]{1,0:T(8,128)S(1)}, f32[128,64]{1,0:T(8,128)S(1)}, u32[]{:S(2)}, u32[]{:S(2)}) %collective-permute-start.18) | collective-permute-done | bytes 32800 | tf_op jit(solution)/shard_map/ppermute | solution.py:363
  163.2 24.3 %all_to_all.20 = bf16[64,24,128]{2,1,0:T(8,128)(2,1)S(1)} all-to-all(bf16[64,24,128]{2,1,0:T(8,128)(2,1)S(1)} %shard_map.142), channel_id=1, replica_groups=mesh['yl'=2,'z'=8,'xh'=2,'xl'=2,'yh'=2,'c'=2] {'yl','z','xh','xl'}, dimensions={0} | all-to-all | bytes 786432 | tf_op jit(solution)/shard_map/all_to_all | solution.py:374
  187.7 0.8 broadcast_in_dim.2
  188.4 5.1 %all-to-all-start.3 = ((bf16[64,24,128]{2,1,0:T(8,128)(2,1)}), bf16[64,24,128]{2,1,0:T(8,128)(2,1)S(1)}, u32[]{:S(2)}, u32[]{:S(2)}) async-start(bf16[64,24,128]{2,1,0:T(8,128)(2,1)} %broadcast_in_dim.2), calls=%async_computation.3 | async-start | bytes 786432 | tf_op jit(solution)/shard_map/all_to_all | solution.py:377
  193.7 1.6 collective-permute-start.20
  195.3 1.8 collective-permute-start.21
  197.0 1.8 collective-permute-done.20
  198.8 0.9 collective-permute-done.21
  199.7 0.6 add_reduce_fusion
  201.0 7.8 %all-to-all-done.3 = bf16[64,24,128]{2,1,0:T(8,128)(2,1)S(1)} async-done(((bf16[64,24,128]{2,1,0:T(8,128)(2,1)}), bf16[64,24,128]{2,1,0:T(8,128)(2,1)S(1)}, u32[]{:S(2)}, u32[]{:S(2)}) %all-to-all-start.3) | async-done | bytes 393248 | tf_op jit(solution)/shard_map/all_to_all | solution.py:377
  208.9 0.7 convert_bitcast_fusion.1
  209.6 0.7 convert_bitcast_fusion
  (68 shorter events, 3.6 us)
Async XLA Ops:
  7.2 2.2 copy-start
  7.2 16.8 %copy-start.10 = (bf16[56,1280]{1,0:T(8,128)(2,1)S(1)}, bf16[56,1280]{1,0:T(8,128)(2,1)}, u32[]{:S(2)}) copy-start(bf16[56,1280]{1,0:T(8,128)(2,1)} %param.17) | copy-start | bytes 430084
  7.2 43.3 %copy-start.8 = (bf16[1280]{0:T(1024)(128)(2,1)S(1)}, bf16[1280]{0:T(1024)(128)(2,1)}, u32[]{:S(2)}) copy-start(bf16[1280]{0:T(1024)(128)(2,1)} %param.19) | copy-start | bytes 7684
  7.2 43.3 %copy-start.4 = (bf16[1280,64]{0,1:T(8,128)(2,1)S(1)}, bf16[1280,64]{0,1:T(8,128)(2,1)}, u32[]{:S(2)}) copy-start(bf16[1280,64]{0,1:T(8,128)(2,1)} %param.20) | copy-start | bytes 491524
  7.2 43.3 %copy-start.2 = (bf16[128,1280]{1,0:T(8,128)(2,1)S(1)}, bf16[128,1280]{1,0:T(8,128)(2,1)}, u32[]{:S(2)}) copy-start(bf16[128,1280]{1,0:T(8,128)(2,1)} %student_ref.3) | copy-start | bytes 983044
  11.3 33.6 %all-to-all-start = ((bf16[64,35,128]{2,1,0:T(8,128)(2,1)}), bf16[64,35,128]{2,1,0:T(8,128)(2,1)S(1)}, u32[]{:S(2)}, u32[]{:S(2)}) async-start(bf16[64,35,128]{2,1,0:T(8,128)(2,1)} %reshape.124), calls=%async_computation | async-start | bytes 1310720 | tf_op jit(solution)/shard_map/all_to_all | solution.py:56
  24.0 109.2 %all-gather.2.cloned.1.call-start = ((), (), s32[]{:S(2)}) async-start(), calls=%async_computation.4 | async-start | bytes 5160960 | tf_op jit(solution)/shard_map/all_gather | solution.py:261
  24.0 0.7 collective-permute-start
  24.7 16.1 %collective-permute-start.1 = (bf16[56,1280]{1,0:T(8,128)(2,1)S(1)}, bf16[56,1280]{1,0:T(8,128)(2,1)S(1)}, u32[]{:S(2)}, u32[]{:S(2)}) collective-permute-start(bf16[56,1280]{1,0:T(8,128)(2,1)S(1)} %collective-permute-done), channel_id=1, source_target_pairs={{0,128},{128,0},{1,129},{129,1},{2,130},{130,2},{3,131},{131,3},{4... | collective-permute-start | bytes 430088 | tf_op jit(solution)/shard_map/ppermute | solution.py:34
  45.5 13.9 %collective-permute-start.3 = (bf16[320,896]{1,0:T(8,128)(2,1)S(1)}, bf16[320,896]{1,0:T(8,128)(2,1)S(1)}, u32[]{:S(2)}, u32[]{:S(2)}) collective-permute-start(bf16[320,896]{1,0:T(8,128)(2,1)S(1)} %reshape.125), channel_id=1, source_target_pairs={{0,2},{2,0},{1,3},{3,1},{4,6},{6,4},{5,7},{7,5},{8,10},{10,8},{9,1... | collective-permute-start | bytes 1720328 | tf_op jit(solution)/shard_map/ppermute | solution.py:34
  48.5 8.1 %collective-permute-start.4 = (bf16[112,1280]{1,0:T(8,128)(2,1)S(1)}, bf16[112,1280]{1,0:T(8,128)(2,1)S(1)}, u32[]{:S(2)}, u32[]{:S(2)}) collective-permute-start(bf16[112,1280]{1,0:T(8,128)(2,1)S(1)} %maximum_select_fusion.1), channel_id=1, source_target_pairs={{0,8},{8,0},{1,9},{9,1},{2,10},{10,2},{3,11},{11,3},{4,12},{12,4},... | collective-permute-start | bytes 860168 | tf_op jit(solution)/shard_map/ppermute | solution.py:34
  50.7 1.3 collective-permute-start.5
  59.4 4.2 %collective-permute-start.2 = (bf16[320,896]{1,0:T(8,128)(2,1)S(1)}, bf16[320,896]{1,0:T(8,128)(2,1)S(1)}, u32[]{:S(2)}, u32[]{:S(2)}) collective-permute-start(bf16[320,896]{1,0:T(8,128)(2,1)S(1)} %reshape.125), channel_id=1, source_target_pairs={{0,1},{1,0},{2,3},{3,2},{4,5},{5,4},{6,7},{7,6},{8,9},{9,8},{10,11... | collective-permute-start | bytes 1720328 | tf_op jit(solution)/shard_map/ppermute | solution.py:34
  59.6 4.1 %copy-start.5 = (bf16[1,3584,512]{2,1,0:T(8,128)(2,1)S(1)}, bf16[1,3584,512]{2,1,0:T(8,128)(2,1)}, u32[]{:S(2)}) copy-start(bf16[1,3584,512]{2,1,0:T(8,128)(2,1)} %param.14) | copy-start | bytes 11010052
  61.4 4.7 %collective-permute-start.6 = (bf16[320,896]{1,0:T(8,128)(2,1)S(1)}, bf16[320,896]{1,0:T(8,128)(2,1)S(1)}, u32[]{:S(2)}, u32[]{:S(2)}) collective-permute-start(bf16[320,896]{1,0:T(8,128)(2,1)S(1)} %collective-permute-done.3), channel_id=1, source_target_pairs={{0,1},{1,0},{2,3},{3,2},{4,5},{5,4},{6,7},{7,6},{8,9},{9,8},{10,11... | collective-permute-start | bytes 1720328 | tf_op jit(solution)/shard_map/ppermute | solution.py:34
  63.6 3.0 %copy-start.7 = (bf16[1,3584,512]{2,1,0:T(8,128)(2,1)S(1)}, bf16[1,3584,512]{2,1,0:T(8,128)(2,1)}, u32[]{:S(2)}) copy-start(bf16[1,3584,512]{2,1,0:T(8,128)(2,1)} %param.15) | copy-start | bytes 11010052
  67.2 2.0 copy-start.6
  69.7 2.1 collective-permute-start.8
  70.4 5.6 %collective-permute-start.7 = (bf16[320,896]{1,0:T(8,128)(2,1)S(1)}, bf16[320,896]{1,0:T(8,128)(2,1)S(1)}, u32[]{:S(2)}, u32[]{:S(2)}) collective-permute-start(bf16[320,896]{1,0:T(8,128)(2,1)S(1)} %convolution_convert_fusion.2), channel_id=1, source_target_pairs={{0,1},{1,0},{2,3},{3,2},{4,5},{5,4},{6,7},{7,6},{8,9},{9,8},{10,11... | collective-permute-start | bytes 1720328 | tf_op jit(solution)/shard_map/ppermute | solution.py:34
  72.3 26.9 %copy-start.9 = (f32[128,2]{0,1:T(2,128)S(1)}, f32[128,2]{0,1:T(2,128)}, u32[]{:S(2)}) copy-start(f32[128,2]{0,1:T(2,128)} %param.13) | copy-start | bytes 3076
  72.3 33.8 %copy-start.3 = (bf16[64,1280]{1,0:T(8,128)(2,1)S(1)}, bf16[64,1280]{1,0:T(8,128)(2,1)}, u32[]{:S(2)}) copy-start(bf16[64,1280]{1,0:T(8,128)(2,1)} %up_ref.3) | copy-start | bytes 491524
  72.3 16.8 %collective-permute-start.9 = (bf16[320,896]{1,0:T(8,128)(2,1)S(1)}, bf16[320,896]{1,0:T(8,128)(2,1)S(1)}, u32[]{:S(2)}, u32[]{:S(2)}) collective-permute-start(bf16[320,896]{1,0:T(8,128)(2,1)S(1)} %add_convert_fusion.1), channel_id=1, source_target_pairs={{0,2},{2,0},{1,3},{3,1},{4,6},{6,4},{5,7},{7,5},{8,10},{10,8},{9,1... | collective-permute-start | bytes 1720328 | tf_op jit(solution)/shard_map/ppermute | solution.py:34
  90.7 33.6 %all-to-all-start.1 = ((bf16[64,35,128]{2,1,0:T(8,128)(2,1)}), bf16[64,35,128]{2,1,0:T(8,128)(2,1)S(1)}, u32[]{:S(2)}, u32[]{:S(2)}) async-start(bf16[64,35,128]{2,1,0:T(8,128)(2,1)} %reshape.127), calls=%async_computation.1 | async-start | bytes 1310720 | tf_op jit(solution)/shard_map/all_to_all | solution.py:56
  99.5 6.6 %collective-permute-start.10 = (f32[128,128]{1,0:T(8,128)S(1)}, f32[128,128]{1,0:T(8,128)S(1)}, u32[]{:S(2)}, u32[]{:S(2)}) collective-permute-start(f32[128,128]{1,0:T(8,128)S(1)} %add.100), channel_id=1, source_target_pairs={{0,2},{2,0},{1,3},{3,1},{4,6},{6,4},{5,7},{7,5},{8,10},{10,8},{9,1... | collective-permute-start | bytes 196616 | tf_op jit(solution)/shard_map/ppermute | solution.py:34
  125.5 6.1 %collective-permute-start.12 = (bf16[128,896]{1,0:T(8,128)(2,1)S(1)}, bf16[128,896]{1,0:T(8,128)(2,1)S(1)}, u32[]{:S(2)}, u32[]{:S(2)}) collective-permute-start(bf16[128,896]{1,0:T(8,128)(2,1)S(1)} %convolution_convert_fusion.5.own_ref), channel_id=1, source_target_pairs={{0,4},{4,0},{1,5},{5,1},{2,6},{6,2},{3,7},{7,3},{8,12},{12,8},{9,1... | collective-permute-start | bytes 688136 | tf_op jit(solution)/shard_map/ppermute | solution.py:34
  126.9 4.9 %collective-permute-start.11 = (bf16[128,896]{1,0:T(8,128)(2,1)S(1)}, bf16[128,896]{1,0:T(8,128)(2,1)S(1)}, u32[]{:S(2)}, u32[]{:S(2)}) collective-permute-start(bf16[128,896]{1,0:T(8,128)(2,1)S(1)} %convolution_convert_fusion.5.own_ref), channel_id=1, source_target_pairs={{0,1},{1,0},{2,3},{3,2},{4,5},{5,4},{6,7},{7,6},{8,9},{9,8},{10,11... | collective-permute-start | bytes 688136 | tf_op jit(solution)/shard_map/ppermute | solution.py:34
  131.6 1.5 collective-permute-start.13
  133.1 2.3 %copy-start.1 = (bf16[1792,1280]{1,0:T(8,128)(2,1)S(1)}, bf16[1792,1280]{1,0:T(8,128)(2,1)}, u32[]{:S(2)}) copy-start(bf16[1792,1280]{1,0:T(8,128)(2,1)} %all-gather.2.cloned.1.call-done.block_ref) | copy-start | bytes 13762564
  139.7 6.1 %collective-permute-start.14 = (bf16[128,1280]{1,0:T(8,128)(2,1)S(1)}, bf16[128,1280]{1,0:T(8,128)(2,1)S(1)}, u32[]{:S(2)}, u32[]{:S(2)}) collective-permute-start(bf16[128,1280]{1,0:T(8,128)(2,1)S(1)} %get-tuple-element.35), channel_id=1, source_target_pairs={{0,0},{1,1},{2,4},{3,5},{4,2},{5,3},{6,6},{7,7},{8,8},{9,9},{10,12... | collective-permute-start | bytes 983048 | tf_op jit(solution)/shard_map/ppermute | solution.py:335
  140.4 13.2 %collective-permute-start.15 = (bf16[128,1280]{1,0:T(8,128)(2,1)S(1)}, bf16[128,1280]{1,0:T(8,128)(2,1)S(1)}, u32[]{:S(2)}, u32[]{:S(2)}) collective-permute-start(bf16[128,1280]{1,0:T(8,128)(2,1)S(1)} %get-tuple-element.36), channel_id=1, source_target_pairs={{0,4},{1,5},{2,0},{3,1},{4,6},{5,7},{6,2},{7,3},{8,12},{9,13},{10,... | collective-permute-start | bytes 983048 | tf_op jit(solution)/shard_map/ppermute | solution.py:335
  154.6 3.4 %collective-permute-start.16 = (f32[128,64]{1,0:T(8,128)S(1)}, f32[128,64]{1,0:T(8,128)S(1)}, u32[]{:S(2)}, u32[]{:S(2)}) collective-permute-start(f32[128,64]{1,0:T(8,128)S(1)} %get-tuple-element.40.own_ref), channel_id=1, source_target_pairs={{0,1},{1,0},{2,3},{3,2},{4,5},{5,4},{6,7},{7,6},{8,9},{9,8},{10,11... | collective-permute-start | bytes 98312 | tf_op jit(solution)/shard_map/ppermute | solution.py:34
  154.6 6.0 %collective-permute-start.17 = (f32[128,64]{1,0:T(8,128)S(1)}, f32[128,64]{1,0:T(8,128)S(1)}, u32[]{:S(2)}, u32[]{:S(2)}) collective-permute-start(f32[128,64]{1,0:T(8,128)S(1)} %get-tuple-element.40.own_ref), channel_id=1, source_target_pairs={{0,2},{2,0},{1,3},{3,1},{4,6},{6,4},{5,7},{7,5},{8,10},{10,8},{9,1... | collective-permute-start | bytes 98312 | tf_op jit(solution)/shard_map/ppermute | solution.py:34
  157.4 5.6 %collective-permute-start.18 = (f32[128,64]{1,0:T(8,128)S(1)}, f32[128,64]{1,0:T(8,128)S(1)}, u32[]{:S(2)}, u32[]{:S(2)}) collective-permute-start(f32[128,64]{1,0:T(8,128)S(1)} %get-tuple-element.40.own_ref), channel_id=1, source_target_pairs={{0,3},{1,2},{2,1},{3,0},{4,7},{5,6},{6,5},{7,4},{8,11},{9,10},{10,... | collective-permute-start | bytes 98312 | tf_op jit(solution)/shard_map/ppermute | solution.py:363
  188.4 20.3 %all-to-all-start.3 = ((bf16[64,24,128]{2,1,0:T(8,128)(2,1)}), bf16[64,24,128]{2,1,0:T(8,128)(2,1)S(1)}, u32[]{:S(2)}, u32[]{:S(2)}) async-start(bf16[64,24,128]{2,1,0:T(8,128)(2,1)} %broadcast_in_dim.2), calls=%async_computation.3 | async-start | bytes 786432 | tf_op jit(solution)/shard_map/all_to_all | solution.py:377
  193.6 3.5 %collective-permute-start.19 = (f32[1,128]{1,0:T(1,128)S(1)}, f32[1,128]{1,0:T(1,128)S(1)}, u32[]{:S(2)}, u32[]{:S(2)}) collective-permute-start(f32[1,128]{1,0:T(1,128)S(1)} %slice.34), channel_id=1, source_target_pairs={{0,1},{1,0},{2,3},{3,2},{4,5},{5,4},{6,7},{7,6},{8,9},{9,8},{10,11... | collective-permute-start | bytes 1544 | tf_op jit(solution)/shard_map/ppermute | solution.py:34
  193.7 5.1 %collective-permute-start.20 = (f32[1,128]{1,0:T(1,128)S(1)}, f32[1,128]{1,0:T(1,128)S(1)}, u32[]{:S(2)}, u32[]{:S(2)}) collective-permute-start(f32[1,128]{1,0:T(1,128)S(1)} %slice.34), channel_id=1, source_target_pairs={{0,2},{2,0},{1,3},{3,1},{4,6},{6,4},{5,7},{7,5},{8,10},{10,8},{9,1... | collective-permute-start | bytes 1544 | tf_op jit(solution)/shard_map/ppermute | solution.py:34
  195.3 4.5 %collective-permute-start.21 = (f32[1,128]{1,0:T(1,128)S(1)}, f32[1,128]{1,0:T(1,128)S(1)}, u32[]{:S(2)}, u32[]{:S(2)}) collective-permute-start(f32[1,128]{1,0:T(1,128)S(1)} %slice.34), channel_id=1, source_target_pairs={{0,3},{1,2},{2,1},{3,0},{4,7},{5,6},{6,5},{7,4},{8,11},{9,10},{10,... | collective-permute-start | bytes 1544 | tf_op jit(solution)/shard_map/ppermute | solution.py:381
Sparse Core Ops, SparseCore 0:
  59.6 69.6 all-gather.1
